TPU v7x, 128 devices: a whole 4x4x4 slice. The times are simulated.
128 devices in a mesh: win: 4 (over x), wide: 32 (over y, z, core).
Axes of the slice: x: 4, y: 4, z: 4, core: 2. Of those that a mesh axis runs over, the one named last changes fastest.
Arguments:
- block_input: bfloat16 [4, 128, 32, 768], P('win', None, 'wide'), may hold values from -6 to 6
- file_lengths: int32 [4, 8], P('win'), may hold values from 0 to 4096, as said below
- file_splits: int32 [4, 8, 2], P('win'), may hold values from 0 to 1024
- ln1_gain: bfloat16 [768], replicated, may hold values from 0.099609375 to 1.8984375
- ln1_bias: bfloat16 [768], replicated, may hold values from -1.25 to 1.25
- w_query: bfloat16 [768, 768], replicated, may hold values from -0.5 to 0.5
- b_query: bfloat16 [768], replicated, may hold values from -1.5 to 1.5
- w_kv: bfloat16 [768, 128], replicated, may hold values from -0.21875 to 0.21875
- b_value: bfloat16 [64], replicated, may hold values from -0.625 to 0.625
- w_out: bfloat16 [768, 768], replicated, may hold values from -0.4375 to 0.4375
- b_out: bfloat16 [768], replicated, may hold values from -0.625 to 0.625
- ln2_gain: bfloat16 [768], replicated, may hold values from 0.099609375 to 1.8984375
- ln2_bias: bfloat16 [768], replicated, may hold values from -1.25 to 1.25
- w_up: bfloat16 [768, 3072], replicated, may hold values from -0.21875 to 0.21875
- b_up: bfloat16 [3072], replicated, may hold values from -1.25 to 1.25
- w_down: bfloat16 [3072, 768], replicated, may hold values from -0.109375 to 0.109375
- b_down: bfloat16 [768], replicated, may hold values from -0.625 to 0.625
- out_cotangent: bfloat16 [4, 128, 32, 768], P('win', None, 'wide'), may hold values from -6 to 6
Outputs:
- block_output: bfloat16 [4, 128, 32, 768], P('win', None, 'wide')
- grad_in: float32 [4, 128, 32, 768], P('win', None, 'wide')
- grad_ln1_gain: float32 [768], replicated
- grad_ln1_bias: float32 [768], replicated
- grad_w_query: float32 [768, 768], replicated
- grad_b_query: float32 [768], replicated
- grad_w_kv: float32 [768, 128], replicated
- grad_b_value: float32 [64], replicated
- grad_w_out: float32 [768, 768], replicated
- grad_b_out: float32 [768], replicated
- grad_ln2_gain: float32 [768], replicated
- grad_ln2_bias: float32 [768], replicated
- grad_w_up: float32 [768, 3072], replicated
- grad_b_up: float32 [3072], replicated
- grad_w_down: float32 [3072, 768], replicated
- grad_b_down: float32 [768], replicated
Inputs may be any that keep to these rules, and one draw needn't show every extreme that they name: `file_lengths`: in each window the lengths add up to 4096; the nonzero ones, two to 8 of them, come first.
All inputs are finite; a program needn't handle non-finite values.
Results may differ from a plain program's by a relative error of at most 0.018.
Values may be sent and summed in bfloat16 or wider, within the bound.
No kernel may reach another device: no remote copies, remote signals or barrier semaphores. Data moves between devices by JAX's collectives and lax.ppermute only.
A program may use at most 192 MiB of HBM per device.

v0:
```python
import jax
import jax.numpy as jnp
from jax import lax
from jax.sharding import PartitionSpec as P

epsilon = 1e-05
masked_score = -1e30


def laid_out(pieces, dim):
    shape = list(pieces.shape[1:])
    shape[dim] *= pieces.shape[0]
    return jnp.moveaxis(pieces, 0, dim).reshape(shape)


def from_everyone(x, axis):
    copies = jnp.broadcast_to(x, (lax.axis_size(axis), *x.shape))
    return lax.all_to_all(copies, axis, split_axis=0, concat_axis=0, tiled=True)


def gathered_copies(x, axis, dim):
    return laid_out(from_everyone(x, axis), dim)


def split_up(x, dim, count):
    shape = x.shape
    pieces = x.reshape(*shape[:dim], count, shape[dim] // count, *shape[dim + 1 :])
    return jnp.moveaxis(pieces, dim, 0)


def summed_on_arrival(x, axis, dim):
    count = lax.axis_size(axis)
    pieces = lax.all_to_all(split_up(x, dim, count), axis, 0, 0, tiled=True)
    return jnp.sum(pieces.astype(jnp.float32), axis=0)


def norm_rows(values, gain_vec, shift_vec):
    row_mean = jnp.mean(values, axis=-1, keepdims=True)
    centered = values - row_mean
    variance = jnp.mean(centered * centered, axis=-1, keepdims=True)
    return centered * lax.rsqrt(variance + epsilon) * gain_vec + shift_vec


def gelu_tanh(values):
    return (
        0.5
        * values
        * (1.0 + jnp.tanh(0.7978845608028654 * (values + 0.044715 * values * values * values)))
    )


def file_positions(lengths, splits, total):
    files = lengths.shape[0]
    slot_index = jnp.arange(files, dtype=jnp.int32)
    is_live = lengths > 0
    live_len = jnp.where(is_live, lengths, 0)
    file_ends = jnp.cumsum(live_len, dtype=jnp.int32)
    file_starts = file_ends - live_len
    cut_first = lengths * jnp.minimum(splits[:, 0], splits[:, 1]) // 1024
    cut_second = lengths * jnp.maximum(splits[:, 0], splits[:, 1]) // 1024
    row_index = jnp.arange(total, dtype=jnp.int32)[:, None]
    inside = (
        is_live[None, :] & (row_index >= file_starts[None, :]) & (row_index < file_ends[None, :])
    )
    offset = row_index - file_starts[None, :]
    moved = jnp.where(
        offset < cut_first[None, :],
        offset,
        jnp.where(
            offset >= cut_second[None, :],
            cut_first[None, :] + offset - cut_second[None, :],
            cut_first[None, :]
            + lengths[None, :]
            - cut_second[None, :]
            + offset
            - cut_first[None, :],
        ),
    )
    hits_count = jnp.sum(inside.astype(jnp.int32), axis=1, dtype=jnp.int32)
    sequence_pos = jnp.sum(
        jnp.where(inside, file_starts[None, :] + moved, 0), axis=1, dtype=jnp.int32
    )
    owner_id = jnp.sum(jnp.where(inside, slot_index[None, :], 0), axis=1, dtype=jnp.int32)
    seqpos = jnp.where(hits_count > 0, sequence_pos, row_index[:, 0])
    fileid = jnp.where(hits_count > 0, owner_id, files)
    return (fileid, seqpos)


def contract_rows(left, right):
    return lax.dot_general(
        left, right, (((0,), (0,)), ((), ())), preferred_element_type=jnp.float32
    )


def contract_last(left, right):
    return lax.dot_general(
        left, right, (((1,), (1,)), ((), ())), preferred_element_type=jnp.float32
    )


def load_block(kv_full, fileid, seqpos, block_index, key_block):
    key_start = block_index * key_block
    kv_block = lax.dynamic_slice_in_dim(kv_full, key_start, key_block, 0)
    file_block = lax.dynamic_slice_in_dim(fileid, key_start, key_block, 0)
    order_block = lax.dynamic_slice_in_dim(seqpos, key_start, key_block, 0)
    return (kv_block, file_block, order_block)


def block_scores(queries, keys, file_rows, order_rows, file_block, order_block, score_scale):
    scores = contract_last(queries, keys) * score_scale
    allowed = (file_rows[:, None] == file_block[None, :]) & (
        order_block[None, :] <= order_rows[:, None]
    )
    return jnp.where(allowed, scores, masked_score)


def attend_forward(
    queries,
    kv_full,
    file_rows,
    order_rows,
    fileid,
    seqpos,
    lower_block,
    upper_block,
    key_block,
    head_dim,
):
    row_count = queries.shape[0]
    score_scale = head_dim ** (-0.5)

    def stats_step(block_index, state):
        row_max, row_total = state
        kv_block, file_block, order_block = load_block(
            kv_full, fileid, seqpos, block_index, key_block
        )
        scores = block_scores(
            queries,
            kv_block[:, :head_dim],
            file_rows,
            order_rows,
            file_block,
            order_block,
            score_scale,
        )
        new_max = jnp.maximum(row_max, jnp.max(scores, axis=1))
        row_total = row_total * jnp.exp(row_max - new_max) + jnp.sum(
            jnp.exp(scores - new_max[:, None]), axis=1
        )
        return (new_max, row_total)

    start_state = (
        jnp.full((row_count,), masked_score, jnp.float32),
        jnp.zeros((row_count,), jnp.float32),
    )
    row_max, row_total = lax.fori_loop(lower_block, upper_block, stats_step, start_state)
    lse = row_max + jnp.log(row_total)

    def value_step(block_index, accum):
        kv_block, file_block, order_block = load_block(
            kv_full, fileid, seqpos, block_index, key_block
        )
        scores = block_scores(
            queries,
            kv_block[:, :head_dim],
            file_rows,
            order_rows,
            file_block,
            order_block,
            score_scale,
        )
        probs = jnp.exp(scores - lse[:, None]).astype(jnp.bfloat16)
        return accum + jnp.dot(probs, kv_block[:, head_dim:], preferred_element_type=jnp.float32)

    accum = lax.fori_loop(
        lower_block, upper_block, value_step, jnp.zeros((row_count, head_dim), jnp.float32)
    )
    return (accum.astype(jnp.bfloat16), lse)


def attend_backward(
    queries,
    grad_rows,
    kv_full,
    file_rows,
    order_rows,
    fileid,
    seqpos,
    lse,
    lower_block,
    upper_block,
    key_block,
    head_dim,
):
    row_count = queries.shape[0]
    score_scale = head_dim ** (-0.5)

    def dot_step(block_index, row_dot):
        kv_block, file_block, order_block = load_block(
            kv_full, fileid, seqpos, block_index, key_block
        )
        scores = block_scores(
            queries,
            kv_block[:, :head_dim],
            file_rows,
            order_rows,
            file_block,
            order_block,
            score_scale,
        )
        probs = jnp.exp(scores - lse[:, None])
        grad_probs = contract_last(grad_rows, kv_block[:, head_dim:])
        return row_dot + jnp.sum(probs * grad_probs, axis=1)

    row_dot = lax.fori_loop(
        lower_block, upper_block, dot_step, jnp.zeros((row_count,), jnp.float32)
    )

    def grad_step(block_index, state):
        grad_query, grad_kv = state
        kv_block, file_block, order_block = load_block(
            kv_full, fileid, seqpos, block_index, key_block
        )
        scores = block_scores(
            queries,
            kv_block[:, :head_dim],
            file_rows,
            order_rows,
            file_block,
            order_block,
            score_scale,
        )
        probs = jnp.exp(scores - lse[:, None])
        grad_probs = contract_last(grad_rows, kv_block[:, head_dim:])
        grad_scores = (probs * (grad_probs - row_dot[:, None])).astype(jnp.bfloat16)
        grad_query = grad_query + jnp.dot(
            grad_scores, kv_block[:, :head_dim], preferred_element_type=jnp.float32
        )
        grad_keys = contract_rows(grad_scores, queries) * score_scale
        grad_values = contract_rows(probs.astype(jnp.bfloat16), grad_rows)
        increment = jnp.concatenate([grad_keys, grad_values], axis=1)
        key_start = block_index * key_block
        previous = lax.dynamic_slice_in_dim(grad_kv, key_start, key_block, 0)
        grad_kv = lax.dynamic_update_slice_in_dim(grad_kv, previous + increment, key_start, 0)
        return (grad_query, grad_kv)

    start_state = (
        jnp.zeros((row_count, head_dim), jnp.float32),
        jnp.zeros((kv_full.shape[0], 2 * head_dim), jnp.float32),
    )
    grad_query, grad_kv = lax.fori_loop(lower_block, upper_block, grad_step, start_state)
    return (grad_query * score_scale, grad_kv)


def body(
    block_input,
    file_lengths,
    file_splits,
    ln1_gain,
    ln1_bias,
    w_query,
    b_query,
    w_kv,
    b_value,
    w_out,
    b_out,
    ln2_gain,
    ln2_bias,
    w_up,
    b_up,
    w_down,
    b_down,
    out_cotangent,
):
    row_count = block_input.shape[1]
    model_width = block_input.shape[3]
    peer_count = lax.axis_size("wide")
    wide_index = lax.axis_index("wide")
    window = row_count * peer_count
    per_peer = row_count // peer_count
    key_block = min(512, window)
    head_dim = b_value.shape[0]
    head_count = model_width // head_dim
    fileid, seqpos = file_positions(file_lengths[0], file_splits[0], window)
    inputs = block_input[0, :, 0, :].astype(jnp.float32)
    normed_full, norm_one_back = jax.vjp(
        norm_rows, inputs, ln1_gain.astype(jnp.float32), ln1_bias.astype(jnp.float32)
    )
    normed_one = normed_full.astype(jnp.bfloat16)
    queries_rows = (
        jnp.dot(normed_one, w_query, preferred_element_type=jnp.float32)
        + b_query.astype(jnp.float32)
    ).astype(jnp.bfloat16)
    kv_shift = jnp.concatenate([jnp.zeros_like(b_value), b_value]).astype(jnp.float32)
    keyvals = (jnp.dot(normed_one, w_kv, preferred_element_type=jnp.float32) + kv_shift).astype(
        jnp.bfloat16
    )
    gathered = gathered_copies(keyvals.reshape(row_count, 1, 2 * head_dim), "wide", 1)
    kv_full = gathered.reshape(window, 2 * head_dim)
    moved = lax.all_to_all(
        queries_rows.reshape(peer_count, per_peer, 1, model_width),
        "wide",
        split_axis=0,
        concat_axis=2,
        tiled=True,
    )
    attn_query = moved.reshape(row_count, model_width)
    file_rows = lax.dynamic_slice_in_dim(fileid, wide_index * row_count, row_count, 0)
    order_rows = lax.dynamic_slice_in_dim(seqpos, wide_index * row_count, row_count, 0)
    key_first = jnp.sum((fileid < file_rows[0]).astype(jnp.int32), dtype=jnp.int32)
    key_end = jnp.sum((fileid <= file_rows[row_count - 1]).astype(jnp.int32), dtype=jnp.int32)
    lower_block = key_first // key_block
    upper_block = (key_end + key_block - 1) // key_block
    head_queries = attn_query.reshape(row_count * head_count, head_dim)
    head_files = jnp.repeat(file_rows, head_count)
    head_orders = jnp.repeat(order_rows, head_count)
    attn_heads, lse = attend_forward(
        head_queries,
        kv_full,
        head_files,
        head_orders,
        fileid,
        seqpos,
        lower_block,
        upper_block,
        key_block,
        head_dim,
    )
    attn_rows = attn_heads.reshape(row_count, model_width)
    attended = lax.all_to_all(
        attn_rows.reshape(1, per_peer, peer_count, model_width),
        "wide",
        split_axis=2,
        concat_axis=0,
        tiled=True,
    ).reshape(row_count, model_width)
    resid = (
        inputs
        + jnp.dot(attended, w_out, preferred_element_type=jnp.float32)
        + b_out.astype(jnp.float32)
    )
    normed_two_full, norm_two_back = jax.vjp(
        norm_rows, resid, ln2_gain.astype(jnp.float32), ln2_bias.astype(jnp.float32)
    )
    normed_two = normed_two_full.astype(jnp.bfloat16)
    pre_act = jnp.dot(normed_two, w_up, preferred_element_type=jnp.float32) + b_up.astype(
        jnp.float32
    )
    activ_full, gelu_back = jax.vjp(gelu_tanh, pre_act)
    activ = activ_full.astype(jnp.bfloat16)
    result = (
        resid
        + jnp.dot(activ, w_down, preferred_element_type=jnp.float32)
        + b_down.astype(jnp.float32)
    )
    block_output = result.astype(jnp.bfloat16).reshape(1, row_count, 1, model_width)
    grad_top = out_cotangent[0, :, 0, :]
    grad_top_full = grad_top.astype(jnp.float32)
    grad_w_down = contract_rows(activ, grad_top)
    grad_b_down = jnp.sum(grad_top_full, axis=0)
    grad_activ = contract_last(grad_top, w_down)
    grad_pre = gelu_back(grad_activ)[0].astype(jnp.bfloat16)
    grad_w_up = contract_rows(normed_two, grad_pre)
    grad_b_up = jnp.sum(grad_pre.astype(jnp.float32), axis=0)
    grad_normed_two = contract_last(grad_pre, w_up)
    grad_resid, grad_ln2_gain, grad_ln2_bias = norm_two_back(grad_normed_two)
    grad_resid = grad_resid + grad_top_full
    grad_branch = grad_resid.astype(jnp.bfloat16)
    grad_w_out = contract_rows(attended, grad_branch)
    grad_b_out = jnp.sum(grad_branch.astype(jnp.float32), axis=0)
    grad_att = contract_last(grad_branch, w_out).astype(jnp.bfloat16)
    grad_att_rows = lax.all_to_all(
        grad_att.reshape(peer_count, per_peer, 1, model_width),
        "wide",
        split_axis=0,
        concat_axis=2,
        tiled=True,
    ).reshape(row_count, model_width)
    grad_heads, grad_kv_part = attend_backward(
        head_queries,
        grad_att_rows.reshape(row_count * head_count, head_dim),
        kv_full,
        head_files,
        head_orders,
        fileid,
        seqpos,
        lse,
        lower_block,
        upper_block,
        key_block,
        head_dim,
    )
    grad_query_rows = grad_heads.reshape(row_count, model_width).astype(jnp.bfloat16)
    grad_queries = lax.all_to_all(
        grad_query_rows.reshape(1, per_peer, peer_count, model_width),
        "wide",
        split_axis=2,
        concat_axis=0,
        tiled=True,
    ).reshape(row_count, model_width)
    summed_kv = summed_on_arrival(
        grad_kv_part.reshape(row_count, peer_count, 2 * head_dim).astype(jnp.bfloat16), "wide", 1
    )
    grad_keyvals = summed_kv.reshape(row_count, 2 * head_dim).astype(jnp.bfloat16)
    grad_w_query = contract_rows(normed_one, grad_queries)
    grad_b_query = jnp.sum(grad_queries.astype(jnp.float32), axis=0)
    grad_w_kv = contract_rows(normed_one, grad_keyvals)
    grad_b_value = jnp.sum(grad_keyvals[:, head_dim:].astype(jnp.float32), axis=0)
    grad_normed_one = contract_last(grad_queries, w_query) + contract_last(grad_keyvals, w_kv)
    grad_inputs, grad_ln1_gain, grad_ln1_bias = norm_one_back(grad_normed_one)
    grad_in = (grad_inputs + grad_resid).reshape(1, row_count, 1, model_width)
    sums = lax.psum(
        (
            grad_ln1_gain,
            grad_ln1_bias,
            grad_w_query,
            grad_b_query,
            grad_w_kv,
            grad_b_value,
            grad_w_out,
            grad_b_out,
            grad_ln2_gain,
            grad_ln2_bias,
            grad_w_up,
            grad_b_up,
            grad_w_down,
            grad_b_down,
        ),
        ("win", "wide"),
    )
    return (
        block_output,
        grad_in,
        sums[0],
        sums[1],
        sums[2],
        sums[3],
        sums[4],
        sums[5],
        sums[6],
        sums[7],
        sums[8],
        sums[9],
        sums[10],
        sums[11],
        sums[12],
        sums[13],
    )


def solution(mesh):
    placed = (
        P("win", None, "wide", None),
        P("win", None),
        P("win", None, None),
        P(),
        P(),
        P(),
        P(),
        P(),
        P(),
        P(),
        P(),
        P(),
        P(),
        P(),
        P(),
        P(),
        P(),
        P("win", None, "wide", None),
    )
    return jax.shard_map(
        body,
        mesh=mesh,
        in_specs=placed,
        out_specs=(
            P("win", None, "wide", None),
            P("win", None, "wide", None),
            P(),
            P(),
            P(),
            P(),
            P(),
            P(),
            P(),
            P(),
            P(),
            P(),
            P(),
            P(),
            P(),
            P(),
        ),
        check_vma=False,
    )
```

profile of v0, /device:TPU:1, one launch (start us, length us, event | category | flops | bytes accessed | tf_op | source)
XLA Modules:
  0.0 509.4 jit_solution(5189061780441896610)
XLA Ops:
  12.1 1.8 fusion.64
  14.6 9.6 %all-to-all-start.1 = ((bf16[32,4,1,768]{3,1,2,0:T(4,128)(2,1)}), bf16[32,4,1,768]{3,1,2,0:T(4,128)(2,1)S(1)}, u32[]{:S(2)}, u32[]{:S(2)}) async-start(bf16[32,4,1,768]{3,1,2,0:T(4,128)(2,1)} %bitcast.16), calls=%async_computation.1 | async-start | bytes 393216 | tf_op jit(solution)/shard_map/all_to_all | solution.py:300
  24.8 7.7 %all-to-all-done.1 = bf16[32,4,1,768]{3,1,2,0:T(4,128)(2,1)S(1)} async-done(((bf16[32,4,1,768]{3,1,2,0:T(4,128)(2,1)}), bf16[32,4,1,768]{3,1,2,0:T(4,128)(2,1)S(1)}, u32[]{:S(2)}, u32[]{:S(2)}) %all-to-all-start.1) | async-done | bytes 196640 | tf_op jit(solution)/shard_map/all_to_all | solution.py:300
  33.8 4.5 all-to-all-start
  39.2 1.9 convert_reduce_fusion.7
  44.8 10.5 %all-to-all-done = bf16[32,128,1,128]{3,1,2,0:T(8,128)(2,1)} async-done(((bf16[32,128,1,128]{3,1,2,0:T(8,128)(2,1)}), bf16[32,128,1,128]{3,1,2,0:T(8,128)(2,1)}, u32[]{:S(2)}, u32[]{:S(2)}) %all-to-all-start) | async-done | bytes 1048608 | tf_op jit(solution)/shard_map/all_to_all | solution.py:18
  55.3 1.9 copy.93
  57.2 15.3 %while.48 = (s32[]{:T(128)}, f32[1536]{0:T(1024)S(1)}, f32[1536]{0:T(1024)S(1)}, s32[]{:T(128)}, s32[4096]{0:T(1024)S(1)}, /*index=5*/s32[4096]{0:T(1024)S(1)}, ...) while((s32[]{:T(128)}, f32[1536]{0:T(1024)S(1)}, ...), condition=%wide.region_11.12_spmd.clone, body=%wide.region_8.11_spmd.clone.sunk | while | flops 106957832 | bytes 6962367 | solution.py:156
  73.2 20.9 %while.49 = (s32[]{:T(128)}, f32[1536,64]{0,1:T(8,128)S(1)}, s32[]{:T(128)}, s32[4096]{0:T(1024)S(1)}, s32[4096]{0:T(1024)S(1)}, /*index=5*/bf16[4096,128]{1,0:T...) while((s32[]{:T(128)}, f32[1536,64]{0,1:T(8,128)S(1)}, ...), condition=%wide.region_13.14_spmd.clone, body=%wide.region_12.13_spmd.clone.sunk | while | flops 206929920 | bytes 1516239 | solution.py:175
  73.7 2.0 convolution_add_fusion.10
  76.3 2.0 convolution_add_fusion.10
  79.0 2.0 convolution_add_fusion.10
  81.6 2.1 convolution_add_fusion.10
  84.2 2.0 convolution_add_fusion.10
  86.8 2.0 convolution_add_fusion.10
  89.4 2.0 convolution_add_fusion.10
  92.0 2.0 convolution_add_fusion.10
  95.5 4.0 all-to-all-start.2
  99.5 8.2 %all-to-all-done.2 = bf16[1,4,32,768]{3,1,0,2:T(4,128)(2,1)S(1)} async-done(((bf16[1,4,32,768]{3,1,0,2:T(4,128)(2,1)}), bf16[1,4,32,768]{3,1,0,2:T(4,128)(2,1)S(1)}, u32[]{:S(2)}, u32[]{:S(2)}) %all-to-all-start.2) | async-done | bytes 196640 | tf_op jit(solution)/shard_map/all_to_all | solution.py:330
  108.5 3.3 convolution_add_fusion.2
  111.9 5.8 %convert_reduce_fusion = (f32[3072]{0:T(1024)}, bf16[128,3072]{1,0:T(8,128)(2,1)S(1)}) fusion(f32[128,3072]{1,0:T(8,128)S(1)} %convolution_add_fusion.2, bf16[3072,768]{1,0:T(8,128)(2,1)} %param.41, bf16[1,128,1,768]{3,1,2,0:T(8,128)(2,1)S(1)} %copy-done.10), kind=kOutput, calls=%fused_computation.70 | convolution fusion | flops 614200320 | bytes 7286784 | tf_op jit(solution)/shard_map/dot_general | solution.py:96
  117.8 1.8 multiply_reduce_fusion
  123.3 3.8 all-to-all-start.3
  127.1 8.4 %all-to-all-done.3 = bf16[32,4,1,768]{3,1,2,0:T(4,128)(2,1)S(1)} async-done(((bf16[32,4,1,768]{3,1,2,0:T(4,128)(2,1)}), bf16[32,4,1,768]{3,1,2,0:T(4,128)(2,1)S(1)}, u32[]{:S(2)}, u32[]{:S(2)}) %all-to-all-start.3) | async-done | bytes 196640 | tf_op jit(solution)/shard_map/all_to_all | solution.py:372
  135.8 25.5 %while.50 = (s32[]{:T(128)}, f32[1536]{0:T(1024)S(1)}, s32[]{:T(128)}, s32[4096]{0:T(1024)S(1)}, s32[4096]{0:T(1024)S(1)}, /*index=5*/bf16[4096,128]{1,0:T(8,128...) while((s32[]{:T(128)}, f32[1536]{0:T(1024)S(1)}, ...), condition=%wide.region_20.21_spmd.clone, body=%wide.region_18.20_spmd.clone.sunk | while | flops 207618048 | bytes 7437539 | solution.py:215
  137.0 2.0 fusion.179
  140.2 2.0 fusion.179
  143.4 2.0 fusion.179
  146.5 2.0 fusion.179
  149.7 2.0 fusion.179
  152.9 2.0 fusion.179
  156.1 2.0 fusion.179
  159.3 2.0 fusion.179
  162.8 53.2 %while.51 = (s32[]{:T(128)}, f32[1536,64]{0,1:T(8,128)S(1)}, f32[4096,128]{1,0:T(8,128)}, s32[]{:T(128)}, s32[4096]{0:T(1024)S(1)}, /*index=5*/s32[4096]{0:T(102...) while((s32[]{:T(128)}, f32[1536,64]{0,1:T(8,128)S(1)}, ...), condition=%wide.region_22.23_spmd.clone, body=%wide.region_21.22_spmd.clone.sunk | while | flops 511442944 | bytes 19741952 | solution.py:251
  210.9 1.8 fusion.190
  217.3 3.9 all-to-all-start.4
  221.2 5.3 %fusion.108 = f32[768,3072]{1,0:T(8,128)} fusion(bf16[128,3072]{1,0:T(8,128)(2,1)S(1)} %copy-done.8, f32[128,768]{1,0:T(8,128)S(1)} %get-tuple-element.610, f32[768]{0:T(1024)S(1)} %convert_element_type.152, f32[768]{0:T(1024)S(1)} %convert_element_type.151, f32[128]{0:T(128)S(1)} %copy-done.23, f32[128]{0:T(128)S(1)} %broadcast_multiply_fusion), kind=kOutput, calls=%fused_computation.170 | convolution fusion | flops 604471296 | bytes 10624000 | tf_op jit(solution)/shard_map/dot_general | solution.py:90
  229.5 6.0 %all-to-all-start.5 = ((bf16[32,128,1,128]{3,1,2,0:T(8,128)(2,1)}), bf16[32,128,1,128]{3,1,2,0:T(8,128)(2,1)S(1)}, u32[]{:S(2)}, u32[]{:S(2)}) async-start(bf16[32,128,1,128]{3,1,2,0:T(8,128)(2,1)} %copy.103), calls=%async_computation.5 | async-start | bytes 2097152 | tf_op jit(solution)/shard_map/all_to_all | solution.py:33
  235.6 1.9 fusion.116
  237.5 6.7 %fusion.85 = f32[3072,768]{1,0:T(8,128)} fusion(bf16[1,128,1,768]{3,1,2,0:T(8,128)(2,1)S(1)} %copy-done.11, f32[128,3072]{1,0:T(8,128)} %copy-done.4), kind=kOutput, calls=%fused_computation.118 | convolution fusion | flops 607518720 | bytes 11206656 | tf_op jit(solution)/shard_map/dot_general | solution.py:90
  244.3 2.0 fusion.105
  246.3 6.1 %all-to-all-done.5 = bf16[32,128,1,128]{3,1,2,0:T(8,128)(2,1)S(1)} async-done(((bf16[32,128,1,128]{3,1,2,0:T(8,128)(2,1)}), bf16[32,128,1,128]{3,1,2,0:T(8,128)(2,1)S(1)}, u32[]{:S(2)}, u32[]{:S(2)}) %all-to-all-start.5) | async-done | bytes 1048608 | tf_op jit(solution)/shard_map/all_to_all | solution.py:33
  254.4 4.6 fusion.65
  262.2 65.7 %all-reduce.1 = (f32[768]{0:T(1024)}, f32[768]{0:T(1024)}, f32[768]{0:T(1024)}, f32[64]{0:T(128)}, f32[768]{0:T(1024)}, /*index=5*/f32[768]{0:T(1024)}, f32[768]{0:T(1024)}, f32[3072]{0:T(1024)}, f32[768]{0:T(1024)}) all-reduce(f32[768]{0:T(1024)S(1)} %get-tuple-element.482, ...), channel_id=1, replica_groups=mesh['win'=4,'wide'=32] {'win','wide'}, use_global_device_ids=true, to_apply=%region_27.28 | all-reduce | flops 8512 | bytes 68096 | tf_op jit(solution)/shard_map/psum | solution.py:412
  327.9 156.0 %all-reduce.5.cloned.1.call-done = (f32[768,768]{1,0:T(8,128)}, f32[768,128]{1,0:T(8,128)}, f32[768,768]{1,0:T(8,128)}, f32[768,3072]{1,0:T(8,128)}, f32[3072,768]{1,0:T(8,128)}) async-done(((f32[768,768]{1,0:T(8,128)}, f32[768,128]{1,0:T(8,128)}, f32[768,768]{1,0:T(8,128)}, f32[768,3072]{1,0:T(8,128)}, f32[3072,768]{1,0:T(8,128)}), (f32[768,768]{1,0:T(8,128)}, f32[768,128]{1,0:T(8,128)}, ...) | async-done | bytes 23986192 | tf_op jit(solution)/shard_map/psum | solution.py:412
  483.9 3.4 copy.167
  489.5 9.3 %copy.170 = f32[768,3072]{1,0:T(8,128)} copy(f32[768,3072]{1,0:T(8,128)} %get-tuple-element.1092) | data formatting | bytes 18874368
  498.8 3.7 copy.171
  (494 shorter events, 107.5 us)
Async XLA Ops:
  7.2 100.6 %copy-start = (bf16[768,768]{1,0:T(8,128)(2,1)S(1)}, bf16[768,768]{1,0:T(8,128)(2,1)}, u32[]{:S(2)}) copy-start(bf16[768,768]{1,0:T(8,128)(2,1)} %param.35) | copy-start | bytes 3538948
  7.2 17.3 %copy-start.3 = (bf16[1,128,1,768]{3,1,2,0:T(8,128)(2,1)S(1)}, bf16[1,128,1,768]{3,1,2,0:T(8,128)(2,1)}, u32[]{:S(2)}) copy-start(bf16[1,128,1,768]{3,1,2,0:T(8,128)(2,1)} %param.26) | copy-start | bytes 589828
  7.2 17.0 %copy-start.38 = (bf16[64]{0:T(256)(128)(2,1)S(1)}, bf16[64]{0:T(256)(128)(2,1)}, u32[]{:S(2)}) copy-start(bf16[64]{0:T(256)(128)(2,1)} %param.34) | copy-start | bytes 388
  7.2 17.1 %copy-start.37 = (s32[1,8]{1,0:T(1,128)S(1)}, s32[1,8]{1,0:T(1,128)}, u32[]{:S(2)}) copy-start(s32[1,8]{1,0:T(1,128)} %param.27) | copy-start | bytes 100
  7.2 17.3 %copy-start.18 = (bf16[768,128]{1,0:T(8,128)(2,1)S(1)}, bf16[768,128]{1,0:T(8,128)(2,1)}, u32[]{:S(2)}) copy-start(bf16[768,128]{1,0:T(8,128)(2,1)} %param.33) | copy-start | bytes 589828
  7.2 17.5 %copy-start.34 = (s32[1,8,2]{1,2,0:T(2,128)S(1)}, s32[1,8,2]{1,2,0:T(2,128)}, u32[]{:S(2)}) copy-start(s32[1,8,2]{1,2,0:T(2,128)} %param.28) | copy-start | bytes 196
  10.1 23.7 %copy-start.25 = (f32[128]{0:T(128)}, f32[128]{0:T(128)S(1)}, u32[]{:S(2)}) copy-start(f32[128]{0:T(128)S(1)} %fusion.99) | copy-start | bytes 1540
  14.6 17.9 %all-to-all-start.1 = ((bf16[32,4,1,768]{3,1,2,0:T(4,128)(2,1)}), bf16[32,4,1,768]{3,1,2,0:T(4,128)(2,1)S(1)}, u32[]{:S(2)}, u32[]{:S(2)}) async-start(bf16[32,4,1,768]{3,1,2,0:T(4,128)(2,1)} %bitcast.16), calls=%async_computation.1 | async-start | bytes 393216 | tf_op jit(solution)/shard_map/all_to_all | solution.py:300
  33.8 21.6 %all-to-all-start = ((bf16[32,128,1,128]{3,1,2,0:T(8,128)(2,1)}), bf16[32,128,1,128]{3,1,2,0:T(8,128)(2,1)}, u32[]{:S(2)}, u32[]{:S(2)}) async-start(bf16[32,128,1,128]{3,1,2,0:T(8,128)(2,1)} %broadcast_in_dim.62), calls=%async_computation | async-start | bytes 2097152 | tf_op jit(solution)/shard_map/all_to_all | solution.py:18
  94.1 5.4 %copy-start.28 = (bf16[768]{0:T(1024)(128)(2,1)S(1)}, bf16[768]{0:T(1024)(128)(2,1)}, u32[]{:S(2)}) copy-start(bf16[768]{0:T(1024)(128)(2,1)} %param.37) | copy-start | bytes 4612
  94.1 5.4 %copy-start.29 = (bf16[768]{0:T(1024)(128)(2,1)S(1)}, bf16[768]{0:T(1024)(128)(2,1)}, u32[]{:S(2)}) copy-start(bf16[768]{0:T(1024)(128)(2,1)} %param.38) | copy-start | bytes 4612
  94.1 5.4 %copy-start.30 = (bf16[768]{0:T(1024)(128)(2,1)S(1)}, bf16[768]{0:T(1024)(128)(2,1)}, u32[]{:S(2)}) copy-start(bf16[768]{0:T(1024)(128)(2,1)} %param.36) | copy-start | bytes 4612
  94.1 5.4 %copy-start.27 = (bf16[3072]{0:T(1024)(128)(2,1)S(1)}, bf16[3072]{0:T(1024)(128)(2,1)}, u32[]{:S(2)}) copy-start(bf16[3072]{0:T(1024)(128)(2,1)} %param.40) | copy-start | bytes 18436
  95.5 12.3 %all-to-all-start.2 = ((bf16[1,4,32,768]{3,1,0,2:T(4,128)(2,1)}), bf16[1,4,32,768]{3,1,0,2:T(4,128)(2,1)S(1)}, u32[]{:S(2)}, u32[]{:S(2)}) async-start(bf16[1,4,32,768]{3,1,0,2:T(4,128)(2,1)} %copy.97), calls=%async_computation.2 | async-start | bytes 393216 | tf_op jit(solution)/shard_map/all_to_all | solution.py:330
  108.5 11.1 %copy-start.22 = (f32[128]{0:T(128)}, f32[128]{0:T(128)S(1)}, u32[]{:S(2)}) copy-start(f32[128]{0:T(128)S(1)} %fusion.100) | copy-start | bytes 1540
  108.5 3.4 copy-start.10
  108.5 9.2 %slice-start = ((s8[4718592]{0:T(1024)(128)(4,1)}), s8[4194304]{0:T(1024)(128)(4,1)S(1)}, s32[]{:S(2)}) async-start(s8[4718592]{0:T(1024)(128)(4,1)} %bitcast.222), calls=%async_computation.7 | async-start | bytes 8388608
  111.9 5.9 %copy-start.4 = (f32[128,3072]{1,0:T(8,128)}, f32[128,3072]{1,0:T(8,128)S(1)}, u32[]{:S(2)}) copy-start(f32[128,3072]{1,0:T(8,128)S(1)} %convolution_add_fusion.2) | copy-start | bytes 4718596
  111.9 5.9 %slice-start.1 = ((s8[4718592]{0:T(1024)(128)(4,1)}), s8[524288]{0:T(1024)(128)(4,1)S(1)}, s32[]{:S(2)}) async-start(s8[4718592]{0:T(1024)(128)(4,1)} %bitcast.222), calls=%async_computation.8 | async-start | bytes 1048576
  117.8 1.8 copy-start.7
  119.9 0.8 copy-start.5
  119.9 15.7 %copy-start.32 = (f32[128]{0:T(128)}, f32[128]{0:T(128)S(1)}, u32[]{:S(2)}) copy-start(f32[128]{0:T(128)S(1)} %negate_multiply_fusion.1) | copy-start | bytes 1540
  123.3 12.2 %all-to-all-start.3 = ((bf16[32,4,1,768]{3,1,2,0:T(4,128)(2,1)}), bf16[32,4,1,768]{3,1,2,0:T(4,128)(2,1)S(1)}, u32[]{:S(2)}, u32[]{:S(2)}) async-start(bf16[32,4,1,768]{3,1,2,0:T(4,128)(2,1)} %bitcast.24), calls=%async_computation.3 | async-start | bytes 393216 | tf_op jit(solution)/shard_map/all_to_all | solution.py:372
  215.9 5.2 %copy-start.8 = (bf16[128,3072]{1,0:T(8,128)(2,1)S(1)}, bf16[128,3072]{1,0:T(8,128)(2,1)}, u32[]{:S(2)}) copy-start(bf16[128,3072]{1,0:T(8,128)(2,1)} %copy-done.7) | copy-start | bytes 2359300
  215.9 5.3 %copy-start.23 = (f32[128]{0:T(128)S(1)}, f32[128]{0:T(128)}, u32[]{:S(2)}) copy-start(f32[128]{0:T(128)} %copy-done.22) | copy-start | bytes 1540
  217.3 12.2 %all-to-all-start.4 = ((bf16[1,4,32,768]{3,1,0,2:T(4,128)(2,1)}), bf16[1,4,32,768]{3,1,0,2:T(4,128)(2,1)S(1)}, u32[]{:S(2)}, u32[]{:S(2)}) async-start(bf16[1,4,32,768]{3,1,0,2:T(4,128)(2,1)} %copy.101), calls=%async_computation.4 | async-start | bytes 393216 | tf_op jit(solution)/shard_map/all_to_all | solution.py:394
  221.2 5.3 %copy-start.2 = (f32[4096,128]{1,0:T(8,128)S(1)}, f32[4096,128]{1,0:T(8,128)}, u32[]{:S(2)}) copy-start(f32[4096,128]{1,0:T(8,128)} %get-tuple-element.255) | copy-start | bytes 6291460
  226.6 9.0 %copy-start.13 = (bf16[128,768]{1,0:T(8,128)(2,1)S(1)}, bf16[128,768]{1,0:T(8,128)(2,1)}, u32[]{:S(2)}) copy-start(bf16[128,768]{1,0:T(8,128)(2,1)} %copy-done.12) | copy-start | bytes 589828
  226.6 9.0 %copy-start.15 = (bf16[128,768]{1,0:T(8,128)(2,1)S(1)}, bf16[128,768]{1,0:T(8,128)(2,1)}, u32[]{:S(2)}) copy-start(bf16[128,768]{1,0:T(8,128)(2,1)} %copy-done.14) | copy-start | bytes 589828
  228.0 9.5 %copy-start.11 = (bf16[1,128,1,768]{3,1,2,0:T(8,128)(2,1)S(1)}, bf16[1,128,1,768]{3,1,2,0:T(8,128)(2,1)}, u32[]{:S(2)}) copy-start(bf16[1,128,1,768]{3,1,2,0:T(8,128)(2,1)} %param.43) | copy-start | bytes 589828
  229.5 22.9 %all-to-all-start.5 = ((bf16[32,128,1,128]{3,1,2,0:T(8,128)(2,1)}), bf16[32,128,1,128]{3,1,2,0:T(8,128)(2,1)S(1)}, u32[]{:S(2)}, u32[]{:S(2)}) async-start(bf16[32,128,1,128]{3,1,2,0:T(8,128)(2,1)} %copy.103), calls=%async_computation.5 | async-start | bytes 2097152 | tf_op jit(solution)/shard_map/all_to_all | solution.py:33
  235.5 248.4 %all-reduce.5.cloned.1.call-start = ((), (), s32[]{:S(2)}) async-start(), calls=%async_computation.6 | async-start | bytes 47972352 | tf_op jit(solution)/shard_map/psum | solution.py:412
  237.5 6.8 %copy-start.26 = (f32[128]{0:T(128)S(1)}, f32[128]{0:T(128)}, u32[]{:S(2)}) copy-start(f32[128]{0:T(128)} %copy-done.25) | copy-start | bytes 1540
  253.7 0.7 copy-start.31
  254.4 4.7 copy-start.16
  259.0 1.0 copy-start.19
  259.0 1.3 copy-start.36
  259.0 1.6 copy-start.6
  259.1 1.6 copy-start.33
  260.0 2.2 copy-start.20
  260.0 2.2 copy-start.21
  260.0 2.2 copy-start.24
  483.9 3.4 copy-start.17
  483.9 4.1 copy-start.9
  488.1 10.7 %slice-start.2 = ((s8[9437184]{0:T(1024)(128)(4,1)}), s8[4194304]{0:T(1024)(128)(4,1)S(1)}, s32[]{:S(2)}) async-start(s8[9437184]{0:T(1024)(128)(4,1)} %bitcast.224), calls=%async_computation.9 | async-start | bytes 8388608
  489.5 9.3 %slice-start.3 = ((s8[9437184]{0:T(1024)(128)(4,1)}), s8[4194304]{0:T(1024)(128)(4,1)S(1)}, s32[]{:S(2)}) async-start(s8[9437184]{0:T(1024)(128)(4,1)} %bitcast.224), calls=%async_computation.10 | async-start | bytes 8388608
  489.5 9.3 %slice-start.4 = ((s8[9437184]{0:T(1024)(128)(4,1)}), s8[1048576]{0:T(1024)(128)(4,1)S(1)}, s32[]{:S(2)}) async-start(s8[9437184]{0:T(1024)(128)(4,1)} %bitcast.224), calls=%async_computation.11 | async-start | bytes 2097152
  498.8 3.8 copy-start.1
  (3 other events, 1.9 us)
Sparse Core Ops, SparseCore 0:
  253.9 230.0 all-reduce.4
where the time goes:
time: 512 us; the launch traced here: 509 us
  waiting for transfers between devices  199 us (39%)
  matrix products  113 us (22%)
  local copies, waits for them, and re-layouts  66.5 us (13%)
  blocking collectives  65.7 us (13%)
  starting transfers between devices  31.8 us (6%)
  between operations  18.1 us (4%)
  other arithmetic  14 us (3%)
    psum x1, waiting for transfers between devices, body(): lax.psum((grad_ln1_gain, grad_ln1_bias, grad_w_query, grad_b_query, grad_...  156 us
    psum x1, blocking collectives, body(): lax.psum((grad_ln1_gain, grad_ln1_bias, grad_w_query, grad_b_query, grad_...  65.7 us
    dot_general x45, matrix products, contract_last(): lax.dot_general(left, right, (((1,), (1,)), ((), ())), preferred_element_...  55.6 us
    dot_general x21, matrix products, contract_rows(): lax.dot_general(left, right, (((0,), (0,)), ((), ())), preferred_element_...  26.8 us
    unnamed x95, local copies, waits for them, and re-layouts  22.7 us
    dot_general x8, matrix products, value_step(): jnp.dot(probs, kv_block[:, head_dim:], preferred_element_type=jnp.float32)  16.4 us
    all_to_all x1, waiting for transfers between devices, from_everyone(): return lax.all_to_all(copies, axis, split_axis=0, concat_axis=0, tiled=True)  10.5 us
  transfers between devices with their start and end apart: 7, of which 7 were waited for; matrix products, arithmetic and copies ran while one was open for 6% of the time, Pallas kernels for 0%

commit v1 on v0

v1 whole, which is shorter than its diff:
```python
import functools

import jax
import jax.numpy as jnp
from jax import lax
from jax.experimental import pallas as pl
from jax.experimental.pallas import tpu as pltpu
from jax.sharding import Mesh, PartitionSpec as P

EPS = 1e-05
MASKED = -1e30
ROWS = 128
WIDE = 32
D = 768
H = 12
HD = 64
FF = 3072
WINDOW = ROWS * WIDE
RB = 4
RBR = ROWS // RB
QB = RBR * H
KB = 8
KBR = ROWS // KB
KEYS = WINDOW // KB
FC = 512
VMEM = pl.BlockSpec(memory_space=pltpu.VMEM)
SMEM = pl.BlockSpec(memory_space=pltpu.SMEM)
f32 = jnp.float32
bf16 = jnp.bfloat16


def params(limit=56):
    return pltpu.CompilerParams(vmem_limit_bytes=limit * 1024 * 1024)


def cost(flops, nbytes):
    return pl.CostEstimate(flops=int(flops), bytes_accessed=int(nbytes), transcendentals=0)


def dot(a, b):
    return jnp.dot(a, b, preferred_element_type=f32)


def dot_nt(a, b):
    return lax.dot_general(a, b, (((1,), (1,)), ((), ())), preferred_element_type=f32)


def dot_tn(a, b):
    return lax.dot_general(a, b, (((0,), (0,)), ((), ())), preferred_element_type=f32)


def norm_parts(x):
    mean = jnp.mean(x, axis=-1, keepdims=True)
    centered = x - mean
    var = jnp.mean(centered * centered, axis=-1, keepdims=True)
    rstd = lax.rsqrt(var + EPS)
    return centered * rstd, rstd


def norm_back(e, n, rstd, gain):
    m = e * gain
    return rstd * (
        m - jnp.mean(m, axis=-1, keepdims=True) - n * jnp.mean(m * n, axis=-1, keepdims=True)
    )


def lanes_low(shape):
    return lax.broadcasted_iota(jnp.int32, shape, len(shape) - 1) < HD


def enter_kernel(x_ref, gain_ref, bias_ref, wkv_ref, bv_ref, n1_ref, kv_ref):
    n, _ = norm_parts(x_ref[...].astype(f32))
    n1 = (n * gain_ref[...].astype(f32) + bias_ref[...].astype(f32)).astype(bf16)
    n1_ref[...] = n1
    kv_ref[...] = (dot(n1, wkv_ref[...]) + bv_ref[...].astype(f32)).astype(bf16)


def query_kernel(n1_ref, wq_ref, bq_ref, q_ref):
    q_ref[...] = (dot(n1_ref[...], wq_ref[...]) + bq_ref[...].astype(f32)).astype(bf16)


def forward_kernel(cls_ref, q_ref, kv_ref, kp_ref, sp_ref, st_ref, att_ref, x_ref, o_ref, lse_ref, m_ref, l_ref, acc_ref):
    low = lanes_low((ROWS, 2 * HD))
    for h in range(H):
        pair = q_ref[:, (h // 2) * 128 : (h // 2) * 128 + 128].astype(f32) * 0.125
        if h % 2:
            pair = pltpu.roll(pair, HD, 1)
        head = jnp.where(low, pair, 0.0).astype(bf16)
        for rb in range(RB):
            x_ref[rb, h * RBR : (h + 1) * RBR, :] = head[rb * RBR : (rb + 1) * RBR, :]

    def row_block(rb, _):
        rows = pl.ds(pl.multiple_of(rb * RBR, RBR), RBR)
        m_ref[...] = jnp.full((QB, 128), MASKED, f32)
        l_ref[...] = jnp.zeros((QB, 128), f32)
        acc_ref[...] = jnp.zeros((QB, 128), f32)

        def step(kb, masked):
            kvb = kv_ref[:, pl.ds(pl.multiple_of(kb * KBR, KBR), KBR), :].reshape(KEYS, 2 * HD)
            s = dot_nt(x_ref[rb], kvb)
            if masked:
                kp = kp_ref[kb]
                allowed = (kp <= sp_ref[rows, :1]) & (kp >= st_ref[rows, :1])
                bias = jnp.where(allowed, 0.0, MASKED)
                s = (s.reshape(H, RBR, KEYS) + bias[None]).reshape(QB, KEYS)
            m_old = m_ref[...]
            m_new = jnp.maximum(m_old, jnp.max(s, axis=1, keepdims=True))
            alpha = jnp.exp(m_old - m_new)
            p = jnp.exp(s - m_new[:, :1])
            l_ref[...] = l_ref[...] * alpha + jnp.sum(p, axis=1, keepdims=True)
            acc_ref[...] = acc_ref[...] * alpha + dot(p.astype(bf16), kvb)
            m_ref[...] = m_new

        def key_block(kb, _):
            kind = cls_ref[rb * KB + kb]

            @pl.when(kind == 2)
            def _():
                step(kb, False)

            @pl.when(kind == 1)
            def _():
                step(kb, True)

            return 0

        lax.fori_loop(0, KB, key_block, 0)
        l = l_ref[...]
        out = acc_ref[...] / l
        lse_ref[rb] = m_ref[...] + jnp.log(l)
        o_ref[rb] = out
        keep = lanes_low((RBR, 2 * HD))
        for h in range(0, H, 2):
            even = out[h * RBR : (h + 1) * RBR, :]
            odd = out[(h + 1) * RBR : (h + 2) * RBR, :]
            att_ref[rows, h * HD : (h + 2) * HD] = jnp.where(keep, pltpu.roll(even, HD, 1), odd).astype(bf16)
        return 0

    lax.fori_loop(0, RB, row_block, 0)


def backward_kernel(cls_ref, x_ref, do_ref, o_ref, lse_ref, kv_ref, kpb_ref, spl_ref, stl_ref, dq_ref, dkv_ref, y_ref, lrow_ref, drow_ref, dqt_ref, acc_ref, kt_ref):
    low = lanes_low((ROWS, 2 * HD))
    for h in range(H):
        pair = do_ref[:, (h // 2) * 128 : (h // 2) * 128 + 128].astype(f32)
        if h % 2 == 0:
            pair = pltpu.roll(pair, HD, 1)
        head = jnp.where(low, 0.0, pair).astype(bf16)
        for rb in range(RB):
            y_ref[rb, h * RBR : (h + 1) * RBR, :] = head[rb * RBR : (rb + 1) * RBR, :]
    for rb in range(RB):
        delta = jnp.sum(y_ref[rb].astype(f32) * o_ref[rb], axis=1, keepdims=True)
        drow_ref[rb] = jnp.transpose(jnp.broadcast_to(delta, (QB, 128)))[:8]
        lrow_ref[rb] = jnp.transpose(lse_ref[rb])[:8]
    dqt_ref[...] = jnp.zeros((RB, 128, QB), f32)

    def key_block(kb, _):
        cols = pl.ds(pl.multiple_of(kb * KBR, KBR), KBR)
        kvb = kv_ref[:, cols, :].reshape(KEYS, 2 * HD)
        kt_ref[...] = jnp.transpose(kvb.astype(f32)).astype(bf16)
        acc_ref[...] = jnp.zeros((KEYS, 2 * HD), f32)

        def step(rb, masked):
            kvb = kv_ref[:, cols, :].reshape(KEYS, 2 * HD)
            xb, yb = x_ref[rb], y_ref[rb]
            s = dot_nt(kvb, xb)
            if masked:
                kp = kpb_ref[kb]
                allowed = (kp <= spl_ref[rb]) & (kp >= stl_ref[rb])
                bias = jnp.where(allowed, 0.0, MASKED)
                s = s + jnp.concatenate([bias] * (QB // 128), axis=1)
            p = jnp.exp(s - lrow_ref[rb, :1])
            ds = (p * (dot_nt(kvb, yb) - drow_ref[rb, :1])).astype(bf16)
            acc_ref[...] += dot(ds, xb) + dot(p.astype(bf16), yb)
            dqt_ref[rb] += dot(kt_ref[...], ds)

        def row_block(rb, _):
            kind = cls_ref[rb * KB + kb]

            @pl.when(kind == 2)
            def _():
                step(rb, False)

            @pl.when(kind == 1)
            def _():
                step(rb, True)

            return 0

        lax.fori_loop(0, RB, row_block, 0)
        dkv_ref[:, cols, :] = acc_ref[...].reshape(WIDE, KBR, 2 * HD).astype(bf16)
        return 0

    lax.fori_loop(0, KB, key_block, 0)
    keep = lanes_low((RBR, 2 * HD))
    for rb in range(RB):
        dq = jnp.transpose(dqt_ref[rb]) * 0.125
        for h in range(0, H, 2):
            even = dq[h * RBR : (h + 1) * RBR, :]
            odd = dq[(h + 1) * RBR : (h + 2) * RBR, :]
            dq_ref[rb * RBR : (rb + 1) * RBR, h * HD : (h + 2) * HD] = jnp.where(
                keep, even, pltpu.roll(odd, HD, 1)
            ).astype(bf16)


def middle_kernel(att_ref, x_ref, g_ref, wout_ref, bout_ref, gain_ref, bias_ref, wup_ref, bup_ref, wdown_ref, bdown_ref,
                  y_ref, n2_ref, act_ref, gp_ref, gr_ref, gb_ref, ga_ref, vec_ref, gbup_ref,
                  resid_ref, out_ref, gn2_ref):
    step = pl.program_id(0)

    @pl.when(step == 0)
    def _():
        resid = x_ref[...].astype(f32) + (dot(att_ref[...], wout_ref[...]) + bout_ref[...].astype(f32))
        resid_ref[...] = resid
        n, _ = norm_parts(resid)
        n2_ref[...] = (n * gain_ref[...].astype(f32) + bias_ref[...].astype(f32)).astype(bf16)
        out_ref[...] = jnp.zeros_like(out_ref)
        gn2_ref[...] = jnp.zeros_like(gn2_ref)

    g = g_ref[...]
    pre = dot(n2_ref[...], wup_ref[...]) + bup_ref[...].astype(f32)
    sq = pre * pre
    t = jnp.tanh(0.7978845608028654 * (pre + 0.044715 * sq * pre))
    half = 0.5 + 0.5 * t
    act = (pre * half).astype(bf16)
    act_ref[...] = act
    slope = half + (0.5 * 0.7978845608028654) * pre * (1.0 - t * t) * (1.0 + (3 * 0.044715) * sq)
    gp = (slope * dot_nt(g, wdown_ref[...])).astype(bf16)
    gp_ref[...] = gp
    gbup_ref[...] = jnp.sum(gp.astype(f32), axis=0, keepdims=True)
    out_ref[...] += dot(act, wdown_ref[...])
    gn2_ref[...] += dot_nt(gp, wup_ref[...])

    @pl.when(step == pl.num_programs(0) - 1)
    def _():
        resid = resid_ref[...]
        gf = g.astype(f32)
        y_ref[...] = (resid + (out_ref[...] + bdown_ref[...].astype(f32))).astype(bf16)
        n, rstd = norm_parts(resid)
        e = gn2_ref[...]
        gr = gf + norm_back(e, n, rstd, gain_ref[...].astype(f32))
        gr_ref[...] = gr
        gb = gr.astype(bf16)
        gb_ref[...] = gb
        ga_ref[...] = dot_nt(gb, wout_ref[...]).astype(bf16)
        vec_ref[0:1, :] = jnp.sum(gf, axis=0, keepdims=True)
        vec_ref[1:2, :] = jnp.sum(e * n, axis=0, keepdims=True)
        vec_ref[2:3, :] = jnp.sum(e, axis=0, keepdims=True)
        vec_ref[3:4, :] = jnp.sum(gb.astype(f32), axis=0, keepdims=True)
        vec_ref[4:8, :] = jnp.zeros((4, D), f32)


def leave_kernel(x_ref, gain_ref, wq_ref, wkv_ref, gq_ref, parts_ref, gr_ref, gin_ref, gkv_ref, vec_ref):
    gkv = jnp.sum(parts_ref[...].astype(f32), axis=0).astype(bf16)
    gkv_ref[...] = gkv
    gq = gq_ref[...]
    e = dot_nt(gq, wq_ref[...]) + dot_nt(gkv, wkv_ref[...])
    n, rstd = norm_parts(x_ref[...].astype(f32))
    gin_ref[...] = gr_ref[...] + norm_back(e, n, rstd, gain_ref[...].astype(f32))
    vec_ref[0:1, :] = jnp.sum(e * n, axis=0, keepdims=True)
    vec_ref[1:2, :] = jnp.sum(e, axis=0, keepdims=True)
    vec_ref[2:3, :] = jnp.sum(gq.astype(f32), axis=0, keepdims=True)
    vec_ref[3:4, 0:128] = jnp.sum(gkv.astype(f32), axis=0, keepdims=True)
    vec_ref[3:4, 128:] = jnp.zeros((1, D - 128), f32)
    vec_ref[4:8, :] = jnp.zeros((4, D), f32)


def shapes(*pairs):
    return tuple(jax.ShapeDtypeStruct(s, t) for s, t in pairs)


def positions(lengths, splits, wide_index):
    ends = jnp.cumsum(lengths, dtype=jnp.int32)
    starts = ends - lengths
    first = lengths * jnp.minimum(splits[:, 0], splits[:, 1]) // 1024
    second = lengths * jnp.maximum(splits[:, 0], splits[:, 1]) // 1024

    def place(row):
        shape = (1,) * row.ndim + (-1,)
        s, e, a, b, n = (v.reshape(shape) for v in (starts, ends, first, second, lengths))
        row = row[..., None]
        inside = (row >= s) & (row < e)
        u = row - s
        moved = jnp.where(u < a, u, jnp.where(u >= b, a + u - b, a + n - b + u - a))
        return (
            jnp.sum(jnp.where(inside, s + moved, 0), axis=-1, dtype=jnp.int32),
            jnp.sum(jnp.where(inside, s, 0), axis=-1, dtype=jnp.int32),
        )

    k = jnp.arange(KB, dtype=jnp.int32)[:, None, None]
    j = jnp.arange(WIDE, dtype=jnp.int32)[None, :, None]
    r = jnp.arange(KBR, dtype=jnp.int32)[None, None, :]
    keys, _ = place(((k * KBR + r) * WIDE + j).reshape(KB, KEYS))
    own, own_start = place(jnp.arange(ROWS, dtype=jnp.int32) * WIDE + wide_index)
    low, high = jnp.min(keys, axis=1), jnp.max(keys, axis=1)
    blocks, block_starts = own.reshape(RB, RBR), own_start.reshape(RB, RBR)
    top, start_low = jnp.max(blocks, axis=1), jnp.min(block_starts, axis=1)
    bottom, start_high = jnp.min(blocks, axis=1), jnp.max(block_starts, axis=1)
    some = (low[None] <= top[:, None]) & (high[None] >= start_low[:, None])
    every = (high[None] <= bottom[:, None]) & (low[None] >= start_high[:, None])
    kinds = jnp.where(every, 2, jnp.where(some, 1, 0)).astype(jnp.int32).reshape(-1)
    return keys, own, own_start, kinds


def body(block_input, file_lengths, file_splits, ln1_gain, ln1_bias, w_query, b_query, w_kv, b_value, w_out, b_out,
         ln2_gain, ln2_bias, w_up, b_up, w_down, b_down, out_cotangent):
    row = lambda v: v.reshape(1, -1)
    x = block_input.reshape(ROWS, D)
    g = out_cotangent.reshape(ROWS, D)
    wide_index = lax.axis_index("wide")
    kv_shift = jnp.concatenate([jnp.zeros_like(b_value), b_value])

    n1, kv = pl.pallas_call(
        enter_kernel,
        out_shape=shapes(((ROWS, D), bf16), ((ROWS, 2 * HD), bf16)),
        in_specs=[VMEM] * 5,
        out_specs=(VMEM, VMEM),
        compiler_params=params(),
        cost_estimate=cost(2 * ROWS * D * 128, 6e5),
        name="enter",
    )(x, row(ln1_gain), row(ln1_bias), w_kv, row(kv_shift))
    copies = jnp.broadcast_to(kv, (WIDE, ROWS, 2 * HD))
    kv_all = lax.all_to_all(copies, "wide", 0, 0, tiled=True)

    q = pl.pallas_call(
        query_kernel,
        out_shape=jax.ShapeDtypeStruct((ROWS, D), bf16),
        in_specs=[VMEM] * 3,
        out_specs=VMEM,
        compiler_params=params(),
        cost_estimate=cost(2 * ROWS * D * D, 2e6),
        name="query",
    )(n1, w_query, row(b_query))
    keys, own, own_start, kinds = positions(file_lengths[0], file_splits[0], wide_index)
    own_cols = jnp.broadcast_to(own[:, None], (ROWS, 128))
    start_cols = jnp.broadcast_to(own_start[:, None], (ROWS, 128))
    key_cols = jnp.broadcast_to(keys[:, :, None], (KB, KEYS, 128))
    own_lanes = jnp.tile(own.reshape(RB, 1, RBR), (1, 1, 4))
    start_lanes = jnp.tile(own_start.reshape(RB, 1, RBR), (1, 1, 4))

    att, xq, o, lse = pl.pallas_call(
        forward_kernel,
        out_shape=shapes(((ROWS, D), bf16), ((RB, QB, 128), bf16), ((RB, QB, 128), f32), ((RB, QB, 128), f32)),
        in_specs=[SMEM] + [VMEM] * 5,
        out_specs=(VMEM,) * 4,
        scratch_shapes=[pltpu.VMEM((QB, 128), f32)] * 3,
        compiler_params=params(),
        cost_estimate=cost(4 * ROWS * H * WINDOW * 64, 4e6),
        name="attend",
    )(kinds, q, kv_all, keys.reshape(KB, 1, KEYS), own_cols, start_cols)

    steps = FF // FC
    whole = lambda *s: pl.BlockSpec(s, lambda i: (0,) * len(s))
    y, n2, act, gp, gr, gb, ga, vec_mid, gb_up = pl.pallas_call(
        middle_kernel,
        grid=(steps,),
        out_shape=shapes(
            ((ROWS, D), bf16), ((ROWS, D), bf16), ((ROWS, FF), bf16), ((ROWS, FF), bf16), ((ROWS, D), f32),
            ((ROWS, D), bf16), ((ROWS, D), bf16), ((8, D), f32), ((1, FF), f32),
        ),
        in_specs=[
            whole(ROWS, D), whole(ROWS, D), whole(ROWS, D), whole(D, D), whole(1, D), whole(1, D), whole(1, D),
            pl.BlockSpec((D, FC), lambda i: (0, i)), pl.BlockSpec((1, FC), lambda i: (0, i)),
            pl.BlockSpec((FC, D), lambda i: (i, 0)), whole(1, D),
        ],
        out_specs=(
            whole(ROWS, D), whole(ROWS, D), pl.BlockSpec((ROWS, FC), lambda i: (0, i)),
            pl.BlockSpec((ROWS, FC), lambda i: (0, i)), whole(ROWS, D), whole(ROWS, D), whole(ROWS, D),
            whole(8, D), pl.BlockSpec((1, FC), lambda i: (0, i)),
        ),
        scratch_shapes=[pltpu.VMEM((ROWS, D), f32)] * 3,
        compiler_params=params(),
        cost_estimate=cost(8 * ROWS * D * FF, 2e7),
        name="middle",
    )(att, x, g, w_out, row(b_out), row(ln2_gain), row(ln2_bias), w_up, row(b_up), w_down, row(b_down))

    gq, dkv = pl.pallas_call(
        backward_kernel,
        out_shape=shapes(((ROWS, D), bf16), ((WIDE, ROWS, 2 * HD), bf16)),
        in_specs=[SMEM] + [VMEM] * 8,
        out_specs=(VMEM, VMEM),
        scratch_shapes=[
            pltpu.VMEM((RB, QB, 128), bf16), pltpu.VMEM((RB, 8, QB), f32), pltpu.VMEM((RB, 8, QB), f32),
            pltpu.VMEM((RB, 128, QB), f32), pltpu.VMEM((KEYS, 2 * HD), f32), pltpu.VMEM((2 * HD, KEYS), bf16),
        ],
        compiler_params=params(),
        cost_estimate=cost(10 * ROWS * H * WINDOW * 64, 8e6),
        name="attend_back",
    )(kinds, xq, ga, o, lse, kv_all, key_cols, own_lanes, start_lanes)
    parts = lax.all_to_all(dkv, "wide", 0, 0, tiled=True)

    gin, gkv, vec_end = pl.pallas_call(
        leave_kernel,
        out_shape=shapes(((ROWS, D), f32), ((ROWS, 2 * HD), bf16), ((8, D), f32)),
        in_specs=[VMEM] * 7,
        out_specs=(VMEM,) * 3,
        compiler_params=params(),
        cost_estimate=cost(2 * ROWS * D * 900, 4e6),
        name="leave",
    )(x, row(ln1_gain), w_query, w_kv, gq, parts, gr)

    grads = [dot_tn(act, g), dot_tn(n2, gp), dot_tn(att, gb), dot_tn(n1, gq), dot_tn(n1, gkv)]
    sums = lax.psum(tuple(v.astype(bf16) for v in grads), ("win", "wide"))
    g_down, g_up, g_out, g_query, g_kv = (v.astype(f32) for v in sums)
    vec_mid, gb_up, vec_end = lax.psum((vec_mid, gb_up, vec_end), ("win", "wide"))
    shape = block_input.shape
    return (
        y.reshape(shape), gin.reshape(shape), vec_end[0], vec_end[1], g_query, vec_end[2], g_kv, vec_end[3, HD : 2 * HD],
        g_out, vec_mid[3], vec_mid[1], vec_mid[2], g_up, gb_up[0], g_down, vec_mid[0],
    )


def solution(mesh):
    split = P("win", None, "wide", None)
    return jax.shard_map(
        body,
        mesh=mesh,
        in_specs=(split, P("win", None), P("win", None, None)) + (P(),) * 14 + (split,),
        out_specs=(split, split) + (P(),) * 14,
        check_vma=False,
    )
```

time: 512 us -> 320 us (0.62)
  matrix products: 113 us -> 11.9 us
  waiting for transfers between devices: 199 us -> 113 us
  Pallas kernels: 0 us -> 61.7 us
  local copies, waits for them, and re-layouts: 66.5 us -> 20.5 us
  starting transfers between devices: 31.8 us -> 13.9 us
    dot_general x87 -> x5, matrix products: 113 us -> 11.9 us  [dot_tn(): lax.dot_general(a, b, (((0,), (0,)), ((), ())), preferred_element_type=f32)]
    pallas_call x0 -> x6, Pallas kernels: none -> 61.7 us  [the longest x1 22.2 us: body(): pl.pallas_call(backward_kernel, out_shape=shapes(((ROWS, D), bf16), ((WID...]
    psum x1, waiting for transfers between devices: 156 us -> 99.4 us  [body(): sums = lax.psum(tuple((v.astype(bf16) for v in grads)), ('win', 'wide'))]
    all_to_all x6 -> x2, waiting for transfers between devices: 42.6 us -> 13.6 us  [the longest x1 7.17 us: body(): kv_all = lax.all_to_all(copies, 'wide', 0, 0, tiled=True)]
    unnamed x95 -> x53, local copies, waits for them, and re-layouts: 22.7 us -> 3.28 us
    all_to_all x6 -> x2, starting transfers between devices: 31.7 us -> 13.7 us  [the longest x1 9.6 us: body(): kv_all = lax.all_to_all(copies, 'wide', 0, 0, tiled=True)]
    dynamic_slice x82 -> x0, local copies, waits for them, and re-layouts: 13.8 us -> none  [the longest x16 8.82 us: grad_step(): previous = lax.dynamic_slice_in_dim(grad_kv, key_start, key_block, 0)]
    convert_element_type x12 -> x5, other arithmetic: 2.29 us -> 15.9 us  [body(): g_down, g_up, g_out, g_query, g_kv = (v.astype(f32) for v in sums)]
  transfers between devices with their start and end apart: 7 -> 3, of which waited for: 7 -> 3; matrix products, arithmetic and copies ran while one was open for 6% -> 6% of each run, Pallas kernels for 0% -> 1%
where the time goes in v1:
time: 320 us; the launch traced here: 321 us
  waiting for transfers between devices  113 us (35%)
  blocking collectives  68.6 us (21%)
  Pallas kernels  61.7 us (19%)
  local copies, waits for them, and re-layouts  20.5 us (6%)
  other arithmetic  16.9 us (5%)
  between operations  14.3 us (4%)
  starting transfers between devices  13.9 us (4%)
  matrix products  11.9 us (4%)
    psum x1, waiting for transfers between devices, body(): sums = lax.psum(tuple((v.astype(bf16) for v in grads)), ('win', 'wide'))  99.4 us
    psum x1, blocking collectives, body(): lax.psum((vec_mid, gb_up, vec_end), ('win', 'wide'))  68.6 us
    pallas_call x1, Pallas kernels, body(): pl.pallas_call(backward_kernel, out_shape=shapes(((ROWS, D), bf16), ((WID...  22.2 us
    pallas_call x1, Pallas kernels, body(): pl.pallas_call(forward_kernel, out_shape=shapes(((ROWS, D), bf16), ((RB,...  20.4 us
    convert_element_type x5, other arithmetic, body(): g_down, g_up, g_out, g_query, g_kv = (v.astype(f32) for v in sums)  15.9 us
    dot_general x5, matrix products, dot_tn(): lax.dot_general(a, b, (((0,), (0,)), ((), ())), preferred_element_type=f32)  11.9 us
    pallas_call x1, Pallas kernels, body(): pl.pallas_call(middle_kernel, grid=(steps,), out_shape=shapes(((ROWS, D),...  11.3 us
    all_to_all x1, starting transfers between devices, body(): kv_all = lax.all_to_all(copies, 'wide', 0, 0, tiled=True)  9.6 us
  transfers between devices with their start and end apart: 3, of which 3 were waited for; matrix products, arithmetic and copies ran while one was open for 6% of the time, Pallas kernels for 1%

profile of v1, /device:TPU:1, one launch (start us, length us, event | category | flops | bytes accessed | tf_op | source)
XLA Modules:
  0.0 320.7 jit_solution(670688811338115938)
XLA Ops:
  7.3 1.3 reshape.327.gain_ref
  8.6 1.3 reshape.328.bias_ref
  9.8 1.2 pad_bitcast_fusion.bv_ref
  11.1 2.0 enter.1
  13.1 2.0 broadcast_in_dim.41
  15.1 9.6 %all-to-all-start = ((bf16[32,128,128]{2,1,0:T(8,128)(2,1)}), bf16[32,128,128]{2,1,0:T(8,128)(2,1)S(1)}, u32[]{:S(2)}, u32[]{:S(2)}) async-start(bf16[32,128,128]{2,1,0:T(8,128)(2,1)} %broadcast_in_dim.41), calls=%async_computation | async-start | bytes 2097152 | tf_op jit(solution)/shard_map/all_to_all | solution.py:323
  24.7 0.2 reduce-window.4
  25.5 0.2 fusion.5
  25.7 0.6 reshape.331.kp_ref
  26.7 0.6 select_n.81.cls_ref
  27.3 0.6 reshape.330.bq_ref
  27.9 0.6 reshape.336.bup_ref
  28.5 0.6 reshape.333.bout_ref
  29.1 0.6 reshape.334.gain_ref
  29.6 0.6 reshape.335.bias_ref
  30.2 0.6 reshape.337.bdown_ref
  30.8 0.7 tile.17.spl_ref
  31.5 0.7 tile.19.stl_ref
  32.1 2.3 query.1.q_ref
  34.4 7.2 %all-to-all-done.kv_ref = bf16[32,128,128]{2,1,0:T(8,128)(2,1)S(1)} async-done(((bf16[32,128,128]{2,1,0:T(8,128)(2,1)}), bf16[32,128,128]{2,1,0:T(8,128)(2,1)S(1)}, u32[]{:S(2)}, u32[]{:S(2)}) %all-to-all-start) | async-done | bytes 1048608 | tf_op jit(solution)/shard_map/all_to_all | solution.py:323
  41.6 0.8 broadcast_in_dim.42.sp_ref
  42.4 0.7 broadcast_in_dim.43.st_ref
  43.1 20.4 %attend.1 = (bf16[128,768]{1,0:T(8,128)(2,1)}, bf16[4,384,128]{2,1,0:T(8,128)(2,1)}, f32[4,384,128]{2,1,0:T(8,128)}, f32[4,384,128]{2,1,0:T(8,128)}) custom-call(s32[32]{0:T(128)} %select_n.81.cls_ref, bf16[128,768]{1,0:T(8,128)(2,1)} %query.1.q_ref, bf16[32,128,128]{2,1,0:T(8,128)(2,1)} %copy-done.6, s32[8,1,512]{2,1,0:T(1,128)} %reshape.331.kp_ref, ...), custom_call_target="tpu_custom_call" | custom-call | flops 1610612736 | bytes 4000000 | tf_op jit(solution)/shard_map/attend/pallas_call | solution.py:341
  63.5 11.3 %middle.1 = (bf16[128,768]{1,0:T(8,128)(2,1)}, bf16[128,768]{1,0:T(8,128)(2,1)}, bf16[128,3072]{1,0:T(8,128)(2,1)}, bf16[128,3072]{1,0:T(8,128)(2,1)}, f32[128,7...) custom-call(bf16[128,768]{1,0:T(8,128)(2,1)} %get-tuple-element.38.a, ...), custom_call_target="tpu_custom_call" | custom-call | flops 2415919104 | bytes 20000000 | tf_op jit(solution)/shard_map/middle/pallas_call | solution.py:354
  74.8 1.7 broadcast_in_dim.70.kpb_ref
  76.5 22.2 %attend_back.1 = (bf16[128,768]{1,0:T(8,128)(2,1)}, bf16[32,128,128]{2,1,0:T(8,128)(2,1)}) custom-call(s32[32]{0:T(128)} %select_n.81.cls_ref, bf16[4,384,128]{2,1,0:T(8,128)(2,1)} %get-tuple-element.40.x_ref, bf16[128,768]{1,0:T(8,128)(2,1)} %get-tuple-element.41.do_ref, f32[4,384,128]{2,1,0:T(8,128)} %get-tuple-element.42.o_ref, ...), custom_call_target="tpu_custom_call" | custom-call | flops 4026531840 | bytes 8000000 | tf_op jit(solution)/shard_map/attend_back/pallas_call | solution.py:377
  98.8 4.1 %all-to-all-start.1 = ((bf16[32,128,128]{2,1,0:T(8,128)(2,1)}), bf16[32,128,128]{2,1,0:T(8,128)(2,1)S(1)}, u32[]{:S(2)}, u32[]{:S(2)}) async-start(bf16[32,128,128]{2,1,0:T(8,128)(2,1)} %get-tuple-element.45), calls=%async_computation.1 | async-start | bytes 2097152 | tf_op jit(solution)/shard_map/all_to_all | solution.py:390
  102.9 0.2 all-reduce.5.cloned.1.call-start
  103.1 1.5 convolution_convert_fusion.2
  104.6 1.5 convolution_convert_fusion.3
  106.2 3.6 %convolution_convert_fusion = bf16[3072,768]{1,0:T(8,128)(2,1)} fusion(bf16[128,3072]{1,0:T(8,128)(2,1)S(1)} %copy-done.2, bf16[1,128,1,768]{3,1,2,0:T(8,128)(2,1)S(1)} %copy-done.10), kind=kOutput, calls=%fused_computation | convolution fusion | flops 606339072 | bytes 5701632 | tf_op jit(solution)/shard_map/dot_general | solution.py:49
  109.8 3.6 %convolution_convert_fusion.1 = bf16[768,3072]{1,0:T(8,128)(2,1)} fusion(bf16[128,768]{1,0:T(8,128)(2,1)S(1)} %copy-done.11, bf16[128,3072]{1,0:T(8,128)(2,1)S(1)} %copy-done.7), kind=kOutput, calls=%fused_computation.1 | convolution fusion | flops 606339072 | bytes 5701632 | tf_op jit(solution)/shard_map/dot_general | solution.py:49
  113.4 6.4 %all-to-all-done.1.parts_ref = bf16[32,128,128]{2,1,0:T(8,128)(2,1)S(1)} async-done(((bf16[32,128,128]{2,1,0:T(8,128)(2,1)}), bf16[32,128,128]{2,1,0:T(8,128)(2,1)S(1)}, u32[]{:S(2)}, u32[]{:S(2)}) %all-to-all-start.1) | async-done | bytes 1048608 | tf_op jit(solution)/shard_map/all_to_all | solution.py:390
  119.8 1.0 copy-done.1
  120.8 3.5 %leave.1 = (f32[128,768]{1,0:T(8,128)}, bf16[128,128]{1,0:T(8,128)(2,1)}, f32[8,768]{1,0:T(8,128)}) custom-call(bf16[128,768]{1,0:T(8,128)(2,1)} %bitcast.69, bf16[1,768]{1,0:T(2,128)(2,1)} %reshape.327.gain_ref, bf16[768,768]{1,0:T(8,128)(2,1)} %wq_ref.3, bf16[768,128]{1,0:T(8,128)(2,1)} %wkv_ref.3, bf16[128,768]{1,0:T(8,128)(2,1)} %get-tuple-element.44.gq_ref, ...), custom_call_target="tpu_custom_call" | custom-call | flops 176947200 | bytes 4000000 | tf_op jit(solution)/shard_map/leave/pallas_call | solution.py:392
  124.2 1.7 convolution_convert_fusion.4
  126.0 1.0 copy-done.12
  126.9 1.1 copy.36
  128.1 68.6 %all-reduce.1 = (f32[8,768]{1,0:T(8,128)S(1)}, f32[8,768]{1,0:T(8,128)S(1)}, f32[3072]{0:T(1024)}) all-reduce(f32[8,768]{1,0:T(8,128)S(1)} %copy-done.16, f32[8,768]{1,0:T(8,128)S(1)} %copy-done.15, f32[3072]{0:T(1024)S(1)} %bitcast.72), channel_id=1, replica_groups=mesh['win'=4,'wide'=32] {'win','wide'}, use_global_device_ids=true, to_apply=%region_10.11 | all-reduce | flops 15360 | bytes 122880 | tf_op jit(solution)/shard_map/psum | solution.py:405
  196.7 0.6 slice_reduce_fusion.4
  197.3 0.6 slice_reduce_fusion
  197.9 0.6 slice_bitcast_fusion
  198.5 99.4 %all-reduce.5.cloned.1.call-done = (bf16[768,768]{1,0:T(8,128)(2,1)}, bf16[768,128]{1,0:T(8,128)(2,1)}, bf16[768,768]{1,0:T(8,128)(2,1)}, bf16[768,3072]{1,0:T(8,128)(2,1)}, bf16[3072,768]{1,0:T(8,128)(2,1)}) async-done(((bf16[768,768]{1,0:T(8,128)(2,1)}, bf16[768,128]{1,0:T(8,128)(2,1)}, bf16[768,768]{1,0:T(8,128)(2,1)}, bf16[768,3072]{1,0:T(8,128)(2,1)}, bf16[3072,768]{1,0:T(8,128)(2,1)}), ...) | async-done | bytes 11993104 | tf_op jit(solution)/shard_map/psum | solution.py:403
  297.9 7.5 %convert_element_type.37 = f32[768,3072]{1,0:T(8,128)} convert(bf16[768,3072]{1,0:T(8,128)(2,1)} %get-tuple-element.125) | non-fusion elementwise | flops 2359296 | bytes 14155776 | tf_op jit(solution)/shard_map/convert_element_type | solution.py:404
  305.4 4.5 %convert_element_type.39 = f32[3072,768]{1,0:T(8,128)} convert(bf16[3072,768]{1,0:T(8,128)(2,1)S(1)} %copy-done) | non-fusion elementwise | flops 2359296 | bytes 14155776 | tf_op jit(solution)/shard_map/convert_element_type | solution.py:404
  309.9 1.6 convert_element_type.31
  311.5 1.6 convert_element_type.35
  313.1 0.8 convert_element_type.33
  (69 shorter events, 1.2 us)
Async XLA Ops:
  7.2 17.5 %copy-start.25 = (s32[1,8]{1,0:T(1,128)S(1)}, s32[1,8]{1,0:T(1,128)}, u32[]{:S(2)}) copy-start(s32[1,8]{1,0:T(1,128)} %param.19) | copy-start | bytes 100
  7.2 17.7 %copy-start.19 = (s32[1,8,2]{1,2,0:T(2,128)S(1)}, s32[1,8,2]{1,2,0:T(2,128)}, u32[]{:S(2)}) copy-start(s32[1,8,2]{1,2,0:T(2,128)} %param.20) | copy-start | bytes 196
  7.2 20.1 %copy-start.20 = (bf16[768]{0:T(1024)(128)(2,1)S(1)}, bf16[768]{0:T(1024)(128)(2,1)}, u32[]{:S(2)}) copy-start(bf16[768]{0:T(1024)(128)(2,1)} %param.24) | copy-start | bytes 4612
  7.2 20.6 %copy-start.18 = (bf16[3072]{0:T(1024)(128)(2,1)S(1)}, bf16[3072]{0:T(1024)(128)(2,1)}, u32[]{:S(2)}) copy-start(bf16[3072]{0:T(1024)(128)(2,1)} %param.32) | copy-start | bytes 18436
  7.2 21.2 %copy-start.21 = (bf16[768]{0:T(1024)(128)(2,1)S(1)}, bf16[768]{0:T(1024)(128)(2,1)}, u32[]{:S(2)}) copy-start(bf16[768]{0:T(1024)(128)(2,1)} %param.28) | copy-start | bytes 4612
  7.2 21.8 %copy-start.22 = (bf16[768]{0:T(1024)(128)(2,1)S(1)}, bf16[768]{0:T(1024)(128)(2,1)}, u32[]{:S(2)}) copy-start(bf16[768]{0:T(1024)(128)(2,1)} %param.29) | copy-start | bytes 4612
  7.2 22.4 %copy-start.23 = (bf16[768]{0:T(1024)(128)(2,1)S(1)}, bf16[768]{0:T(1024)(128)(2,1)}, u32[]{:S(2)}) copy-start(bf16[768]{0:T(1024)(128)(2,1)} %param.30) | copy-start | bytes 4612
  7.3 23.0 %copy-start.24 = (bf16[768]{0:T(1024)(128)(2,1)S(1)}, bf16[768]{0:T(1024)(128)(2,1)}, u32[]{:S(2)}) copy-start(bf16[768]{0:T(1024)(128)(2,1)} %param.34) | copy-start | bytes 4612
  15.1 26.5 %all-to-all-start = ((bf16[32,128,128]{2,1,0:T(8,128)(2,1)}), bf16[32,128,128]{2,1,0:T(8,128)(2,1)S(1)}, u32[]{:S(2)}, u32[]{:S(2)}) async-start(bf16[32,128,128]{2,1,0:T(8,128)(2,1)} %broadcast_in_dim.41), calls=%async_computation | async-start | bytes 2097152 | tf_op jit(solution)/shard_map/all_to_all | solution.py:323
  41.6 1.5 copy-start.6
  76.5 26.6 %copy-start.9 = (bf16[128,768]{1,0:T(8,128)(2,1)S(1)}, bf16[128,768]{1,0:T(8,128)(2,1)}, u32[]{:S(2)}) copy-start(bf16[128,768]{1,0:T(8,128)(2,1)} %get-tuple-element.38.att_ref) | copy-start | bytes 589828
  76.5 26.6 %copy-start.13 = (bf16[128,768]{1,0:T(8,128)(2,1)S(1)}, bf16[128,768]{1,0:T(8,128)(2,1)}, u32[]{:S(2)}) copy-start(bf16[128,768]{1,0:T(8,128)(2,1)} %get-tuple-element.50) | copy-start | bytes 589828
  98.7 5.9 %copy-start.3 = (bf16[128,768]{1,0:T(8,128)(2,1)S(1)}, bf16[128,768]{1,0:T(8,128)(2,1)}, u32[]{:S(2)}) copy-start(bf16[128,768]{1,0:T(8,128)(2,1)} %get-tuple-element.36.n1_ref) | copy-start | bytes 589828
  98.7 5.9 %copy-start.8 = (bf16[128,768]{1,0:T(8,128)(2,1)S(1)}, bf16[128,768]{1,0:T(8,128)(2,1)}, u32[]{:S(2)}) copy-start(bf16[128,768]{1,0:T(8,128)(2,1)} %get-tuple-element.44.gq_ref) | copy-start | bytes 589828
  98.7 7.4 %copy-start.2 = (bf16[128,3072]{1,0:T(8,128)(2,1)S(1)}, bf16[128,3072]{1,0:T(8,128)(2,1)}, u32[]{:S(2)}) copy-start(bf16[128,3072]{1,0:T(8,128)(2,1)} %get-tuple-element.55) | copy-start | bytes 2359300
  98.7 7.4 %copy-start.10 = (bf16[1,128,1,768]{3,1,2,0:T(8,128)(2,1)S(1)}, bf16[1,128,1,768]{3,1,2,0:T(8,128)(2,1)}, u32[]{:S(2)}) copy-start(bf16[1,128,1,768]{3,1,2,0:T(8,128)(2,1)} %param.35) | copy-start | bytes 589828
  98.8 21.0 %all-to-all-start.1 = ((bf16[32,128,128]{2,1,0:T(8,128)(2,1)}), bf16[32,128,128]{2,1,0:T(8,128)(2,1)S(1)}, u32[]{:S(2)}, u32[]{:S(2)}) async-start(bf16[32,128,128]{2,1,0:T(8,128)(2,1)} %get-tuple-element.45), calls=%async_computation.1 | async-start | bytes 2097152 | tf_op jit(solution)/shard_map/all_to_all | solution.py:390
  102.9 195.0 %all-reduce.5.cloned.1.call-start = ((), (), s32[]{:S(2)}) async-start(), calls=%async_computation.2 | async-start | bytes 23986176 | tf_op jit(solution)/shard_map/psum | solution.py:403
  106.1 3.6 %copy-start.7 = (bf16[128,3072]{1,0:T(8,128)(2,1)S(1)}, bf16[128,3072]{1,0:T(8,128)(2,1)}, u32[]{:S(2)}) copy-start(bf16[128,3072]{1,0:T(8,128)(2,1)} %get-tuple-element.53) | copy-start | bytes 2359300
  106.1 3.6 %copy-start.11 = (bf16[128,768]{1,0:T(8,128)(2,1)S(1)}, bf16[128,768]{1,0:T(8,128)(2,1)}, u32[]{:S(2)}) copy-start(bf16[128,768]{1,0:T(8,128)(2,1)} %get-tuple-element.52) | copy-start | bytes 589828
  119.8 1.0 copy-start.1
  125.9 1.0 copy-start.12
  125.9 2.1 copy-start.15
  125.9 2.1 copy-start.16
  125.9 2.1 copy-start.17
  297.9 7.5 %copy-start = (bf16[3072,768]{1,0:T(8,128)(2,1)S(1)}, bf16[3072,768]{1,0:T(8,128)(2,1)}, u32[]{:S(2)}) copy-start(bf16[3072,768]{1,0:T(8,128)(2,1)} %get-tuple-element.126) | copy-start | bytes 14155780
  305.4 4.5 %copy-start.5 = (bf16[768,768]{1,0:T(8,128)(2,1)S(1)}, bf16[768,768]{1,0:T(8,128)(2,1)}, u32[]{:S(2)}) copy-start(bf16[768,768]{1,0:T(8,128)(2,1)} %get-tuple-element.122) | copy-start | bytes 3538948
  309.9 1.7 copy-start.4
  311.5 1.7 copy-start.14
Sparse Core Ops, SparseCore 0:
  126.1 171.7 all-reduce.4

commit v2 on v1

v2 whole, which is shorter than its diff:
```python
import itertools

import jax
import jax.numpy as jnp
from jax import lax
from jax.experimental import pallas as pl
from jax.experimental.pallas import tpu as pltpu
from jax.sharding import Mesh, PartitionSpec as P

EPS = 1e-05
MASKED = -1e30
ROWS = 128
WIDE = 32
CHIPS = 16
D = 768
H = 12
HD = 64
FF = 3072
WINDOW = ROWS * WIDE
RB = 2
RBR = ROWS // RB
QB = RBR * H
KB = 4
KBR = ROWS // KB
KEYS = WINDOW // KB
FC = 512
VMEM = pl.BlockSpec(memory_space=pltpu.VMEM)
SMEM = pl.BlockSpec(memory_space=pltpu.SMEM)
ANY = pl.BlockSpec(memory_space=pl.ANY)
f32 = jnp.float32
bf16 = jnp.bfloat16


def params(limit=56):
    return pltpu.CompilerParams(vmem_limit_bytes=limit * 1024 * 1024)


def cost(flops, nbytes):
    return pl.CostEstimate(flops=1, bytes_accessed=1, transcendentals=0)


def dot(a, b):
    return jnp.dot(a, b, preferred_element_type=f32)


def dot_nt(a, b):
    return lax.dot_general(a, b, (((1,), (1,)), ((), ())), preferred_element_type=f32)


def dot_tn(a, b):
    return lax.dot_general(a, b, (((0,), (0,)), ((), ())), preferred_element_type=f32)


def norm_parts(x):
    mean = jnp.mean(x, axis=-1, keepdims=True)
    centered = x - mean
    var = jnp.mean(centered * centered, axis=-1, keepdims=True)
    rstd = lax.rsqrt(var + EPS)
    return centered * rstd, rstd


def norm_back(e, n, rstd, gain):
    m = e * gain
    return rstd * (
        m - jnp.mean(m, axis=-1, keepdims=True) - n * jnp.mean(m * n, axis=-1, keepdims=True)
    )


AXES = ("x", "y", "z", "c")
ORDER = ((2, 1, 0), (1, 0, 2))
FROM = (0, 3, 1, 2)


def ring(place, shift):
    pairs = []
    for at in itertools.product(range(4), range(4), range(4), range(2)):
        to = list(at)
        axis = ORDER[at[3]][place]
        to[axis] = (to[axis] + shift) % 4
        index = lambda v: ((v[0] * 4 + v[1]) * 4 + v[2]) * 2 + v[3]
        pairs.append((index(at), index(to)))
    return pairs


def ring_groups(place):
    groups = {}
    for at in itertools.product(range(4), range(4), range(4), range(2)):
        key = list(at)
        key[ORDER[at[3]][place]] = -1
        groups.setdefault(tuple(key), []).append(((at[0] * 4 + at[1]) * 4 + at[2]) * 2 + at[3])
    return list(groups.values())


def send(v, place, shift):
    return lax.ppermute(v, AXES, ring(place, shift))


def swap(v):
    return lax.ppermute(v, "c", [(0, 1), (1, 0)])


def spread(place, plus, minus, far):
    return send(plus, place, 1), send(minus, place, 3), send(far, place, 2)


def gather4(v, place):
    return (v,) + spread(place, v, v, v)


def lanes_low(shape):
    return lax.broadcasted_iota(jnp.int32, shape, len(shape) - 1) < HD


def vec(ref):
    return ref[...].astype(f32).reshape(1, -1)


def enter_kernel(x_ref, gain_ref, bias_ref, wkv_ref, bv_ref, n1_ref, kv_ref):
    n, _ = norm_parts(x_ref[...].astype(f32))
    n1 = (n * vec(gain_ref) + vec(bias_ref)).astype(bf16)
    n1_ref[...] = n1
    shift = jnp.concatenate([jnp.zeros((1, HD), f32), vec(bv_ref)], axis=1)
    kv = (dot(n1, wkv_ref[...]) + shift).astype(bf16)
    for i in range(CHIPS):
        kv_ref[i] = kv


def query_kernel(n1_ref, wq_ref, bq_ref, q_ref):
    q_ref[...] = (dot(n1_ref[...], wq_ref[...]) + vec(bq_ref)).astype(bf16)


def block_bias(kp, sp, st):
    bias = jnp.where((kp <= sp) & (kp >= st), 0.0, MASKED)
    return jnp.concatenate([bias] * (QB // 128), axis=1)


def visit(cls_ref, kb, step):
    def row_block(rb, _):
        kind = cls_ref[rb * KB + kb]

        @pl.when(kind == 2)
        def _():
            step(rb, False)

        @pl.when(kind == 1)
        def _():
            step(rb, True)

        return 0

    lax.fori_loop(0, RB, row_block, 0)


def forward_kernel(at_ref, cls_ref, q_ref, same_ref, other_ref, kpb_ref, spl_ref, stl_ref, n1_ref,
                   att_ref, keep_ref, send_ref, x_ref, o_ref, lse_ref, kv_ref, m_ref, l_ref, acc_ref, kt_ref):
    kv_ref[:CHIPS] = same_ref[...]
    kv_ref[CHIPS:] = other_ref[...]
    low = lanes_low((ROWS, 2 * HD))
    for h in range(H):
        pair = q_ref[:, (h // 2) * 128 : (h // 2) * 128 + 128].astype(f32) * 0.125
        if h % 2:
            pair = pltpu.roll(pair, HD, 1)
        head = jnp.where(low, pair, 0.0).astype(bf16)
        for rb in range(RB):
            x_ref[rb, h * RBR : (h + 1) * RBR, :] = head[rb * RBR : (rb + 1) * RBR, :]
    m_ref[...] = jnp.full((RB, 1, QB), MASKED, f32)
    l_ref[...] = jnp.zeros((RB, 1, QB), f32)
    acc_ref[...] = jnp.zeros((RB, 2 * HD, QB), f32)

    def key_block(kb, _):
        cols = pl.ds(pl.multiple_of(kb * KBR, KBR), KBR)
        kt_ref[...] = jnp.transpose(kv_ref[:, cols, :].reshape(KEYS, 2 * HD).astype(f32)).astype(bf16)

        def step(rb, masked):
            s = dot_nt(kv_ref[:, cols, :].reshape(KEYS, 2 * HD), x_ref[rb])
            if masked:
                s = s + block_bias(kpb_ref[kb], spl_ref[rb], stl_ref[rb])
            m_old = m_ref[rb]
            m_new = jnp.maximum(m_old, jnp.max(s, axis=0, keepdims=True))
            alpha = jnp.exp(m_old - m_new)
            p = jnp.exp(s - m_new)
            l_ref[rb] = l_ref[rb] * alpha + jnp.sum(p, axis=0, keepdims=True)
            acc_ref[rb] = acc_ref[rb] * alpha + dot(kt_ref[...], p.astype(bf16))
            m_ref[rb] = m_new

        visit(cls_ref, kb, step)
        return 0

    lax.fori_loop(0, KB, key_block, 0)
    keep = lanes_low((RBR, 2 * HD))
    first = at_ref[0] == 0
    for rb in range(RB):
        rows = slice(rb * RBR, (rb + 1) * RBR)
        l = l_ref[rb]
        lse_ref[rb] = m_ref[rb] + jnp.log(l)
        out = jnp.transpose(acc_ref[rb] / l)
        o_ref[rb] = out
        for h in range(0, H, 2):
            even = out[h * RBR : (h + 1) * RBR, :]
            odd = out[(h + 1) * RBR : (h + 2) * RBR, :]
            att_ref[rows, h * HD : (h + 2) * HD] = jnp.where(keep, pltpu.roll(even, HD, 1), odd).astype(bf16)
    n1, att = n1_ref[...], att_ref[...]
    keep_ref[...] = jnp.where(first, n1, att)
    send_ref[...] = jnp.where(first, att, n1)


def backward_kernel(at_ref, cls_ref, x_ref, do_ref, o_ref, lse_ref, kv_ref, kpb_ref, spl_ref, stl_ref, gb_ref,
                    dq_ref, keep_ref, send_ref, dkv_ref, y_ref, drow_ref, dqt_ref, acc_ref, kt_ref):
    low = lanes_low((ROWS, 2 * HD))
    for h in range(H):
        pair = do_ref[:, (h // 2) * 128 : (h // 2) * 128 + 128].astype(f32)
        if h % 2 == 0:
            pair = pltpu.roll(pair, HD, 1)
        head = jnp.where(low, 0.0, pair).astype(bf16)
        for rb in range(RB):
            y_ref[rb, h * RBR : (h + 1) * RBR, :] = head[rb * RBR : (rb + 1) * RBR, :]
    for rb in range(RB):
        delta = jnp.sum(y_ref[rb].astype(f32) * o_ref[rb], axis=1, keepdims=True)
        drow_ref[rb] = jnp.transpose(jnp.broadcast_to(delta, (QB, 128)))[:8]
    dqt_ref[...] = jnp.zeros((RB, 128, QB), f32)

    def key_block(kb, _):
        cols = pl.ds(pl.multiple_of(kb * KBR, KBR), KBR)
        kvb = kv_ref[:, cols, :].reshape(KEYS, 2 * HD)
        kt_ref[...] = jnp.transpose(kvb.astype(f32)).astype(bf16)
        acc_ref[...] = jnp.zeros((KEYS, 2 * HD), f32)

        def step(rb, masked):
            kvb = kv_ref[:, cols, :].reshape(KEYS, 2 * HD)
            xb, yb = x_ref[rb], y_ref[rb]
            s = dot_nt(kvb, xb)
            if masked:
                s = s + block_bias(kpb_ref[kb], spl_ref[rb], stl_ref[rb])
            p = jnp.exp(s - lse_ref[rb])
            ds = (p * (dot_nt(kvb, yb) - drow_ref[rb, :1])).astype(bf16)
            acc_ref[...] += dot(ds, xb) + dot(p.astype(bf16), yb)
            dqt_ref[rb] += dot(kt_ref[...], ds)

        visit(cls_ref, kb, step)
        sums = acc_ref[...].reshape(WIDE, KBR, 2 * HD).astype(bf16)
        for i in range(CHIPS):
            dkv_ref[2 * i + at_ref[0], cols, :] = sums[i]
            dkv_ref[2 * i + 1 - at_ref[0], cols, :] = sums[CHIPS + i]
        return 0

    lax.fori_loop(0, KB, key_block, 0)
    keep = lanes_low((RBR, 2 * HD))
    for rb in range(RB):
        dq = jnp.transpose(dqt_ref[rb]) * 0.125
        for h in range(0, H, 2):
            even = dq[h * RBR : (h + 1) * RBR, :]
            odd = dq[(h + 1) * RBR : (h + 2) * RBR, :]
            dq_ref[rb * RBR : (rb + 1) * RBR, h * HD : (h + 2) * HD] = jnp.where(
                keep, even, pltpu.roll(odd, HD, 1)
            ).astype(bf16)
    first = at_ref[0] == 0
    dq, gb = dq_ref[...], gb_ref[...]
    keep_ref[...] = jnp.where(first, dq, gb)
    send_ref[...] = jnp.where(first, gb, dq)


def put_rows(ref, at, row):
    for i in range(row.shape[1] // 128):
        ref[pl.ds(at + i, 1), :] = row[:, i * 128 : (i + 1) * 128]


def middle_kernel(at_ref, att_ref, x_ref, g_ref, wout_ref, bout_ref, gain_ref, bias_ref, wup_ref, bup_ref, wdown_ref, bdown_ref,
                  y_ref, bk_ref, bs_ref, sk_ref, ss_ref, gr_ref, gb_ref, ga_ref, vec_ref,
                  resid_ref, out_ref, gn2_ref, n2_ref):
    step = pl.program_id(0)
    first = at_ref[0] == 0

    @pl.when(step == 0)
    def _():
        resid = x_ref[...].astype(f32) + (dot(att_ref[...], wout_ref[...]) + vec(bout_ref))
        resid_ref[...] = resid
        n, _ = norm_parts(resid)
        n2 = (n * vec(gain_ref) + vec(bias_ref)).astype(bf16)
        n2_ref[...] = n2
        sk_ref[...] = jnp.where(first, g_ref[...], n2)
        ss_ref[...] = jnp.where(first, n2, g_ref[...])
        out_ref[...] = jnp.zeros_like(out_ref)
        gn2_ref[...] = jnp.zeros_like(gn2_ref)

    g = g_ref[...]
    pre = dot(n2_ref[...], wup_ref[...]) + vec(bup_ref)
    sq = pre * pre
    t = jnp.tanh(0.7978845608028654 * (pre + 0.044715 * sq * pre))
    half = 0.5 + 0.5 * t
    act = (pre * half).astype(bf16)
    slope = half + (0.5 * 0.7978845608028654) * pre * (1.0 - t * t) * (1.0 + (3 * 0.044715) * sq)
    gp = (slope * dot_nt(g, wdown_ref[...])).astype(bf16)
    bk_ref[...] = jnp.where(first, act, gp)
    bs_ref[...] = jnp.where(first, gp, act)
    put_rows(vec_ref, 24 + step * (FC // 128), jnp.sum(gp.astype(f32), axis=0, keepdims=True))
    out_ref[...] += dot(act, wdown_ref[...])
    gn2_ref[...] += dot_nt(gp, wup_ref[...])

    @pl.when(step == pl.num_programs(0) - 1)
    def _():
        resid = resid_ref[...]
        gf = g.astype(f32)
        y_ref[...] = (resid + (out_ref[...] + vec(bdown_ref))).astype(bf16)
        n, rstd = norm_parts(resid)
        e = gn2_ref[...]
        gr = gf + norm_back(e, n, rstd, vec(gain_ref))
        gr_ref[...] = gr
        gb = gr.astype(bf16)
        gb_ref[...] = gb
        ga_ref[...] = dot_nt(gb, wout_ref[...]).astype(bf16)
        put_rows(vec_ref, 0, jnp.sum(gf, axis=0, keepdims=True))
        put_rows(vec_ref, 6, jnp.sum(e * n, axis=0, keepdims=True))
        put_rows(vec_ref, 12, jnp.sum(e, axis=0, keepdims=True))
        put_rows(vec_ref, 18, jnp.sum(gb.astype(f32), axis=0, keepdims=True))


def leave_kernel(at_ref, x_ref, gain_ref, wq_ref, wkv_ref, gq_ref, parts_ref, gr_ref, mid_ref, gin_ref, keep_ref, send_ref, vec_ref):
    gkv = jnp.sum(parts_ref[...].astype(f32), axis=0).astype(bf16)
    gq = gq_ref[...]
    e = dot_nt(gq, wq_ref[...]) + dot_nt(gkv, wkv_ref[...])
    n, rstd = norm_parts(x_ref[...].astype(f32))
    gin_ref[...] = gr_ref[...] + norm_back(e, n, rstd, vec(gain_ref))
    gkv = gkv.astype(f32)
    vec_ref[0:48, :] = mid_ref[...]
    vec_ref[48:128, :] = jnp.zeros((80, 128), f32)
    put_rows(vec_ref, 48, jnp.sum(e * n, axis=0, keepdims=True))
    put_rows(vec_ref, 54, jnp.sum(e, axis=0, keepdims=True))
    put_rows(vec_ref, 60, jnp.sum(gq.astype(f32), axis=0, keepdims=True))
    put_rows(vec_ref, 66, jnp.sum(gkv, axis=0, keepdims=True))
    first = at_ref[0] == 0
    vecs = vec_ref[...]
    keep_ref[...] = jnp.where(first, gkv, vecs)
    send_ref[...] = jnp.where(first, vecs, gkv)


def pack_kernel(bk_ref, sk_ref, bp_ref, sp_ref, out_ref):
    for i in range(4):
        cols = slice(i * D, (i + 1) * D)
        out_ref[i, 0:ROWS, 0:D] = bk_ref[:, cols]
        out_ref[i, ROWS:, 0:D] = bp_ref[:, cols]
        out_ref[i, 0:ROWS, D:] = sk_ref[...]
        out_ref[i, ROWS:, D:] = sp_ref[...]

def quarters(at, which, total_ref, outs):
    rows = total_ref.shape[0]//4
    for rel, out in zip((0,1,3,2), outs):
        out[...] = total_ref[pl.ds(pl.multiple_of(((at[which]+rel)&3)*rows, rows), rows), :].astype(out.dtype)

def weight_kernel(at_ref, slab_ref, own_ref, plus_ref, minus_ref, far_ref, total_ref):
    @pl.when(at_ref[0] == 0)
    def _():
        total_ref[...] = sum(dot_tn(slab_ref[i, :, :D], slab_ref[i, :, D:]) for i in range(4))

    @pl.when(at_ref[0] == 1)
    def _():
        total_ref[...] = sum(dot_tn(slab_ref[i, :, D:], slab_ref[i, :, :D]) for i in range(4))

    quarters(at_ref, 2, total_ref, (own_ref, plus_ref, minus_ref, far_ref))


def join_kernel(at_ref,a_ref,b_ref,c_ref,d_ref,out_ref):
    rows=a_ref.shape[0]
    for rel, v in zip(FROM,(a_ref,b_ref,c_ref,d_ref)):
        out_ref[pl.ds(pl.multiple_of(((at_ref[2]+rel)&3)*rows,rows),rows),:] = v[...]

def place_kernel(at_ref, own_ref, other_ref, *rest):
    down_ref, up_ref = rest[-2:]
    first = at_ref[0]==0
    own, other = own_ref[...], other_ref[...]
    down_ref[...] = jnp.where(first, own, other).astype(f32)
    up_ref[...] = jnp.where(first, other, own).astype(f32)

def place(at, rel, own, other, kept):
    tile=256
    n=D//tile
    piece=pl.BlockSpec((tile,D), lambda i,at: (i,0))
    outs=(pl.BlockSpec((tile,D), lambda i,at: (((at[4]+rel)&3)*n+i,0)), pl.BlockSpec((tile,D), lambda i,at: (i,(at[5]+rel)&3)))
    anyspec=pl.BlockSpec(memory_space=pl.ANY)
    return pl.pallas_call(place_kernel,
        grid_spec=pltpu.PrefetchScalarGridSpec(num_scalar_prefetch=1, grid=(n,), in_specs=[piece,piece]+[anyspec]*len(kept), out_specs=outs),
        out_shape=shapes(((FF,D),f32),((D,FF),f32)),
        input_output_aliases={3:0,4:1} if kept else {},
        compiler_params=params(), cost_estimate=cost(0,8e6), name="place")(at, own, other, *kept)


def late_kernel(at_ref, lk_ref, lo_ref, rk_ref, ro_ref, tk_ref, to_ref, out_ref, total_ref):
    first = at_ref[0] == 0
    lk, lo = lk_ref[...], lo_ref[...]
    total_ref[:, 0:D] = dot_tn(lk, rk_ref[...]) + dot_tn(lo, ro_ref[...])

    @pl.when(first)
    def _():
        total_ref[:, D : D + 128] = dot_tn(lk, tk_ref[...].astype(bf16)) + dot_tn(lo, to_ref[...].astype(bf16))

    @pl.when(jnp.logical_not(first))
    def _():
        total_ref[0:128, D : D + 128] = tk_ref[...] + to_ref[...]
        total_ref[128:, D : D + 128] = jnp.zeros((D - 128, 128), f32)

    total_ref[:, D + 128 :] = jnp.zeros((D, 128), f32)
    for a in range(8):
        for b in range(8):
            out_ref[a * 8 + b] = total_ref[a * 96 : a * 96 + 96, b * 128 : b * 128 + 128].astype(bf16)


def late_sum_kernel(parts_ref, out_ref):
    total = jnp.sum(parts_ref[...].astype(f32), axis=0).astype(bf16)
    for i in range(64):
        out_ref[i] = total


VECTORS = ((0, 6), (6, 6), (12, 6), (18, 6), (24, 24), (48, 6), (54, 6), (60, 6))


def late_place_kernel(at_ref, own_ref, other_ref, query_ref, out_ref, kv_ref, value_ref, *vec_refs):
    first = at_ref[0] == 0
    for a in range(8):
        rows = slice(a * 96, a * 96 + 96)
        for b in range(7):
            own, other = own_ref[a * 8 + b].astype(f32), other_ref[a * 8 + b].astype(f32)
            zero, one = jnp.where(first, own, other), jnp.where(first, other, own)
            if b < 6:
                cols = slice(b * 128, b * 128 + 128)
                query_ref[rows, cols] = zero
                out_ref[rows, cols] = one
            else:
                kv_ref[rows, :] = zero
            if b == 6 and a == 0:
                value_ref[...] = one[66, HD:]
                for ref, (at, count) in zip(vec_refs, VECTORS):
                    for i in range(count):
                        ref[i * 128 : (i + 1) * 128] = one[at + i]


def call(kernel, args, outs, scratch=(), name=None, flops=0, nbytes=2e6, after=()):
    given, extra = len(args), len(after)
    run = lambda *refs: kernel(*refs[:given], *refs[given + extra :])
    return pl.pallas_call(
        run,
        out_shape=outs,
        in_specs=[SMEM if v.dtype == jnp.int32 and v.ndim == 1 else VMEM for v in args] + [ANY] * extra,
        out_specs=jax.tree.map(lambda _: VMEM, outs),
        scratch_shapes=list(scratch),
        compiler_params=params(),
        cost_estimate=cost(flops, nbytes),
        name=name,
    )(*args, *after)


def shapes(*pairs):
    return tuple(jax.ShapeDtypeStruct(s, t) for s, t in pairs)


def positions(lengths, splits, wide_index, core):
    ends = jnp.cumsum(lengths, dtype=jnp.int32)
    starts = ends - lengths
    first = lengths * jnp.minimum(splits[:, 0], splits[:, 1]) // 1024
    second = lengths * jnp.maximum(splits[:, 0], splits[:, 1]) // 1024

    def place(row):
        shape = (1,) * row.ndim + (-1,)
        s, e, a, b, n = (v.reshape(shape) for v in (starts, ends, first, second, lengths))
        row = row[..., None]
        inside = (row >= s) & (row < e)
        u = row - s
        moved = jnp.where(u < a, u, jnp.where(u >= b, a + u - b, a + n - b + u - a))
        return (
            jnp.sum(jnp.where(inside, s + moved, 0), axis=-1, dtype=jnp.int32),
            jnp.sum(jnp.where(inside, s, 0), axis=-1, dtype=jnp.int32),
        )

    k = jnp.arange(KB, dtype=jnp.int32)[:, None, None]
    j = jnp.arange(CHIPS, dtype=jnp.int32) * 2
    j = jnp.concatenate([j + core, j + 1 - core])[None, :, None]
    r = jnp.arange(KBR, dtype=jnp.int32)[None, None, :]
    keys, _ = place(((k * KBR + r) * WIDE + j).reshape(KB, KEYS))
    own, own_start = place(jnp.arange(ROWS, dtype=jnp.int32) * WIDE + wide_index)
    low, high = jnp.min(keys, axis=1), jnp.max(keys, axis=1)
    blocks, block_starts = own.reshape(RB, RBR), own_start.reshape(RB, RBR)
    top, start_low = jnp.max(blocks, axis=1), jnp.min(block_starts, axis=1)
    bottom, start_high = jnp.min(blocks, axis=1), jnp.max(block_starts, axis=1)
    some = (low[None] <= top[:, None]) & (high[None] >= start_low[:, None])
    every = (high[None] <= bottom[:, None]) & (low[None] >= start_high[:, None])
    kinds = jnp.where(every, 2, jnp.where(some, 1, 0)).astype(jnp.int32).reshape(-1)
    return keys, own, own_start, kinds


NARROW = ((ROWS, D), bf16)


def attend(*args):
    stat = pltpu.VMEM((RB, 1, QB), f32)
    return call(
        forward_kernel, args,
        shapes(NARROW, NARROW, NARROW, ((RB, QB, 128), bf16), ((RB, QB, 128), f32), ((RB, 1, QB), f32), ((WIDE, ROWS, 2 * HD), bf16)),
        [stat, stat, pltpu.VMEM((RB, 2 * HD, QB), f32), pltpu.VMEM((2 * HD, KEYS), bf16)],
        name="attend", flops=4 * ROWS * H * WINDOW * 64, nbytes=4e6,
    )


def attend_back(*args, after=()):
    return call(
        backward_kernel, args,
        shapes(NARROW, NARROW, NARROW, ((WIDE, ROWS, 2 * HD), bf16)),
        [
            pltpu.VMEM((RB, QB, 128), bf16), pltpu.VMEM((RB, 8, QB), f32),
            pltpu.VMEM((RB, 128, QB), f32), pltpu.VMEM((KEYS, 2 * HD), f32), pltpu.VMEM((2 * HD, KEYS), bf16),
        ],
        name="attend_back", flops=10 * ROWS * H * WINDOW * 64, nbytes=8e6, after=after,
    )


def coords():
    x, y, z, c = (lax.axis_index(a) for a in AXES)
    first = c == 0
    at = (c, jnp.where(first, z, y), jnp.where(first, y, x), jnp.where(first, x, z), z, y)
    return jnp.stack(at).astype(jnp.int32)


def halves_kernel(before_ref, after_ref, low_ref, high_ref):
    low_ref[...] = before_ref[D // 2 :, :]
    high_ref[...] = after_ref[: D // 2, :]


def stack_kernel(high_ref, low_ref, out_ref):
    out_ref[: D // 2, :] = high_ref[...]
    out_ref[D // 2 :, :] = low_ref[...]


QUARTER = ((D // 4, D), bf16)
HALF = ((D // 2, D), bf16)


def pair_sums(a, b, c, d):
    a, b, c, d = (v.astype(f32) for v in (a, b, c, d))
    return ((a + d) + (b + c)).astype(bf16)


def tie_kernel(v_ref, *refs):
    pass


def tie(v, *after):
    return pl.pallas_call(
        tie_kernel,
        out_shape=jax.ShapeDtypeStruct(v.shape, v.dtype),
        in_specs=[ANY] * (1 + len(after)),
        out_specs=ANY,
        input_output_aliases={0: 0},
        cost_estimate=cost(0, 0),
        name="tie",
    )(v, *after)


def feed_forward_spread(at, totals, before_join, before_far):
    u = call(join_kernel, (at,) + totals, shapes(((D, D), bf16))[0], name="join", after=before_join)
    before, after = send(u, 0, 1), send(u, 0, 3)
    kept = place(at, 0, u, swap(u), ())
    low, high = call(halves_kernel, (before, after), shapes(HALF, HALF), name="halves", after=kept[:1])
    low, high = send(low, 0, 1), send(high, 0, 3)
    kept = place(at, 3, before, swap(before), kept)
    kept = place(at, 1, after, swap(after), kept)
    far = call(stack_kernel, (high, low), shapes(((D, D), bf16))[0], name="stack", after=kept[:1] + tuple(before_far))
    return place(at, 2, far, swap(far), kept)


def body(block_input, file_lengths, file_splits, ln1_gain, ln1_bias, w_query, b_query, w_kv, b_value, w_out, b_out,
         ln2_gain, ln2_bias, w_up, b_up, w_down, b_down, out_cotangent):
    x = block_input.reshape(ROWS, D)
    g = out_cotangent.reshape(ROWS, D)
    wide = ("y", "z", "c")
    at = coords()
    narrow = NARROW

    n1, copies = call(enter_kernel, (x, ln1_gain, ln1_bias, w_kv, b_value), shapes(narrow, ((CHIPS, ROWS, 2 * HD), bf16)),
                      name="enter", flops=2 * ROWS * D * 128)
    kv_same = lax.all_to_all(copies, ("y", "z"), 0, 0, tiled=True)
    keys, own, own_start, kinds = positions(file_lengths[0], file_splits[0], lax.axis_index(wide), at[0])
    key_cols = jnp.broadcast_to(keys[:, :, None], (KB, KEYS, 128))
    own_lanes = jnp.tile(own.reshape(RB, 1, RBR), (1, 1, 128 // RBR))
    start_lanes = jnp.tile(own_start.reshape(RB, 1, RBR), (1, 1, 128 // RBR))
    q = call(query_kernel, (n1, w_query, b_query), shapes(narrow)[0], name="query", flops=2 * ROWS * D * D,
             after=(key_cols, own_lanes, start_lanes, kinds))
    kv_other = swap(tie(kv_same, q))

    att, left, left_send, xq, o, lse, kv_all = attend(at, kinds, q, kv_same, kv_other, key_cols, own_lanes, start_lanes, n1)
    left_other = swap(left_send)

    steps = FF // FC
    whole = lambda *s: pl.BlockSpec(s, lambda i: (0,) * len(s))
    wide_cols = pl.BlockSpec((ROWS, FC), lambda i: (0, i))
    y, big, big_send, small, small_send, gr, gb, ga, vec_mid = pl.pallas_call(
        middle_kernel,
        grid=(steps,),
        out_shape=shapes(narrow, ((ROWS, FF), bf16), ((ROWS, FF), bf16), narrow, narrow, ((ROWS, D), f32), narrow, narrow, ((48, 128), f32)),
        in_specs=[
            SMEM, whole(ROWS, D), whole(ROWS, D), whole(ROWS, D), whole(D, D), whole(D), whole(D), whole(D),
            pl.BlockSpec((D, FC), lambda i: (0, i)), pl.BlockSpec((FC,), lambda i: (i,)),
            pl.BlockSpec((FC, D), lambda i: (i, 0)), whole(D),
        ],
        out_specs=(
            whole(ROWS, D), wide_cols, wide_cols, whole(ROWS, D), whole(ROWS, D), whole(ROWS, D), whole(ROWS, D),
            whole(ROWS, D), whole(48, 128),
        ),
        scratch_shapes=[pltpu.VMEM((ROWS, D), f32)] * 3 + [pltpu.VMEM((ROWS, D), bf16)],
        compiler_params=params(),
        cost_estimate=cost(8 * ROWS * D * FF, 2e7),
        name="middle",
    )(at, att, x, g, w_out, b_out, ln2_gain, ln2_bias, w_up, b_up, w_down, b_down)

    packed = call(pack_kernel, (big, small, swap(big_send), swap(small_send)), shapes(((4, 2 * ROWS, 2 * D), bf16))[0], name="pack")
    slabs = lax.all_to_all(packed, AXES, 0, 0, axis_index_groups=ring_groups(0), tiled=True)

    gq, right, right_send, dkv = attend_back(at, kinds, xq, ga, o, lse, kv_all, key_cols, own_lanes, start_lanes, gb, after=(packed,))
    parts = lax.all_to_all(tie(dkv, slabs), wide, 0, 0, tiled=True)
    right_other = swap(right_send)

    pieces = call(weight_kernel, (at, slabs), shapes(*[QUARTER] * 4), [pltpu.VMEM((D, D), f32)], name="weights")
    ff_parts = (pieces[0],) + spread(1, *pieces[1:])
    gin, tail, tail_send, _ = call(
        leave_kernel, (at, x, ln1_gain, w_query, w_kv, gq, parts, gr, vec_mid),
        shapes(((ROWS, D), f32), ((128, 128), f32), ((128, 128), f32), ((128, 128), f32)),
        name="leave", flops=2 * ROWS * D * 900, nbytes=4e6, after=pieces[:1],
    )

    late_pieces = call(late_kernel, (at, left, left_other, right, right_other, tail, swap(tail_send)),
                  shapes(((64, 96, 128), bf16))[0], [pltpu.VMEM((D, 1024), f32)], name="late", after=ff_parts[1:])
    space = ("x", "y", "z")
    arrived = lax.all_to_all(late_pieces, space, 0, 0, tiled=True)
    ff_total = pair_sums(*gather4(pair_sums(*ff_parts), 2))
    ff_totals = gather4(ff_total, 1)
    copies = call(late_sum_kernel, (arrived,), shapes(((64, 96, 128), bf16))[0], name="late_sum", after=ff_totals[1:])
    late = lax.all_to_all(copies, space, 0, 0, tiled=True)
    one = lambda n: ((n,), f32)
    outs = call(
        late_place_kernel, (at, late, swap(late)),
        shapes(((D, D), f32), ((D, D), f32), ((D, 128), f32), one(HD), *[one(128 * n) for _, n in VECTORS]), name="late_place",
    )
    g_query, g_out, g_kv, g_value, g_bdown, g_gain2, g_bias2, g_bout, g_bup, g_gain1, g_bias1, g_bq = outs
    g_down, g_up = feed_forward_spread(at, ff_totals, (copies,), outs[:1])
    shape = block_input.shape
    return (
        y.reshape(shape), gin.reshape(shape), g_gain1, g_bias1, g_query, g_bq, g_kv, g_value,
        g_out, g_bout, g_gain2, g_bias2, g_up, g_bup, g_down, g_bdown,
    )


def solution(mesh):
    split = P("x", None, ("y", "z", "c"), None)
    return jax.shard_map(
        body,
        mesh=Mesh(mesh.devices.reshape(4, 4, 4, 2), AXES),
        in_specs=(split, P("x", None), P("x", None, None)) + (P(),) * 14 + (split,),
        out_specs=(split, split) + (P(),) * 14,
        check_vma=False,
    )
```

time: 320 us -> 257 us (0.80)
  blocking collectives: 68.6 us -> 0 us
  starting transfers between devices: 13.9 us -> 62.9 us
  waiting for transfers between devices: 113 us -> 64.5 us
  Pallas kernels: 61.7 us -> 104 us
  other arithmetic: 16.9 us -> 3.48 us
  between operations: 14.3 us -> 1.04 us
  matrix products: 11.9 us -> 0 us
    psum x1 -> x0, waiting for transfers between devices: 99.4 us -> none  [body(): sums = lax.psum(tuple((v.astype(bf16) for v in grads)), ('win', 'wide'))]
    psum x1 -> x0, blocking collectives: 68.6 us -> none  [body(): lax.psum((vec_mid, gb_up, vec_end), ('win', 'wide'))]
    ppermute x0 -> x24, waiting for transfers between devices: none -> 44 us  [the longest x13 37.8 us: send(): return lax.ppermute(v, AXES, ring(place, shift))]
    pallas_call x6 -> x20, Pallas kernels: 61.7 us -> 104 us  [the longest x13 73.4 us: call(): pl.pallas_call(run, out_shape=outs, in_specs=[SMEM if v.dtype == jnp.int3...]
    ppermute x0 -> x24, starting transfers between devices: none -> 29.5 us  [the longest x13 16 us: send(): return lax.ppermute(v, AXES, ring(place, shift))]
    all_to_all x2 -> x5, starting transfers between devices: 13.7 us -> 33.4 us  [the longest x1 8.6 us: body(): kv_same = lax.all_to_all(copies, ('y', 'z'), 0, 0, tiled=True)]
    convert_element_type x5 -> x2, other arithmetic: 15.9 us -> 0.29 us  [pair_sums(): return (a + d + (b + c)).astype(bf16)]
    dot_general x5 -> x0, matrix products: 11.9 us -> none  [dot_tn(): lax.dot_general(a, b, (((0,), (0,)), ((), ())), preferred_element_type=f32)]
  transfers between devices with their start and end apart: 3 -> 29, of which waited for: 3 -> 13; matrix products, arithmetic and copies ran while one was open for 6% -> 4% of each run, Pallas kernels for 1% -> 22%
where the time goes in v2:
time: 257 us; the launch traced here: 256 us
  Pallas kernels  104 us (40%)
  waiting for transfers between devices  64.5 us (25%)
  starting transfers between devices  62.9 us (24%)
  local copies, waits for them, and re-layouts  19.3 us (8%)
  other arithmetic  3.48 us (1%)
    pallas_call x13, Pallas kernels, call(): pl.pallas_call(run, out_shape=outs, in_specs=[SMEM if v.dtype == jnp.int3...  73.4 us
    ppermute x13, waiting for transfers between devices, send(): return lax.ppermute(v, AXES, ring(place, shift))  37.8 us
    pallas_call x4, Pallas kernels, place(): pl.pallas_call(place_kernel, grid_spec=pltpu.PrefetchScalarGridSpec(num_s...  19.4 us
    ppermute x13, starting transfers between devices, send(): return lax.ppermute(v, AXES, ring(place, shift))  16 us
    unnamed x66, local copies, waits for them, and re-layouts  14.1 us
    all_to_all x1, waiting for transfers between devices, body(): late = lax.all_to_all(copies, space, 0, 0, tiled=True)  13.6 us
    ppermute x11, starting transfers between devices, swap(): return lax.ppermute(v, 'c', [(0, 1), (1, 0)])  13.5 us
    pallas_call x1, Pallas kernels, body(): pl.pallas_call(middle_kernel, grid=(steps,), out_shape=shapes(narrow, ((R...  11.5 us
  transfers between devices with their start and end apart: 29, of which 13 were waited for; matrix products, arithmetic and copies ran while one was open for 4% of the time, Pallas kernels for 22%

profile of v2, /device:TPU:1, one launch (start us, length us, event | category | flops | bytes accessed | tf_op | source)
XLA Modules:
  0.0 255.6 jit_solution(1153929616673335672)
XLA Ops:
  0.6 2.2 enter.1
  2.9 8.6 %all-to-all-start = ((bf16[16,128,128]{2,1,0:T(8,128)(2,1)}), bf16[16,128,128]{2,1,0:T(8,128)(2,1)S(1)}, u32[]{:S(2)}, u32[]{:S(2)}) async-start(bf16[16,128,128]{2,1,0:T(8,128)(2,1)} %get-tuple-element.68), calls=%async_computation | async-start | bytes 1048576 | tf_op jit(solution)/shard_map/all_to_all | solution.py:577
  17.1 2.2 broadcast_in_dim.28.refs_3_.refs_5_.refs_7_
  19.3 2.3 query.1.refs_0_.refs_2_
  22.6 2.1 collective-permute-start
  27.3 17.8 %attend.1 = (bf16[128,768]{1,0:T(8,128)(2,1)}, bf16[128,768]{1,0:T(8,128)(2,1)}, bf16[128,768]{1,0:T(8,128)(2,1)}, bf16[2,768,128]{2,1,0:T(8,128)(2,1)}, f32[2,7...) custom-call(s32[6]{0:T(128)} %stack.28.refs_0_.at_ref, s32[8]{0:T(128)} %select_n.94.refs_6_.refs_1_, ...), custom_call_target="tpu_custom_call" | custom-call | flops 1 | bytes 1 | tf_op jit(solution)/shard_map/attend/pallas_call | solution.py:438
  45.1 11.5 %middle.1 = (bf16[128,768]{1,0:T(8,128)(2,1)}, bf16[128,3072]{1,0:T(8,128)(2,1)}, bf16[128,3072]{1,0:T(8,128)(2,1)}, bf16[128,768]{1,0:T(8,128)(2,1)}, bf16[128,...) custom-call(s32[6]{0:T(128)} %stack.28.refs_0_.at_ref, ...), custom_call_target="tpu_custom_call" | custom-call | flops 1 | bytes 1 | tf_op jit(solution)/shard_map/middle/pallas_call | solution.py:592
  57.2 2.3 collective-permute-done.2.refs_3_
  60.5 3.4 %pack.1.refs_11_ = bf16[4,256,1536]{2,1,0:T(8,128)(2,1)} custom-call(bf16[128,3072]{1,0:T(8,128)(2,1)} %get-tuple-element.77.refs_0_, bf16[128,768]{1,0:T(8,128)(2,1)} %get-tuple-element.78.refs_1_, bf16[128,3072]{1,0:T(8,128)(2,1)} %copy-done.21, bf16[128,768]{1,0:T(8,128)(2,1)} %copy-done.26), custom_call_target="tpu_custom_call" | custom-call | flops 1 | bytes 1 | tf_op jit(solution)/shard_map/pack/pallas_call | solution.py:438
  63.8 3.9 %all-to-all-start.1 = ((bf16[4,256,1536]{2,1,0:T(8,128)(2,1)}), bf16[4,256,1536]{2,1,0:T(8,128)(2,1)S(1)}, u32[]{:S(2)}, u32[]{:S(2)}) async-start(bf16[4,256,1536]{2,1,0:T(8,128)(2,1)} %pack.1.refs_11_), calls=%async_computation.1 | async-start | bytes 6291456 | tf_op jit(solution)/shard_map/all_to_all | solution.py:612
  67.7 21.5 %attend_back.1 = (bf16[128,768]{1,0:T(8,128)(2,1)}, bf16[128,768]{1,0:T(8,128)(2,1)}, bf16[128,768]{1,0:T(8,128)(2,1)}, bf16[32,128,128]{2,1,0:T(8,128)(2,1)}) custom-call(s32[6]{0:T(128)} %stack.28.refs_0_.at_ref, s32[8]{0:T(128)} %select_n.94.refs_6_.refs_1_, bf16[2,768,128]{2,1,0:T(8,128)(2,1)} %get-tuple-element.71.refs_2_, ...), custom_call_target="tpu_custom_call" | custom-call | flops 1 | bytes 1 | tf_op jit(solution)/shard_map/attend_back/pallas_call | solution.py:438
  89.2 1.7 copy-done
  90.9 7.2 %all-to-all-start.2 = ((bf16[32,128,128]{2,1,0:T(8,128)(2,1)}), bf16[32,128,128]{2,1,0:T(8,128)(2,1)S(1)}, u32[]{:S(2)}, u32[]{:S(2)}) async-start(bf16[32,128,128]{2,1,0:T(8,128)(2,1)} %tie.3), calls=%async_computation.2 | async-start | bytes 2097152 | tf_op jit(solution)/shard_map/all_to_all | solution.py:615
  98.1 4.5 %weights.1 = (bf16[192,768]{1,0:T(8,128)(2,1)}, bf16[192,768]{1,0:T(8,128)(2,1)}, bf16[192,768]{1,0:T(8,128)(2,1)}, bf16[192,768]{1,0:T(8,128)(2,1)}) custom-call(s32[6]{0:T(128)} %stack.28.refs_0_.at_ref, bf16[4,256,1536]{2,1,0:T(8,128)(2,1)} %copy-done), custom_call_target="tpu_custom_call" | custom-call | flops 1 | bytes 1 | tf_op jit(solution)/shard_map/weights/pallas_call | solution.py:438
  103.8 1.4 collective-permute-start.7
  106.3 1.9 collective-permute-start.3
  108.2 6.7 %all-to-all-done.2.refs_6_ = bf16[32,128,128]{2,1,0:T(8,128)(2,1)S(1)} async-done(((bf16[32,128,128]{2,1,0:T(8,128)(2,1)}), bf16[32,128,128]{2,1,0:T(8,128)(2,1)S(1)}, u32[]{:S(2)}, u32[]{:S(2)}) %all-to-all-start.2) | async-done | bytes 1048608 | tf_op jit(solution)/shard_map/all_to_all | solution.py:615
  115.9 3.5 %leave.1 = (f32[128,768]{1,0:T(8,128)}, f32[128,128]{1,0:T(8,128)}, f32[128,128]{1,0:T(8,128)}, f32[128,128]{1,0:T(8,128)}) custom-call(s32[6]{0:T(128)} %stack.28.refs_0_.at_ref, bf16[128,768]{1,0:T(8,128)(2,1)} %bitcast.59, bf16[768]{0:T(1024)(128)(2,1)} %refs_2_.5, bf16[768,768]{1,0:T(8,128)(2,1)} %refs_3_.3, bf16[768,128]{1,0:T(8,128)(2,1)} %refs_4_.3, ...), custom_call_target="tpu_custom_call" | custom-call | flops 1 | bytes 1 | tf_op jit(solution)/shard_map/leave/pallas_call | solution.py:438
  119.7 1.3 collective-permute-done.5.refs_6_
  121.6 3.4 %late.1 = bf16[64,96,128]{2,1,0:T(8,128)(2,1)} custom-call(s32[6]{0:T(128)} %stack.28.refs_0_.at_ref, bf16[128,768]{1,0:T(8,128)(2,1)} %get-tuple-element.87.refs_1_, bf16[128,768]{1,0:T(8,128)(2,1)} %copy-done.27, bf16[128,768]{1,0:T(8,128)(2,1)} %get-tuple-element.89.refs_3_, bf16[128,768]{1,0:T(8,128)(2,1)} %copy-done.28, ...), custom_call_target="tpu_custom_call" | custom-call | flops 1 | bytes 1 | tf_op jit(solution)/shard_map/late/pallas_call | solution.py:438
  125.0 6.8 %all-to-all-start.3 = ((bf16[64,96,128]{2,1,0:T(8,128)(2,1)}), bf16[64,96,128]{2,1,0:T(8,128)(2,1)S(1)}, u32[]{:S(2)}, u32[]{:S(2)}) async-start(bf16[64,96,128]{2,1,0:T(8,128)(2,1)} %late.1), calls=%async_computation.3 | async-start | bytes 3145728 | tf_op jit(solution)/shard_map/all_to_all | solution.py:629
  133.1 1.7 collective-permute-start.11
  134.8 1.3 collective-permute-start.9
  136.1 18.7 %collective-permute-done.10 = bf16[192,768]{1,0:T(8,128)(2,1)S(1)} collective-permute-done((bf16[192,768]{1,0:T(8,128)(2,1)S(1)}, bf16[192,768]{1,0:T(8,128)(2,1)S(1)}, u32[]{:S(2)}, u32[]{:S(2)}) %collective-permute-start.10) | collective-permute-done | bytes 294944 | tf_op jit(solution)/shard_map/ppermute | solution.py:95
  154.8 2.6 %collective-permute-done.11 = bf16[192,768]{1,0:T(8,128)(2,1)S(1)} collective-permute-done((bf16[192,768]{1,0:T(8,128)(2,1)S(1)}, bf16[192,768]{1,0:T(8,128)(2,1)S(1)}, u32[]{:S(2)}, u32[]{:S(2)}) %collective-permute-start.11) | collective-permute-done | bytes 294944 | tf_op jit(solution)/shard_map/ppermute | solution.py:95
  157.4 1.6 collective-permute-done.9
  159.1 1.3 collective-permute-start.12
  160.4 1.5 collective-permute-start.13
  161.9 1.4 collective-permute-start.14
  163.2 3.0 %collective-permute-done.12.refs_1_.refs_2_ = bf16[192,768]{1,0:T(8,128)(2,1)S(1)} collective-permute-done((bf16[192,768]{1,0:T(8,128)(2,1)S(1)}, bf16[192,768]{1,0:T(8,128)(2,1)S(1)}, u32[]{:S(2)}, u32[]{:S(2)}) %collective-permute-start.12) | collective-permute-done | bytes 294944 | tf_op jit(solution)/shard_map/ppermute | solution.py:95
  166.3 3.8 %collective-permute-done.14.refs_3_.refs_4_ = bf16[192,768]{1,0:T(8,128)(2,1)S(1)} collective-permute-done((bf16[192,768]{1,0:T(8,128)(2,1)S(1)}, bf16[192,768]{1,0:T(8,128)(2,1)S(1)}, u32[]{:S(2)}, u32[]{:S(2)}) %collective-permute-start.14) | collective-permute-done | bytes 294944 | tf_op jit(solution)/shard_map/ppermute | solution.py:95
  171.9 2.8 %late_sum.1.refs_5_ = bf16[64,96,128]{2,1,0:T(8,128)(2,1)} custom-call(bf16[64,96,128]{2,1,0:T(8,128)(2,1)} %copy-done.2, bf16[192,768]{1,0:T(8,128)(2,1)} %copy-done.18, bf16[192,768]{1,0:T(8,128)(2,1)} %copy-done.19, bf16[192,768]{1,0:T(8,128)(2,1)} %copy-done.20), custom_call_target="tpu_custom_call" | custom-call | flops 1 | bytes 1 | tf_op jit(solution)/shard_map/late_sum/pallas_call | solution.py:438
  174.7 7.0 %all-to-all-start.4 = ((bf16[64,96,128]{2,1,0:T(8,128)(2,1)}), bf16[64,96,128]{2,1,0:T(8,128)(2,1)S(1)}, u32[]{:S(2)}, u32[]{:S(2)}) async-start(bf16[64,96,128]{2,1,0:T(8,128)(2,1)} %late_sum.1.refs_5_), calls=%async_computation.4 | async-start | bytes 3145728 | tf_op jit(solution)/shard_map/all_to_all | solution.py:633
  181.7 2.3 join.1.own_ref
  185.1 1.7 collective-permute-start.17
  186.7 2.7 %collective-permute-start.18 = (bf16[768,768]{1,0:T(8,128)(2,1)}, bf16[768,768]{1,0:T(8,128)(2,1)}, u32[]{:S(2)}, u32[]{:S(2)}) collective-permute-start(bf16[768,768]{1,0:T(8,128)(2,1)} %join.1.own_ref), channel_id=1, source_target_pairs={{0,1},{1,0},{2,3},{3,2},{4,5},{5,4},{6,7},{7,6},{8,9},{9,8},{10,11... | collective-permute-start | bytes 3538952 | tf_op jit(solution)/shard_map/ppermute | solution.py:99
  189.4 13.6 %all-to-all-done.4.refs_1_ = bf16[64,96,128]{2,1,0:T(8,128)(2,1)S(1)} async-done(((bf16[64,96,128]{2,1,0:T(8,128)(2,1)}), bf16[64,96,128]{2,1,0:T(8,128)(2,1)S(1)}, u32[]{:S(2)}, u32[]{:S(2)}) %all-to-all-start.4) | async-done | bytes 1572896 | tf_op jit(solution)/shard_map/all_to_all | solution.py:633
  203.0 3.9 %collective-permute-start.15 = (bf16[64,96,128]{2,1,0:T(8,128)(2,1)S(1)}, bf16[64,96,128]{2,1,0:T(8,128)(2,1)S(1)}, u32[]{:S(2)}, u32[]{:S(2)}) collective-permute-start(bf16[64,96,128]{2,1,0:T(8,128)(2,1)S(1)} %all-to-all-done.4.refs_1_), channel_id=1, source_target_pairs={{0,1},{1,0},{2,3},{3,2},{4,5},{5,4},{6,7},{7,6},{8,9},{9,8},{10,11... | collective-permute-start | bytes 4718600 | tf_op jit(solution)/shard_map/ppermute | solution.py:99
  206.9 8.1 %collective-permute-done.16.refs_0_.own_ref = bf16[768,768]{1,0:T(8,128)(2,1)} collective-permute-done((bf16[768,768]{1,0:T(8,128)(2,1)}, bf16[768,768]{1,0:T(8,128)(2,1)}, u32[]{:S(2)}, u32[]{:S(2)}) %collective-permute-start.16) | collective-permute-done | bytes 1179680 | tf_op jit(solution)/shard_map/ppermute | solution.py:95
  216.1 4.8 %place.4 = (f32[3072,768]{1,0:T(8,128)}, f32[768,3072]{1,0:T(8,128)}) custom-call(s32[6]{0:T(128)} %stack.28.refs_0_.at_ref, bf16[768,768]{1,0:T(8,128)(2,1)} %join.1.own_ref, bf16[768,768]{1,0:T(8,128)(2,1)} %collective-permute-done.18.other_ref), custom_call_target="tpu_custom_call" | custom-call | flops 1 | bytes 1 | tf_op jit(solution)/shard_map/place/pallas_call | solution.py:379
  220.9 2.7 %halves.1 = (bf16[384,768]{1,0:T(8,128)(2,1)}, bf16[384,768]{1,0:T(8,128)(2,1)}) custom-call(bf16[768,768]{1,0:T(8,128)(2,1)} %collective-permute-done.16.refs_0_.own_ref, bf16[768,768]{1,0:T(8,128)(2,1)} %copy-done.3, f32[3072,768]{1,0:T(8,128)} %get-tuple-element.106.refs_2_.rest_0_), custom_call_target="tpu_custom_call" | custom-call | flops 1 | bytes 1 | tf_op jit(solution)/shard_map/halves/pallas_call | solution.py:438
  223.6 1.5 collective-permute-start.19
  226.1 4.8 %place.5 = (f32[3072,768]{1,0:T(8,128)}, f32[768,3072]{1,0:T(8,128)}) custom-call(s32[6]{0:T(128)} %stack.28.refs_0_.at_ref, bf16[768,768]{1,0:T(8,128)(2,1)} %collective-permute-done.16.refs_0_.own_ref, bf16[768,768]{1,0:T(8,128)(2,1)} %copy-done.8, f32[3072,768]{1,0:T(8,128)} %get-tuple-element.106.refs_2_.rest_0_, ...), custom_call_target="tpu_custom_call", output_to_operand_aliasing={{0}: (3, {}), {1}: (4, {})} | custom-call | flops 1 | bytes 1 | tf_op jit(solution)/shard_map/place/pallas_call | solution.py:379
  232.0 4.8 %place.6 = (f32[3072,768]{1,0:T(8,128)}, f32[768,3072]{1,0:T(8,128)}) custom-call(s32[6]{0:T(128)} %stack.28.refs_0_.at_ref, bf16[768,768]{1,0:T(8,128)(2,1)} %copy-done.3, bf16[768,768]{1,0:T(8,128)(2,1)} %copy-done.7, f32[3072,768]{1,0:T(8,128)} %get-tuple-element.110.rest_0_, ...), custom_call_target="tpu_custom_call", output_to_operand_aliasing={{0}: (3, {}), {1}: (4, {})} | custom-call | flops 1 | bytes 1 | tf_op jit(solution)/shard_map/place/pallas_call | solution.py:379
  238.0 4.5 %late_place.1 = (f32[768,768]{1,0:T(8,128)}, f32[768,768]{1,0:T(8,128)}, f32[768,128]{1,0:T(8,128)}, f32[64]{0:T(128)}, f32[768]{0:T(1024)}, /*index=5*/f32[768]...) custom-call(s32[6]{0:T(128)} %stack.28.refs_0_.at_ref, ...), custom_call_target="tpu_custom_call" | custom-call | flops 1 | bytes 1 | tf_op jit(solution)/shard_map/late_place/pallas_call | solution.py:438
  243.6 2.5 stack.29.own_ref
  248.1 1.5 collective-permute-done.23.other_ref
  250.7 4.8 %place.7 = (f32[3072,768]{1,0:T(8,128)}, f32[768,3072]{1,0:T(8,128)}) custom-call(s32[6]{0:T(128)} %stack.28.refs_0_.at_ref, bf16[768,768]{1,0:T(8,128)(2,1)} %stack.29.own_ref, bf16[768,768]{1,0:T(8,128)(2,1)} %copy-done.9, f32[3072,768]{1,0:T(8,128)} %get-tuple-element.112.refs_2_.rest_0_, ...), custom_call_target="tpu_custom_call", output_to_operand_aliasing={{0}: (3, {}), {1}: (4, {})} | custom-call | flops 1 | bytes 1 | tf_op jit(solution)/shard_map/place/pallas_call | solution.py:379
  (125 shorter events, 27.5 us)
Async XLA Ops:
  2.9 18.9 %all-to-all-start = ((bf16[16,128,128]{2,1,0:T(8,128)(2,1)}), bf16[16,128,128]{2,1,0:T(8,128)(2,1)S(1)}, u32[]{:S(2)}, u32[]{:S(2)}) async-start(bf16[16,128,128]{2,1,0:T(8,128)(2,1)} %get-tuple-element.68), calls=%async_computation | async-start | bytes 1048576 | tf_op jit(solution)/shard_map/all_to_all | solution.py:577
  21.8 4.7 %copy-start.4 = (bf16[16,128,128]{2,1,0:T(8,128)(2,1)}, bf16[16,128,128]{2,1,0:T(8,128)(2,1)S(1)}, u32[]{:S(2)}) copy-start(bf16[16,128,128]{2,1,0:T(8,128)(2,1)S(1)} %all-to-all-done.refs_3_) | copy-start | bytes 1572868
  22.6 3.9 %collective-permute-start = (bf16[16,128,128]{2,1,0:T(8,128)(2,1)}, bf16[16,128,128]{2,1,0:T(8,128)(2,1)S(1)}, u32[]{:S(2)}, u32[]{:S(2)}) collective-permute-start(bf16[16,128,128]{2,1,0:T(8,128)(2,1)} %tie.2), channel_id=1, source_target_pairs={{0,1},{1,0},{2,3},{3,2},{4,5},{5,4},{6,7},{7,6},{8,9},{9,8},{10,11... | collective-permute-start | bytes 1572872 | tf_op jit(solution)/shard_map/ppermute | solution.py:99
  56.6 2.9 %collective-permute-start.1 = (bf16[128,3072]{1,0:T(8,128)(2,1)}, bf16[128,3072]{1,0:T(8,128)(2,1)S(1)}, u32[]{:S(2)}, u32[]{:S(2)}) collective-permute-start(bf16[128,3072]{1,0:T(8,128)(2,1)} %get-tuple-element.79), channel_id=1, source_target_pairs={{0,1},{1,0},{2,3},{3,2},{4,5},{5,4},{6,7},{7,6},{8,9},{9,8},{10,11... | collective-permute-start | bytes 2359304 | tf_op jit(solution)/shard_map/ppermute | solution.py:99
  57.1 2.4 collective-permute-start.2
  63.8 25.4 %all-to-all-start.1 = ((bf16[4,256,1536]{2,1,0:T(8,128)(2,1)}), bf16[4,256,1536]{2,1,0:T(8,128)(2,1)S(1)}, u32[]{:S(2)}, u32[]{:S(2)}) async-start(bf16[4,256,1536]{2,1,0:T(8,128)(2,1)} %pack.1.refs_11_), calls=%async_computation.1 | async-start | bytes 6291456 | tf_op jit(solution)/shard_map/all_to_all | solution.py:612
  89.2 1.7 copy-start
  90.9 24.1 %all-to-all-start.2 = ((bf16[32,128,128]{2,1,0:T(8,128)(2,1)}), bf16[32,128,128]{2,1,0:T(8,128)(2,1)S(1)}, u32[]{:S(2)}, u32[]{:S(2)}) async-start(bf16[32,128,128]{2,1,0:T(8,128)(2,1)} %tie.3), calls=%async_computation.2 | async-start | bytes 2097152 | tf_op jit(solution)/shard_map/all_to_all | solution.py:615
  98.0 8.3 %copy-start.30 = (bf16[128,768]{1,0:T(8,128)(2,1)S(1)}, bf16[128,768]{1,0:T(8,128)(2,1)}, u32[]{:S(2)}) copy-start(bf16[128,768]{1,0:T(8,128)(2,1)} %get-tuple-element.88) | copy-start | bytes 589828
  98.0 10.1 %copy-start.31 = (bf16[128,768]{1,0:T(8,128)(2,1)S(1)}, bf16[128,768]{1,0:T(8,128)(2,1)}, u32[]{:S(2)}) copy-start(bf16[128,768]{1,0:T(8,128)(2,1)} %get-tuple-element.90) | copy-start | bytes 589828
  102.6 17.1 %collective-permute-start.6 = (bf16[192,768]{1,0:T(8,128)(2,1)}, bf16[192,768]{1,0:T(8,128)(2,1)S(1)}, u32[]{:S(2)}, u32[]{:S(2)}) collective-permute-start(bf16[192,768]{1,0:T(8,128)(2,1)} %get-tuple-element.93), channel_id=1, source_target_pairs={{0,8},{1,33},{2,10},{3,35},{4,12},{5,37},{6,14},{7,39},{8,16},{9,4... | collective-permute-start | bytes 884744 | tf_op jit(solution)/shard_map/ppermute | solution.py:95
  103.8 15.8 %collective-permute-start.7 = (bf16[192,768]{1,0:T(8,128)(2,1)}, bf16[192,768]{1,0:T(8,128)(2,1)S(1)}, u32[]{:S(2)}, u32[]{:S(2)}) collective-permute-start(bf16[192,768]{1,0:T(8,128)(2,1)} %get-tuple-element.94), channel_id=1, source_target_pairs={{0,24},{1,97},{2,26},{3,99},{4,28},{5,101},{6,30},{7,103},{8,0},{9... | collective-permute-start | bytes 884744 | tf_op jit(solution)/shard_map/ppermute | solution.py:95
  105.3 14.4 %collective-permute-start.8 = (bf16[192,768]{1,0:T(8,128)(2,1)}, bf16[192,768]{1,0:T(8,128)(2,1)S(1)}, u32[]{:S(2)}, u32[]{:S(2)}) collective-permute-start(bf16[192,768]{1,0:T(8,128)(2,1)} %get-tuple-element.95), channel_id=1, source_target_pairs={{0,16},{1,65},{2,18},{3,67},{4,20},{5,69},{6,22},{7,71},{8,24},{9,... | collective-permute-start | bytes 884744 | tf_op jit(solution)/shard_map/ppermute | solution.py:95
  106.3 13.1 %collective-permute-start.3 = (bf16[128,768]{1,0:T(8,128)(2,1)S(1)}, bf16[128,768]{1,0:T(8,128)(2,1)S(1)}, u32[]{:S(2)}, u32[]{:S(2)}) collective-permute-start(bf16[128,768]{1,0:T(8,128)(2,1)S(1)} %copy-done.30), channel_id=1, source_target_pairs={{0,1},{1,0},{2,3},{3,2},{4,5},{5,4},{6,7},{7,6},{8,9},{9,8},{10,11... | collective-permute-start | bytes 589832 | tf_op jit(solution)/shard_map/ppermute | solution.py:99
  108.2 11.5 %collective-permute-start.4 = (bf16[128,768]{1,0:T(8,128)(2,1)S(1)}, bf16[128,768]{1,0:T(8,128)(2,1)S(1)}, u32[]{:S(2)}, u32[]{:S(2)}) collective-permute-start(bf16[128,768]{1,0:T(8,128)(2,1)S(1)} %copy-done.31), channel_id=1, source_target_pairs={{0,1},{1,0},{2,3},{3,2},{4,5},{5,4},{6,7},{7,6},{8,9},{9,8},{10,11... | collective-permute-start | bytes 589832 | tf_op jit(solution)/shard_map/ppermute | solution.py:99
  119.4 1.6 copy-start.27
  119.4 1.5 collective-permute-start.5
  119.7 1.3 copy-start.28
  119.7 1.3 copy-start.12
  119.7 1.3 copy-start.14
  119.7 1.3 copy-start.16
  125.0 6.8 %copy-start.10 = (bf16[192,768]{1,0:T(8,128)(2,1)S(1)}, bf16[192,768]{1,0:T(8,128)(2,1)}, u32[]{:S(2)}) copy-start(bf16[192,768]{1,0:T(8,128)(2,1)} %get-tuple-element.85.refs_9_) | copy-start | bytes 884740
  125.0 6.9 %copy-start.13 = (bf16[192,768]{1,0:T(8,128)(2,1)S(1)}, bf16[192,768]{1,0:T(8,128)(2,1)}, u32[]{:S(2)}) copy-start(bf16[192,768]{1,0:T(8,128)(2,1)} %copy-done.12) | copy-start | bytes 884740
  125.0 6.9 %copy-start.15 = (bf16[192,768]{1,0:T(8,128)(2,1)S(1)}, bf16[192,768]{1,0:T(8,128)(2,1)}, u32[]{:S(2)}) copy-start(bf16[192,768]{1,0:T(8,128)(2,1)} %copy-done.14) | copy-start | bytes 884740
  125.0 6.9 %copy-start.17 = (bf16[192,768]{1,0:T(8,128)(2,1)S(1)}, bf16[192,768]{1,0:T(8,128)(2,1)}, u32[]{:S(2)}) copy-start(bf16[192,768]{1,0:T(8,128)(2,1)} %copy-done.16) | copy-start | bytes 884740
  125.0 45.1 %all-to-all-start.3 = ((bf16[64,96,128]{2,1,0:T(8,128)(2,1)}), bf16[64,96,128]{2,1,0:T(8,128)(2,1)S(1)}, u32[]{:S(2)}, u32[]{:S(2)}) async-start(bf16[64,96,128]{2,1,0:T(8,128)(2,1)} %late.1), calls=%async_computation.3 | async-start | bytes 3145728 | tf_op jit(solution)/shard_map/all_to_all | solution.py:629
  132.0 22.8 %collective-permute-start.10 = (bf16[192,768]{1,0:T(8,128)(2,1)S(1)}, bf16[192,768]{1,0:T(8,128)(2,1)S(1)}, u32[]{:S(2)}, u32[]{:S(2)}) collective-permute-start(bf16[192,768]{1,0:T(8,128)(2,1)S(1)} %add_convert_fusion.1), channel_id=1, source_target_pairs={{0,32},{1,3},{2,34},{3,5},{4,36},{5,7},{6,38},{7,1},{8,40},{9,11},... | collective-permute-start | bytes 884744 | tf_op jit(solution)/shard_map/ppermute | solution.py:95
  133.1 24.3 %collective-permute-start.11 = (bf16[192,768]{1,0:T(8,128)(2,1)S(1)}, bf16[192,768]{1,0:T(8,128)(2,1)S(1)}, u32[]{:S(2)}, u32[]{:S(2)}) collective-permute-start(bf16[192,768]{1,0:T(8,128)(2,1)S(1)} %add_convert_fusion.1), channel_id=1, source_target_pairs={{0,96},{1,7},{2,98},{3,1},{4,100},{5,3},{6,102},{7,5},{8,104},{9,1... | collective-permute-start | bytes 884744 | tf_op jit(solution)/shard_map/ppermute | solution.py:95
  134.8 24.2 %collective-permute-start.9 = (bf16[192,768]{1,0:T(8,128)(2,1)S(1)}, bf16[192,768]{1,0:T(8,128)(2,1)S(1)}, u32[]{:S(2)}, u32[]{:S(2)}) collective-permute-start(bf16[192,768]{1,0:T(8,128)(2,1)S(1)} %add_convert_fusion.1), channel_id=1, source_target_pairs={{0,64},{1,5},{2,66},{3,7},{4,68},{5,1},{6,70},{7,3},{8,72},{9,13},... | collective-permute-start | bytes 884744 | tf_op jit(solution)/shard_map/ppermute | solution.py:95
  159.1 22.6 %copy-start.11 = (bf16[192,768]{1,0:T(8,128)(2,1)}, bf16[192,768]{1,0:T(8,128)(2,1)S(1)}, u32[]{:S(2)}) copy-start(bf16[192,768]{1,0:T(8,128)(2,1)S(1)} %add_convert_fusion.refs_1_) | copy-start | bytes 884740
  159.1 7.1 %collective-permute-start.12 = (bf16[192,768]{1,0:T(8,128)(2,1)S(1)}, bf16[192,768]{1,0:T(8,128)(2,1)S(1)}, u32[]{:S(2)}, u32[]{:S(2)}) collective-permute-start(bf16[192,768]{1,0:T(8,128)(2,1)S(1)} %add_convert_fusion.refs_1_), channel_id=1, source_target_pairs={{0,8},{1,33},{2,10},{3,35},{4,12},{5,37},{6,14},{7,39},{8,16},{9,4... | collective-permute-start | bytes 884744 | tf_op jit(solution)/shard_map/ppermute | solution.py:95
  160.4 5.9 %collective-permute-start.13 = (bf16[192,768]{1,0:T(8,128)(2,1)S(1)}, bf16[192,768]{1,0:T(8,128)(2,1)S(1)}, u32[]{:S(2)}, u32[]{:S(2)}) collective-permute-start(bf16[192,768]{1,0:T(8,128)(2,1)S(1)} %add_convert_fusion.refs_1_), channel_id=1, source_target_pairs={{0,24},{1,97},{2,26},{3,99},{4,28},{5,101},{6,30},{7,103},{8,0},{9... | collective-permute-start | bytes 884744 | tf_op jit(solution)/shard_map/ppermute | solution.py:95
  161.9 8.2 %collective-permute-start.14 = (bf16[192,768]{1,0:T(8,128)(2,1)S(1)}, bf16[192,768]{1,0:T(8,128)(2,1)S(1)}, u32[]{:S(2)}, u32[]{:S(2)}) collective-permute-start(bf16[192,768]{1,0:T(8,128)(2,1)S(1)} %add_convert_fusion.refs_1_), channel_id=1, source_target_pairs={{0,16},{1,65},{2,18},{3,67},{4,20},{5,69},{6,22},{7,71},{8,24},{9,... | collective-permute-start | bytes 884744 | tf_op jit(solution)/shard_map/ppermute | solution.py:95
  166.3 3.8 %copy-start.18 = (bf16[192,768]{1,0:T(8,128)(2,1)}, bf16[192,768]{1,0:T(8,128)(2,1)S(1)}, u32[]{:S(2)}) copy-start(bf16[192,768]{1,0:T(8,128)(2,1)S(1)} %collective-permute-done.12.refs_1_.refs_2_) | copy-start | bytes 884740
  166.3 3.8 %copy-start.19 = (bf16[192,768]{1,0:T(8,128)(2,1)}, bf16[192,768]{1,0:T(8,128)(2,1)S(1)}, u32[]{:S(2)}) copy-start(bf16[192,768]{1,0:T(8,128)(2,1)S(1)} %collective-permute-done.13.refs_2_.refs_3_) | copy-start | bytes 884740
  174.7 28.3 %all-to-all-start.4 = ((bf16[64,96,128]{2,1,0:T(8,128)(2,1)}), bf16[64,96,128]{2,1,0:T(8,128)(2,1)S(1)}, u32[]{:S(2)}, u32[]{:S(2)}) async-start(bf16[64,96,128]{2,1,0:T(8,128)(2,1)} %late_sum.1.refs_5_), calls=%async_computation.4 | async-start | bytes 3145728 | tf_op jit(solution)/shard_map/all_to_all | solution.py:633
  184.1 30.9 %collective-permute-start.16 = (bf16[768,768]{1,0:T(8,128)(2,1)}, bf16[768,768]{1,0:T(8,128)(2,1)}, u32[]{:S(2)}, u32[]{:S(2)}) collective-permute-start(bf16[768,768]{1,0:T(8,128)(2,1)} %join.1.own_ref), channel_id=1, source_target_pairs={{0,2},{1,9},{2,4},{3,11},{4,6},{5,13},{6,0},{7,15},{8,10},{9,17},{... | collective-permute-start | bytes 3538952 | tf_op jit(solution)/shard_map/ppermute | solution.py:95
  185.1 30.9 %collective-permute-start.17 = (bf16[768,768]{1,0:T(8,128)(2,1)}, bf16[768,768]{1,0:T(8,128)(2,1)S(1)}, u32[]{:S(2)}, u32[]{:S(2)}) collective-permute-start(bf16[768,768]{1,0:T(8,128)(2,1)} %join.1.own_ref), channel_id=1, source_target_pairs={{0,6},{1,25},{2,0},{3,27},{4,2},{5,29},{6,4},{7,31},{8,14},{9,1},{... | collective-permute-start | bytes 3538952 | tf_op jit(solution)/shard_map/ppermute | solution.py:95
  186.7 29.3 %collective-permute-start.18 = (bf16[768,768]{1,0:T(8,128)(2,1)}, bf16[768,768]{1,0:T(8,128)(2,1)}, u32[]{:S(2)}, u32[]{:S(2)}) collective-permute-start(bf16[768,768]{1,0:T(8,128)(2,1)} %join.1.own_ref), channel_id=1, source_target_pairs={{0,1},{1,0},{2,3},{3,2},{4,5},{5,4},{6,7},{7,6},{8,9},{9,8},{10,11... | collective-permute-start | bytes 3538952 | tf_op jit(solution)/shard_map/ppermute | solution.py:99
  203.0 20.6 %copy-start.1 = (bf16[64,96,128]{2,1,0:T(8,128)(2,1)}, bf16[64,96,128]{2,1,0:T(8,128)(2,1)S(1)}, u32[]{:S(2)}) copy-start(bf16[64,96,128]{2,1,0:T(8,128)(2,1)S(1)} %all-to-all-done.4.refs_1_) | copy-start | bytes 4718596
  203.0 33.8 %collective-permute-start.15 = (bf16[64,96,128]{2,1,0:T(8,128)(2,1)S(1)}, bf16[64,96,128]{2,1,0:T(8,128)(2,1)S(1)}, u32[]{:S(2)}, u32[]{:S(2)}) collective-permute-start(bf16[64,96,128]{2,1,0:T(8,128)(2,1)S(1)} %all-to-all-done.4.refs_1_), channel_id=1, source_target_pairs={{0,1},{1,0},{2,3},{3,2},{4,5},{5,4},{6,7},{7,6},{8,9},{9,8},{10,11... | collective-permute-start | bytes 4718600 | tf_op jit(solution)/shard_map/ppermute | solution.py:99
  215.0 10.1 %collective-permute-start.22 = (bf16[768,768]{1,0:T(8,128)(2,1)}, bf16[768,768]{1,0:T(8,128)(2,1)S(1)}, u32[]{:S(2)}, u32[]{:S(2)}) collective-permute-start(bf16[768,768]{1,0:T(8,128)(2,1)} %collective-permute-done.16.refs_0_.own_ref), channel_id=1, source_target_pairs={{0,1},{1,0},{2,3},{3,2},{4,5},{5,4},{6,7},{7,6},{8,9},{9,8},{10,11... | collective-permute-start | bytes 3538952 | tf_op jit(solution)/shard_map/ppermute | solution.py:99
  216.0 4.9 %copy-start.3 = (bf16[768,768]{1,0:T(8,128)(2,1)}, bf16[768,768]{1,0:T(8,128)(2,1)S(1)}, u32[]{:S(2)}) copy-start(bf16[768,768]{1,0:T(8,128)(2,1)S(1)} %collective-permute-done.17.refs_1_.own_ref) | copy-start | bytes 3538948
  216.0 15.0 %collective-permute-start.21 = (bf16[768,768]{1,0:T(8,128)(2,1)S(1)}, bf16[768,768]{1,0:T(8,128)(2,1)S(1)}, u32[]{:S(2)}, u32[]{:S(2)}) collective-permute-start(bf16[768,768]{1,0:T(8,128)(2,1)S(1)} %collective-permute-done.17.refs_1_.own_ref), channel_id=1, source_target_pairs={{0,1},{1,0},{2,3},{3,2},{4,5},{5,4},{6,7},{7,6},{8,9},{9,8},{10,11... | collective-permute-start | bytes 3538952 | tf_op jit(solution)/shard_map/ppermute | solution.py:99
  223.6 18.9 %collective-permute-start.19 = (bf16[384,768]{1,0:T(8,128)(2,1)}, bf16[384,768]{1,0:T(8,128)(2,1)S(1)}, u32[]{:S(2)}, u32[]{:S(2)}) collective-permute-start(bf16[384,768]{1,0:T(8,128)(2,1)} %get-tuple-element.107), channel_id=1, source_target_pairs={{0,6},{1,25},{2,0},{3,27},{4,2},{5,29},{6,4},{7,31},{8,14},{9,1},{... | collective-permute-start | bytes 1769480 | tf_op jit(solution)/shard_map/ppermute | solution.py:95
  225.1 17.4 %collective-permute-start.20 = (bf16[384,768]{1,0:T(8,128)(2,1)}, bf16[384,768]{1,0:T(8,128)(2,1)S(1)}, u32[]{:S(2)}, u32[]{:S(2)}) collective-permute-start(bf16[384,768]{1,0:T(8,128)(2,1)} %get-tuple-element.108), channel_id=1, source_target_pairs={{0,2},{1,9},{2,4},{3,11},{4,6},{5,13},{6,0},{7,15},{8,10},{9,17},{... | collective-permute-start | bytes 1769480 | tf_op jit(solution)/shard_map/ppermute | solution.py:95
  243.6 3.4 %copy-start.25 = (f32[128,768]{1,0:T(8,128)S(1)}, f32[128,768]{1,0:T(8,128)}, u32[]{:S(2)}) copy-start(f32[128,768]{1,0:T(8,128)} %get-tuple-element.86) | copy-start | bytes 1179652
  246.1 3.6 %collective-permute-start.23 = (bf16[768,768]{1,0:T(8,128)(2,1)}, bf16[768,768]{1,0:T(8,128)(2,1)S(1)}, u32[]{:S(2)}, u32[]{:S(2)}) collective-permute-start(bf16[768,768]{1,0:T(8,128)(2,1)} %stack.29.own_ref), channel_id=1, source_target_pairs={{0,1},{1,0},{2,3},{3,2},{4,5},{5,4},{6,7},{7,6},{8,9},{9,8},{10,11... | collective-permute-start | bytes 3538952 | tf_op jit(solution)/shard_map/ppermute | solution.py:99
  (13 other events, 11.9 us)

commit v3 on v2

--- a/solution.py
+++ b/solution.py
@@ -23,7 +23,8 @@
 KB = 4
 KBR = ROWS // KB
 KEYS = WINDOW // KB
-FC = 512
+STRIP = D // CHIPS
+FC = 1024
 VMEM = pl.BlockSpec(memory_space=pltpu.VMEM)
 SMEM = pl.BlockSpec(memory_space=pltpu.SMEM)
 ANY = pl.BlockSpec(memory_space=pl.ANY)
@@ -67,7 +68,7 @@
 
 
 AXES = ("x", "y", "z", "c")
-ORDER = ((2, 1, 0), (1, 0, 2))
+ORDER = ((2, 1, 0, 0), (1, 0, 2, 0))
 FROM = (0, 3, 1, 2)
 
 
@@ -205,7 +206,7 @@
 
 
 def backward_kernel(at_ref, cls_ref, x_ref, do_ref, o_ref, lse_ref, kv_ref, kpb_ref, spl_ref, stl_ref, gb_ref,
-                    dq_ref, keep_ref, send_ref, dkv_ref, y_ref, drow_ref, dqt_ref, acc_ref, kt_ref):
+                    dq_ref, keep_ref, send_ref, same_ref, other_ref, y_ref, drow_ref, dqt_ref, acc_ref, kt_ref):
     low = lanes_low((ROWS, 2 * HD))
     for h in range(H):
         pair = do_ref[:, (h // 2) * 128 : (h // 2) * 128 + 128].astype(f32)
@@ -238,9 +239,8 @@
 
         visit(cls_ref, kb, step)
         sums = acc_ref[...].reshape(WIDE, KBR, 2 * HD).astype(bf16)
-        for i in range(CHIPS):
-            dkv_ref[2 * i + at_ref[0], cols, :] = sums[i]
-            dkv_ref[2 * i + 1 - at_ref[0], cols, :] = sums[CHIPS + i]
+        same_ref[:, cols, :] = sums[:CHIPS]
+        other_ref[:, cols, :] = sums[CHIPS:]
         return 0
 
     lax.fori_loop(0, KB, key_block, 0)
@@ -314,12 +314,14 @@
         put_rows(vec_ref, 18, jnp.sum(gb.astype(f32), axis=0, keepdims=True))
 
 
-def leave_kernel(at_ref, x_ref, gain_ref, wq_ref, wkv_ref, gq_ref, parts_ref, gr_ref, mid_ref, gin_ref, keep_ref, send_ref, vec_ref):
+def leave_kernel(at_ref, x_ref, gain_ref, wq_ref, wkv_ref, gq_ref, gr_ref, mid_ref, parts_ref, _, gin_ref, keep_ref, send_ref, vec_ref):
     gkv = jnp.sum(parts_ref[...].astype(f32), axis=0).astype(bf16)
     gq = gq_ref[...]
     e = dot_nt(gq, wq_ref[...]) + dot_nt(gkv, wkv_ref[...])
     n, rstd = norm_parts(x_ref[...].astype(f32))
-    gin_ref[...] = gr_ref[...] + norm_back(e, n, rstd, vec(gain_ref))
+    gin = gr_ref[...] + norm_back(e, n, rstd, vec(gain_ref))
+    for i in range(D // 128):
+        gin_ref[pl.ds(i, ROWS, stride=D // 128), :] = gin[:, i * 128 : (i + 1) * 128]
     gkv = gkv.astype(f32)
     vec_ref[0:48, :] = mid_ref[...]
     vec_ref[48:128, :] = jnp.zeros((80, 128), f32)
@@ -370,42 +372,63 @@
     down_ref[...] = jnp.where(first, own, other).astype(f32)
     up_ref[...] = jnp.where(first, other, own).astype(f32)
 
-def place(at, rel, own, other, kept):
-    tile=256
-    n=D//tile
-    piece=pl.BlockSpec((tile,D), lambda i,at: (i,0))
-    outs=(pl.BlockSpec((tile,D), lambda i,at: (((at[4]+rel)&3)*n+i,0)), pl.BlockSpec((tile,D), lambda i,at: (i,(at[5]+rel)&3)))
-    anyspec=pl.BlockSpec(memory_space=pl.ANY)
-    return pl.pallas_call(place_kernel,
-        grid_spec=pltpu.PrefetchScalarGridSpec(num_scalar_prefetch=1, grid=(n,), in_specs=[piece,piece]+[anyspec]*len(kept), out_specs=outs),
-        out_shape=shapes(((FF,D),f32),((D,FF),f32)),
-        input_output_aliases={3:0,4:1} if kept else {},
-        compiler_params=params(), cost_estimate=cost(0,8e6), name="place")(at, own, other, *kept)
-
-
-def late_kernel(at_ref, lk_ref, lo_ref, rk_ref, ro_ref, tk_ref, to_ref, out_ref, total_ref):
+def place(at, rel, own, other, kept, part=0):
+    tile = D // 2
+    n = own.shape[0] // tile
+    piece = pl.BlockSpec((tile, D), lambda i, at: (i, 0))
+    outs = (
+        pl.BlockSpec((tile, D), lambda i, at: (((at[4] + rel) & 3) * 2 + part + i, 0)),
+        pl.BlockSpec((tile, D), lambda i, at: (part + i, (at[5] + rel) & 3)),
+    )
+    return pl.pallas_call(
+        place_kernel,
+        grid_spec=pltpu.PrefetchScalarGridSpec(
+            num_scalar_prefetch=1, grid=(n,), in_specs=[piece, piece] + [ANY] * len(kept), out_specs=outs
+        ),
+        out_shape=shapes(((FF, D), f32), ((D, FF), f32)),
+        input_output_aliases={3: 0, 4: 1} if kept else {},
+        compiler_params=params(),
+        cost_estimate=cost(0, 8e6),
+        name="place",
+    )(at, own, other, *kept)
+
+
+def share_kernel(same_ref, other_ref, lk_ref, lo_ref, rk_ref, ro_ref, out_ref, total_ref):
+    out_ref[:, 0:ROWS, :] = (same_ref[...].astype(f32) + other_ref[...].astype(f32)).astype(bf16)
+    total_ref[...] = dot_tn(lk_ref[...], rk_ref[...]) + dot_tn(lo_ref[...], ro_ref[...])
+    for i in range(CHIPS):
+        for b in range(6):
+            out_ref[i, ROWS + STRIP * b : ROWS + STRIP * (b + 1), :] = total_ref[
+                STRIP * i : STRIP * (i + 1), 128 * b : 128 * (b + 1)
+            ].astype(bf16)
+
+
+def late_kernel(at_ref, lk_ref, lo_ref, tk_ref, to_ref, out_ref, total_ref):
     first = at_ref[0] == 0
-    lk, lo = lk_ref[...], lo_ref[...]
-    total_ref[:, 0:D] = dot_tn(lk, rk_ref[...]) + dot_tn(lo, ro_ref[...])
 
     @pl.when(first)
     def _():
-        total_ref[:, D : D + 128] = dot_tn(lk, tk_ref[...].astype(bf16)) + dot_tn(lo, to_ref[...].astype(bf16))
+        total_ref[...] = dot_tn(lk_ref[...], tk_ref[...].astype(bf16)) + dot_tn(lo_ref[...], to_ref[...].astype(bf16))
 
     @pl.when(jnp.logical_not(first))
     def _():
-        total_ref[0:128, D : D + 128] = tk_ref[...] + to_ref[...]
-        total_ref[128:, D : D + 128] = jnp.zeros((D - 128, 128), f32)
-
-    total_ref[:, D + 128 :] = jnp.zeros((D, 128), f32)
-    for a in range(8):
-        for b in range(8):
-            out_ref[a * 8 + b] = total_ref[a * 96 : a * 96 + 96, b * 128 : b * 128 + 128].astype(bf16)
-
-
-def late_sum_kernel(parts_ref, out_ref):
-    total = jnp.sum(parts_ref[...].astype(f32), axis=0).astype(bf16)
-    for i in range(64):
+        total_ref[0:128, :] = tk_ref[...] + to_ref[...]
+        total_ref[128:, :] = jnp.zeros((D - 128, 128), f32)
+
+    for i in range(CHIPS):
+        out_ref[i] = total_ref[STRIP * i : STRIP * (i + 1), :].astype(bf16)
+
+
+def strip_kernel(parts_ref, tail_ref, out_ref):
+    for b in range(6):
+        rows = slice(ROWS + STRIP * b, ROWS + STRIP * (b + 1))
+        out_ref[:, 128 * b : 128 * (b + 1)] = jnp.sum(parts_ref[:, rows, :].astype(f32), axis=0).astype(bf16)
+    out_ref[:, D:] = jnp.sum(tail_ref[...].astype(f32), axis=0).astype(bf16)
+
+
+def copies_kernel(a_ref, b_ref, c_ref, d_ref, out_ref):
+    total = pair_sums(a_ref[...], b_ref[...], c_ref[...], d_ref[...])
+    for i in range(CHIPS):
         out_ref[i] = total
 
 
@@ -414,22 +437,21 @@
 
 def late_place_kernel(at_ref, own_ref, other_ref, query_ref, out_ref, kv_ref, value_ref, *vec_refs):
     first = at_ref[0] == 0
-    for a in range(8):
-        rows = slice(a * 96, a * 96 + 96)
-        for b in range(7):
-            own, other = own_ref[a * 8 + b].astype(f32), other_ref[a * 8 + b].astype(f32)
-            zero, one = jnp.where(first, own, other), jnp.where(first, other, own)
-            if b < 6:
-                cols = slice(b * 128, b * 128 + 128)
-                query_ref[rows, cols] = zero
-                out_ref[rows, cols] = one
-            else:
-                kv_ref[rows, :] = zero
-            if b == 6 and a == 0:
-                value_ref[...] = one[66, HD:]
-                for ref, (at, count) in zip(vec_refs, VECTORS):
-                    for i in range(count):
-                        ref[i * 128 : (i + 1) * 128] = one[at + i]
+    vecs = []
+    for a in range(CHIPS):
+        rows = slice(STRIP * a, STRIP * (a + 1))
+        own, other = own_ref[a].astype(f32), other_ref[a].astype(f32)
+        zero, one = jnp.where(first, own, other), jnp.where(first, other, own)
+        query_ref[rows, :] = zero[:, :D]
+        out_ref[rows, :] = one[:, :D]
+        kv_ref[rows, :] = zero[:, D:]
+        if a < 2:
+            vecs.append(one[:, D:])
+    row = lambda i: vecs[i // STRIP][i % STRIP]
+    value_ref[...] = row(66)[HD:]
+    for ref, (at, count) in zip(vec_refs, VECTORS):
+        for i in range(count):
+            ref[i * 128 : (i + 1) * 128] = row(at + i)
 
 
 def call(kernel, args, outs, scratch=(), name=None, flops=0, nbytes=2e6, after=()):
@@ -486,6 +508,7 @@
 
 
 NARROW = ((ROWS, D), bf16)
+KV_HALF = ((CHIPS, ROWS, 2 * HD), bf16)
 
 
 def attend(*args):
@@ -501,7 +524,7 @@
 def attend_back(*args, after=()):
     return call(
         backward_kernel, args,
-        shapes(NARROW, NARROW, NARROW, ((WIDE, ROWS, 2 * HD), bf16)),
+        shapes(NARROW, NARROW, NARROW, KV_HALF, KV_HALF),
         [
             pltpu.VMEM((RB, QB, 128), bf16), pltpu.VMEM((RB, 8, QB), f32),
             pltpu.VMEM((RB, 128, QB), f32), pltpu.VMEM((KEYS, 2 * HD), f32), pltpu.VMEM((2 * HD, KEYS), bf16),
@@ -520,11 +543,6 @@
 def halves_kernel(before_ref, after_ref, low_ref, high_ref):
     low_ref[...] = before_ref[D // 2 :, :]
     high_ref[...] = after_ref[: D // 2, :]
-
-
-def stack_kernel(high_ref, low_ref, out_ref):
-    out_ref[: D // 2, :] = high_ref[...]
-    out_ref[D // 2 :, :] = low_ref[...]
 
 
 QUARTER = ((D // 4, D), bf16)
@@ -560,8 +578,9 @@
     low, high = send(low, 0, 1), send(high, 0, 3)
     kept = place(at, 3, before, swap(before), kept)
     kept = place(at, 1, after, swap(after), kept)
-    far = call(stack_kernel, (high, low), shapes(((D, D), bf16))[0], name="stack", after=kept[:1] + tuple(before_far))
-    return place(at, 2, far, swap(far), kept)
+    low, high = (tie(v, kept[0], *before_far) for v in (low, high))
+    kept = place(at, 2, high, swap(high), kept)
+    return place(at, 2, low, swap(low), kept, part=1)
 
 
 def body(block_input, file_lengths, file_splits, ln1_gain, ln1_bias, w_query, b_query, w_kv, b_value, w_out, b_out,
@@ -611,26 +630,33 @@
     packed = call(pack_kernel, (big, small, swap(big_send), swap(small_send)), shapes(((4, 2 * ROWS, 2 * D), bf16))[0], name="pack")
     slabs = lax.all_to_all(packed, AXES, 0, 0, axis_index_groups=ring_groups(0), tiled=True)
 
-    gq, right, right_send, dkv = attend_back(at, kinds, xq, ga, o, lse, kv_all, key_cols, own_lanes, start_lanes, gb, after=(packed,))
-    parts = lax.all_to_all(tie(dkv, slabs), wide, 0, 0, tiled=True)
-    right_other = swap(right_send)
+    gq, right, right_send, kv_grads, kv_send = attend_back(at, kinds, xq, ga, o, lse, kv_all, key_cols, own_lanes, start_lanes, gb, after=(packed,))
+    shares = call(share_kernel, (kv_grads, swap(kv_send), left, left_other, right, swap(right_send)),
+                  shapes(((CHIPS, ROWS + 6 * STRIP, 128), bf16))[0], [pltpu.VMEM((D, D), f32)], name="share", after=(slabs,))
+    parts = lax.all_to_all(shares, ("y", "z"), 0, 0, tiled=True)
 
     pieces = call(weight_kernel, (at, slabs), shapes(*[QUARTER] * 4), [pltpu.VMEM((D, D), f32)], name="weights")
     ff_parts = (pieces[0],) + spread(1, *pieces[1:])
-    gin, tail, tail_send, _ = call(
-        leave_kernel, (at, x, ln1_gain, w_query, w_kv, gq, parts, gr, vec_mid),
-        shapes(((ROWS, D), f32), ((128, 128), f32), ((128, 128), f32), ((128, 128), f32)),
-        name="leave", flops=2 * ROWS * D * 900, nbytes=4e6, after=pieces[:1],
-    )
-
-    late_pieces = call(late_kernel, (at, left, left_other, right, right_other, tail, swap(tail_send)),
-                  shapes(((64, 96, 128), bf16))[0], [pltpu.VMEM((D, 1024), f32)], name="late", after=ff_parts[1:])
-    space = ("x", "y", "z")
-    arrived = lax.all_to_all(late_pieces, space, 0, 0, tiled=True)
-    ff_total = pair_sums(*gather4(pair_sums(*ff_parts), 2))
-    ff_totals = gather4(ff_total, 1)
-    copies = call(late_sum_kernel, (arrived,), shapes(((64, 96, 128), bf16))[0], name="late_sum", after=ff_totals[1:])
-    late = lax.all_to_all(copies, space, 0, 0, tiled=True)
+    ff_crossed = gather4(pair_sums(*ff_parts), 2)
+    gin, tail, tail_send, _ = pl.pallas_call(
+        leave_kernel,
+        grid=(1,),
+        out_shape=shapes(((ROWS * D // 128, 128), f32), ((128, 128), f32), ((128, 128), f32), ((128, 128), f32)),
+        in_specs=[SMEM] + [VMEM] * 7 + [pl.BlockSpec((CHIPS, ROWS, 128), lambda i: (0, 0, 0)), ANY],
+        out_specs=(VMEM,) * 4,
+        compiler_params=params(),
+        cost_estimate=cost(2 * ROWS * D * 900, 4e6),
+        name="leave",
+    )(at, x, ln1_gain, w_query, w_kv, gq, gr, vec_mid, parts, pieces[0])
+
+    late_parts = call(late_kernel, (at, left, left_other, tail, swap(tail_send)), shapes(((CHIPS, STRIP, 128), bf16))[0],
+                      [pltpu.VMEM((D, 128), f32)], name="late", after=ff_parts[1:])
+    late_parts = lax.all_to_all(late_parts, ("y", "z"), 0, 0, tiled=True)
+    ff_totals = gather4(pair_sums(*ff_crossed), 1)
+    strip = call(strip_kernel, (parts, late_parts), shapes(((STRIP, D + 128), bf16))[0], name="strip", after=ff_crossed[1:])
+    strips = gather4(strip, 3)
+    copies = call(copies_kernel, strips, shapes(((CHIPS, STRIP, D + 128), bf16))[0], name="copies", after=ff_totals[1:])
+    late = lax.all_to_all(copies, ("y", "z"), 0, 0, tiled=True)
     one = lambda n: ((n,), f32)
     outs = call(
         late_place_kernel, (at, late, swap(late)),

time: 257 us -> 260 us (1.012)
  waiting for transfers between devices: 64.5 us -> 42 us
  starting transfers between devices: 62.9 us -> 76.9 us
  blocking collectives: 0 us -> 11.6 us
    ppermute x11 -> x13, starting transfers between devices: 13.5 us -> 34.7 us  [swap(): return lax.ppermute(v, 'c', [(0, 1), (1, 0)])]
    all_to_all x3 -> x2, waiting for transfers between devices: 20.3 us -> 6 us  [the longest x1 6 us: body(): late = lax.all_to_all(copies, ('y', 'z'), 0, 0, tiled=True)]
    all_to_all x0 -> x1, blocking collectives: none -> 11.6 us  [body(): late_parts = lax.all_to_all(late_parts, ('y', 'z'), 0, 0, tiled=True)]
    all_to_all x3 -> x2, starting transfers between devices: 21 us -> 10.1 us  [the longest x1 6.43 us: body(): parts = lax.all_to_all(shares, ('y', 'z'), 0, 0, tiled=True)]
    ppermute x13 -> x16, waiting for transfers between devices: 37.8 us -> 29 us  [send(): return lax.ppermute(v, AXES, ring(place, shift))]
    ppermute x13 -> x16, starting transfers between devices: 16 us -> 19.6 us  [send(): return lax.ppermute(v, AXES, ring(place, shift))]
    pallas_call x0 -> x1, Pallas kernels: none -> 3.28 us  [body(): pl.pallas_call(leave_kernel, grid=(1,), out_shape=shapes(((ROWS * D // 12...]
    unnamed x66 -> x61, local copies, waits for them, and re-layouts: 14.1 us -> 13.1 us
  transfers between devices with their start and end apart: 29 -> 33, of which waited for: 13 -> 16; matrix products, arithmetic and copies ran while one was open for 4% -> 4% of each run, Pallas kernels for 22% -> 24%
where the time goes in v3:
time: 260 us; the launch traced here: 259 us
  Pallas kernels  104 us (40%)
  starting transfers between devices  76.9 us (30%)
  waiting for transfers between devices  42 us (16%)
  local copies, waits for them, and re-layouts  18.3 us (7%)
  blocking collectives  11.6 us (4%)
  other arithmetic  5.25 us (2%)
    pallas_call x13, Pallas kernels, call(): pl.pallas_call(run, out_shape=outs, in_specs=[SMEM if v.dtype == jnp.int3...  71.1 us
    ppermute x13, starting transfers between devices, swap(): return lax.ppermute(v, 'c', [(0, 1), (1, 0)])  34.7 us
    ppermute x16, waiting for transfers between devices, send(): return lax.ppermute(v, AXES, ring(place, shift))  29 us
    ppermute x16, starting transfers between devices, send(): return lax.ppermute(v, AXES, ring(place, shift))  19.6 us
    pallas_call x5, Pallas kernels, place(): pl.pallas_call(place_kernel, grid_spec=pltpu.PrefetchScalarGridSpec(num_s...  19.3 us
    unnamed x61, local copies, waits for them, and re-layouts  13.1 us
    all_to_all x1, blocking collectives, body(): late_parts = lax.all_to_all(late_parts, ('y', 'z'), 0, 0, tiled=True)  11.6 us
    pallas_call x1, Pallas kernels, body(): pl.pallas_call(middle_kernel, grid=(steps,), out_shape=shapes(narrow, ((R...  10.5 us
  transfers between devices with their start and end apart: 33, of which 16 were waited for; matrix products, arithmetic and copies ran while one was open for 4% of the time, Pallas kernels for 24%

profile of v3, /device:TPU:1, one launch (start us, length us, event | category | flops | bytes accessed | tf_op | source)
XLA Modules:
  0.0 259.3 jit_solution(16684093372393827897)
XLA Ops:
  0.6 2.2 enter.1
  2.9 8.6 %all-to-all-start = ((bf16[16,128,128]{2,1,0:T(8,128)(2,1)}), bf16[16,128,128]{2,1,0:T(8,128)(2,1)S(1)}, u32[]{:S(2)}, u32[]{:S(2)}) async-start(bf16[16,128,128]{2,1,0:T(8,128)(2,1)} %get-tuple-element.71), calls=%async_computation | async-start | bytes 1048576 | tf_op jit(solution)/shard_map/all_to_all | solution.py:596
  17.1 2.2 broadcast_in_dim.28.refs_3_.refs_5_.refs_7_
  19.3 2.3 query.1.refs_0_.refs_2_
  22.6 2.1 collective-permute-start
  27.3 17.8 %attend.1 = (bf16[128,768]{1,0:T(8,128)(2,1)}, bf16[128,768]{1,0:T(8,128)(2,1)}, bf16[128,768]{1,0:T(8,128)(2,1)}, bf16[2,768,128]{2,1,0:T(8,128)(2,1)}, f32[2,7...) custom-call(s32[6]{0:T(128)} %stack.27.refs_0_.at_ref, s32[8]{0:T(128)} %select_n.94.refs_6_.refs_1_, ...), custom_call_target="tpu_custom_call" | custom-call | flops 1 | bytes 1 | tf_op jit(solution)/shard_map/attend/pallas_call | solution.py:460
  45.2 10.5 %middle.1 = (bf16[128,768]{1,0:T(8,128)(2,1)}, bf16[128,3072]{1,0:T(8,128)(2,1)}, bf16[128,3072]{1,0:T(8,128)(2,1)}, bf16[128,768]{1,0:T(8,128)(2,1)}, bf16[128,...) custom-call(s32[6]{0:T(128)} %stack.27.refs_0_.at_ref, ...), custom_call_target="tpu_custom_call" | custom-call | flops 1 | bytes 1 | tf_op jit(solution)/shard_map/middle/pallas_call | solution.py:611
  56.3 2.3 collective-permute-done.2.refs_3_
  59.5 3.4 %pack.1.refs_11_ = bf16[4,256,1536]{2,1,0:T(8,128)(2,1)} custom-call(bf16[128,3072]{1,0:T(8,128)(2,1)} %get-tuple-element.80.refs_0_, bf16[128,768]{1,0:T(8,128)(2,1)} %get-tuple-element.81.refs_1_, bf16[128,3072]{1,0:T(8,128)(2,1)} %copy-done.19, bf16[128,768]{1,0:T(8,128)(2,1)} %copy-done.24), custom_call_target="tpu_custom_call" | custom-call | flops 1 | bytes 1 | tf_op jit(solution)/shard_map/pack/pallas_call | solution.py:460
  62.9 3.9 %all-to-all-start.1 = ((bf16[4,256,1536]{2,1,0:T(8,128)(2,1)}), bf16[4,256,1536]{2,1,0:T(8,128)(2,1)S(1)}, u32[]{:S(2)}, u32[]{:S(2)}) async-start(bf16[4,256,1536]{2,1,0:T(8,128)(2,1)} %pack.1.refs_11_), calls=%async_computation.1 | async-start | bytes 6291456 | tf_op jit(solution)/shard_map/all_to_all | solution.py:631
  66.8 21.4 %attend_back.1 = (bf16[128,768]{1,0:T(8,128)(2,1)}, bf16[128,768]{1,0:T(8,128)(2,1)}, bf16[128,768]{1,0:T(8,128)(2,1)}, bf16[16,128,128]{2,1,0:T(8,128)(2,1)}, bf16[16,128,128]{2,1,0:T(8,128)(2,1)}) custom-call(s32[6]{0:T(128)} %stack.27.refs_0_.at_ref, s32[8]{0:T(128)} %select_n.94.refs_6_.refs_1_, bf16[2,768,128]{2,1,0:T(8,128)(2,1)} %get-tuple-element.74.refs_2_, ...), custom_call_target="tpu_custom_call" | custom-call | flops 1 | bytes 1 | tf_op jit(solution)/shard_map/attend_back/pallas_call | solution.py:460
  89.1 1.6 collective-permute-done.4.refs_3_.refs_2_
  92.6 3.6 %share.1 = bf16[16,416,128]{2,1,0:T(8,128)(2,1)} custom-call(bf16[16,128,128]{2,1,0:T(8,128)(2,1)} %get-tuple-element.87.refs_0_, bf16[16,128,128]{2,1,0:T(8,128)(2,1)} %collective-permute-done.3.refs_1_, bf16[128,768]{1,0:T(8,128)(2,1)} %get-tuple-element.89.refs_2_.refs_1_, bf16[128,768]{1,0:T(8,128)(2,1)} %copy-done.18, ...), custom_call_target="tpu_custom_call" | custom-call | flops 1 | bytes 1 | tf_op jit(solution)/shard_map/share/pallas_call | solution.py:460
  96.2 6.4 %all-to-all-start.2 = ((bf16[16,416,128]{2,1,0:T(8,128)(2,1)}), bf16[16,416,128]{2,1,0:T(8,128)(2,1)S(1)}, u32[]{:S(2)}, u32[]{:S(2)}) async-start(bf16[16,416,128]{2,1,0:T(8,128)(2,1)} %share.1), calls=%async_computation.2 | async-start | bytes 3407872 | tf_op jit(solution)/shard_map/all_to_all | solution.py:636
  102.7 4.5 %weights.1 = (bf16[192,768]{1,0:T(8,128)(2,1)}, bf16[192,768]{1,0:T(8,128)(2,1)}, bf16[192,768]{1,0:T(8,128)(2,1)}, bf16[192,768]{1,0:T(8,128)(2,1)}) custom-call(s32[6]{0:T(128)} %stack.27.refs_0_.at_ref, bf16[4,256,1536]{2,1,0:T(8,128)(2,1)} %copy-done), custom_call_target="tpu_custom_call" | custom-call | flops 1 | bytes 1 | tf_op jit(solution)/shard_map/weights/pallas_call | solution.py:460
  108.4 1.5 collective-permute-start.8
  109.8 1.5 collective-permute-start.9
  111.4 3.1 %collective-permute-done.7.refs_5_ = bf16[192,768]{1,0:T(8,128)(2,1)S(1)} collective-permute-done((bf16[192,768]{1,0:T(8,128)(2,1)}, bf16[192,768]{1,0:T(8,128)(2,1)S(1)}, u32[]{:S(2)}, u32[]{:S(2)}) %collective-permute-start.7) | collective-permute-done | bytes 294944 | tf_op jit(solution)/shard_map/ppermute | solution.py:96
  114.5 4.1 %collective-permute-done.9.refs_7_ = bf16[192,768]{1,0:T(8,128)(2,1)S(1)} collective-permute-done((bf16[192,768]{1,0:T(8,128)(2,1)}, bf16[192,768]{1,0:T(8,128)(2,1)S(1)}, u32[]{:S(2)}, u32[]{:S(2)}) %collective-permute-start.9) | collective-permute-done | bytes 294944 | tf_op jit(solution)/shard_map/ppermute | solution.py:96
  119.8 1.4 collective-permute-start.10
  121.3 1.3 collective-permute-start.11
  122.6 1.7 collective-permute-start.12
  124.2 5.4 %collective-permute-done.10.refs_2_ = bf16[192,768]{1,0:T(8,128)(2,1)S(1)} collective-permute-done((bf16[192,768]{1,0:T(8,128)(2,1)S(1)}, bf16[192,768]{1,0:T(8,128)(2,1)S(1)}, u32[]{:S(2)}, u32[]{:S(2)}) %collective-permute-start.10) | collective-permute-done | bytes 294944 | tf_op jit(solution)/shard_map/ppermute | solution.py:96
  129.6 1.6 collective-permute-done.11.refs_3_
  131.2 3.7 %collective-permute-done.12.refs_4_ = bf16[192,768]{1,0:T(8,128)(2,1)S(1)} collective-permute-done((bf16[192,768]{1,0:T(8,128)(2,1)S(1)}, bf16[192,768]{1,0:T(8,128)(2,1)S(1)}, u32[]{:S(2)}, u32[]{:S(2)}) %collective-permute-start.12) | collective-permute-done | bytes 294944 | tf_op jit(solution)/shard_map/ppermute | solution.py:96
  138.9 3.3 %leave.1 = (f32[768,128]{1,0:T(8,128)}, f32[128,128]{1,0:T(8,128)}, f32[128,128]{1,0:T(8,128)}, f32[128,128]{1,0:T(8,128)}) custom-call(s32[6]{0:T(128)} %stack.27.refs_0_.at_ref, bf16[128,768]{1,0:T(8,128)(2,1)} %bitcast.59, bf16[768]{0:T(1024)(128)(2,1)} %gain_ref.3, bf16[768,768]{1,0:T(8,128)(2,1)} %wq_ref.1, bf16[768,128]{1,0:T(8,128)(2,1)} %wkv_ref.1, ...), custom_call_target="tpu_custom_call" | custom-call | flops 1 | bytes 1 | tf_op jit(solution)/shard_map/leave/pallas_call | solution.py:641
  142.3 14.9 %collective-permute-start.6 = (f32[128,128]{1,0:T(8,128)}, f32[128,128]{1,0:T(8,128)S(1)}, u32[]{:S(2)}, u32[]{:S(2)}) collective-permute-start(f32[128,128]{1,0:T(8,128)} %get-tuple-element.96), channel_id=1, source_target_pairs={{0,1},{1,0},{2,3},{3,2},{4,5},{5,4},{6,7},{7,6},{8,9},{9,8},{10,11... | collective-permute-start | bytes 196616 | tf_op jit(solution)/shard_map/ppermute | solution.py:100
  158.9 1.8 late.1
  160.7 11.6 %all_to_all.25.refs_1_ = bf16[16,48,128]{2,1,0:T(8,128)(2,1)} all-to-all(bf16[16,48,128]{2,1,0:T(8,128)(2,1)} %late.1), channel_id=1, replica_groups=mesh['x'=4,'y'=4,'z'=4,'c'=2] {'y','z'}, dimensions={0} | all-to-all | bytes 393216 | tf_op jit(solution)/shard_map/all_to_all | solution.py:654
  172.2 2.3 strip.1.refs_0_
  175.0 3.3 %collective-permute-start.14 = (bf16[48,896]{1,0:T(8,128)(2,1)}, bf16[48,896]{1,0:T(8,128)(2,1)S(1)}, u32[]{:S(2)}, u32[]{:S(2)}) collective-permute-start(bf16[48,896]{1,0:T(8,128)(2,1)} %strip.1.refs_0_), channel_id=1, source_target_pairs={{0,96},{1,97},{2,98},{3,99},{4,100},{5,101},{6,102},{7,103},{8,104... | collective-permute-start | bytes 258056 | tf_op jit(solution)/shard_map/ppermute | solution.py:96
  180.4 3.3 %collective-permute-done.15.refs_3_ = bf16[48,896]{1,0:T(8,128)(2,1)S(1)} collective-permute-done((bf16[48,896]{1,0:T(8,128)(2,1)}, bf16[48,896]{1,0:T(8,128)(2,1)S(1)}, u32[]{:S(2)}, u32[]{:S(2)}) %collective-permute-start.15) | collective-permute-done | bytes 86048 | tf_op jit(solution)/shard_map/ppermute | solution.py:96
  184.4 2.2 copies.1.refs_5_
  186.6 3.7 %all-to-all-start.4 = ((bf16[16,48,896]{2,1,0:T(8,128)(2,1)}), bf16[16,48,896]{2,1,0:T(8,128)(2,1)S(1)}, u32[]{:S(2)}, u32[]{:S(2)}) async-start(bf16[16,48,896]{2,1,0:T(8,128)(2,1)} %copies.1.refs_5_), calls=%async_computation.4 | async-start | bytes 2752512 | tf_op jit(solution)/shard_map/all_to_all | solution.py:659
  190.3 2.3 join.1.own_ref
  193.9 1.4 collective-permute-start.21
  195.3 5.0 %collective-permute-start.22 = (bf16[768,768]{1,0:T(8,128)(2,1)}, bf16[768,768]{1,0:T(8,128)(2,1)}, u32[]{:S(2)}, u32[]{:S(2)}) collective-permute-start(bf16[768,768]{1,0:T(8,128)(2,1)} %join.1.own_ref), channel_id=1, source_target_pairs={{0,1},{1,0},{2,3},{3,2},{4,5},{5,4},{6,7},{7,6},{8,9},{9,8},{10,11... | collective-permute-start | bytes 3538952 | tf_op jit(solution)/shard_map/ppermute | solution.py:100
  200.3 6.0 %all-to-all-done.4.refs_1_ = bf16[16,48,896]{2,1,0:T(8,128)(2,1)S(1)} async-done(((bf16[16,48,896]{2,1,0:T(8,128)(2,1)}), bf16[16,48,896]{2,1,0:T(8,128)(2,1)S(1)}, u32[]{:S(2)}, u32[]{:S(2)}) %all-to-all-start.4) | async-done | bytes 1376288 | tf_op jit(solution)/shard_map/all_to_all | solution.py:659
  206.3 8.5 %collective-permute-start.19 = (bf16[16,48,896]{2,1,0:T(8,128)(2,1)S(1)}, bf16[16,48,896]{2,1,0:T(8,128)(2,1)S(1)}, u32[]{:S(2)}, u32[]{:S(2)}) collective-permute-start(bf16[16,48,896]{2,1,0:T(8,128)(2,1)S(1)} %all-to-all-done.4.refs_1_), channel_id=1, source_target_pairs={{0,1},{1,0},{2,3},{3,2},{4,5},{5,4},{6,7},{7,6},{8,9},{9,8},{10,11... | collective-permute-start | bytes 4128776 | tf_op jit(solution)/shard_map/ppermute | solution.py:100
  214.8 7.0 %collective-permute-done.20.refs_0_.own_ref = bf16[768,768]{1,0:T(8,128)(2,1)} collective-permute-done((bf16[768,768]{1,0:T(8,128)(2,1)}, bf16[768,768]{1,0:T(8,128)(2,1)}, u32[]{:S(2)}, u32[]{:S(2)}) %collective-permute-start.20) | collective-permute-done | bytes 1179680 | tf_op jit(solution)/shard_map/ppermute | solution.py:96
  221.8 1.6 collective-permute-start.25
  223.5 4.2 %place.5 = (f32[3072,768]{1,0:T(8,128)}, f32[768,3072]{1,0:T(8,128)}) custom-call(s32[6]{0:T(128)} %stack.27.refs_0_.at_ref, bf16[768,768]{1,0:T(8,128)(2,1)} %join.1.own_ref, bf16[768,768]{1,0:T(8,128)(2,1)} %collective-permute-done.22.other_ref), custom_call_target="tpu_custom_call" | custom-call | flops 1 | bytes 1 | tf_op jit(solution)/shard_map/place/pallas_call | solution.py:383
  227.7 2.7 %halves.1 = (bf16[384,768]{1,0:T(8,128)(2,1)}, bf16[384,768]{1,0:T(8,128)(2,1)}) custom-call(bf16[768,768]{1,0:T(8,128)(2,1)} %collective-permute-done.20.refs_0_.own_ref, bf16[768,768]{1,0:T(8,128)(2,1)} %copy-done.3, f32[3072,768]{1,0:T(8,128)} %get-tuple-element.110.refs_2_.rest_0_), custom_call_target="tpu_custom_call" | custom-call | flops 1 | bytes 1 | tf_op jit(solution)/shard_map/halves/pallas_call | solution.py:460
  232.9 4.2 %place.6 = (f32[3072,768]{1,0:T(8,128)}, f32[768,3072]{1,0:T(8,128)}) custom-call(s32[6]{0:T(128)} %stack.27.refs_0_.at_ref, bf16[768,768]{1,0:T(8,128)(2,1)} %collective-permute-done.20.refs_0_.own_ref, bf16[768,768]{1,0:T(8,128)(2,1)} %copy-done.8, f32[3072,768]{1,0:T(8,128)} %get-tuple-element.110.refs_2_.rest_0_, ...), custom_call_target="tpu_custom_call", output_to_operand_aliasing={{0}: (3, {}), {1}: (4, {})} | custom-call | flops 1 | bytes 1 | tf_op jit(solution)/shard_map/place/pallas_call | solution.py:383
  238.1 4.2 %place.7 = (f32[3072,768]{1,0:T(8,128)}, f32[768,3072]{1,0:T(8,128)}) custom-call(s32[6]{0:T(128)} %stack.27.refs_0_.at_ref, bf16[768,768]{1,0:T(8,128)(2,1)} %copy-done.3, bf16[768,768]{1,0:T(8,128)(2,1)} %copy-done.7, f32[3072,768]{1,0:T(8,128)} %get-tuple-element.113.rest_0_, ...), custom_call_target="tpu_custom_call", output_to_operand_aliasing={{0}: (3, {}), {1}: (4, {})} | custom-call | flops 1 | bytes 1 | tf_op jit(solution)/shard_map/place/pallas_call | solution.py:383
  243.4 4.6 %late_place.1 = (f32[768,768]{1,0:T(8,128)}, f32[768,768]{1,0:T(8,128)}, f32[768,128]{1,0:T(8,128)}, f32[64]{0:T(128)}, f32[768]{0:T(1024)}, /*index=5*/f32[768]...) custom-call(s32[6]{0:T(128)} %stack.27.refs_0_.at_ref, ...), custom_call_target="tpu_custom_call" | custom-call | flops 1 | bytes 1 | tf_op jit(solution)/shard_map/late_place/pallas_call | solution.py:460
  251.7 3.4 %place.8 = (f32[3072,768]{1,0:T(8,128)}, f32[768,3072]{1,0:T(8,128)}) custom-call(s32[6]{0:T(128)} %stack.27.refs_0_.at_ref, bf16[384,768]{1,0:T(8,128)(2,1)} %tie.5.own_ref, bf16[384,768]{1,0:T(8,128)(2,1)} %copy-done.20, f32[3072,768]{1,0:T(8,128)} %get-tuple-element.115.refs_0_.rest_0_, ...), custom_call_target="tpu_custom_call", output_to_operand_aliasing={{0}: (3, {}), {1}: (4, {})} | custom-call | flops 1 | bytes 1 | tf_op jit(solution)/shard_map/place/pallas_call | solution.py:383
  255.9 3.4 %place.9 = (f32[3072,768]{1,0:T(8,128)}, f32[768,3072]{1,0:T(8,128)}) custom-call(s32[6]{0:T(128)} %stack.27.refs_0_.at_ref, bf16[384,768]{1,0:T(8,128)(2,1)} %tie.4.own_ref, bf16[384,768]{1,0:T(8,128)(2,1)} %copy-done.21, f32[3072,768]{1,0:T(8,128)} %get-tuple-element.118.rest_0_, ...), custom_call_target="tpu_custom_call", output_to_operand_aliasing={{0}: (3, {}), {1}: (4, {})} | custom-call | flops 1 | bytes 1 | tf_op jit(solution)/shard_map/place/pallas_call | solution.py:383
  (132 shorter events, 35.4 us)
Async XLA Ops:
  2.9 18.9 %all-to-all-start = ((bf16[16,128,128]{2,1,0:T(8,128)(2,1)}), bf16[16,128,128]{2,1,0:T(8,128)(2,1)S(1)}, u32[]{:S(2)}, u32[]{:S(2)}) async-start(bf16[16,128,128]{2,1,0:T(8,128)(2,1)} %get-tuple-element.71), calls=%async_computation | async-start | bytes 1048576 | tf_op jit(solution)/shard_map/all_to_all | solution.py:596
  21.8 4.7 %copy-start.4 = (bf16[16,128,128]{2,1,0:T(8,128)(2,1)}, bf16[16,128,128]{2,1,0:T(8,128)(2,1)S(1)}, u32[]{:S(2)}) copy-start(bf16[16,128,128]{2,1,0:T(8,128)(2,1)S(1)} %all-to-all-done.refs_3_) | copy-start | bytes 1572868
  22.6 3.9 %collective-permute-start = (bf16[16,128,128]{2,1,0:T(8,128)(2,1)}, bf16[16,128,128]{2,1,0:T(8,128)(2,1)S(1)}, u32[]{:S(2)}, u32[]{:S(2)}) collective-permute-start(bf16[16,128,128]{2,1,0:T(8,128)(2,1)} %tie.3), channel_id=1, source_target_pairs={{0,1},{1,0},{2,3},{3,2},{4,5},{5,4},{6,7},{7,6},{8,9},{9,8},{10,11... | collective-permute-start | bytes 1572872 | tf_op jit(solution)/shard_map/ppermute | solution.py:100
  55.7 2.9 %collective-permute-start.1 = (bf16[128,3072]{1,0:T(8,128)(2,1)}, bf16[128,3072]{1,0:T(8,128)(2,1)S(1)}, u32[]{:S(2)}, u32[]{:S(2)}) collective-permute-start(bf16[128,3072]{1,0:T(8,128)(2,1)} %get-tuple-element.82), channel_id=1, source_target_pairs={{0,1},{1,0},{2,3},{3,2},{4,5},{5,4},{6,7},{7,6},{8,9},{9,8},{10,11... | collective-permute-start | bytes 2359304 | tf_op jit(solution)/shard_map/ppermute | solution.py:100
  56.1 2.4 collective-permute-start.2
  62.9 28.0 %all-to-all-start.1 = ((bf16[4,256,1536]{2,1,0:T(8,128)(2,1)}), bf16[4,256,1536]{2,1,0:T(8,128)(2,1)S(1)}, u32[]{:S(2)}, u32[]{:S(2)}) async-start(bf16[4,256,1536]{2,1,0:T(8,128)(2,1)} %pack.1.refs_11_), calls=%async_computation.1 | async-start | bytes 6291456 | tf_op jit(solution)/shard_map/all_to_all | solution.py:631
  66.8 21.8 %copy-start.29 = (bf16[128,768]{1,0:T(8,128)(2,1)S(1)}, bf16[128,768]{1,0:T(8,128)(2,1)}, u32[]{:S(2)}) copy-start(bf16[128,768]{1,0:T(8,128)(2,1)} %get-tuple-element.90) | copy-start | bytes 589828
  88.2 2.7 %collective-permute-start.3 = (bf16[16,128,128]{2,1,0:T(8,128)(2,1)}, bf16[16,128,128]{2,1,0:T(8,128)(2,1)}, u32[]{:S(2)}, u32[]{:S(2)}) collective-permute-start(bf16[16,128,128]{2,1,0:T(8,128)(2,1)} %get-tuple-element.88), channel_id=1, source_target_pairs={{0,1},{1,0},{2,3},{3,2},{4,5},{5,4},{6,7},{7,6},{8,9},{9,8},{10,11... | collective-permute-start | bytes 1572872 | tf_op jit(solution)/shard_map/ppermute | solution.py:100
  88.6 2.1 collective-permute-start.4
  88.7 2.2 collective-permute-start.5
  90.9 1.7 copy-start
  96.2 41.5 %all-to-all-start.2 = ((bf16[16,416,128]{2,1,0:T(8,128)(2,1)}), bf16[16,416,128]{2,1,0:T(8,128)(2,1)S(1)}, u32[]{:S(2)}, u32[]{:S(2)}) async-start(bf16[16,416,128]{2,1,0:T(8,128)(2,1)} %share.1), calls=%async_computation.2 | async-start | bytes 3407872 | tf_op jit(solution)/shard_map/all_to_all | solution.py:636
  107.2 7.3 %collective-permute-start.7 = (bf16[192,768]{1,0:T(8,128)(2,1)}, bf16[192,768]{1,0:T(8,128)(2,1)S(1)}, u32[]{:S(2)}, u32[]{:S(2)}) collective-permute-start(bf16[192,768]{1,0:T(8,128)(2,1)} %get-tuple-element.97), channel_id=1, source_target_pairs={{0,8},{1,33},{2,10},{3,35},{4,12},{5,37},{6,14},{7,39},{8,16},{9,4... | collective-permute-start | bytes 884744 | tf_op jit(solution)/shard_map/ppermute | solution.py:96
  108.4 6.1 %collective-permute-start.8 = (bf16[192,768]{1,0:T(8,128)(2,1)}, bf16[192,768]{1,0:T(8,128)(2,1)S(1)}, u32[]{:S(2)}, u32[]{:S(2)}) collective-permute-start(bf16[192,768]{1,0:T(8,128)(2,1)} %get-tuple-element.98), channel_id=1, source_target_pairs={{0,24},{1,97},{2,26},{3,99},{4,28},{5,101},{6,30},{7,103},{8,0},{9... | collective-permute-start | bytes 884744 | tf_op jit(solution)/shard_map/ppermute | solution.py:96
  109.8 8.8 %collective-permute-start.9 = (bf16[192,768]{1,0:T(8,128)(2,1)}, bf16[192,768]{1,0:T(8,128)(2,1)S(1)}, u32[]{:S(2)}, u32[]{:S(2)}) collective-permute-start(bf16[192,768]{1,0:T(8,128)(2,1)} %get-tuple-element.99), channel_id=1, source_target_pairs={{0,16},{1,65},{2,18},{3,67},{4,20},{5,69},{6,22},{7,71},{8,24},{9,... | collective-permute-start | bytes 884744 | tf_op jit(solution)/shard_map/ppermute | solution.py:96
  114.5 27.8 %copy-start.10 = (bf16[192,768]{1,0:T(8,128)(2,1)}, bf16[192,768]{1,0:T(8,128)(2,1)S(1)}, u32[]{:S(2)}) copy-start(bf16[192,768]{1,0:T(8,128)(2,1)S(1)} %collective-permute-done.7.refs_5_) | copy-start | bytes 884740
  114.5 27.7 %copy-start.11 = (bf16[192,768]{1,0:T(8,128)(2,1)}, bf16[192,768]{1,0:T(8,128)(2,1)S(1)}, u32[]{:S(2)}) copy-start(bf16[192,768]{1,0:T(8,128)(2,1)S(1)} %collective-permute-done.8.refs_6_) | copy-start | bytes 884740
  118.6 23.6 %copy-start.12 = (bf16[192,768]{1,0:T(8,128)(2,1)}, bf16[192,768]{1,0:T(8,128)(2,1)S(1)}, u32[]{:S(2)}) copy-start(bf16[192,768]{1,0:T(8,128)(2,1)S(1)} %collective-permute-done.9.refs_7_) | copy-start | bytes 884740
  119.8 9.8 %collective-permute-start.10 = (bf16[192,768]{1,0:T(8,128)(2,1)S(1)}, bf16[192,768]{1,0:T(8,128)(2,1)S(1)}, u32[]{:S(2)}, u32[]{:S(2)}) collective-permute-start(bf16[192,768]{1,0:T(8,128)(2,1)S(1)} %add_convert_fusion.1), channel_id=1, source_target_pairs={{0,32},{1,3},{2,34},{3,5},{4,36},{5,7},{6,38},{7,1},{8,40},{9,11},... | collective-permute-start | bytes 884744 | tf_op jit(solution)/shard_map/ppermute | solution.py:96
  121.3 10.0 %collective-permute-start.11 = (bf16[192,768]{1,0:T(8,128)(2,1)S(1)}, bf16[192,768]{1,0:T(8,128)(2,1)S(1)}, u32[]{:S(2)}, u32[]{:S(2)}) collective-permute-start(bf16[192,768]{1,0:T(8,128)(2,1)S(1)} %add_convert_fusion.1), channel_id=1, source_target_pairs={{0,96},{1,7},{2,98},{3,1},{4,100},{5,3},{6,102},{7,5},{8,104},{9,1... | collective-permute-start | bytes 884744 | tf_op jit(solution)/shard_map/ppermute | solution.py:96
  122.6 12.4 %collective-permute-start.12 = (bf16[192,768]{1,0:T(8,128)(2,1)S(1)}, bf16[192,768]{1,0:T(8,128)(2,1)S(1)}, u32[]{:S(2)}, u32[]{:S(2)}) collective-permute-start(bf16[192,768]{1,0:T(8,128)(2,1)S(1)} %add_convert_fusion.1), channel_id=1, source_target_pairs={{0,64},{1,5},{2,66},{3,7},{4,68},{5,1},{6,70},{7,3},{8,72},{9,13},... | collective-permute-start | bytes 884744 | tf_op jit(solution)/shard_map/ppermute | solution.py:96
  129.6 12.7 %copy-start.13 = (bf16[192,768]{1,0:T(8,128)(2,1)}, bf16[192,768]{1,0:T(8,128)(2,1)S(1)}, u32[]{:S(2)}) copy-start(bf16[192,768]{1,0:T(8,128)(2,1)S(1)} %collective-permute-done.10.refs_2_) | copy-start | bytes 884740
  131.2 11.0 %copy-start.15 = (bf16[192,768]{1,0:T(8,128)(2,1)}, bf16[192,768]{1,0:T(8,128)(2,1)S(1)}, u32[]{:S(2)}) copy-start(bf16[192,768]{1,0:T(8,128)(2,1)S(1)} %collective-permute-done.11.refs_3_) | copy-start | bytes 884740
  136.5 41.8 %collective-permute-start.16 = (bf16[192,768]{1,0:T(8,128)(2,1)}, bf16[192,768]{1,0:T(8,128)(2,1)S(1)}, u32[]{:S(2)}, u32[]{:S(2)}) collective-permute-start(bf16[192,768]{1,0:T(8,128)(2,1)} %add_convert_fusion.refs_1_), channel_id=1, source_target_pairs={{0,8},{1,33},{2,10},{3,35},{4,12},{5,37},{6,14},{7,39},{8,16},{9,4... | collective-permute-start | bytes 884744 | tf_op jit(solution)/shard_map/ppermute | solution.py:96
  142.3 16.0 %collective-permute-start.6 = (f32[128,128]{1,0:T(8,128)}, f32[128,128]{1,0:T(8,128)S(1)}, u32[]{:S(2)}, u32[]{:S(2)}) collective-permute-start(f32[128,128]{1,0:T(8,128)} %get-tuple-element.96), channel_id=1, source_target_pairs={{0,1},{1,0},{2,3},{3,2},{4,5},{5,4},{6,7},{7,6},{8,9},{9,8},{10,11... | collective-permute-start | bytes 196616 | tf_op jit(solution)/shard_map/ppermute | solution.py:100
  157.1 22.5 %collective-permute-start.17 = (bf16[192,768]{1,0:T(8,128)(2,1)}, bf16[192,768]{1,0:T(8,128)(2,1)S(1)}, u32[]{:S(2)}, u32[]{:S(2)}) collective-permute-start(bf16[192,768]{1,0:T(8,128)(2,1)} %add_convert_fusion.refs_1_), channel_id=1, source_target_pairs={{0,24},{1,97},{2,26},{3,99},{4,28},{5,101},{6,30},{7,103},{8,0},{9... | collective-permute-start | bytes 884744 | tf_op jit(solution)/shard_map/ppermute | solution.py:96
  157.1 22.5 %collective-permute-start.18 = (bf16[192,768]{1,0:T(8,128)(2,1)}, bf16[192,768]{1,0:T(8,128)(2,1)S(1)}, u32[]{:S(2)}, u32[]{:S(2)}) collective-permute-start(bf16[192,768]{1,0:T(8,128)(2,1)} %add_convert_fusion.refs_1_), channel_id=1, source_target_pairs={{0,16},{1,65},{2,18},{3,67},{4,20},{5,69},{6,22},{7,71},{8,24},{9,... | collective-permute-start | bytes 884744 | tf_op jit(solution)/shard_map/ppermute | solution.py:96
  174.5 5.9 %collective-permute-start.13 = (bf16[48,896]{1,0:T(8,128)(2,1)}, bf16[48,896]{1,0:T(8,128)(2,1)S(1)}, u32[]{:S(2)}, u32[]{:S(2)}) collective-permute-start(bf16[48,896]{1,0:T(8,128)(2,1)} %strip.1.refs_0_), channel_id=1, source_target_pairs={{0,32},{1,33},{2,34},{3,35},{4,36},{5,37},{6,38},{7,39},{8,40},{9,... | collective-permute-start | bytes 258056 | tf_op jit(solution)/shard_map/ppermute | solution.py:96
  175.0 5.4 %collective-permute-start.14 = (bf16[48,896]{1,0:T(8,128)(2,1)}, bf16[48,896]{1,0:T(8,128)(2,1)S(1)}, u32[]{:S(2)}, u32[]{:S(2)}) collective-permute-start(bf16[48,896]{1,0:T(8,128)(2,1)} %strip.1.refs_0_), channel_id=1, source_target_pairs={{0,96},{1,97},{2,98},{3,99},{4,100},{5,101},{6,102},{7,103},{8,104... | collective-permute-start | bytes 258056 | tf_op jit(solution)/shard_map/ppermute | solution.py:96
  178.4 5.4 %copy-start.9 = (bf16[192,768]{1,0:T(8,128)(2,1)}, bf16[192,768]{1,0:T(8,128)(2,1)S(1)}, u32[]{:S(2)}) copy-start(bf16[192,768]{1,0:T(8,128)(2,1)S(1)} %collective-permute-done.16.refs_4_.refs_2_) | copy-start | bytes 884740
  178.4 5.4 %collective-permute-start.15 = (bf16[48,896]{1,0:T(8,128)(2,1)}, bf16[48,896]{1,0:T(8,128)(2,1)S(1)}, u32[]{:S(2)}, u32[]{:S(2)}) collective-permute-start(bf16[48,896]{1,0:T(8,128)(2,1)} %strip.1.refs_0_), channel_id=1, source_target_pairs={{0,64},{1,65},{2,66},{3,67},{4,68},{5,69},{6,70},{7,71},{8,72},{9,... | collective-permute-start | bytes 258056 | tf_op jit(solution)/shard_map/ppermute | solution.py:96
  179.6 4.1 %copy-start.14 = (bf16[192,768]{1,0:T(8,128)(2,1)}, bf16[192,768]{1,0:T(8,128)(2,1)S(1)}, u32[]{:S(2)}) copy-start(bf16[192,768]{1,0:T(8,128)(2,1)S(1)} %collective-permute-done.17.refs_5_.refs_3_) | copy-start | bytes 884740
  179.6 4.1 %copy-start.16 = (bf16[192,768]{1,0:T(8,128)(2,1)}, bf16[192,768]{1,0:T(8,128)(2,1)S(1)}, u32[]{:S(2)}) copy-start(bf16[192,768]{1,0:T(8,128)(2,1)S(1)} %collective-permute-done.18.refs_6_.refs_4_) | copy-start | bytes 884740
  180.4 3.3 %copy-start.25 = (bf16[48,896]{1,0:T(8,128)(2,1)}, bf16[48,896]{1,0:T(8,128)(2,1)S(1)}, u32[]{:S(2)}) copy-start(bf16[48,896]{1,0:T(8,128)(2,1)S(1)} %collective-permute-done.13.refs_1_) | copy-start | bytes 258052
  180.4 3.3 %copy-start.26 = (bf16[48,896]{1,0:T(8,128)(2,1)}, bf16[48,896]{1,0:T(8,128)(2,1)S(1)}, u32[]{:S(2)}) copy-start(bf16[48,896]{1,0:T(8,128)(2,1)S(1)} %collective-permute-done.14.refs_2_) | copy-start | bytes 258052
  186.6 19.7 %all-to-all-start.4 = ((bf16[16,48,896]{2,1,0:T(8,128)(2,1)}), bf16[16,48,896]{2,1,0:T(8,128)(2,1)S(1)}, u32[]{:S(2)}, u32[]{:S(2)}) async-start(bf16[16,48,896]{2,1,0:T(8,128)(2,1)} %copies.1.refs_5_), calls=%async_computation.4 | async-start | bytes 2752512 | tf_op jit(solution)/shard_map/all_to_all | solution.py:659
  192.7 29.1 %collective-permute-start.20 = (bf16[768,768]{1,0:T(8,128)(2,1)}, bf16[768,768]{1,0:T(8,128)(2,1)}, u32[]{:S(2)}, u32[]{:S(2)}) collective-permute-start(bf16[768,768]{1,0:T(8,128)(2,1)} %join.1.own_ref), channel_id=1, source_target_pairs={{0,2},{1,9},{2,4},{3,11},{4,6},{5,13},{6,0},{7,15},{8,10},{9,17},{... | collective-permute-start | bytes 3538952 | tf_op jit(solution)/shard_map/ppermute | solution.py:96
  193.9 29.5 %collective-permute-start.21 = (bf16[768,768]{1,0:T(8,128)(2,1)}, bf16[768,768]{1,0:T(8,128)(2,1)S(1)}, u32[]{:S(2)}, u32[]{:S(2)}) collective-permute-start(bf16[768,768]{1,0:T(8,128)(2,1)} %join.1.own_ref), channel_id=1, source_target_pairs={{0,6},{1,25},{2,0},{3,27},{4,2},{5,29},{6,4},{7,31},{8,14},{9,1},{... | collective-permute-start | bytes 3538952 | tf_op jit(solution)/shard_map/ppermute | solution.py:96
  195.3 28.1 %collective-permute-start.22 = (bf16[768,768]{1,0:T(8,128)(2,1)}, bf16[768,768]{1,0:T(8,128)(2,1)}, u32[]{:S(2)}, u32[]{:S(2)}) collective-permute-start(bf16[768,768]{1,0:T(8,128)(2,1)} %join.1.own_ref), channel_id=1, source_target_pairs={{0,1},{1,0},{2,3},{3,2},{4,5},{5,4},{6,7},{7,6},{8,9},{9,8},{10,11... | collective-permute-start | bytes 3538952 | tf_op jit(solution)/shard_map/ppermute | solution.py:100
  206.3 24.1 %copy-start.2 = (bf16[16,48,896]{2,1,0:T(8,128)(2,1)}, bf16[16,48,896]{2,1,0:T(8,128)(2,1)S(1)}, u32[]{:S(2)}) copy-start(bf16[16,48,896]{2,1,0:T(8,128)(2,1)S(1)} %all-to-all-done.4.refs_1_) | copy-start | bytes 4128772
  206.3 35.9 %collective-permute-start.19 = (bf16[16,48,896]{2,1,0:T(8,128)(2,1)S(1)}, bf16[16,48,896]{2,1,0:T(8,128)(2,1)S(1)}, u32[]{:S(2)}, u32[]{:S(2)}) collective-permute-start(bf16[16,48,896]{2,1,0:T(8,128)(2,1)S(1)} %all-to-all-done.4.refs_1_), channel_id=1, source_target_pairs={{0,1},{1,0},{2,3},{3,2},{4,5},{5,4},{6,7},{7,6},{8,9},{9,8},{10,11... | collective-permute-start | bytes 4128776 | tf_op jit(solution)/shard_map/ppermute | solution.py:100
  221.8 10.1 %collective-permute-start.25 = (bf16[768,768]{1,0:T(8,128)(2,1)}, bf16[768,768]{1,0:T(8,128)(2,1)S(1)}, u32[]{:S(2)}, u32[]{:S(2)}) collective-permute-start(bf16[768,768]{1,0:T(8,128)(2,1)} %collective-permute-done.20.refs_0_.own_ref), channel_id=1, source_target_pairs={{0,1},{1,0},{2,3},{3,2},{4,5},{5,4},{6,7},{7,6},{8,9},{9,8},{10,11... | collective-permute-start | bytes 3538952 | tf_op jit(solution)/shard_map/ppermute | solution.py:100
  223.4 4.3 %copy-start.3 = (bf16[768,768]{1,0:T(8,128)(2,1)}, bf16[768,768]{1,0:T(8,128)(2,1)S(1)}, u32[]{:S(2)}) copy-start(bf16[768,768]{1,0:T(8,128)(2,1)S(1)} %collective-permute-done.21.refs_1_.own_ref) | copy-start | bytes 3538948
  223.4 13.7 %collective-permute-start.24 = (bf16[768,768]{1,0:T(8,128)(2,1)S(1)}, bf16[768,768]{1,0:T(8,128)(2,1)S(1)}, u32[]{:S(2)}, u32[]{:S(2)}) collective-permute-start(bf16[768,768]{1,0:T(8,128)(2,1)S(1)} %collective-permute-done.21.refs_1_.own_ref), channel_id=1, source_target_pairs={{0,1},{1,0},{2,3},{3,2},{4,5},{5,4},{6,7},{7,6},{8,9},{9,8},{10,11... | collective-permute-start | bytes 3538952 | tf_op jit(solution)/shard_map/ppermute | solution.py:100
  230.4 17.5 %collective-permute-start.27 = (bf16[384,768]{1,0:T(8,128)(2,1)}, bf16[384,768]{1,0:T(8,128)(2,1)}, u32[]{:S(2)}, u32[]{:S(2)}) collective-permute-start(bf16[384,768]{1,0:T(8,128)(2,1)} %get-tuple-element.116), channel_id=1, source_target_pairs={{0,6},{1,25},{2,0},{3,27},{4,2},{5,29},{6,4},{7,31},{8,14},{9,1},{... | collective-permute-start | bytes 1769480 | tf_op jit(solution)/shard_map/ppermute | solution.py:96
  231.6 17.4 %collective-permute-start.23 = (bf16[384,768]{1,0:T(8,128)(2,1)}, bf16[384,768]{1,0:T(8,128)(2,1)S(1)}, u32[]{:S(2)}, u32[]{:S(2)}) collective-permute-start(bf16[384,768]{1,0:T(8,128)(2,1)} %get-tuple-element.111), channel_id=1, source_target_pairs={{0,2},{1,9},{2,4},{3,11},{4,6},{5,13},{6,0},{7,15},{8,10},{9,17},{... | collective-permute-start | bytes 1769480 | tf_op jit(solution)/shard_map/ppermute | solution.py:96
  247.9 2.9 %collective-permute-start.28 = (bf16[384,768]{1,0:T(8,128)(2,1)}, bf16[384,768]{1,0:T(8,128)(2,1)S(1)}, u32[]{:S(2)}, u32[]{:S(2)}) collective-permute-start(bf16[384,768]{1,0:T(8,128)(2,1)} %tie.5.own_ref), channel_id=1, source_target_pairs={{0,1},{1,0},{2,3},{3,2},{4,5},{5,4},{6,7},{7,6},{8,9},{9,8},{10,11... | collective-permute-start | bytes 1769480 | tf_op jit(solution)/shard_map/ppermute | solution.py:100
  249.8 5.2 %collective-permute-start.26 = (bf16[384,768]{1,0:T(8,128)(2,1)}, bf16[384,768]{1,0:T(8,128)(2,1)S(1)}, u32[]{:S(2)}, u32[]{:S(2)}) collective-permute-start(bf16[384,768]{1,0:T(8,128)(2,1)} %tie.4.own_ref), channel_id=1, source_target_pairs={{0,1},{1,0},{2,3},{3,2},{4,5},{5,4},{6,7},{7,6},{8,9},{9,8},{10,11... | collective-permute-start | bytes 1769480 | tf_op jit(solution)/shard_map/ppermute | solution.py:100
  (15 other events, 12.6 us)

commit v4 on v3

--- a/solution.py
+++ b/solution.py
@@ -426,6 +426,10 @@
     out_ref[:, D:] = jnp.sum(tail_ref[...].astype(f32), axis=0).astype(bf16)
 
 
+def part_kernel(a_ref, b_ref, c_ref, d_ref, out_ref):
+    out_ref[...] = pair_sums(a_ref[...], b_ref[...], c_ref[...], d_ref[...])
+
+
 def copies_kernel(a_ref, b_ref, c_ref, d_ref, out_ref):
     total = pair_sums(a_ref[...], b_ref[...], c_ref[...], d_ref[...])
     for i in range(CHIPS):
@@ -570,15 +574,17 @@
     )(v, *after)
 
 
-def feed_forward_spread(at, totals, before_join, before_far):
+def feed_forward_spread(at, totals, before_join, beside):
     u = call(join_kernel, (at,) + totals, shapes(((D, D), bf16))[0], name="join", after=before_join)
     before, after = send(u, 0, 1), send(u, 0, 3)
     kept = place(at, 0, u, swap(u), ())
-    low, high = call(halves_kernel, (before, after), shapes(HALF, HALF), name="halves", after=kept[:1])
+    marks = (swap(kept[0][:8, :128]),)
+    low, high = call(halves_kernel, (before, after), shapes(HALF, HALF), name="halves", after=marks)
+    before, after = tie(before, low), tie(after, low)
     low, high = send(low, 0, 1), send(high, 0, 3)
     kept = place(at, 3, before, swap(before), kept)
     kept = place(at, 1, after, swap(after), kept)
-    low, high = (tie(v, kept[0], *before_far) for v in (low, high))
+    low, high = (tie(v, kept[0], beside) for v in (low, high))
     kept = place(at, 2, high, swap(high), kept)
     return place(at, 2, low, swap(low), kept, part=1)
 
@@ -600,7 +606,8 @@
     start_lanes = jnp.tile(own_start.reshape(RB, 1, RBR), (1, 1, 128 // RBR))
     q = call(query_kernel, (n1, w_query, b_query), shapes(narrow)[0], name="query", flops=2 * ROWS * D * D,
              after=(key_cols, own_lanes, start_lanes, kinds))
-    kv_other = swap(tie(kv_same, q))
+    kv_same = tie(kv_same, q)
+    kv_other = swap(kv_same)
 
     att, left, left_send, xq, o, lse, kv_all = attend(at, kinds, q, kv_same, kv_other, key_cols, own_lanes, start_lanes, n1)
     left_other = swap(left_send)
@@ -637,7 +644,6 @@
 
     pieces = call(weight_kernel, (at, slabs), shapes(*[QUARTER] * 4), [pltpu.VMEM((D, D), f32)], name="weights")
     ff_parts = (pieces[0],) + spread(1, *pieces[1:])
-    ff_crossed = gather4(pair_sums(*ff_parts), 2)
     gin, tail, tail_send, _ = pl.pallas_call(
         leave_kernel,
         grid=(1,),
@@ -651,6 +657,8 @@
 
     late_parts = call(late_kernel, (at, left, left_other, tail, swap(tail_send)), shapes(((CHIPS, STRIP, 128), bf16))[0],
                       [pltpu.VMEM((D, 128), f32)], name="late", after=ff_parts[1:])
+    ff_part = call(part_kernel, ff_parts, shapes(QUARTER)[0], name="part", after=(late_parts,))
+    ff_crossed = gather4(ff_part, 2)
     late_parts = lax.all_to_all(late_parts, ("y", "z"), 0, 0, tiled=True)
     ff_totals = gather4(pair_sums(*ff_crossed), 1)
     strip = call(strip_kernel, (parts, late_parts), shapes(((STRIP, D + 128), bf16))[0], name="strip", after=ff_crossed[1:])
@@ -663,7 +671,7 @@
         shapes(((D, D), f32), ((D, D), f32), ((D, 128), f32), one(HD), *[one(128 * n) for _, n in VECTORS]), name="late_place",
     )
     g_query, g_out, g_kv, g_value, g_bdown, g_gain2, g_bias2, g_bout, g_bup, g_gain1, g_bias1, g_bq = outs
-    g_down, g_up = feed_forward_spread(at, ff_totals, (copies,), outs[:1])
+    g_down, g_up = feed_forward_spread(at, ff_totals, (copies,), outs[2])
     shape = block_input.shape
     return (
         y.reshape(shape), gin.reshape(shape), g_gain1, g_bias1, g_query, g_bq, g_kv, g_value,

time: 260 us -> 245 us (0.942)
  blocking collectives: 11.6 us -> 0 us
  Pallas kernels: 104 us -> 99.1 us
  local copies, waits for them, and re-layouts: 18.3 us -> 22.3 us
    ppermute x13 -> x14, starting transfers between devices: 34.7 us -> 15.1 us  [swap(): return lax.ppermute(v, 'c', [(0, 1), (1, 0)])]
    ppermute x16, waiting for transfers between devices: 29 us -> 11.9 us  [send(): return lax.ppermute(v, AXES, ring(place, shift))]
    ppermute x16, starting transfers between devices: 19.6 us -> 33.8 us  [send(): return lax.ppermute(v, AXES, ring(place, shift))]
    all_to_all x1 -> x0, blocking collectives: 11.6 us -> none  [body(): late_parts = lax.all_to_all(late_parts, ('y', 'z'), 0, 0, tiled=True)]
    all_to_all x1, waiting for transfers between devices: 0.01 us -> 7.98 us  [body(): parts = lax.all_to_all(shares, ('y', 'z'), 0, 0, tiled=True)]
    pallas_call x13 -> x14, Pallas kernels: 71.1 us -> 65.9 us  [call(): pl.pallas_call(run, out_shape=outs, in_specs=[SMEM if v.dtype == jnp.int3...]
    all_to_all x1, waiting for transfers between devices: 6 us -> 10.9 us  [body(): late = lax.all_to_all(copies, ('y', 'z'), 0, 0, tiled=True)]
    all_to_all x0 -> x1, starting transfers between devices: none -> 4.86 us  [body(): late_parts = lax.all_to_all(late_parts, ('y', 'z'), 0, 0, tiled=True)]
  transfers between devices with their start and end apart: 33 -> 35, of which waited for: 16 -> 15; matrix products, arithmetic and copies ran while one was open for 4% -> 4% of each run, Pallas kernels for 24% -> 23%
where the time goes in v4:
time: 245 us; the launch traced here: 244 us
  Pallas kernels  99.1 us (40%)
  starting transfers between devices  77.2 us (32%)
  waiting for transfers between devices  40.4 us (16%)
  local copies, waits for them, and re-layouts  22.3 us (9%)
  other arithmetic  4.53 us (2%)
    pallas_call x14, Pallas kernels, call(): pl.pallas_call(run, out_shape=outs, in_specs=[SMEM if v.dtype == jnp.int3...  65.9 us
    ppermute x16, starting transfers between devices, send(): return lax.ppermute(v, AXES, ring(place, shift))  33.8 us
    pallas_call x5, Pallas kernels, place(): pl.pallas_call(place_kernel, grid_spec=pltpu.PrefetchScalarGridSpec(num_s...  19.3 us
    unnamed x72, local copies, waits for them, and re-layouts  16.5 us
    ppermute x14, starting transfers between devices, swap(): return lax.ppermute(v, 'c', [(0, 1), (1, 0)])  15.1 us
    ppermute x16, waiting for transfers between devices, send(): return lax.ppermute(v, AXES, ring(place, shift))  11.9 us
    all_to_all x1, waiting for transfers between devices, body(): late = lax.all_to_all(copies, ('y', 'z'), 0, 0, tiled=True)  10.9 us
    pallas_call x1, Pallas kernels, body(): pl.pallas_call(middle_kernel, grid=(steps,), out_shape=shapes(narrow, ((R...  10.6 us
  transfers between devices with their start and end apart: 35, of which 15 were waited for; matrix products, arithmetic and copies ran while one was open for 4% of the time, Pallas kernels for 23%

profile of v4, /device:TPU:1, one launch (start us, length us, event | category | flops | bytes accessed | tf_op | source)
XLA Modules:
  0.0 244.4 jit_solution(2010434558150837895)
XLA Ops:
  0.6 2.2 enter.1
  2.9 8.6 %all-to-all-start = ((bf16[16,128,128]{2,1,0:T(8,128)(2,1)}), bf16[16,128,128]{2,1,0:T(8,128)(2,1)S(1)}, u32[]{:S(2)}, u32[]{:S(2)}) async-start(bf16[16,128,128]{2,1,0:T(8,128)(2,1)} %get-tuple-element.71), calls=%async_computation | async-start | bytes 1048576 | tf_op jit(solution)/shard_map/all_to_all | solution.py:602
  17.0 2.2 broadcast_in_dim.28.refs_3_.refs_5_.refs_7_
  19.2 2.3 query.1.refs_0_.refs_2_
  22.6 2.1 collective-permute-start
  27.3 14.4 %attend.1 = (bf16[128,768]{1,0:T(8,128)(2,1)}, bf16[128,768]{1,0:T(8,128)(2,1)}, bf16[128,768]{1,0:T(8,128)(2,1)}, bf16[2,768,128]{2,1,0:T(8,128)(2,1)}, f32[2,7...) custom-call(s32[6]{0:T(128)} %stack.27.refs_0_.at_ref, s32[8]{0:T(128)} %select_n.94.refs_6_.refs_1_, ...), custom_call_target="tpu_custom_call" | custom-call | flops 1 | bytes 1 | tf_op jit(solution)/shard_map/attend/pallas_call | solution.py:464
  41.7 10.6 %middle.1 = (bf16[128,768]{1,0:T(8,128)(2,1)}, bf16[128,3072]{1,0:T(8,128)(2,1)}, bf16[128,3072]{1,0:T(8,128)(2,1)}, bf16[128,768]{1,0:T(8,128)(2,1)}, bf16[128,...) custom-call(s32[6]{0:T(128)} %stack.27.refs_0_.at_ref, ...), custom_call_target="tpu_custom_call" | custom-call | flops 1 | bytes 1 | tf_op jit(solution)/shard_map/middle/pallas_call | solution.py:618
  52.9 2.3 collective-permute-done.2.refs_3_
  56.1 3.4 %pack.1.refs_11_ = bf16[4,256,1536]{2,1,0:T(8,128)(2,1)} custom-call(bf16[128,3072]{1,0:T(8,128)(2,1)} %get-tuple-element.80.refs_0_, bf16[128,768]{1,0:T(8,128)(2,1)} %get-tuple-element.81.refs_1_, bf16[128,3072]{1,0:T(8,128)(2,1)} %copy-done.22, bf16[128,768]{1,0:T(8,128)(2,1)} %copy-done.28), custom_call_target="tpu_custom_call" | custom-call | flops 1 | bytes 1 | tf_op jit(solution)/shard_map/pack/pallas_call | solution.py:464
  59.5 3.9 %all-to-all-start.1 = ((bf16[4,256,1536]{2,1,0:T(8,128)(2,1)}), bf16[4,256,1536]{2,1,0:T(8,128)(2,1)S(1)}, u32[]{:S(2)}, u32[]{:S(2)}) async-start(bf16[4,256,1536]{2,1,0:T(8,128)(2,1)} %pack.1.refs_11_), calls=%async_computation.1 | async-start | bytes 6291456 | tf_op jit(solution)/shard_map/all_to_all | solution.py:638
  63.4 17.3 %attend_back.1 = (bf16[128,768]{1,0:T(8,128)(2,1)}, bf16[128,768]{1,0:T(8,128)(2,1)}, bf16[128,768]{1,0:T(8,128)(2,1)}, bf16[16,128,128]{2,1,0:T(8,128)(2,1)}, bf16[16,128,128]{2,1,0:T(8,128)(2,1)}) custom-call(s32[6]{0:T(128)} %stack.27.refs_0_.at_ref, s32[8]{0:T(128)} %select_n.94.refs_6_.refs_1_, bf16[2,768,128]{2,1,0:T(8,128)(2,1)} %get-tuple-element.74.refs_2_, ...), custom_call_target="tpu_custom_call" | custom-call | flops 1 | bytes 1 | tf_op jit(solution)/shard_map/attend_back/pallas_call | solution.py:464
  81.6 1.6 collective-permute-done.4.refs_3_.refs_2_
  84.4 1.7 copy-done
  86.1 3.6 %share.1 = bf16[16,416,128]{2,1,0:T(8,128)(2,1)} custom-call(bf16[16,128,128]{2,1,0:T(8,128)(2,1)} %get-tuple-element.87.refs_0_, bf16[16,128,128]{2,1,0:T(8,128)(2,1)} %collective-permute-done.3.refs_1_, bf16[128,768]{1,0:T(8,128)(2,1)} %get-tuple-element.89.refs_2_.refs_1_, bf16[128,768]{1,0:T(8,128)(2,1)} %copy-done.21, ...), custom_call_target="tpu_custom_call" | custom-call | flops 1 | bytes 1 | tf_op jit(solution)/shard_map/share/pallas_call | solution.py:464
  89.7 5.5 %all-to-all-start.2 = ((bf16[16,416,128]{2,1,0:T(8,128)(2,1)}), bf16[16,416,128]{2,1,0:T(8,128)(2,1)S(1)}, u32[]{:S(2)}, u32[]{:S(2)}) async-start(bf16[16,416,128]{2,1,0:T(8,128)(2,1)} %share.1), calls=%async_computation.2 | async-start | bytes 3407872 | tf_op jit(solution)/shard_map/all_to_all | solution.py:643
  95.2 4.5 %weights.1 = (bf16[192,768]{1,0:T(8,128)(2,1)}, bf16[192,768]{1,0:T(8,128)(2,1)}, bf16[192,768]{1,0:T(8,128)(2,1)}, bf16[192,768]{1,0:T(8,128)(2,1)}) custom-call(s32[6]{0:T(128)} %stack.27.refs_0_.at_ref, bf16[4,256,1536]{2,1,0:T(8,128)(2,1)} %copy-done), custom_call_target="tpu_custom_call" | custom-call | flops 1 | bytes 1 | tf_op jit(solution)/shard_map/weights/pallas_call | solution.py:464
  99.7 8.6 %collective-permute-start.7 = (bf16[192,768]{1,0:T(8,128)(2,1)}, bf16[192,768]{1,0:T(8,128)(2,1)S(1)}, u32[]{:S(2)}, u32[]{:S(2)}) collective-permute-start(bf16[192,768]{1,0:T(8,128)(2,1)} %get-tuple-element.97), channel_id=1, source_target_pairs={{0,8},{1,33},{2,10},{3,35},{4,12},{5,37},{6,14},{7,39},{8,16},{9,4... | collective-permute-start | bytes 884744 | tf_op jit(solution)/shard_map/ppermute | solution.py:96
  108.3 3.0 %collective-permute-start.9 = (bf16[192,768]{1,0:T(8,128)(2,1)}, bf16[192,768]{1,0:T(8,128)(2,1)S(1)}, u32[]{:S(2)}, u32[]{:S(2)}) collective-permute-start(bf16[192,768]{1,0:T(8,128)(2,1)} %get-tuple-element.99), channel_id=1, source_target_pairs={{0,16},{1,65},{2,18},{3,67},{4,20},{5,69},{6,22},{7,71},{8,24},{9,... | collective-permute-start | bytes 884744 | tf_op jit(solution)/shard_map/ppermute | solution.py:96
  111.3 8.0 %all-to-all-done.2.parts_ref.refs_0_ = bf16[16,416,128]{2,1,0:T(8,128)(2,1)S(1)} async-done(((bf16[16,416,128]{2,1,0:T(8,128)(2,1)}), bf16[16,416,128]{2,1,0:T(8,128)(2,1)S(1)}, u32[]{:S(2)}, u32[]{:S(2)}) %all-to-all-start.2) | async-done | bytes 1703968 | tf_op jit(solution)/shard_map/all_to_all | solution.py:643
  120.4 3.3 %leave.1 = (f32[768,128]{1,0:T(8,128)}, f32[128,128]{1,0:T(8,128)}, f32[128,128]{1,0:T(8,128)}, f32[128,128]{1,0:T(8,128)}) custom-call(s32[6]{0:T(128)} %stack.27.refs_0_.at_ref, bf16[128,768]{1,0:T(8,128)(2,1)} %bitcast.59, bf16[768]{0:T(1024)(128)(2,1)} %gain_ref.3, bf16[768,768]{1,0:T(8,128)(2,1)} %wq_ref.1, bf16[768,128]{1,0:T(8,128)(2,1)} %wkv_ref.1, ...), custom_call_target="tpu_custom_call" | custom-call | flops 1 | bytes 1 | tf_op jit(solution)/shard_map/leave/pallas_call | solution.py:647
  123.7 2.5 %collective-permute-start.6 = (f32[128,128]{1,0:T(8,128)}, f32[128,128]{1,0:T(8,128)S(1)}, u32[]{:S(2)}, u32[]{:S(2)}) collective-permute-start(f32[128,128]{1,0:T(8,128)} %get-tuple-element.96), channel_id=1, source_target_pairs={{0,1},{1,0},{2,3},{3,2},{4,5},{5,4},{6,7},{7,6},{8,9},{9,8},{10,11... | collective-permute-start | bytes 196616 | tf_op jit(solution)/shard_map/ppermute | solution.py:100
  128.0 2.0 late.1.refs_4_
  130.0 2.1 part.1
  132.4 2.4 collective-permute-start.11
  134.8 4.9 %all-to-all-start.3 = ((bf16[16,48,128]{2,1,0:T(8,128)(2,1)}), bf16[16,48,128]{2,1,0:T(8,128)(2,1)S(1)}, u32[]{:S(2)}, u32[]{:S(2)}) async-start(bf16[16,48,128]{2,1,0:T(8,128)(2,1)} %late.1.refs_4_), calls=%async_computation.3 | async-start | bytes 393216 | tf_op jit(solution)/shard_map/all_to_all | solution.py:662
  139.6 2.9 %collective-permute-done.10.refs_2_ = bf16[192,768]{1,0:T(8,128)(2,1)S(1)} collective-permute-done((bf16[192,768]{1,0:T(8,128)(2,1)}, bf16[192,768]{1,0:T(8,128)(2,1)S(1)}, u32[]{:S(2)}, u32[]{:S(2)}) %collective-permute-start.10) | collective-permute-done | bytes 294944 | tf_op jit(solution)/shard_map/ppermute | solution.py:96
  143.9 8.5 %collective-permute-start.16 = (bf16[192,768]{1,0:T(8,128)(2,1)S(1)}, bf16[192,768]{1,0:T(8,128)(2,1)S(1)}, u32[]{:S(2)}, u32[]{:S(2)}) collective-permute-start(bf16[192,768]{1,0:T(8,128)(2,1)S(1)} %add_convert_fusion.refs_1_), channel_id=1, source_target_pairs={{0,8},{1,33},{2,10},{3,35},{4,12},{5,37},{6,14},{7,39},{8,16},{9,4... | collective-permute-start | bytes 884744 | tf_op jit(solution)/shard_map/ppermute | solution.py:96
  152.5 3.3 %collective-permute-start.18 = (bf16[192,768]{1,0:T(8,128)(2,1)S(1)}, bf16[192,768]{1,0:T(8,128)(2,1)S(1)}, u32[]{:S(2)}, u32[]{:S(2)}) collective-permute-start(bf16[192,768]{1,0:T(8,128)(2,1)S(1)} %add_convert_fusion.refs_1_), channel_id=1, source_target_pairs={{0,16},{1,65},{2,18},{3,67},{4,20},{5,69},{6,22},{7,71},{8,24},{9,... | collective-permute-start | bytes 884744 | tf_op jit(solution)/shard_map/ppermute | solution.py:96
  156.5 2.3 strip.1.refs_0_
  159.1 2.3 collective-permute-start.14
  161.4 2.2 collective-permute-done.13.refs_1_
  164.2 4.4 %collective-permute-done.15.refs_3_ = bf16[48,896]{1,0:T(8,128)(2,1)S(1)} collective-permute-done((bf16[48,896]{1,0:T(8,128)(2,1)}, bf16[48,896]{1,0:T(8,128)(2,1)S(1)}, u32[]{:S(2)}, u32[]{:S(2)}) %collective-permute-start.15) | collective-permute-done | bytes 86048 | tf_op jit(solution)/shard_map/ppermute | solution.py:96
  170.2 2.2 copies.1.refs_5_
  172.4 5.5 %all-to-all-start.4 = ((bf16[16,48,896]{2,1,0:T(8,128)(2,1)}), bf16[16,48,896]{2,1,0:T(8,128)(2,1)}, u32[]{:S(2)}, u32[]{:S(2)}) async-start(bf16[16,48,896]{2,1,0:T(8,128)(2,1)} %copies.1.refs_5_), calls=%async_computation.4 | async-start | bytes 2752512 | tf_op jit(solution)/shard_map/all_to_all | solution.py:667
  177.9 2.3 join.1.own_ref
  180.3 2.3 collective-permute-start.22
  182.5 1.6 collective-permute-start.20
  185.3 10.9 %all-to-all-done.4.refs_1_ = bf16[16,48,896]{2,1,0:T(8,128)(2,1)} async-done(((bf16[16,48,896]{2,1,0:T(8,128)(2,1)}), bf16[16,48,896]{2,1,0:T(8,128)(2,1)}, u32[]{:S(2)}, u32[]{:S(2)}) %all-to-all-start.4) | async-done | bytes 1376288 | tf_op jit(solution)/shard_map/all_to_all | solution.py:667
  196.2 4.8 %collective-permute-start.19 = (bf16[16,48,896]{2,1,0:T(8,128)(2,1)}, bf16[16,48,896]{2,1,0:T(8,128)(2,1)}, u32[]{:S(2)}, u32[]{:S(2)}) collective-permute-start(bf16[16,48,896]{2,1,0:T(8,128)(2,1)} %all-to-all-done.4.refs_1_), channel_id=1, source_target_pairs={{0,1},{1,0},{2,3},{3,2},{4,5},{5,4},{6,7},{7,6},{8,9},{9,8},{10,11... | collective-permute-start | bytes 4128776 | tf_op jit(solution)/shard_map/ppermute | solution.py:100
  202.0 4.2 %place.5 = (f32[3072,768]{1,0:T(8,128)}, f32[768,3072]{1,0:T(8,128)}) custom-call(s32[6]{0:T(128)} %stack.27.refs_0_.at_ref, bf16[768,768]{1,0:T(8,128)(2,1)} %join.1.own_ref, bf16[768,768]{1,0:T(8,128)(2,1)} %copy-done.10), custom_call_target="tpu_custom_call" | custom-call | flops 1 | bytes 1 | tf_op jit(solution)/shard_map/place/pallas_call | solution.py:383
  206.9 2.4 collective-permute-done.20.refs_0_.v_ref
  211.3 2.7 %halves.1 = (bf16[384,768]{1,0:T(8,128)(2,1)}, bf16[384,768]{1,0:T(8,128)(2,1)}) custom-call(bf16[768,768]{1,0:T(8,128)(2,1)} %copy-done.3, bf16[768,768]{1,0:T(8,128)(2,1)} %copy-done.2, f32[8,128]{1,0:T(8,128)} %copy-done.33), custom_call_target="tpu_custom_call" | custom-call | flops 1 | bytes 1 | tf_op jit(solution)/shard_map/halves/pallas_call | solution.py:464
  215.4 1.5 collective-permute-start.28
  219.0 4.2 %place.6 = (f32[3072,768]{1,0:T(8,128)}, f32[768,3072]{1,0:T(8,128)}) custom-call(s32[6]{0:T(128)} %stack.27.refs_0_.at_ref, bf16[768,768]{1,0:T(8,128)(2,1)} %tie.7.own_ref, bf16[768,768]{1,0:T(8,128)(2,1)} %copy-done.9, f32[3072,768]{1,0:T(8,128)} %get-tuple-element.110.rest_0_, ...), custom_call_target="tpu_custom_call", output_to_operand_aliasing={{0}: (3, {}), {1}: (4, {})} | custom-call | flops 1 | bytes 1 | tf_op jit(solution)/shard_map/place/pallas_call | solution.py:383
  224.2 4.2 %place.7 = (f32[3072,768]{1,0:T(8,128)}, f32[768,3072]{1,0:T(8,128)}) custom-call(s32[6]{0:T(128)} %stack.27.refs_0_.at_ref, bf16[768,768]{1,0:T(8,128)(2,1)} %tie.6.own_ref, bf16[768,768]{1,0:T(8,128)(2,1)} %copy-done.8, f32[3072,768]{1,0:T(8,128)} %get-tuple-element.113.rest_0_, ...), custom_call_target="tpu_custom_call", output_to_operand_aliasing={{0}: (3, {}), {1}: (4, {})} | custom-call | flops 1 | bytes 1 | tf_op jit(solution)/shard_map/place/pallas_call | solution.py:383
  228.4 4.6 %late_place.1 = (f32[768,768]{1,0:T(8,128)}, f32[768,768]{1,0:T(8,128)}, f32[768,128]{1,0:T(8,128)}, f32[64]{0:T(128)}, f32[768]{0:T(1024)}, /*index=5*/f32[768]...) custom-call(s32[6]{0:T(128)} %stack.27.refs_0_.at_ref, ...), custom_call_target="tpu_custom_call" | custom-call | flops 1 | bytes 1 | tf_op jit(solution)/shard_map/late_place/pallas_call | solution.py:464
  236.8 3.4 %place.8 = (f32[3072,768]{1,0:T(8,128)}, f32[768,3072]{1,0:T(8,128)}) custom-call(s32[6]{0:T(128)} %stack.27.refs_0_.at_ref, bf16[384,768]{1,0:T(8,128)(2,1)} %tie.9.own_ref, bf16[384,768]{1,0:T(8,128)(2,1)} %copy-done.24, f32[3072,768]{1,0:T(8,128)} %get-tuple-element.115.refs_0_.rest_0_, ...), custom_call_target="tpu_custom_call", output_to_operand_aliasing={{0}: (3, {}), {1}: (4, {})} | custom-call | flops 1 | bytes 1 | tf_op jit(solution)/shard_map/place/pallas_call | solution.py:383
  241.0 3.4 %place.9 = (f32[3072,768]{1,0:T(8,128)}, f32[768,3072]{1,0:T(8,128)}) custom-call(s32[6]{0:T(128)} %stack.27.refs_0_.at_ref, bf16[384,768]{1,0:T(8,128)(2,1)} %tie.8.own_ref, bf16[384,768]{1,0:T(8,128)(2,1)} %copy-done.25, f32[3072,768]{1,0:T(8,128)} %get-tuple-element.118.rest_0_, ...), custom_call_target="tpu_custom_call", output_to_operand_aliasing={{0}: (3, {}), {1}: (4, {})} | custom-call | flops 1 | bytes 1 | tf_op jit(solution)/shard_map/place/pallas_call | solution.py:383
  (149 shorter events, 34.7 us)
Async XLA Ops:
  2.9 18.9 %all-to-all-start = ((bf16[16,128,128]{2,1,0:T(8,128)(2,1)}), bf16[16,128,128]{2,1,0:T(8,128)(2,1)S(1)}, u32[]{:S(2)}, u32[]{:S(2)}) async-start(bf16[16,128,128]{2,1,0:T(8,128)(2,1)} %get-tuple-element.71), calls=%async_computation | async-start | bytes 1048576 | tf_op jit(solution)/shard_map/all_to_all | solution.py:602
  22.6 3.9 %collective-permute-start = (bf16[16,128,128]{2,1,0:T(8,128)(2,1)}, bf16[16,128,128]{2,1,0:T(8,128)(2,1)S(1)}, u32[]{:S(2)}, u32[]{:S(2)}) collective-permute-start(bf16[16,128,128]{2,1,0:T(8,128)(2,1)} %tie.5.refs_3_), channel_id=1, source_target_pairs={{0,1},{1,0},{2,3},{3,2},{4,5},{5,4},{6,7},{7,6},{8,9},{9,8},{10,11... | collective-permute-start | bytes 1572872 | tf_op jit(solution)/shard_map/ppermute | solution.py:100
  52.3 2.9 %collective-permute-start.1 = (bf16[128,3072]{1,0:T(8,128)(2,1)}, bf16[128,3072]{1,0:T(8,128)(2,1)S(1)}, u32[]{:S(2)}, u32[]{:S(2)}) collective-permute-start(bf16[128,3072]{1,0:T(8,128)(2,1)} %get-tuple-element.82), channel_id=1, source_target_pairs={{0,1},{1,0},{2,3},{3,2},{4,5},{5,4},{6,7},{7,6},{8,9},{9,8},{10,11... | collective-permute-start | bytes 2359304 | tf_op jit(solution)/shard_map/ppermute | solution.py:100
  52.7 2.4 collective-permute-start.2
  59.5 24.9 %all-to-all-start.1 = ((bf16[4,256,1536]{2,1,0:T(8,128)(2,1)}), bf16[4,256,1536]{2,1,0:T(8,128)(2,1)S(1)}, u32[]{:S(2)}, u32[]{:S(2)}) async-start(bf16[4,256,1536]{2,1,0:T(8,128)(2,1)} %pack.1.refs_11_), calls=%async_computation.1 | async-start | bytes 6291456 | tf_op jit(solution)/shard_map/all_to_all | solution.py:638
  63.4 17.7 %copy-start.35 = (bf16[128,768]{1,0:T(8,128)(2,1)S(1)}, bf16[128,768]{1,0:T(8,128)(2,1)}, u32[]{:S(2)}) copy-start(bf16[128,768]{1,0:T(8,128)(2,1)} %get-tuple-element.90) | copy-start | bytes 589828
  80.7 2.7 %collective-permute-start.3 = (bf16[16,128,128]{2,1,0:T(8,128)(2,1)}, bf16[16,128,128]{2,1,0:T(8,128)(2,1)}, u32[]{:S(2)}, u32[]{:S(2)}) collective-permute-start(bf16[16,128,128]{2,1,0:T(8,128)(2,1)} %get-tuple-element.88), channel_id=1, source_target_pairs={{0,1},{1,0},{2,3},{3,2},{4,5},{5,4},{6,7},{7,6},{8,9},{9,8},{10,11... | collective-permute-start | bytes 1572872 | tf_op jit(solution)/shard_map/ppermute | solution.py:100
  81.1 2.1 collective-permute-start.4
  81.2 2.2 collective-permute-start.5
  83.2 1.3 copy-start.21
  84.4 1.7 copy-start
  89.7 29.5 %all-to-all-start.2 = ((bf16[16,416,128]{2,1,0:T(8,128)(2,1)}), bf16[16,416,128]{2,1,0:T(8,128)(2,1)S(1)}, u32[]{:S(2)}, u32[]{:S(2)}) async-start(bf16[16,416,128]{2,1,0:T(8,128)(2,1)} %share.1), calls=%async_computation.2 | async-start | bytes 3407872 | tf_op jit(solution)/shard_map/all_to_all | solution.py:643
  99.7 26.6 %collective-permute-start.7 = (bf16[192,768]{1,0:T(8,128)(2,1)}, bf16[192,768]{1,0:T(8,128)(2,1)S(1)}, u32[]{:S(2)}, u32[]{:S(2)}) collective-permute-start(bf16[192,768]{1,0:T(8,128)(2,1)} %get-tuple-element.97), channel_id=1, source_target_pairs={{0,8},{1,33},{2,10},{3,35},{4,12},{5,37},{6,14},{7,39},{8,16},{9,4... | collective-permute-start | bytes 884744 | tf_op jit(solution)/shard_map/ppermute | solution.py:96
  108.3 18.0 %collective-permute-start.8 = (bf16[192,768]{1,0:T(8,128)(2,1)}, bf16[192,768]{1,0:T(8,128)(2,1)S(1)}, u32[]{:S(2)}, u32[]{:S(2)}) collective-permute-start(bf16[192,768]{1,0:T(8,128)(2,1)} %get-tuple-element.98), channel_id=1, source_target_pairs={{0,24},{1,97},{2,26},{3,99},{4,28},{5,101},{6,30},{7,103},{8,0},{9... | collective-permute-start | bytes 884744 | tf_op jit(solution)/shard_map/ppermute | solution.py:96
  108.3 18.0 %collective-permute-start.9 = (bf16[192,768]{1,0:T(8,128)(2,1)}, bf16[192,768]{1,0:T(8,128)(2,1)S(1)}, u32[]{:S(2)}, u32[]{:S(2)}) collective-permute-start(bf16[192,768]{1,0:T(8,128)(2,1)} %get-tuple-element.99), channel_id=1, source_target_pairs={{0,16},{1,65},{2,18},{3,67},{4,20},{5,69},{6,22},{7,71},{8,24},{9,... | collective-permute-start | bytes 884744 | tf_op jit(solution)/shard_map/ppermute | solution.py:96
  119.3 1.2 copy-start.1
  123.7 3.7 %collective-permute-start.6 = (f32[128,128]{1,0:T(8,128)}, f32[128,128]{1,0:T(8,128)S(1)}, u32[]{:S(2)}, u32[]{:S(2)}) collective-permute-start(f32[128,128]{1,0:T(8,128)} %get-tuple-element.96), channel_id=1, source_target_pairs={{0,1},{1,0},{2,3},{3,2},{4,5},{5,4},{6,7},{7,6},{8,9},{9,8},{10,11... | collective-permute-start | bytes 196616 | tf_op jit(solution)/shard_map/ppermute | solution.py:100
  132.1 10.4 %collective-permute-start.10 = (bf16[192,768]{1,0:T(8,128)(2,1)}, bf16[192,768]{1,0:T(8,128)(2,1)S(1)}, u32[]{:S(2)}, u32[]{:S(2)}) collective-permute-start(bf16[192,768]{1,0:T(8,128)(2,1)} %part.1), channel_id=1, source_target_pairs={{0,32},{1,3},{2,34},{3,5},{4,36},{5,7},{6,38},{7,1},{8,40},{9,11},... | collective-permute-start | bytes 884744 | tf_op jit(solution)/shard_map/ppermute | solution.py:96
  132.4 10.2 %collective-permute-start.11 = (bf16[192,768]{1,0:T(8,128)(2,1)}, bf16[192,768]{1,0:T(8,128)(2,1)S(1)}, u32[]{:S(2)}, u32[]{:S(2)}) collective-permute-start(bf16[192,768]{1,0:T(8,128)(2,1)} %part.1), channel_id=1, source_target_pairs={{0,96},{1,7},{2,98},{3,1},{4,100},{5,3},{6,102},{7,5},{8,104},{9,1... | collective-permute-start | bytes 884744 | tf_op jit(solution)/shard_map/ppermute | solution.py:96
  134.8 7.8 %collective-permute-start.12 = (bf16[192,768]{1,0:T(8,128)(2,1)}, bf16[192,768]{1,0:T(8,128)(2,1)S(1)}, u32[]{:S(2)}, u32[]{:S(2)}) collective-permute-start(bf16[192,768]{1,0:T(8,128)(2,1)} %part.1), channel_id=1, source_target_pairs={{0,64},{1,5},{2,66},{3,7},{4,68},{5,1},{6,70},{7,3},{8,72},{9,13},... | collective-permute-start | bytes 884744 | tf_op jit(solution)/shard_map/ppermute | solution.py:96
  134.8 21.0 %all-to-all-start.3 = ((bf16[16,48,128]{2,1,0:T(8,128)(2,1)}), bf16[16,48,128]{2,1,0:T(8,128)(2,1)S(1)}, u32[]{:S(2)}, u32[]{:S(2)}) async-start(bf16[16,48,128]{2,1,0:T(8,128)(2,1)} %late.1.refs_4_), calls=%async_computation.3 | async-start | bytes 393216 | tf_op jit(solution)/shard_map/all_to_all | solution.py:662
  142.6 13.2 %copy-start.17 = (bf16[192,768]{1,0:T(8,128)(2,1)}, bf16[192,768]{1,0:T(8,128)(2,1)S(1)}, u32[]{:S(2)}) copy-start(bf16[192,768]{1,0:T(8,128)(2,1)S(1)} %collective-permute-done.10.refs_2_) | copy-start | bytes 884740
  142.6 13.2 %copy-start.18 = (bf16[192,768]{1,0:T(8,128)(2,1)}, bf16[192,768]{1,0:T(8,128)(2,1)S(1)}, u32[]{:S(2)}) copy-start(bf16[192,768]{1,0:T(8,128)(2,1)S(1)} %collective-permute-done.11.refs_3_) | copy-start | bytes 884740
  142.6 13.2 %copy-start.19 = (bf16[192,768]{1,0:T(8,128)(2,1)}, bf16[192,768]{1,0:T(8,128)(2,1)S(1)}, u32[]{:S(2)}) copy-start(bf16[192,768]{1,0:T(8,128)(2,1)S(1)} %collective-permute-done.12.refs_4_) | copy-start | bytes 884740
  143.9 28.5 %copy-start.20 = (bf16[192,768]{1,0:T(8,128)(2,1)}, bf16[192,768]{1,0:T(8,128)(2,1)S(1)}, u32[]{:S(2)}) copy-start(bf16[192,768]{1,0:T(8,128)(2,1)S(1)} %add_convert_fusion.refs_1_) | copy-start | bytes 884740
  143.9 24.7 %collective-permute-start.16 = (bf16[192,768]{1,0:T(8,128)(2,1)S(1)}, bf16[192,768]{1,0:T(8,128)(2,1)S(1)}, u32[]{:S(2)}, u32[]{:S(2)}) collective-permute-start(bf16[192,768]{1,0:T(8,128)(2,1)S(1)} %add_convert_fusion.refs_1_), channel_id=1, source_target_pairs={{0,8},{1,33},{2,10},{3,35},{4,12},{5,37},{6,14},{7,39},{8,16},{9,4... | collective-permute-start | bytes 884744 | tf_op jit(solution)/shard_map/ppermute | solution.py:96
  152.5 16.2 %collective-permute-start.17 = (bf16[192,768]{1,0:T(8,128)(2,1)S(1)}, bf16[192,768]{1,0:T(8,128)(2,1)S(1)}, u32[]{:S(2)}, u32[]{:S(2)}) collective-permute-start(bf16[192,768]{1,0:T(8,128)(2,1)S(1)} %add_convert_fusion.refs_1_), channel_id=1, source_target_pairs={{0,24},{1,97},{2,26},{3,99},{4,28},{5,101},{6,30},{7,103},{8,0},{9... | collective-permute-start | bytes 884744 | tf_op jit(solution)/shard_map/ppermute | solution.py:96
  152.5 16.2 %collective-permute-start.18 = (bf16[192,768]{1,0:T(8,128)(2,1)S(1)}, bf16[192,768]{1,0:T(8,128)(2,1)S(1)}, u32[]{:S(2)}, u32[]{:S(2)}) collective-permute-start(bf16[192,768]{1,0:T(8,128)(2,1)S(1)} %add_convert_fusion.refs_1_), channel_id=1, source_target_pairs={{0,16},{1,65},{2,18},{3,67},{4,20},{5,69},{6,22},{7,71},{8,24},{9,... | collective-permute-start | bytes 884744 | tf_op jit(solution)/shard_map/ppermute | solution.py:96
  158.7 4.9 %collective-permute-start.13 = (bf16[48,896]{1,0:T(8,128)(2,1)}, bf16[48,896]{1,0:T(8,128)(2,1)S(1)}, u32[]{:S(2)}, u32[]{:S(2)}) collective-permute-start(bf16[48,896]{1,0:T(8,128)(2,1)} %strip.1.refs_0_), channel_id=1, source_target_pairs={{0,32},{1,33},{2,34},{3,35},{4,36},{5,37},{6,38},{7,39},{8,40},{9,... | collective-permute-start | bytes 258056 | tf_op jit(solution)/shard_map/ppermute | solution.py:96
  159.1 5.1 %collective-permute-start.14 = (bf16[48,896]{1,0:T(8,128)(2,1)}, bf16[48,896]{1,0:T(8,128)(2,1)S(1)}, u32[]{:S(2)}, u32[]{:S(2)}) collective-permute-start(bf16[48,896]{1,0:T(8,128)(2,1)} %strip.1.refs_0_), channel_id=1, source_target_pairs={{0,96},{1,97},{2,98},{3,99},{4,100},{5,101},{6,102},{7,103},{8,104... | collective-permute-start | bytes 258056 | tf_op jit(solution)/shard_map/ppermute | solution.py:96
  163.6 5.1 %copy-start.29 = (bf16[48,896]{1,0:T(8,128)(2,1)}, bf16[48,896]{1,0:T(8,128)(2,1)S(1)}, u32[]{:S(2)}) copy-start(bf16[48,896]{1,0:T(8,128)(2,1)S(1)} %collective-permute-done.13.refs_1_) | copy-start | bytes 258052
  163.6 5.1 %collective-permute-start.15 = (bf16[48,896]{1,0:T(8,128)(2,1)}, bf16[48,896]{1,0:T(8,128)(2,1)S(1)}, u32[]{:S(2)}, u32[]{:S(2)}) collective-permute-start(bf16[48,896]{1,0:T(8,128)(2,1)} %strip.1.refs_0_), channel_id=1, source_target_pairs={{0,64},{1,65},{2,66},{3,67},{4,68},{5,69},{6,70},{7,71},{8,72},{9,... | collective-permute-start | bytes 258056 | tf_op jit(solution)/shard_map/ppermute | solution.py:96
  164.2 4.5 %copy-start.30 = (bf16[48,896]{1,0:T(8,128)(2,1)}, bf16[48,896]{1,0:T(8,128)(2,1)S(1)}, u32[]{:S(2)}) copy-start(bf16[48,896]{1,0:T(8,128)(2,1)S(1)} %collective-permute-done.14.refs_2_) | copy-start | bytes 258052
  172.4 23.8 %all-to-all-start.4 = ((bf16[16,48,896]{2,1,0:T(8,128)(2,1)}), bf16[16,48,896]{2,1,0:T(8,128)(2,1)}, u32[]{:S(2)}, u32[]{:S(2)}) async-start(bf16[16,48,896]{2,1,0:T(8,128)(2,1)} %copies.1.refs_5_), calls=%async_computation.4 | async-start | bytes 2752512 | tf_op jit(solution)/shard_map/all_to_all | solution.py:667
  180.3 20.7 %collective-permute-start.22 = (bf16[768,768]{1,0:T(8,128)(2,1)}, bf16[768,768]{1,0:T(8,128)(2,1)S(1)}, u32[]{:S(2)}, u32[]{:S(2)}) collective-permute-start(bf16[768,768]{1,0:T(8,128)(2,1)} %join.1.own_ref), channel_id=1, source_target_pairs={{0,1},{1,0},{2,3},{3,2},{4,5},{5,4},{6,7},{7,6},{8,9},{9,8},{10,11... | collective-permute-start | bytes 3538952 | tf_op jit(solution)/shard_map/ppermute | solution.py:100
  182.5 26.8 %collective-permute-start.20 = (bf16[768,768]{1,0:T(8,128)(2,1)}, bf16[768,768]{1,0:T(8,128)(2,1)S(1)}, u32[]{:S(2)}, u32[]{:S(2)}) collective-permute-start(bf16[768,768]{1,0:T(8,128)(2,1)} %join.1.own_ref), channel_id=1, source_target_pairs={{0,2},{1,9},{2,4},{3,11},{4,6},{5,13},{6,0},{7,15},{8,10},{9,17},{... | collective-permute-start | bytes 3538952 | tf_op jit(solution)/shard_map/ppermute | solution.py:96
  184.1 25.2 %collective-permute-start.21 = (bf16[768,768]{1,0:T(8,128)(2,1)}, bf16[768,768]{1,0:T(8,128)(2,1)S(1)}, u32[]{:S(2)}, u32[]{:S(2)}) collective-permute-start(bf16[768,768]{1,0:T(8,128)(2,1)} %join.1.own_ref), channel_id=1, source_target_pairs={{0,6},{1,25},{2,0},{3,27},{4,2},{5,29},{6,4},{7,31},{8,14},{9,1},{... | collective-permute-start | bytes 3538952 | tf_op jit(solution)/shard_map/ppermute | solution.py:96
  196.2 32.2 %collective-permute-start.19 = (bf16[16,48,896]{2,1,0:T(8,128)(2,1)}, bf16[16,48,896]{2,1,0:T(8,128)(2,1)}, u32[]{:S(2)}, u32[]{:S(2)}) collective-permute-start(bf16[16,48,896]{2,1,0:T(8,128)(2,1)} %all-to-all-done.4.refs_1_), channel_id=1, source_target_pairs={{0,1},{1,0},{2,3},{3,2},{4,5},{5,4},{6,7},{7,6},{8,9},{9,8},{10,11... | collective-permute-start | bytes 4128776 | tf_op jit(solution)/shard_map/ppermute | solution.py:100
  206.9 2.4 collective-permute-start.23
  209.3 1.4 copy-start.2
  214.0 1.4 copy-start.34
  214.0 2.9 %copy-start.5 = (bf16[384,768]{1,0:T(8,128)(2,1)S(1)}, bf16[384,768]{1,0:T(8,128)(2,1)}, u32[]{:S(2)}) copy-start(bf16[384,768]{1,0:T(8,128)(2,1)} %get-tuple-element.111.refs_0_) | copy-start | bytes 1769476
  214.0 4.0 %collective-permute-start.26 = (bf16[768,768]{1,0:T(8,128)(2,1)}, bf16[768,768]{1,0:T(8,128)(2,1)S(1)}, u32[]{:S(2)}, u32[]{:S(2)}) collective-permute-start(bf16[768,768]{1,0:T(8,128)(2,1)} %tie.7.own_ref), channel_id=1, source_target_pairs={{0,1},{1,0},{2,3},{3,2},{4,5},{5,4},{6,7},{7,6},{8,9},{9,8},{10,11... | collective-permute-start | bytes 3538952 | tf_op jit(solution)/shard_map/ppermute | solution.py:100
  215.3 7.9 %collective-permute-start.25 = (bf16[768,768]{1,0:T(8,128)(2,1)}, bf16[768,768]{1,0:T(8,128)(2,1)S(1)}, u32[]{:S(2)}, u32[]{:S(2)}) collective-permute-start(bf16[768,768]{1,0:T(8,128)(2,1)} %tie.6.own_ref), channel_id=1, source_target_pairs={{0,1},{1,0},{2,3},{3,2},{4,5},{5,4},{6,7},{7,6},{8,9},{9,8},{10,11... | collective-permute-start | bytes 3538952 | tf_op jit(solution)/shard_map/ppermute | solution.py:100
  215.4 17.6 %collective-permute-start.28 = (bf16[384,768]{1,0:T(8,128)(2,1)S(1)}, bf16[384,768]{1,0:T(8,128)(2,1)S(1)}, u32[]{:S(2)}, u32[]{:S(2)}) collective-permute-start(bf16[384,768]{1,0:T(8,128)(2,1)S(1)} %copy-done.34), channel_id=1, source_target_pairs={{0,6},{1,25},{2,0},{3,27},{4,2},{5,29},{6,4},{7,31},{8,14},{9,1},{... | collective-permute-start | bytes 1769480 | tf_op jit(solution)/shard_map/ppermute | solution.py:96
  216.9 17.3 %collective-permute-start.24 = (bf16[384,768]{1,0:T(8,128)(2,1)S(1)}, bf16[384,768]{1,0:T(8,128)(2,1)S(1)}, u32[]{:S(2)}, u32[]{:S(2)}) collective-permute-start(bf16[384,768]{1,0:T(8,128)(2,1)S(1)} %copy-done.5), channel_id=1, source_target_pairs={{0,2},{1,9},{2,4},{3,11},{4,6},{5,13},{6,0},{7,15},{8,10},{9,17},{... | collective-permute-start | bytes 1769480 | tf_op jit(solution)/shard_map/ppermute | solution.py:96
  233.8 2.2 collective-permute-start.29
  235.0 5.2 %collective-permute-start.27 = (bf16[384,768]{1,0:T(8,128)(2,1)}, bf16[384,768]{1,0:T(8,128)(2,1)S(1)}, u32[]{:S(2)}, u32[]{:S(2)}) collective-permute-start(bf16[384,768]{1,0:T(8,128)(2,1)} %tie.8.own_ref), channel_id=1, source_target_pairs={{0,1},{1,0},{2,3},{3,2},{4,5},{5,4},{6,7},{7,6},{8,9},{9,8},{10,11... | collective-permute-start | bytes 1769480 | tf_op jit(solution)/shard_map/ppermute | solution.py:100
  (23 other events, 19.7 us)

commit v5 on v4

--- a/solution.py
+++ b/solution.py
@@ -314,7 +314,7 @@
         put_rows(vec_ref, 18, jnp.sum(gb.astype(f32), axis=0, keepdims=True))
 
 
-def leave_kernel(at_ref, x_ref, gain_ref, wq_ref, wkv_ref, gq_ref, gr_ref, mid_ref, parts_ref, _, gin_ref, keep_ref, send_ref, vec_ref):
+def leave_kernel(at_ref, x_ref, gain_ref, wq_ref, wkv_ref, gq_ref, gr_ref, mid_ref, parts_ref, gin_ref, keep_ref, send_ref, vec_ref):
     gkv = jnp.sum(parts_ref[...].astype(f32), axis=0).astype(bf16)
     gq = gq_ref[...]
     e = dot_nt(gq, wq_ref[...]) + dot_nt(gkv, wkv_ref[...])
@@ -393,17 +393,15 @@
     )(at, own, other, *kept)
 
 
-def share_kernel(same_ref, other_ref, lk_ref, lo_ref, rk_ref, ro_ref, out_ref, total_ref):
-    out_ref[:, 0:ROWS, :] = (same_ref[...].astype(f32) + other_ref[...].astype(f32)).astype(bf16)
-    total_ref[...] = dot_tn(lk_ref[...], rk_ref[...]) + dot_tn(lo_ref[...], ro_ref[...])
-    for i in range(CHIPS):
-        for b in range(6):
-            out_ref[i, ROWS + STRIP * b : ROWS + STRIP * (b + 1), :] = total_ref[
-                STRIP * i : STRIP * (i + 1), 128 * b : 128 * (b + 1)
-            ].astype(bf16)
-
-
-def late_kernel(at_ref, lk_ref, lo_ref, tk_ref, to_ref, out_ref, total_ref):
+def share_kernel(same_ref, other_ref, out_ref):
+    out_ref[...] = (same_ref[...].astype(f32) + other_ref[...].astype(f32)).astype(bf16)
+
+
+def square_kernel(lk_ref, lo_ref, rk_ref, ro_ref, out_ref):
+    out_ref[...] = (dot_tn(lk_ref[...], rk_ref[...]) + dot_tn(lo_ref[...], ro_ref[...])).astype(bf16)
+
+
+def late_kernel(at_ref, lk_ref, lo_ref, tk_ref, to_ref, square_ref, out_ref, total_ref):
     first = at_ref[0] == 0
 
     @pl.when(first)
@@ -416,14 +414,13 @@
         total_ref[128:, :] = jnp.zeros((D - 128, 128), f32)
 
     for i in range(CHIPS):
-        out_ref[i] = total_ref[STRIP * i : STRIP * (i + 1), :].astype(bf16)
-
-
-def strip_kernel(parts_ref, tail_ref, out_ref):
-    for b in range(6):
-        rows = slice(ROWS + STRIP * b, ROWS + STRIP * (b + 1))
-        out_ref[:, 128 * b : 128 * (b + 1)] = jnp.sum(parts_ref[:, rows, :].astype(f32), axis=0).astype(bf16)
-    out_ref[:, D:] = jnp.sum(tail_ref[...].astype(f32), axis=0).astype(bf16)
+        rows = slice(STRIP * i, STRIP * (i + 1))
+        out_ref[i, :, :D] = square_ref[rows, :]
+        out_ref[i, :, D:] = total_ref[rows, :].astype(bf16)
+
+
+def strip_kernel(parts_ref, out_ref):
+    out_ref[...] = jnp.sum(parts_ref[...].astype(f32), axis=0).astype(bf16)
 
 
 def part_kernel(a_ref, b_ref, c_ref, d_ref, out_ref):
@@ -574,13 +571,15 @@
     )(v, *after)
 
 
-def feed_forward_spread(at, totals, before_join, beside):
-    u = call(join_kernel, (at,) + totals, shapes(((D, D), bf16))[0], name="join", after=before_join)
+def feed_forward_spread(at, u):
     before, after = send(u, 0, 1), send(u, 0, 3)
     kept = place(at, 0, u, swap(u), ())
-    marks = (swap(kept[0][:8, :128]),)
-    low, high = call(halves_kernel, (before, after), shapes(HALF, HALF), name="halves", after=marks)
-    before, after = tie(before, low), tie(after, low)
+    return before, after, kept, swap(kept[0][:8, :128])
+
+
+def feed_forward_rest(at, before, after, kept, mark, beside):
+    low, high = call(halves_kernel, (before, after), shapes(HALF, HALF), name="halves", after=(mark,))
+    before, after = tie(before, low), tie(after, high)
     low, high = send(low, 0, 1), send(high, 0, 3)
     kept = place(at, 3, before, swap(before), kept)
     kept = place(at, 1, after, swap(after), kept)
@@ -638,40 +637,36 @@
     slabs = lax.all_to_all(packed, AXES, 0, 0, axis_index_groups=ring_groups(0), tiled=True)
 
     gq, right, right_send, kv_grads, kv_send = attend_back(at, kinds, xq, ga, o, lse, kv_all, key_cols, own_lanes, start_lanes, gb, after=(packed,))
-    shares = call(share_kernel, (kv_grads, swap(kv_send), left, left_other, right, swap(right_send)),
-                  shapes(((CHIPS, ROWS + 6 * STRIP, 128), bf16))[0], [pltpu.VMEM((D, D), f32)], name="share", after=(slabs,))
+    shares = call(share_kernel, (kv_grads, swap(kv_send)), shapes(KV_HALF)[0], name="share", after=(slabs,))
     parts = lax.all_to_all(shares, ("y", "z"), 0, 0, tiled=True)
 
     pieces = call(weight_kernel, (at, slabs), shapes(*[QUARTER] * 4), [pltpu.VMEM((D, D), f32)], name="weights")
     ff_parts = (pieces[0],) + spread(1, *pieces[1:])
-    gin, tail, tail_send, _ = pl.pallas_call(
-        leave_kernel,
-        grid=(1,),
-        out_shape=shapes(((ROWS * D // 128, 128), f32), ((128, 128), f32), ((128, 128), f32), ((128, 128), f32)),
-        in_specs=[SMEM] + [VMEM] * 7 + [pl.BlockSpec((CHIPS, ROWS, 128), lambda i: (0, 0, 0)), ANY],
-        out_specs=(VMEM,) * 4,
-        compiler_params=params(),
-        cost_estimate=cost(2 * ROWS * D * 900, 4e6),
-        name="leave",
-    )(at, x, ln1_gain, w_query, w_kv, gq, gr, vec_mid, parts, pieces[0])
-
-    late_parts = call(late_kernel, (at, left, left_other, tail, swap(tail_send)), shapes(((CHIPS, STRIP, 128), bf16))[0],
-                      [pltpu.VMEM((D, 128), f32)], name="late", after=ff_parts[1:])
-    ff_part = call(part_kernel, ff_parts, shapes(QUARTER)[0], name="part", after=(late_parts,))
+    square = call(square_kernel, (left, left_other, right, swap(right_send)), shapes(((D, D), bf16))[0], name="square")
+    gin, tail, tail_send, _ = call(
+        leave_kernel, (at, x, ln1_gain, w_query, w_kv, gq, gr, vec_mid, parts),
+        shapes(((ROWS * D // 128, 128), f32), ((128, 128), f32), ((128, 128), f32), ((128, 128), f32)),
+        name="leave", after=(pieces[0], square),
+    )
+
+    shares = call(late_kernel, (at, left, left_other, tail, swap(tail_send), square), shapes(((CHIPS, STRIP, D + 128), bf16))[0],
+                  [pltpu.VMEM((D, 128), f32)], name="late", after=ff_parts[1:])
+    ff_part = call(part_kernel, ff_parts, shapes(QUARTER)[0], name="part", after=(shares,))
     ff_crossed = gather4(ff_part, 2)
-    late_parts = lax.all_to_all(late_parts, ("y", "z"), 0, 0, tiled=True)
+    late_parts = lax.all_to_all(shares, ("y", "z"), 0, 0, tiled=True)
     ff_totals = gather4(pair_sums(*ff_crossed), 1)
-    strip = call(strip_kernel, (parts, late_parts), shapes(((STRIP, D + 128), bf16))[0], name="strip", after=ff_crossed[1:])
-    strips = gather4(strip, 3)
-    copies = call(copies_kernel, strips, shapes(((CHIPS, STRIP, D + 128), bf16))[0], name="copies", after=ff_totals[1:])
-    late = lax.all_to_all(copies, ("y", "z"), 0, 0, tiled=True)
+    strip = call(strip_kernel, (late_parts,), shapes(((STRIP, D + 128), bf16))[0], name="strip", after=ff_crossed[1:])
+    u = call(join_kernel, (at,) + ff_totals, shapes(((D, D), bf16))[0], name="join")
+    copies = call(copies_kernel, gather4(strip, 3), shapes(((CHIPS, STRIP, D + 128), bf16))[0], name="copies", after=(u,))
+    spreading = feed_forward_spread(at, u)
+    late = tie(lax.all_to_all(copies, ("y", "z"), 0, 0, tiled=True), spreading[-1])
     one = lambda n: ((n,), f32)
     outs = call(
         late_place_kernel, (at, late, swap(late)),
         shapes(((D, D), f32), ((D, D), f32), ((D, 128), f32), one(HD), *[one(128 * n) for _, n in VECTORS]), name="late_place",
     )
     g_query, g_out, g_kv, g_value, g_bdown, g_gain2, g_bias2, g_bout, g_bup, g_gain1, g_bias1, g_bq = outs
-    g_down, g_up = feed_forward_spread(at, ff_totals, (copies,), outs[2])
+    g_down, g_up = feed_forward_rest(at, *spreading, outs[2])
     shape = block_input.shape
     return (
         y.reshape(shape), gin.reshape(shape), g_gain1, g_bias1, g_query, g_bq, g_kv, g_value,

time: 245 us -> 243 us (level)
  starting transfers between devices: 77.2 us -> 57.7 us
  Pallas kernels: 99.1 us -> 109 us
  waiting for transfers between devices: 40.4 us -> 47.6 us
    ppermute x16, waiting for transfers between devices: 11.9 us -> 29.9 us  [send(): return lax.ppermute(v, AXES, ring(place, shift))]
    ppermute x16, starting transfers between devices: 33.8 us -> 19.5 us  [send(): return lax.ppermute(v, AXES, ring(place, shift))]
    pallas_call x14 -> x16, Pallas kernels: 65.9 us -> 78.8 us  [call(): pl.pallas_call(run, out_shape=outs, in_specs=[SMEM if v.dtype == jnp.int3...]
    all_to_all x1, waiting for transfers between devices: 7.98 us -> 0.01 us  [body(): parts = lax.all_to_all(shares, ('y', 'z'), 0, 0, tiled=True)]
    ppermute x14, starting transfers between devices: 15.1 us -> 8.69 us  [swap(): return lax.ppermute(v, 'c', [(0, 1), (1, 0)])]
    all_to_all x2, waiting for transfers between devices: 10.9 us -> 6.15 us  [the longest x1 6.15 us: body(): lax.all_to_all(copies, ('y', 'z'), 0, 0, tiled=True)]
    pallas_call x1 -> x0, Pallas kernels: 3.28 us -> none  [body(): pl.pallas_call(leave_kernel, grid=(1,), out_shape=shapes(((ROWS * D // 12...]
    ppermute x14, waiting for transfers between devices: 8.29 us -> 11.3 us  [swap(): return lax.ppermute(v, 'c', [(0, 1), (1, 0)])]
  transfers between devices with their start and end apart: 35 -> 35, of which waited for: 15 -> 19; matrix products, arithmetic and copies ran while one was open for 4% -> 4% of each run, Pallas kernels for 23% -> 27%
where the time goes in v5:
time: 243 us; the launch traced here: 242 us
  Pallas kernels  109 us (45%)
  starting transfers between devices  57.7 us (24%)
  waiting for transfers between devices  47.6 us (20%)
  local copies, waits for them, and re-layouts  22.7 us (9%)
  other arithmetic  4.4 us (2%)
    pallas_call x16, Pallas kernels, call(): pl.pallas_call(run, out_shape=outs, in_specs=[SMEM if v.dtype == jnp.int3...  78.8 us
    ppermute x16, waiting for transfers between devices, send(): return lax.ppermute(v, AXES, ring(place, shift))  29.9 us
    ppermute x16, starting transfers between devices, send(): return lax.ppermute(v, AXES, ring(place, shift))  19.5 us
    pallas_call x5, Pallas kernels, place(): pl.pallas_call(place_kernel, grid_spec=pltpu.PrefetchScalarGridSpec(num_s...  19.3 us
    unnamed x74, local copies, waits for them, and re-layouts  16.9 us
    ppermute x14, waiting for transfers between devices, swap(): return lax.ppermute(v, 'c', [(0, 1), (1, 0)])  11.3 us
    pallas_call x1, Pallas kernels, body(): pl.pallas_call(middle_kernel, grid=(steps,), out_shape=shapes(narrow, ((R...  10.5 us
    ppermute x14, starting transfers between devices, swap(): return lax.ppermute(v, 'c', [(0, 1), (1, 0)])  8.69 us
  transfers between devices with their start and end apart: 35, of which 19 were waited for; matrix products, arithmetic and copies ran while one was open for 4% of the time, Pallas kernels for 27%

profile of v5, /device:TPU:1, one launch (start us, length us, event | category | flops | bytes accessed | tf_op | source)
XLA Modules:
  0.0 242.0 jit_solution(14041921108029759970)
XLA Ops:
  0.6 2.2 enter.1
  2.9 8.6 %all-to-all-start = ((bf16[16,128,128]{2,1,0:T(8,128)(2,1)}), bf16[16,128,128]{2,1,0:T(8,128)(2,1)S(1)}, u32[]{:S(2)}, u32[]{:S(2)}) async-start(bf16[16,128,128]{2,1,0:T(8,128)(2,1)} %get-tuple-element.71), calls=%async_computation | async-start | bytes 1048576 | tf_op jit(solution)/shard_map/all_to_all | solution.py:601
  17.1 2.2 broadcast_in_dim.28.refs_3_.refs_5_.refs_7_
  19.3 2.3 query.1.refs_0_.refs_2_
  22.6 2.1 collective-permute-start
  27.3 17.7 %attend.1 = (bf16[128,768]{1,0:T(8,128)(2,1)}, bf16[128,768]{1,0:T(8,128)(2,1)}, bf16[128,768]{1,0:T(8,128)(2,1)}, bf16[2,768,128]{2,1,0:T(8,128)(2,1)}, f32[2,7...) custom-call(s32[6]{0:T(128)} %stack.27.refs_0_.at_ref, s32[8]{0:T(128)} %select_n.94.refs_6_.refs_1_, ...), custom_call_target="tpu_custom_call" | custom-call | flops 1 | bytes 1 | tf_op jit(solution)/shard_map/attend/pallas_call | solution.py:461
  45.0 10.5 %middle.1 = (bf16[128,768]{1,0:T(8,128)(2,1)}, bf16[128,3072]{1,0:T(8,128)(2,1)}, bf16[128,3072]{1,0:T(8,128)(2,1)}, bf16[128,768]{1,0:T(8,128)(2,1)}, bf16[128,...) custom-call(s32[6]{0:T(128)} %stack.27.refs_0_.at_ref, ...), custom_call_target="tpu_custom_call" | custom-call | flops 1 | bytes 1 | tf_op jit(solution)/shard_map/middle/pallas_call | solution.py:617
  56.2 2.3 collective-permute-done.2.refs_3_
  59.4 3.4 %pack.1.refs_11_ = bf16[4,256,1536]{2,1,0:T(8,128)(2,1)} custom-call(bf16[128,3072]{1,0:T(8,128)(2,1)} %get-tuple-element.80.refs_0_, bf16[128,768]{1,0:T(8,128)(2,1)} %get-tuple-element.81.refs_1_, bf16[128,3072]{1,0:T(8,128)(2,1)} %copy-done.18, bf16[128,768]{1,0:T(8,128)(2,1)} %copy-done.28), custom_call_target="tpu_custom_call" | custom-call | flops 1 | bytes 1 | tf_op jit(solution)/shard_map/pack/pallas_call | solution.py:461
  62.8 3.9 %all-to-all-start.1 = ((bf16[4,256,1536]{2,1,0:T(8,128)(2,1)}), bf16[4,256,1536]{2,1,0:T(8,128)(2,1)S(1)}, u32[]{:S(2)}, u32[]{:S(2)}) async-start(bf16[4,256,1536]{2,1,0:T(8,128)(2,1)} %pack.1.refs_11_), calls=%async_computation.1 | async-start | bytes 6291456 | tf_op jit(solution)/shard_map/all_to_all | solution.py:637
  66.7 21.4 %attend_back.1 = (bf16[128,768]{1,0:T(8,128)(2,1)}, bf16[128,768]{1,0:T(8,128)(2,1)}, bf16[128,768]{1,0:T(8,128)(2,1)}, bf16[16,128,128]{2,1,0:T(8,128)(2,1)}, bf16[16,128,128]{2,1,0:T(8,128)(2,1)}) custom-call(s32[6]{0:T(128)} %stack.27.refs_0_.at_ref, s32[8]{0:T(128)} %select_n.94.refs_6_.refs_1_, bf16[2,768,128]{2,1,0:T(8,128)(2,1)} %get-tuple-element.74.refs_2_, ...), custom_call_target="tpu_custom_call" | custom-call | flops 1 | bytes 1 | tf_op jit(solution)/shard_map/attend_back/pallas_call | solution.py:461
  88.4 1.9 collective-permute-done.3.refs_1_
  90.3 1.7 copy-done
  92.0 2.1 share.1
  94.1 6.6 %all-to-all-start.2 = ((bf16[16,128,128]{2,1,0:T(8,128)(2,1)}), bf16[16,128,128]{2,1,0:T(8,128)(2,1)S(1)}, u32[]{:S(2)}, u32[]{:S(2)}) async-start(bf16[16,128,128]{2,1,0:T(8,128)(2,1)} %share.1), calls=%async_computation.2 | async-start | bytes 1048576 | tf_op jit(solution)/shard_map/all_to_all | solution.py:641
  100.7 4.5 %weights.1 = (bf16[192,768]{1,0:T(8,128)(2,1)}, bf16[192,768]{1,0:T(8,128)(2,1)}, bf16[192,768]{1,0:T(8,128)(2,1)}, bf16[192,768]{1,0:T(8,128)(2,1)}) custom-call(s32[6]{0:T(128)} %stack.27.refs_0_.at_ref, bf16[4,256,1536]{2,1,0:T(8,128)(2,1)} %copy-done), custom_call_target="tpu_custom_call" | custom-call | flops 1 | bytes 1 | tf_op jit(solution)/shard_map/weights/pallas_call | solution.py:461
  105.2 1.3 collective-permute-start.7
  106.5 1.4 collective-permute-start.8
  108.9 2.4 collective-permute-start.4
  113.4 3.0 %square.1.refs_10_.refs_5_ = bf16[768,768]{1,0:T(8,128)(2,1)} custom-call(bf16[128,768]{1,0:T(8,128)(2,1)} %get-tuple-element.90.refs_0_.refs_1_, bf16[128,768]{1,0:T(8,128)(2,1)} %copy-done.19, bf16[128,768]{1,0:T(8,128)(2,1)} %get-tuple-element.92.refs_2_, bf16[128,768]{1,0:T(8,128)(2,1)} %copy-done.29), custom_call_target="tpu_custom_call" | custom-call | flops 1 | bytes 1 | tf_op jit(solution)/shard_map/square/pallas_call | solution.py:461
  117.2 3.3 %leave.1 = (f32[768,128]{1,0:T(8,128)}, f32[128,128]{1,0:T(8,128)}, f32[128,128]{1,0:T(8,128)}, f32[128,128]{1,0:T(8,128)}) custom-call(s32[6]{0:T(128)} %stack.27.refs_0_.at_ref, bf16[128,768]{1,0:T(8,128)(2,1)} %bitcast.59, bf16[768]{0:T(1024)(128)(2,1)} %refs_2_.5, bf16[768,768]{1,0:T(8,128)(2,1)} %refs_3_.3, bf16[768,128]{1,0:T(8,128)(2,1)} %refs_4_.3, ...), custom_call_target="tpu_custom_call" | custom-call | flops 1 | bytes 1 | tf_op jit(solution)/shard_map/leave/pallas_call | solution.py:461
  122.6 2.8 %late.1.refs_4_ = bf16[16,48,896]{2,1,0:T(8,128)(2,1)} custom-call(s32[6]{0:T(128)} %stack.27.refs_0_.at_ref, bf16[128,768]{1,0:T(8,128)(2,1)} %get-tuple-element.90.refs_0_.refs_1_, bf16[128,768]{1,0:T(8,128)(2,1)} %copy-done.19, f32[128,128]{1,0:T(8,128)} %get-tuple-element.95.refs_3_, f32[128,128]{1,0:T(8,128)} %copy-done.33, ...), custom_call_target="tpu_custom_call" | custom-call | flops 1 | bytes 1 | tf_op jit(solution)/shard_map/late/pallas_call | solution.py:461
  125.4 5.3 %all-to-all-start.3 = ((bf16[16,48,896]{2,1,0:T(8,128)(2,1)}), bf16[16,48,896]{2,1,0:T(8,128)(2,1)S(1)}, u32[]{:S(2)}, u32[]{:S(2)}) async-start(bf16[16,48,896]{2,1,0:T(8,128)(2,1)} %late.1.refs_4_), calls=%async_computation.3 | async-start | bytes 2752512 | tf_op jit(solution)/shard_map/all_to_all | solution.py:656
  130.7 2.1 part.1
  132.8 2.9 %collective-permute-start.12 = (bf16[192,768]{1,0:T(8,128)(2,1)}, bf16[192,768]{1,0:T(8,128)(2,1)S(1)}, u32[]{:S(2)}, u32[]{:S(2)}) collective-permute-start(bf16[192,768]{1,0:T(8,128)(2,1)} %part.1), channel_id=1, source_target_pairs={{0,64},{1,5},{2,66},{3,7},{4,68},{5,1},{6,70},{7,3},{8,72},{9,13},... | collective-permute-start | bytes 884744 | tf_op jit(solution)/shard_map/ppermute | solution.py:96
  137.1 16.7 %collective-permute-done.12.refs_3_ = bf16[192,768]{1,0:T(8,128)(2,1)S(1)} collective-permute-done((bf16[192,768]{1,0:T(8,128)(2,1)}, bf16[192,768]{1,0:T(8,128)(2,1)S(1)}, u32[]{:S(2)}, u32[]{:S(2)}) %collective-permute-start.12) | collective-permute-done | bytes 294944 | tf_op jit(solution)/shard_map/ppermute | solution.py:96
  153.8 1.4 collective-permute-done.11.refs_2_
  155.5 1.2 add_convert_fusion.refs_1_
  156.7 1.3 collective-permute-start.18
  158.0 2.8 %collective-permute-start.17 = (bf16[192,768]{1,0:T(8,128)(2,1)S(1)}, bf16[192,768]{1,0:T(8,128)(2,1)S(1)}, u32[]{:S(2)}, u32[]{:S(2)}) collective-permute-start(bf16[192,768]{1,0:T(8,128)(2,1)S(1)} %add_convert_fusion.refs_1_), channel_id=1, source_target_pairs={{0,24},{1,97},{2,26},{3,99},{4,28},{5,101},{6,30},{7,103},{8,0},{9... | collective-permute-start | bytes 884744 | tf_op jit(solution)/shard_map/ppermute | solution.py:96
  161.8 2.2 strip.1.refs_0_
  164.0 1.3 collective-permute-start.15
  165.3 2.1 collective-permute-start.14
  167.3 2.0 collective-permute-done.17.refs_3_
  171.0 2.3 join.1.refs_4_.own_ref
  174.6 2.2 copies.1
  176.8 5.2 %all-to-all-start.4 = ((bf16[16,48,896]{2,1,0:T(8,128)(2,1)}), bf16[16,48,896]{2,1,0:T(8,128)(2,1)S(1)}, u32[]{:S(2)}, u32[]{:S(2)}) async-start(bf16[16,48,896]{2,1,0:T(8,128)(2,1)} %copies.1), calls=%async_computation.4 | async-start | bytes 2752512 | tf_op jit(solution)/shard_map/all_to_all | solution.py:662
  182.1 2.6 %collective-permute-start.23 = (bf16[768,768]{1,0:T(8,128)(2,1)}, bf16[768,768]{1,0:T(8,128)(2,1)S(1)}, u32[]{:S(2)}, u32[]{:S(2)}) collective-permute-start(bf16[768,768]{1,0:T(8,128)(2,1)} %join.1.refs_4_.own_ref), channel_id=1, source_target_pairs={{0,6},{1,25},{2,0},{3,27},{4,2},{5,29},{6,4},{7,31},{8,14},{9,1},{... | collective-permute-start | bytes 3538952 | tf_op jit(solution)/shard_map/ppermute | solution.py:96
  186.2 4.2 %place.5 = (f32[3072,768]{1,0:T(8,128)}, f32[768,3072]{1,0:T(8,128)}) custom-call(s32[6]{0:T(128)} %stack.27.refs_0_.at_ref, bf16[768,768]{1,0:T(8,128)(2,1)} %join.1.refs_4_.own_ref, bf16[768,768]{1,0:T(8,128)(2,1)} %copy-done.17), custom_call_target="tpu_custom_call" | custom-call | flops 1 | bytes 1 | tf_op jit(solution)/shard_map/place/pallas_call | solution.py:383
  192.3 6.2 %all-to-all-done.4.v_ref = bf16[16,48,896]{2,1,0:T(8,128)(2,1)S(1)} async-done(((bf16[16,48,896]{2,1,0:T(8,128)(2,1)}), bf16[16,48,896]{2,1,0:T(8,128)(2,1)S(1)}, u32[]{:S(2)}, u32[]{:S(2)}) %all-to-all-start.4) | async-done | bytes 1376288 | tf_op jit(solution)/shard_map/all_to_all | solution.py:662
  199.5 7.5 %collective-permute-done.23.refs_1_.v_ref = bf16[768,768]{1,0:T(8,128)(2,1)S(1)} collective-permute-done((bf16[768,768]{1,0:T(8,128)(2,1)}, bf16[768,768]{1,0:T(8,128)(2,1)S(1)}, u32[]{:S(2)}, u32[]{:S(2)}) %collective-permute-start.23) | collective-permute-done | bytes 1179680 | tf_op jit(solution)/shard_map/ppermute | solution.py:96
  208.1 2.7 %halves.1 = (bf16[384,768]{1,0:T(8,128)(2,1)}, bf16[384,768]{1,0:T(8,128)(2,1)}) custom-call(bf16[768,768]{1,0:T(8,128)(2,1)} %collective-permute-done.22.refs_0_.v_ref, bf16[768,768]{1,0:T(8,128)(2,1)} %copy-done.2, f32[8,128]{1,0:T(8,128)} %copy-done.34), custom_call_target="tpu_custom_call" | custom-call | flops 1 | bytes 1 | tf_op jit(solution)/shard_map/halves/pallas_call | solution.py:461
  210.8 1.6 collective-permute-start.26
  216.1 4.2 %place.6 = (f32[3072,768]{1,0:T(8,128)}, f32[768,3072]{1,0:T(8,128)}) custom-call(s32[6]{0:T(128)} %stack.27.refs_0_.at_ref, bf16[768,768]{1,0:T(8,128)(2,1)} %tie.9.own_ref, bf16[768,768]{1,0:T(8,128)(2,1)} %copy-done.9, f32[3072,768]{1,0:T(8,128)} %get-tuple-element.100.rest_0_, ...), custom_call_target="tpu_custom_call", output_to_operand_aliasing={{0}: (3, {}), {1}: (4, {})} | custom-call | flops 1 | bytes 1 | tf_op jit(solution)/shard_map/place/pallas_call | solution.py:383
  221.3 4.2 %place.7 = (f32[3072,768]{1,0:T(8,128)}, f32[768,3072]{1,0:T(8,128)}) custom-call(s32[6]{0:T(128)} %stack.27.refs_0_.at_ref, bf16[768,768]{1,0:T(8,128)(2,1)} %tie.8.own_ref, bf16[768,768]{1,0:T(8,128)(2,1)} %copy-done.8, f32[3072,768]{1,0:T(8,128)} %get-tuple-element.114.rest_0_, ...), custom_call_target="tpu_custom_call", output_to_operand_aliasing={{0}: (3, {}), {1}: (4, {})} | custom-call | flops 1 | bytes 1 | tf_op jit(solution)/shard_map/place/pallas_call | solution.py:383
  225.5 4.6 %late_place.1 = (f32[768,768]{1,0:T(8,128)}, f32[768,768]{1,0:T(8,128)}, f32[768,128]{1,0:T(8,128)}, f32[64]{0:T(128)}, f32[768]{0:T(1024)}, /*index=5*/f32[768]...) custom-call(s32[6]{0:T(128)} %stack.27.refs_0_.at_ref, ...), custom_call_target="tpu_custom_call" | custom-call | flops 1 | bytes 1 | tf_op jit(solution)/shard_map/late_place/pallas_call | solution.py:461
  234.4 3.4 %place.8 = (f32[3072,768]{1,0:T(8,128)}, f32[768,3072]{1,0:T(8,128)}) custom-call(s32[6]{0:T(128)} %stack.27.refs_0_.at_ref, bf16[384,768]{1,0:T(8,128)(2,1)} %tie.11.own_ref, bf16[384,768]{1,0:T(8,128)(2,1)} %copy-done.20, f32[3072,768]{1,0:T(8,128)} %get-tuple-element.116.refs_0_.rest_0_, ...), custom_call_target="tpu_custom_call", output_to_operand_aliasing={{0}: (3, {}), {1}: (4, {})} | custom-call | flops 1 | bytes 1 | tf_op jit(solution)/shard_map/place/pallas_call | solution.py:383
  238.6 3.4 %place.9 = (f32[3072,768]{1,0:T(8,128)}, f32[768,3072]{1,0:T(8,128)}) custom-call(s32[6]{0:T(128)} %stack.27.refs_0_.at_ref, bf16[384,768]{1,0:T(8,128)(2,1)} %tie.10.own_ref, bf16[384,768]{1,0:T(8,128)(2,1)} %copy-done.21, f32[3072,768]{1,0:T(8,128)} %get-tuple-element.118.rest_0_, ...), custom_call_target="tpu_custom_call", output_to_operand_aliasing={{0}: (3, {}), {1}: (4, {})} | custom-call | flops 1 | bytes 1 | tf_op jit(solution)/shard_map/place/pallas_call | solution.py:383
  (153 shorter events, 38.3 us)
Async XLA Ops:
  2.9 18.9 %all-to-all-start = ((bf16[16,128,128]{2,1,0:T(8,128)(2,1)}), bf16[16,128,128]{2,1,0:T(8,128)(2,1)S(1)}, u32[]{:S(2)}, u32[]{:S(2)}) async-start(bf16[16,128,128]{2,1,0:T(8,128)(2,1)} %get-tuple-element.71), calls=%async_computation | async-start | bytes 1048576 | tf_op jit(solution)/shard_map/all_to_all | solution.py:601
  22.6 3.9 %collective-permute-start = (bf16[16,128,128]{2,1,0:T(8,128)(2,1)}, bf16[16,128,128]{2,1,0:T(8,128)(2,1)S(1)}, u32[]{:S(2)}, u32[]{:S(2)}) collective-permute-start(bf16[16,128,128]{2,1,0:T(8,128)(2,1)} %tie.6.refs_3_), channel_id=1, source_target_pairs={{0,1},{1,0},{2,3},{3,2},{4,5},{5,4},{6,7},{7,6},{8,9},{9,8},{10,11... | collective-permute-start | bytes 1572872 | tf_op jit(solution)/shard_map/ppermute | solution.py:100
  55.6 2.9 %collective-permute-start.1 = (bf16[128,3072]{1,0:T(8,128)(2,1)}, bf16[128,3072]{1,0:T(8,128)(2,1)S(1)}, u32[]{:S(2)}, u32[]{:S(2)}) collective-permute-start(bf16[128,3072]{1,0:T(8,128)(2,1)} %get-tuple-element.82), channel_id=1, source_target_pairs={{0,1},{1,0},{2,3},{3,2},{4,5},{5,4},{6,7},{7,6},{8,9},{9,8},{10,11... | collective-permute-start | bytes 2359304 | tf_op jit(solution)/shard_map/ppermute | solution.py:100
  56.0 2.4 collective-permute-start.2
  62.8 27.6 %all-to-all-start.1 = ((bf16[4,256,1536]{2,1,0:T(8,128)(2,1)}), bf16[4,256,1536]{2,1,0:T(8,128)(2,1)S(1)}, u32[]{:S(2)}, u32[]{:S(2)}) async-start(bf16[4,256,1536]{2,1,0:T(8,128)(2,1)} %pack.1.refs_11_), calls=%async_computation.1 | async-start | bytes 6291456 | tf_op jit(solution)/shard_map/all_to_all | solution.py:637
  88.1 2.3 collective-permute-start.3
  90.3 1.7 copy-start
  94.1 14.8 %copy-start.35 = (bf16[128,768]{1,0:T(8,128)(2,1)S(1)}, bf16[128,768]{1,0:T(8,128)(2,1)}, u32[]{:S(2)}) copy-start(bf16[128,768]{1,0:T(8,128)(2,1)} %get-tuple-element.91) | copy-start | bytes 589828
  94.1 17.2 %copy-start.36 = (bf16[128,768]{1,0:T(8,128)(2,1)S(1)}, bf16[128,768]{1,0:T(8,128)(2,1)}, u32[]{:S(2)}) copy-start(bf16[128,768]{1,0:T(8,128)(2,1)} %get-tuple-element.93) | copy-start | bytes 589828
  94.1 22.3 %all-to-all-start.2 = ((bf16[16,128,128]{2,1,0:T(8,128)(2,1)}), bf16[16,128,128]{2,1,0:T(8,128)(2,1)S(1)}, u32[]{:S(2)}, u32[]{:S(2)}) async-start(bf16[16,128,128]{2,1,0:T(8,128)(2,1)} %share.1), calls=%async_computation.2 | async-start | bytes 1048576 | tf_op jit(solution)/shard_map/all_to_all | solution.py:641
  105.2 15.6 %collective-permute-start.7 = (bf16[192,768]{1,0:T(8,128)(2,1)}, bf16[192,768]{1,0:T(8,128)(2,1)S(1)}, u32[]{:S(2)}, u32[]{:S(2)}) collective-permute-start(bf16[192,768]{1,0:T(8,128)(2,1)} %get-tuple-element.97), channel_id=1, source_target_pairs={{0,8},{1,33},{2,10},{3,35},{4,12},{5,37},{6,14},{7,39},{8,16},{9,4... | collective-permute-start | bytes 884744 | tf_op jit(solution)/shard_map/ppermute | solution.py:96
  106.5 14.4 %collective-permute-start.8 = (bf16[192,768]{1,0:T(8,128)(2,1)}, bf16[192,768]{1,0:T(8,128)(2,1)S(1)}, u32[]{:S(2)}, u32[]{:S(2)}) collective-permute-start(bf16[192,768]{1,0:T(8,128)(2,1)} %get-tuple-element.98), channel_id=1, source_target_pairs={{0,24},{1,97},{2,26},{3,99},{4,28},{5,101},{6,30},{7,103},{8,0},{9... | collective-permute-start | bytes 884744 | tf_op jit(solution)/shard_map/ppermute | solution.py:96
  107.9 13.0 %collective-permute-start.9 = (bf16[192,768]{1,0:T(8,128)(2,1)}, bf16[192,768]{1,0:T(8,128)(2,1)S(1)}, u32[]{:S(2)}, u32[]{:S(2)}) collective-permute-start(bf16[192,768]{1,0:T(8,128)(2,1)} %get-tuple-element.99), channel_id=1, source_target_pairs={{0,16},{1,65},{2,18},{3,67},{4,20},{5,69},{6,22},{7,71},{8,24},{9,... | collective-permute-start | bytes 884744 | tf_op jit(solution)/shard_map/ppermute | solution.py:96
  108.9 3.4 %collective-permute-start.4 = (bf16[128,768]{1,0:T(8,128)(2,1)S(1)}, bf16[128,768]{1,0:T(8,128)(2,1)S(1)}, u32[]{:S(2)}, u32[]{:S(2)}) collective-permute-start(bf16[128,768]{1,0:T(8,128)(2,1)S(1)} %copy-done.35), channel_id=1, source_target_pairs={{0,1},{1,0},{2,3},{3,2},{4,5},{5,4},{6,7},{7,6},{8,9},{9,8},{10,11... | collective-permute-start | bytes 589832 | tf_op jit(solution)/shard_map/ppermute | solution.py:100
  111.3 1.4 collective-permute-start.5
  120.5 1.5 collective-permute-start.6
  120.8 1.2 copy-start.10
  120.8 1.2 copy-start.11
  125.4 35.4 %all-to-all-start.3 = ((bf16[16,48,896]{2,1,0:T(8,128)(2,1)}), bf16[16,48,896]{2,1,0:T(8,128)(2,1)S(1)}, u32[]{:S(2)}, u32[]{:S(2)}) async-start(bf16[16,48,896]{2,1,0:T(8,128)(2,1)} %late.1.refs_4_), calls=%async_computation.3 | async-start | bytes 2752512 | tf_op jit(solution)/shard_map/all_to_all | solution.py:656
  132.8 21.0 %collective-permute-start.12 = (bf16[192,768]{1,0:T(8,128)(2,1)}, bf16[192,768]{1,0:T(8,128)(2,1)S(1)}, u32[]{:S(2)}, u32[]{:S(2)}) collective-permute-start(bf16[192,768]{1,0:T(8,128)(2,1)} %part.1), channel_id=1, source_target_pairs={{0,64},{1,5},{2,66},{3,7},{4,68},{5,1},{6,70},{7,3},{8,72},{9,13},... | collective-permute-start | bytes 884744 | tf_op jit(solution)/shard_map/ppermute | solution.py:96
  135.6 19.6 %collective-permute-start.11 = (bf16[192,768]{1,0:T(8,128)(2,1)}, bf16[192,768]{1,0:T(8,128)(2,1)S(1)}, u32[]{:S(2)}, u32[]{:S(2)}) collective-permute-start(bf16[192,768]{1,0:T(8,128)(2,1)} %part.1), channel_id=1, source_target_pairs={{0,96},{1,7},{2,98},{3,1},{4,100},{5,3},{6,102},{7,5},{8,104},{9,1... | collective-permute-start | bytes 884744 | tf_op jit(solution)/shard_map/ppermute | solution.py:96
  136.5 19.0 %collective-permute-start.10 = (bf16[192,768]{1,0:T(8,128)(2,1)}, bf16[192,768]{1,0:T(8,128)(2,1)S(1)}, u32[]{:S(2)}, u32[]{:S(2)}) collective-permute-start(bf16[192,768]{1,0:T(8,128)(2,1)} %part.1), channel_id=1, source_target_pairs={{0,32},{1,3},{2,34},{3,5},{4,36},{5,7},{6,38},{7,1},{8,40},{9,11},... | collective-permute-start | bytes 884744 | tf_op jit(solution)/shard_map/ppermute | solution.py:96
  153.8 7.0 %copy-start.14 = (bf16[192,768]{1,0:T(8,128)(2,1)}, bf16[192,768]{1,0:T(8,128)(2,1)S(1)}, u32[]{:S(2)}) copy-start(bf16[192,768]{1,0:T(8,128)(2,1)S(1)} %collective-permute-done.12.refs_3_) | copy-start | bytes 884740
  155.2 5.5 %copy-start.15 = (bf16[192,768]{1,0:T(8,128)(2,1)}, bf16[192,768]{1,0:T(8,128)(2,1)S(1)}, u32[]{:S(2)}) copy-start(bf16[192,768]{1,0:T(8,128)(2,1)S(1)} %collective-permute-done.11.refs_2_) | copy-start | bytes 884740
  155.5 5.3 %copy-start.16 = (bf16[192,768]{1,0:T(8,128)(2,1)}, bf16[192,768]{1,0:T(8,128)(2,1)S(1)}, u32[]{:S(2)}) copy-start(bf16[192,768]{1,0:T(8,128)(2,1)S(1)} %collective-permute-done.10.refs_1_) | copy-start | bytes 884740
  156.7 13.6 %copy-start.13 = (bf16[192,768]{1,0:T(8,128)(2,1)}, bf16[192,768]{1,0:T(8,128)(2,1)S(1)}, u32[]{:S(2)}) copy-start(bf16[192,768]{1,0:T(8,128)(2,1)S(1)} %add_convert_fusion.refs_1_) | copy-start | bytes 884740
  156.7 10.6 %collective-permute-start.18 = (bf16[192,768]{1,0:T(8,128)(2,1)S(1)}, bf16[192,768]{1,0:T(8,128)(2,1)S(1)}, u32[]{:S(2)}, u32[]{:S(2)}) collective-permute-start(bf16[192,768]{1,0:T(8,128)(2,1)S(1)} %add_convert_fusion.refs_1_), channel_id=1, source_target_pairs={{0,16},{1,65},{2,18},{3,67},{4,20},{5,69},{6,22},{7,71},{8,24},{9,... | collective-permute-start | bytes 884744 | tf_op jit(solution)/shard_map/ppermute | solution.py:96
  158.0 11.3 %collective-permute-start.17 = (bf16[192,768]{1,0:T(8,128)(2,1)S(1)}, bf16[192,768]{1,0:T(8,128)(2,1)S(1)}, u32[]{:S(2)}, u32[]{:S(2)}) collective-permute-start(bf16[192,768]{1,0:T(8,128)(2,1)S(1)} %add_convert_fusion.refs_1_), channel_id=1, source_target_pairs={{0,24},{1,97},{2,26},{3,99},{4,28},{5,101},{6,30},{7,103},{8,0},{9... | collective-permute-start | bytes 884744 | tf_op jit(solution)/shard_map/ppermute | solution.py:96
  160.7 9.5 %collective-permute-start.16 = (bf16[192,768]{1,0:T(8,128)(2,1)S(1)}, bf16[192,768]{1,0:T(8,128)(2,1)S(1)}, u32[]{:S(2)}, u32[]{:S(2)}) collective-permute-start(bf16[192,768]{1,0:T(8,128)(2,1)S(1)} %add_convert_fusion.refs_1_), channel_id=1, source_target_pairs={{0,8},{1,33},{2,10},{3,35},{4,12},{5,37},{6,14},{7,39},{8,16},{9,4... | collective-permute-start | bytes 884744 | tf_op jit(solution)/shard_map/ppermute | solution.py:96
  164.0 9.3 %collective-permute-start.15 = (bf16[48,896]{1,0:T(8,128)(2,1)}, bf16[48,896]{1,0:T(8,128)(2,1)S(1)}, u32[]{:S(2)}, u32[]{:S(2)}) collective-permute-start(bf16[48,896]{1,0:T(8,128)(2,1)} %strip.1.refs_0_), channel_id=1, source_target_pairs={{0,64},{1,65},{2,66},{3,67},{4,68},{5,69},{6,70},{7,71},{8,72},{9,... | collective-permute-start | bytes 258056 | tf_op jit(solution)/shard_map/ppermute | solution.py:96
  165.3 8.1 %collective-permute-start.14 = (bf16[48,896]{1,0:T(8,128)(2,1)}, bf16[48,896]{1,0:T(8,128)(2,1)S(1)}, u32[]{:S(2)}, u32[]{:S(2)}) collective-permute-start(bf16[48,896]{1,0:T(8,128)(2,1)} %strip.1.refs_0_), channel_id=1, source_target_pairs={{0,96},{1,97},{2,98},{3,99},{4,100},{5,101},{6,102},{7,103},{8,104... | collective-permute-start | bytes 258056 | tf_op jit(solution)/shard_map/ppermute | solution.py:96
  167.3 2.9 %copy-start.25 = (bf16[192,768]{1,0:T(8,128)(2,1)}, bf16[192,768]{1,0:T(8,128)(2,1)S(1)}, u32[]{:S(2)}) copy-start(bf16[192,768]{1,0:T(8,128)(2,1)S(1)} %collective-permute-done.18.refs_4_) | copy-start | bytes 884740
  167.3 6.0 %collective-permute-start.13 = (bf16[48,896]{1,0:T(8,128)(2,1)}, bf16[48,896]{1,0:T(8,128)(2,1)S(1)}, u32[]{:S(2)}, u32[]{:S(2)}) collective-permute-start(bf16[48,896]{1,0:T(8,128)(2,1)} %strip.1.refs_0_), channel_id=1, source_target_pairs={{0,32},{1,33},{2,34},{3,35},{4,36},{5,37},{6,38},{7,39},{8,40},{9,... | collective-permute-start | bytes 258056 | tf_op jit(solution)/shard_map/ppermute | solution.py:96
  176.8 21.6 %all-to-all-start.4 = ((bf16[16,48,896]{2,1,0:T(8,128)(2,1)}), bf16[16,48,896]{2,1,0:T(8,128)(2,1)S(1)}, u32[]{:S(2)}, u32[]{:S(2)}) async-start(bf16[16,48,896]{2,1,0:T(8,128)(2,1)} %copies.1), calls=%async_computation.4 | async-start | bytes 2752512 | tf_op jit(solution)/shard_map/all_to_all | solution.py:662
  182.0 3.1 %collective-permute-start.19 = (bf16[768,768]{1,0:T(8,128)(2,1)}, bf16[768,768]{1,0:T(8,128)(2,1)S(1)}, u32[]{:S(2)}, u32[]{:S(2)}) collective-permute-start(bf16[768,768]{1,0:T(8,128)(2,1)} %join.1.refs_4_.own_ref), channel_id=1, source_target_pairs={{0,1},{1,0},{2,3},{3,2},{4,5},{5,4},{6,7},{7,6},{8,9},{9,8},{10,11... | collective-permute-start | bytes 3538952 | tf_op jit(solution)/shard_map/ppermute | solution.py:100
  182.1 24.9 %collective-permute-start.23 = (bf16[768,768]{1,0:T(8,128)(2,1)}, bf16[768,768]{1,0:T(8,128)(2,1)S(1)}, u32[]{:S(2)}, u32[]{:S(2)}) collective-permute-start(bf16[768,768]{1,0:T(8,128)(2,1)} %join.1.refs_4_.own_ref), channel_id=1, source_target_pairs={{0,6},{1,25},{2,0},{3,27},{4,2},{5,29},{6,4},{7,31},{8,14},{9,1},{... | collective-permute-start | bytes 3538952 | tf_op jit(solution)/shard_map/ppermute | solution.py:96
  184.7 23.4 %collective-permute-start.22 = (bf16[768,768]{1,0:T(8,128)(2,1)}, bf16[768,768]{1,0:T(8,128)(2,1)}, u32[]{:S(2)}, u32[]{:S(2)}) collective-permute-start(bf16[768,768]{1,0:T(8,128)(2,1)} %join.1.refs_4_.own_ref), channel_id=1, source_target_pairs={{0,2},{1,9},{2,4},{3,11},{4,6},{5,13},{6,0},{7,15},{8,10},{9,17},{... | collective-permute-start | bytes 3538952 | tf_op jit(solution)/shard_map/ppermute | solution.py:96
  191.1 1.2 collective-permute-start.20
  192.3 6.2 %copy-start.34 = (f32[8,128]{1,0:T(8,128)}, f32[8,128]{1,0:T(8,128)S(1)}, u32[]{:S(2)}) copy-start(f32[8,128]{1,0:T(8,128)S(1)} %collective-permute-done.20.refs_0_.refs_2_) | copy-start | bytes 12292
  199.5 25.9 %collective-permute-start.21 = (bf16[16,48,896]{2,1,0:T(8,128)(2,1)}, bf16[16,48,896]{2,1,0:T(8,128)(2,1)}, u32[]{:S(2)}, u32[]{:S(2)}) collective-permute-start(bf16[16,48,896]{2,1,0:T(8,128)(2,1)} %tie.7.refs_1_), channel_id=1, source_target_pairs={{0,1},{1,0},{2,3},{3,2},{4,5},{5,4},{6,7},{7,6},{8,9},{9,8},{10,11... | collective-permute-start | bytes 4128776 | tf_op jit(solution)/shard_map/ppermute | solution.py:100
  210.8 1.7 copy-start.23
  210.8 2.9 %copy-start.22 = (bf16[384,768]{1,0:T(8,128)(2,1)S(1)}, bf16[384,768]{1,0:T(8,128)(2,1)}, u32[]{:S(2)}) copy-start(bf16[384,768]{1,0:T(8,128)(2,1)} %get-tuple-element.111.refs_0_) | copy-start | bytes 1769476
  210.8 4.3 %collective-permute-start.26 = (bf16[768,768]{1,0:T(8,128)(2,1)}, bf16[768,768]{1,0:T(8,128)(2,1)S(1)}, u32[]{:S(2)}, u32[]{:S(2)}) collective-permute-start(bf16[768,768]{1,0:T(8,128)(2,1)} %tie.9.own_ref), channel_id=1, source_target_pairs={{0,1},{1,0},{2,3},{3,2},{4,5},{5,4},{6,7},{7,6},{8,9},{9,8},{10,11... | collective-permute-start | bytes 3538952 | tf_op jit(solution)/shard_map/ppermute | solution.py:100
  212.4 7.9 %collective-permute-start.25 = (bf16[768,768]{1,0:T(8,128)(2,1)}, bf16[768,768]{1,0:T(8,128)(2,1)S(1)}, u32[]{:S(2)}, u32[]{:S(2)}) collective-permute-start(bf16[768,768]{1,0:T(8,128)(2,1)} %tie.8.own_ref), channel_id=1, source_target_pairs={{0,1},{1,0},{2,3},{3,2},{4,5},{5,4},{6,7},{7,6},{8,9},{9,8},{10,11... | collective-permute-start | bytes 3538952 | tf_op jit(solution)/shard_map/ppermute | solution.py:100
  212.5 17.6 %collective-permute-start.28 = (bf16[384,768]{1,0:T(8,128)(2,1)S(1)}, bf16[384,768]{1,0:T(8,128)(2,1)S(1)}, u32[]{:S(2)}, u32[]{:S(2)}) collective-permute-start(bf16[384,768]{1,0:T(8,128)(2,1)S(1)} %copy-done.23), channel_id=1, source_target_pairs={{0,6},{1,25},{2,0},{3,27},{4,2},{5,29},{6,4},{7,31},{8,14},{9,1},{... | collective-permute-start | bytes 1769480 | tf_op jit(solution)/shard_map/ppermute | solution.py:96
  213.7 18.0 %collective-permute-start.24 = (bf16[384,768]{1,0:T(8,128)(2,1)S(1)}, bf16[384,768]{1,0:T(8,128)(2,1)S(1)}, u32[]{:S(2)}, u32[]{:S(2)}) collective-permute-start(bf16[384,768]{1,0:T(8,128)(2,1)S(1)} %copy-done.22), channel_id=1, source_target_pairs={{0,2},{1,9},{2,4},{3,11},{4,6},{5,13},{6,0},{7,15},{8,10},{9,17},{... | collective-permute-start | bytes 1769480 | tf_op jit(solution)/shard_map/ppermute | solution.py:96
  230.8 2.7 %collective-permute-start.29 = (bf16[384,768]{1,0:T(8,128)(2,1)}, bf16[384,768]{1,0:T(8,128)(2,1)S(1)}, u32[]{:S(2)}, u32[]{:S(2)}) collective-permute-start(bf16[384,768]{1,0:T(8,128)(2,1)} %tie.11.own_ref), channel_id=1, source_target_pairs={{0,1},{1,0},{2,3},{3,2},{4,5},{5,4},{6,7},{7,6},{8,9},{9,8},{10,11... | collective-permute-start | bytes 1769480 | tf_op jit(solution)/shard_map/ppermute | solution.py:100
  232.5 5.2 %collective-permute-start.27 = (bf16[384,768]{1,0:T(8,128)(2,1)}, bf16[384,768]{1,0:T(8,128)(2,1)S(1)}, u32[]{:S(2)}, u32[]{:S(2)}) collective-permute-start(bf16[384,768]{1,0:T(8,128)(2,1)} %tie.10.own_ref), channel_id=1, source_target_pairs={{0,1},{1,0},{2,3},{3,2},{4,5},{5,4},{6,7},{7,6},{8,9},{9,8},{10,11... | collective-permute-start | bytes 1769480 | tf_op jit(solution)/shard_map/ppermute | solution.py:100
  (24 other events, 20.4 us)

commit v6 on v5

--- a/solution.py
+++ b/solution.py
@@ -349,15 +349,23 @@
         out[...] = total_ref[pl.ds(pl.multiple_of(((at[which]+rel)&3)*rows, rows), rows), :].astype(out.dtype)
 
 def weight_kernel(at_ref, slab_ref, own_ref, plus_ref, minus_ref, far_ref, total_ref):
+    step = pl.program_id(0)
+
+    @pl.when(step == 0)
+    def _():
+        total_ref[...] = jnp.zeros_like(total_ref)
+
     @pl.when(at_ref[0] == 0)
     def _():
-        total_ref[...] = sum(dot_tn(slab_ref[i, :, :D], slab_ref[i, :, D:]) for i in range(4))
+        total_ref[...] += dot_tn(slab_ref[0, :, :D], slab_ref[0, :, D:])
 
     @pl.when(at_ref[0] == 1)
     def _():
-        total_ref[...] = sum(dot_tn(slab_ref[i, :, D:], slab_ref[i, :, :D]) for i in range(4))
-
-    quarters(at_ref, 2, total_ref, (own_ref, plus_ref, minus_ref, far_ref))
+        total_ref[...] += dot_tn(slab_ref[0, :, D:], slab_ref[0, :, :D])
+
+    @pl.when(step == pl.num_programs(0) - 1)
+    def _():
+        quarters(at_ref, 2, total_ref, (own_ref, plus_ref, minus_ref, far_ref))
 
 
 def join_kernel(at_ref,a_ref,b_ref,c_ref,d_ref,out_ref):
@@ -374,7 +382,6 @@
 
 def place(at, rel, own, other, kept, part=0):
     tile = D // 2
-    n = own.shape[0] // tile
     piece = pl.BlockSpec((tile, D), lambda i, at: (i, 0))
     outs = (
         pl.BlockSpec((tile, D), lambda i, at: (((at[4] + rel) & 3) * 2 + part + i, 0)),
@@ -383,12 +390,12 @@
     return pl.pallas_call(
         place_kernel,
         grid_spec=pltpu.PrefetchScalarGridSpec(
-            num_scalar_prefetch=1, grid=(n,), in_specs=[piece, piece] + [ANY] * len(kept), out_specs=outs
+            num_scalar_prefetch=1, grid=(own.shape[0] // tile,), in_specs=[piece, piece] + [ANY] * len(kept), out_specs=outs
         ),
         out_shape=shapes(((FF, D), f32), ((D, FF), f32)),
         input_output_aliases={3: 0, 4: 1} if kept else {},
-        compiler_params=params(),
-        cost_estimate=cost(0, 8e6),
+        compiler_params=params(62),
+        cost_estimate=cost(0, 0),
         name="place",
     )(at, own, other, *kept)
 
@@ -541,11 +548,6 @@
     return jnp.stack(at).astype(jnp.int32)
 
 
-def halves_kernel(before_ref, after_ref, low_ref, high_ref):
-    low_ref[...] = before_ref[D // 2 :, :]
-    high_ref[...] = after_ref[: D // 2, :]
-
-
 QUARTER = ((D // 4, D), bf16)
 HALF = ((D // 2, D), bf16)
 
@@ -571,21 +573,24 @@
     )(v, *after)
 
 
-def feed_forward_spread(at, u):
-    before, after = send(u, 0, 1), send(u, 0, 3)
-    kept = place(at, 0, u, swap(u), ())
-    return before, after, kept, swap(kept[0][:8, :128])
-
-
-def feed_forward_rest(at, before, after, kept, mark, beside):
+def corner(v):
+    return swap(v[:8, :128])
+
+
+def halves_kernel(before_ref, after_ref, low_ref, high_ref):
+    low_ref[...] = before_ref[D // 2 :, :]
+    high_ref[...] = after_ref[: D // 2, :]
+
+
+def feed_forward_rest(at, before, after, kept, mark):
     low, high = call(halves_kernel, (before, after), shapes(HALF, HALF), name="halves", after=(mark,))
     before, after = tie(before, low), tie(after, high)
     low, high = send(low, 0, 1), send(high, 0, 3)
     kept = place(at, 3, before, swap(before), kept)
     kept = place(at, 1, after, swap(after), kept)
-    low, high = (tie(v, kept[0], beside) for v in (low, high))
+    low, high = (tie(v, kept[0]) for v in (low, high))
     kept = place(at, 2, high, swap(high), kept)
-    return place(at, 2, low, swap(low), kept, part=1)
+    return *place(at, 2, low, swap(low), kept, part=1), low, high
 
 
 def body(block_input, file_lengths, file_splits, ln1_gain, ln1_bias, w_query, b_query, w_kv, b_value, w_out, b_out,
@@ -640,7 +645,17 @@
     shares = call(share_kernel, (kv_grads, swap(kv_send)), shapes(KV_HALF)[0], name="share", after=(slabs,))
     parts = lax.all_to_all(shares, ("y", "z"), 0, 0, tiled=True)
 
-    pieces = call(weight_kernel, (at, slabs), shapes(*[QUARTER] * 4), [pltpu.VMEM((D, D), f32)], name="weights")
+    pieces = pl.pallas_call(
+        weight_kernel,
+        grid=(4,),
+        out_shape=shapes(*[QUARTER] * 4),
+        in_specs=[SMEM, pl.BlockSpec((1, 2 * ROWS, 2 * D), lambda i: (i, 0, 0))],
+        out_specs=(VMEM,) * 4,
+        scratch_shapes=[pltpu.VMEM((D, D), f32)],
+        compiler_params=params(62),
+        cost_estimate=cost(0, 0),
+        name="weights",
+    )(at, slabs)
     ff_parts = (pieces[0],) + spread(1, *pieces[1:])
     square = call(square_kernel, (left, left_other, right, swap(right_send)), shapes(((D, D), bf16))[0], name="square")
     gin, tail, tail_send, _ = call(
@@ -656,17 +671,21 @@
     late_parts = lax.all_to_all(shares, ("y", "z"), 0, 0, tiled=True)
     ff_totals = gather4(pair_sums(*ff_crossed), 1)
     strip = call(strip_kernel, (late_parts,), shapes(((STRIP, D + 128), bf16))[0], name="strip", after=ff_crossed[1:])
-    u = call(join_kernel, (at,) + ff_totals, shapes(((D, D), bf16))[0], name="join")
-    copies = call(copies_kernel, gather4(strip, 3), shapes(((CHIPS, STRIP, D + 128), bf16))[0], name="copies", after=(u,))
-    spreading = feed_forward_spread(at, u)
-    late = tie(lax.all_to_all(copies, ("y", "z"), 0, 0, tiled=True), spreading[-1])
+    u = call(join_kernel, (at,) + ff_totals, shapes(((D, D), bf16))[0], name="join", after=(strip,))
+    before, after = send(u, 0, 1), send(u, 0, 3)
+    kept = place(at, 0, u, swap(u), ())
+    mark = corner(kept[0])
+    copies = call(copies_kernel, gather4(strip, 3), shapes(((CHIPS, STRIP, D + 128), bf16))[0], name="copies",
+                  after=(before, after, mark))
+    late = lax.all_to_all(copies, ("y", "z"), 0, 0, tiled=True)
+    g_down, g_up, *rest = feed_forward_rest(at, before, after, kept, mark)
+    late = tie(late, *rest)
     one = lambda n: ((n,), f32)
     outs = call(
         late_place_kernel, (at, late, swap(late)),
         shapes(((D, D), f32), ((D, D), f32), ((D, 128), f32), one(HD), *[one(128 * n) for _, n in VECTORS]), name="late_place",
     )
     g_query, g_out, g_kv, g_value, g_bdown, g_gain2, g_bias2, g_bout, g_bup, g_gain1, g_bias1, g_bq = outs
-    g_down, g_up = feed_forward_rest(at, *spreading, outs[2])
     shape = block_input.shape
     return (
         y.reshape(shape), gin.reshape(shape), g_gain1, g_bias1, g_query, g_bq, g_kv, g_value,

time: 243 us -> 244 us (level)
  starting transfers between devices: 57.7 us -> 63.2 us
  local copies, waits for them, and re-layouts: 22.7 us -> 17.8 us
    all_to_all x1, waiting for transfers between devices: 6.15 us -> 0.01 us  [body(): late = lax.all_to_all(copies, ('y', 'z'), 0, 0, tiled=True)]
    pallas_call x0 -> x1, Pallas kernels: none -> 5.31 us  [body(): pl.pallas_call(weight_kernel, grid=(4,), out_shape=shapes(*[QUARTER] * 4)...]
    unnamed x74 -> x62, local copies, waits for them, and re-layouts: 16.9 us -> 12 us
    ppermute x14, starting transfers between devices: 8.69 us -> 13.5 us  [swap(): return lax.ppermute(v, 'c', [(0, 1), (1, 0)])]
    ppermute x16, waiting for transfers between devices: 29.9 us -> 34.3 us  [send(): return lax.ppermute(v, AXES, ring(place, shift))]
    pallas_call x16 -> x15, Pallas kernels: 78.8 us -> 74.4 us  [call(): pl.pallas_call(run, out_shape=outs, in_specs=[SMEM if v.dtype == jnp.int3...]
  transfers between devices with their start and end apart: 35 -> 35, of which waited for: 19 -> 15; matrix products, arithmetic and copies ran while one was open for 4% -> 4% of each run, Pallas kernels for 27% -> 25%
where the time goes in v6:
time: 244 us; the launch traced here: 243 us
  Pallas kernels  110 us (45%)
  starting transfers between devices  63.2 us (26%)
  waiting for transfers between devices  46.5 us (19%)
  local copies, waits for them, and re-layouts  17.8 us (7%)
  other arithmetic  4.4 us (2%)
    pallas_call x15, Pallas kernels, call(): pl.pallas_call(run, out_shape=outs, in_specs=[SMEM if v.dtype == jnp.int3...  74.4 us
    ppermute x16, waiting for transfers between devices, send(): return lax.ppermute(v, AXES, ring(place, shift))  34.3 us
    ppermute x16, starting transfers between devices, send(): return lax.ppermute(v, AXES, ring(place, shift))  21.2 us
    pallas_call x5, Pallas kernels, place(): pl.pallas_call(place_kernel, grid_spec=pltpu.PrefetchScalarGridSpec(num_s...  19.3 us
    ppermute x14, starting transfers between devices, swap(): return lax.ppermute(v, 'c', [(0, 1), (1, 0)])  13.5 us
    unnamed x62, local copies, waits for them, and re-layouts  12 us
    ppermute x14, waiting for transfers between devices, swap(): return lax.ppermute(v, 'c', [(0, 1), (1, 0)])  11.9 us
    pallas_call x1, Pallas kernels, body(): pl.pallas_call(middle_kernel, grid=(steps,), out_shape=shapes(narrow, ((R...  10.5 us
  transfers between devices with their start and end apart: 35, of which 15 were waited for; matrix products, arithmetic and copies ran while one was open for 4% of the time, Pallas kernels for 25%

profile of v6, /device:TPU:1, one launch (start us, length us, event | category | flops | bytes accessed | tf_op | source)
XLA Modules:
  0.0 242.7 jit_solution(3170463706130158703)
XLA Ops:
  0.6 2.2 enter.1
  2.9 8.6 %all-to-all-start = ((bf16[16,128,128]{2,1,0:T(8,128)(2,1)}), bf16[16,128,128]{2,1,0:T(8,128)(2,1)S(1)}, u32[]{:S(2)}, u32[]{:S(2)}) async-start(bf16[16,128,128]{2,1,0:T(8,128)(2,1)} %get-tuple-element.71), calls=%async_computation | async-start | bytes 1048576 | tf_op jit(solution)/shard_map/all_to_all | solution.py:606
  17.1 2.2 broadcast_in_dim.28.refs_3_.refs_5_.refs_7_
  19.3 2.3 query.1.refs_0_.refs_2_
  22.6 2.1 collective-permute-start
  27.3 17.8 %attend.1 = (bf16[128,768]{1,0:T(8,128)(2,1)}, bf16[128,768]{1,0:T(8,128)(2,1)}, bf16[128,768]{1,0:T(8,128)(2,1)}, bf16[2,768,128]{2,1,0:T(8,128)(2,1)}, f32[2,7...) custom-call(s32[6]{0:T(128)} %stack.27.refs_0_.at_ref, s32[8]{0:T(128)} %select_n.94.refs_6_.refs_1_, ...), custom_call_target="tpu_custom_call" | custom-call | flops 1 | bytes 1 | tf_op jit(solution)/shard_map/attend/pallas_call | solution.py:468
  45.1 10.5 %middle.1 = (bf16[128,768]{1,0:T(8,128)(2,1)}, bf16[128,3072]{1,0:T(8,128)(2,1)}, bf16[128,3072]{1,0:T(8,128)(2,1)}, bf16[128,768]{1,0:T(8,128)(2,1)}, bf16[128,...) custom-call(s32[6]{0:T(128)} %stack.27.refs_0_.at_ref, ...), custom_call_target="tpu_custom_call" | custom-call | flops 1 | bytes 1 | tf_op jit(solution)/shard_map/middle/pallas_call | solution.py:622
  56.3 2.3 collective-permute-done.2.refs_3_
  59.5 3.4 %pack.1.refs_11_ = bf16[4,256,1536]{2,1,0:T(8,128)(2,1)} custom-call(bf16[128,3072]{1,0:T(8,128)(2,1)} %get-tuple-element.80.refs_0_, bf16[128,768]{1,0:T(8,128)(2,1)} %get-tuple-element.81.refs_1_, bf16[128,3072]{1,0:T(8,128)(2,1)} %copy-done.16, bf16[128,768]{1,0:T(8,128)(2,1)} %copy-done.22), custom_call_target="tpu_custom_call" | custom-call | flops 1 | bytes 1 | tf_op jit(solution)/shard_map/pack/pallas_call | solution.py:468
  62.9 3.9 %all-to-all-start.1 = ((bf16[4,256,1536]{2,1,0:T(8,128)(2,1)}), bf16[4,256,1536]{2,1,0:T(8,128)(2,1)S(1)}, u32[]{:S(2)}, u32[]{:S(2)}) async-start(bf16[4,256,1536]{2,1,0:T(8,128)(2,1)} %pack.1.refs_11_), calls=%async_computation.1 | async-start | bytes 6291456 | tf_op jit(solution)/shard_map/all_to_all | solution.py:642
  66.8 21.4 %attend_back.1 = (bf16[128,768]{1,0:T(8,128)(2,1)}, bf16[128,768]{1,0:T(8,128)(2,1)}, bf16[128,768]{1,0:T(8,128)(2,1)}, bf16[16,128,128]{2,1,0:T(8,128)(2,1)}, bf16[16,128,128]{2,1,0:T(8,128)(2,1)}) custom-call(s32[6]{0:T(128)} %stack.27.refs_0_.at_ref, s32[8]{0:T(128)} %select_n.94.refs_6_.refs_1_, bf16[2,768,128]{2,1,0:T(8,128)(2,1)} %get-tuple-element.74.refs_2_, ...), custom_call_target="tpu_custom_call" | custom-call | flops 1 | bytes 1 | tf_op jit(solution)/shard_map/attend_back/pallas_call | solution.py:468
  88.6 1.9 collective-permute-done.3.refs_1_
  90.5 1.7 copy-done
  92.1 2.1 share.1
  94.2 6.5 %all-to-all-start.2 = ((bf16[16,128,128]{2,1,0:T(8,128)(2,1)}), bf16[16,128,128]{2,1,0:T(8,128)(2,1)S(1)}, u32[]{:S(2)}, u32[]{:S(2)}) async-start(bf16[16,128,128]{2,1,0:T(8,128)(2,1)} %share.1), calls=%async_computation.2 | async-start | bytes 1048576 | tf_op jit(solution)/shard_map/all_to_all | solution.py:646
  100.8 5.3 %weights.1 = (bf16[192,768]{1,0:T(8,128)(2,1)}, bf16[192,768]{1,0:T(8,128)(2,1)}, bf16[192,768]{1,0:T(8,128)(2,1)}, bf16[192,768]{1,0:T(8,128)(2,1)}) custom-call(s32[6]{0:T(128)} %stack.27.refs_0_.at_ref, bf16[4,256,1536]{2,1,0:T(8,128)(2,1)} %copy-done), custom_call_target="tpu_custom_call" | custom-call | flops 1 | bytes 1 | tf_op jit(solution)/shard_map/weights/pallas_call | solution.py:648
  106.1 2.7 %collective-permute-start.8 = (bf16[192,768]{1,0:T(8,128)(2,1)}, bf16[192,768]{1,0:T(8,128)(2,1)S(1)}, u32[]{:S(2)}, u32[]{:S(2)}) collective-permute-start(bf16[192,768]{1,0:T(8,128)(2,1)} %get-tuple-element.98), channel_id=1, source_target_pairs={{0,24},{1,97},{2,26},{3,99},{4,28},{5,101},{6,30},{7,103},{8,0},{9... | collective-permute-start | bytes 884744 | tf_op jit(solution)/shard_map/ppermute | solution.py:96
  109.7 2.4 %collective-permute-start.4 = (bf16[128,768]{1,0:T(8,128)(2,1)S(1)}, bf16[128,768]{1,0:T(8,128)(2,1)S(1)}, u32[]{:S(2)}, u32[]{:S(2)}) collective-permute-start(bf16[128,768]{1,0:T(8,128)(2,1)S(1)} %copy-done.29), channel_id=1, source_target_pairs={{0,1},{1,0},{2,3},{3,2},{4,5},{5,4},{6,7},{7,6},{8,9},{9,8},{10,11... | collective-permute-start | bytes 589832 | tf_op jit(solution)/shard_map/ppermute | solution.py:100
  114.3 3.0 %square.1.refs_10_.refs_5_ = bf16[768,768]{1,0:T(8,128)(2,1)} custom-call(bf16[128,768]{1,0:T(8,128)(2,1)} %get-tuple-element.90.refs_0_.refs_1_, bf16[128,768]{1,0:T(8,128)(2,1)} %copy-done.17, bf16[128,768]{1,0:T(8,128)(2,1)} %get-tuple-element.92.refs_2_, bf16[128,768]{1,0:T(8,128)(2,1)} %copy-done.23), custom_call_target="tpu_custom_call" | custom-call | flops 1 | bytes 1 | tf_op jit(solution)/shard_map/square/pallas_call | solution.py:468
  118.1 3.3 %leave.1 = (f32[768,128]{1,0:T(8,128)}, f32[128,128]{1,0:T(8,128)}, f32[128,128]{1,0:T(8,128)}, f32[128,128]{1,0:T(8,128)}) custom-call(s32[6]{0:T(128)} %stack.27.refs_0_.at_ref, bf16[128,768]{1,0:T(8,128)(2,1)} %bitcast.59, bf16[768]{0:T(1024)(128)(2,1)} %refs_2_.5, bf16[768,768]{1,0:T(8,128)(2,1)} %refs_3_.3, bf16[768,128]{1,0:T(8,128)(2,1)} %refs_4_.3, ...), custom_call_target="tpu_custom_call" | custom-call | flops 1 | bytes 1 | tf_op jit(solution)/shard_map/leave/pallas_call | solution.py:468
  123.5 2.8 %late.1.refs_4_ = bf16[16,48,896]{2,1,0:T(8,128)(2,1)} custom-call(s32[6]{0:T(128)} %stack.27.refs_0_.at_ref, bf16[128,768]{1,0:T(8,128)(2,1)} %get-tuple-element.90.refs_0_.refs_1_, bf16[128,768]{1,0:T(8,128)(2,1)} %copy-done.17, f32[128,128]{1,0:T(8,128)} %get-tuple-element.95.refs_3_, f32[128,128]{1,0:T(8,128)} %copy-done.27, ...), custom_call_target="tpu_custom_call" | custom-call | flops 1 | bytes 1 | tf_op jit(solution)/shard_map/late/pallas_call | solution.py:468
  126.3 5.3 %all-to-all-start.3 = ((bf16[16,48,896]{2,1,0:T(8,128)(2,1)}), bf16[16,48,896]{2,1,0:T(8,128)(2,1)S(1)}, u32[]{:S(2)}, u32[]{:S(2)}) async-start(bf16[16,48,896]{2,1,0:T(8,128)(2,1)} %late.1.refs_4_), calls=%async_computation.3 | async-start | bytes 2752512 | tf_op jit(solution)/shard_map/all_to_all | solution.py:671
  131.5 2.1 part.1
  136.3 1.7 collective-permute-start.12
  138.0 14.9 %collective-permute-done.10.refs_1_ = bf16[192,768]{1,0:T(8,128)(2,1)S(1)} collective-permute-done((bf16[192,768]{1,0:T(8,128)(2,1)}, bf16[192,768]{1,0:T(8,128)(2,1)S(1)}, u32[]{:S(2)}, u32[]{:S(2)}) %collective-permute-start.10) | collective-permute-done | bytes 294944 | tf_op jit(solution)/shard_map/ppermute | solution.py:96
  152.9 3.8 %collective-permute-done.12.refs_3_ = bf16[192,768]{1,0:T(8,128)(2,1)S(1)} collective-permute-done((bf16[192,768]{1,0:T(8,128)(2,1)}, bf16[192,768]{1,0:T(8,128)(2,1)S(1)}, u32[]{:S(2)}, u32[]{:S(2)}) %collective-permute-start.12) | collective-permute-done | bytes 294944 | tf_op jit(solution)/shard_map/ppermute | solution.py:96
  158.2 2.9 %collective-permute-start.17 = (bf16[192,768]{1,0:T(8,128)(2,1)S(1)}, bf16[192,768]{1,0:T(8,128)(2,1)S(1)}, u32[]{:S(2)}, u32[]{:S(2)}) collective-permute-start(bf16[192,768]{1,0:T(8,128)(2,1)S(1)} %add_convert_fusion.refs_1_), channel_id=1, source_target_pairs={{0,24},{1,97},{2,26},{3,99},{4,28},{5,101},{6,30},{7,103},{8,0},{9... | collective-permute-start | bytes 884744 | tf_op jit(solution)/shard_map/ppermute | solution.py:96
  163.3 2.1 strip.1.refs_5_.refs_0_
  165.5 2.5 %collective-permute-done.17.refs_3_ = bf16[192,768]{1,0:T(8,128)(2,1)S(1)} collective-permute-done((bf16[192,768]{1,0:T(8,128)(2,1)S(1)}, bf16[192,768]{1,0:T(8,128)(2,1)S(1)}, u32[]{:S(2)}, u32[]{:S(2)}) %collective-permute-start.17) | collective-permute-done | bytes 294944 | tf_op jit(solution)/shard_map/ppermute | solution.py:96
  168.0 1.6 collective-permute-done.18.refs_4_
  169.6 2.4 join.1.own_ref
  172.8 1.9 collective-permute-start.20
  175.5 1.8 collective-permute-start.14
  178.0 4.2 %place.5 = (f32[3072,768]{1,0:T(8,128)}, f32[768,3072]{1,0:T(8,128)}) custom-call(s32[6]{0:T(128)} %stack.27.refs_0_.at_ref, bf16[768,768]{1,0:T(8,128)(2,1)} %join.1.own_ref, bf16[768,768]{1,0:T(8,128)(2,1)} %collective-permute-done.21.other_ref), custom_call_target="tpu_custom_call" | custom-call | flops 1 | bytes 1 | tf_op jit(solution)/shard_map/place/pallas_call | solution.py:390
  182.9 1.6 collective-permute-start.22
  184.5 4.3 %collective-permute-done.19.refs_4_.refs_0_.v_ref = bf16[768,768]{1,0:T(8,128)(2,1)} collective-permute-done((bf16[768,768]{1,0:T(8,128)(2,1)}, bf16[768,768]{1,0:T(8,128)(2,1)}, u32[]{:S(2)}, u32[]{:S(2)}) %collective-permute-start.19) | collective-permute-done | bytes 1179680 | tf_op jit(solution)/shard_map/ppermute | solution.py:96
  190.5 2.2 copies.1
  192.6 4.2 %all-to-all-start.4 = ((bf16[16,48,896]{2,1,0:T(8,128)(2,1)}), bf16[16,48,896]{2,1,0:T(8,128)(2,1)S(1)}, u32[]{:S(2)}, u32[]{:S(2)}) async-start(bf16[16,48,896]{2,1,0:T(8,128)(2,1)} %copies.1), calls=%async_computation.4 | async-start | bytes 2752512 | tf_op jit(solution)/shard_map/all_to_all | solution.py:680
  196.8 2.7 %halves.1 = (bf16[384,768]{1,0:T(8,128)(2,1)}, bf16[384,768]{1,0:T(8,128)(2,1)}) custom-call(bf16[768,768]{1,0:T(8,128)(2,1)} %collective-permute-done.19.refs_4_.refs_0_.v_ref, bf16[768,768]{1,0:T(8,128)(2,1)} %copy-done.1, f32[8,128]{1,0:T(8,128)} %copy-done.28), custom_call_target="tpu_custom_call" | custom-call | flops 1 | bytes 1 | tf_op jit(solution)/shard_map/halves/pallas_call | solution.py:468
  199.5 3.9 %collective-permute-start.25 = (bf16[768,768]{1,0:T(8,128)(2,1)}, bf16[768,768]{1,0:T(8,128)(2,1)}, u32[]{:S(2)}, u32[]{:S(2)}) collective-permute-start(bf16[768,768]{1,0:T(8,128)(2,1)} %tie.8.own_ref), channel_id=1, source_target_pairs={{0,1},{1,0},{2,3},{3,2},{4,5},{5,4},{6,7},{7,6},{8,9},{9,8},{10,11... | collective-permute-start | bytes 3538952 | tf_op jit(solution)/shard_map/ppermute | solution.py:100
  203.4 2.9 %collective-permute-start.26 = (bf16[384,768]{1,0:T(8,128)(2,1)}, bf16[384,768]{1,0:T(8,128)(2,1)}, u32[]{:S(2)}, u32[]{:S(2)}) collective-permute-start(bf16[384,768]{1,0:T(8,128)(2,1)} %get-tuple-element.102.refs_0_), channel_id=1, source_target_pairs={{0,6},{1,25},{2,0},{3,27},{4,2},{5,29},{6,4},{7,31},{8,14},{9,1},{... | collective-permute-start | bytes 1769480 | tf_op jit(solution)/shard_map/ppermute | solution.py:96
  206.3 4.2 %place.6 = (f32[3072,768]{1,0:T(8,128)}, f32[768,3072]{1,0:T(8,128)}) custom-call(s32[6]{0:T(128)} %stack.27.refs_0_.at_ref, bf16[768,768]{1,0:T(8,128)(2,1)} %tie.8.own_ref, bf16[768,768]{1,0:T(8,128)(2,1)} %collective-permute-done.25.other_ref, f32[3072,768]{1,0:T(8,128)} %get-tuple-element.100.rest_0_, ...), custom_call_target="tpu_custom_call", output_to_operand_aliasing={{0}: (3, {}), {1}: (4, {})} | custom-call | flops 1 | bytes 1 | tf_op jit(solution)/shard_map/place/pallas_call | solution.py:390
  210.5 4.2 %place.7 = (f32[3072,768]{1,0:T(8,128)}, f32[768,3072]{1,0:T(8,128)}) custom-call(s32[6]{0:T(128)} %stack.27.refs_0_.at_ref, bf16[768,768]{1,0:T(8,128)(2,1)} %tie.7.own_ref, bf16[768,768]{1,0:T(8,128)(2,1)} %collective-permute-done.24.other_ref, f32[3072,768]{1,0:T(8,128)} %get-tuple-element.104.rest_0_, ...), custom_call_target="tpu_custom_call", output_to_operand_aliasing={{0}: (3, {}), {1}: (4, {})} | custom-call | flops 1 | bytes 1 | tf_op jit(solution)/shard_map/place/pallas_call | solution.py:390
  214.7 6.2 %collective-permute-done.26.v_ref = bf16[384,768]{1,0:T(8,128)(2,1)} collective-permute-done((bf16[384,768]{1,0:T(8,128)(2,1)}, bf16[384,768]{1,0:T(8,128)(2,1)}, u32[]{:S(2)}, u32[]{:S(2)}) %collective-permute-start.26) | collective-permute-done | bytes 589856 | tf_op jit(solution)/shard_map/ppermute | solution.py:96
  225.9 4.1 %collective-permute-done.29.other_ref = bf16[384,768]{1,0:T(8,128)(2,1)} collective-permute-done((bf16[384,768]{1,0:T(8,128)(2,1)}, bf16[384,768]{1,0:T(8,128)(2,1)}, u32[]{:S(2)}, u32[]{:S(2)}) %collective-permute-start.29) | collective-permute-done | bytes 589856 | tf_op jit(solution)/shard_map/ppermute | solution.py:100
  230.1 3.4 %place.8 = (f32[3072,768]{1,0:T(8,128)}, f32[768,3072]{1,0:T(8,128)}) custom-call(s32[6]{0:T(128)} %stack.27.refs_0_.at_ref, bf16[384,768]{1,0:T(8,128)(2,1)} %tie.10.refs_1_.own_ref, bf16[384,768]{1,0:T(8,128)(2,1)} %collective-permute-done.29.other_ref, ...), custom_call_target="tpu_custom_call", output_to_operand_aliasing={{0}: (3, {}), {1}: (4, {})} | custom-call | flops 1 | bytes 1 | tf_op jit(solution)/shard_map/place/pallas_call | solution.py:390
  233.4 3.4 %place.9 = (f32[3072,768]{1,0:T(8,128)}, f32[768,3072]{1,0:T(8,128)}) custom-call(s32[6]{0:T(128)} %stack.27.refs_0_.at_ref, bf16[384,768]{1,0:T(8,128)(2,1)} %tie.9.refs_0_.own_ref, bf16[384,768]{1,0:T(8,128)(2,1)} %collective-permute-done.28.other_ref, f32[3072,768]{1,0:T(8,128)} %get-tuple-element.118.rest_0_, ...), custom_call_target="tpu_custom_call", output_to_operand_aliasing={{0}: (3, {}), {1}: (4, {})} | custom-call | flops 1 | bytes 1 | tf_op jit(solution)/shard_map/place/pallas_call | solution.py:390
  237.9 4.6 %late_place.1 = (f32[768,768]{1,0:T(8,128)}, f32[768,768]{1,0:T(8,128)}, f32[768,128]{1,0:T(8,128)}, f32[64]{0:T(128)}, f32[768]{0:T(1024)}, /*index=5*/f32[768]...) custom-call(s32[6]{0:T(128)} %stack.27.refs_0_.at_ref, ...), custom_call_target="tpu_custom_call" | custom-call | flops 1 | bytes 1 | tf_op jit(solution)/shard_map/late_place/pallas_call | solution.py:468
  (141 shorter events, 34.2 us)
Async XLA Ops:
  2.9 18.9 %all-to-all-start = ((bf16[16,128,128]{2,1,0:T(8,128)(2,1)}), bf16[16,128,128]{2,1,0:T(8,128)(2,1)S(1)}, u32[]{:S(2)}, u32[]{:S(2)}) async-start(bf16[16,128,128]{2,1,0:T(8,128)(2,1)} %get-tuple-element.71), calls=%async_computation | async-start | bytes 1048576 | tf_op jit(solution)/shard_map/all_to_all | solution.py:606
  22.6 3.9 %collective-permute-start = (bf16[16,128,128]{2,1,0:T(8,128)(2,1)}, bf16[16,128,128]{2,1,0:T(8,128)(2,1)S(1)}, u32[]{:S(2)}, u32[]{:S(2)}) collective-permute-start(bf16[16,128,128]{2,1,0:T(8,128)(2,1)} %tie.6.refs_3_), channel_id=1, source_target_pairs={{0,1},{1,0},{2,3},{3,2},{4,5},{5,4},{6,7},{7,6},{8,9},{9,8},{10,11... | collective-permute-start | bytes 1572872 | tf_op jit(solution)/shard_map/ppermute | solution.py:100
  55.7 2.9 %collective-permute-start.1 = (bf16[128,3072]{1,0:T(8,128)(2,1)}, bf16[128,3072]{1,0:T(8,128)(2,1)S(1)}, u32[]{:S(2)}, u32[]{:S(2)}) collective-permute-start(bf16[128,3072]{1,0:T(8,128)(2,1)} %get-tuple-element.82), channel_id=1, source_target_pairs={{0,1},{1,0},{2,3},{3,2},{4,5},{5,4},{6,7},{7,6},{8,9},{9,8},{10,11... | collective-permute-start | bytes 2359304 | tf_op jit(solution)/shard_map/ppermute | solution.py:100
  56.1 2.4 collective-permute-start.2
  62.9 27.6 %all-to-all-start.1 = ((bf16[4,256,1536]{2,1,0:T(8,128)(2,1)}), bf16[4,256,1536]{2,1,0:T(8,128)(2,1)S(1)}, u32[]{:S(2)}, u32[]{:S(2)}) async-start(bf16[4,256,1536]{2,1,0:T(8,128)(2,1)} %pack.1.refs_11_), calls=%async_computation.1 | async-start | bytes 6291456 | tf_op jit(solution)/shard_map/all_to_all | solution.py:642
  88.2 2.3 collective-permute-start.3
  90.5 1.7 copy-start
  94.2 15.5 %copy-start.29 = (bf16[128,768]{1,0:T(8,128)(2,1)S(1)}, bf16[128,768]{1,0:T(8,128)(2,1)}, u32[]{:S(2)}) copy-start(bf16[128,768]{1,0:T(8,128)(2,1)} %get-tuple-element.91) | copy-start | bytes 589828
  94.2 18.0 %copy-start.30 = (bf16[128,768]{1,0:T(8,128)(2,1)S(1)}, bf16[128,768]{1,0:T(8,128)(2,1)}, u32[]{:S(2)}) copy-start(bf16[128,768]{1,0:T(8,128)(2,1)} %get-tuple-element.93) | copy-start | bytes 589828
  94.2 23.1 %all-to-all-start.2 = ((bf16[16,128,128]{2,1,0:T(8,128)(2,1)}), bf16[16,128,128]{2,1,0:T(8,128)(2,1)S(1)}, u32[]{:S(2)}, u32[]{:S(2)}) async-start(bf16[16,128,128]{2,1,0:T(8,128)(2,1)} %share.1), calls=%async_computation.2 | async-start | bytes 1048576 | tf_op jit(solution)/shard_map/all_to_all | solution.py:646
  106.1 15.6 %collective-permute-start.7 = (bf16[192,768]{1,0:T(8,128)(2,1)}, bf16[192,768]{1,0:T(8,128)(2,1)S(1)}, u32[]{:S(2)}, u32[]{:S(2)}) collective-permute-start(bf16[192,768]{1,0:T(8,128)(2,1)} %get-tuple-element.97), channel_id=1, source_target_pairs={{0,8},{1,33},{2,10},{3,35},{4,12},{5,37},{6,14},{7,39},{8,16},{9,4... | collective-permute-start | bytes 884744 | tf_op jit(solution)/shard_map/ppermute | solution.py:96
  106.1 15.6 %collective-permute-start.8 = (bf16[192,768]{1,0:T(8,128)(2,1)}, bf16[192,768]{1,0:T(8,128)(2,1)S(1)}, u32[]{:S(2)}, u32[]{:S(2)}) collective-permute-start(bf16[192,768]{1,0:T(8,128)(2,1)} %get-tuple-element.98), channel_id=1, source_target_pairs={{0,24},{1,97},{2,26},{3,99},{4,28},{5,101},{6,30},{7,103},{8,0},{9... | collective-permute-start | bytes 884744 | tf_op jit(solution)/shard_map/ppermute | solution.py:96
  108.8 13.0 %collective-permute-start.9 = (bf16[192,768]{1,0:T(8,128)(2,1)}, bf16[192,768]{1,0:T(8,128)(2,1)S(1)}, u32[]{:S(2)}, u32[]{:S(2)}) collective-permute-start(bf16[192,768]{1,0:T(8,128)(2,1)} %get-tuple-element.99), channel_id=1, source_target_pairs={{0,16},{1,65},{2,18},{3,67},{4,20},{5,69},{6,22},{7,71},{8,24},{9,... | collective-permute-start | bytes 884744 | tf_op jit(solution)/shard_map/ppermute | solution.py:96
  109.7 3.5 %collective-permute-start.4 = (bf16[128,768]{1,0:T(8,128)(2,1)S(1)}, bf16[128,768]{1,0:T(8,128)(2,1)S(1)}, u32[]{:S(2)}, u32[]{:S(2)}) collective-permute-start(bf16[128,768]{1,0:T(8,128)(2,1)S(1)} %copy-done.29), channel_id=1, source_target_pairs={{0,1},{1,0},{2,3},{3,2},{4,5},{5,4},{6,7},{7,6},{8,9},{9,8},{10,11... | collective-permute-start | bytes 589832 | tf_op jit(solution)/shard_map/ppermute | solution.py:100
  112.2 1.4 collective-permute-start.5
  121.4 1.5 collective-permute-start.6
  126.3 36.0 %all-to-all-start.3 = ((bf16[16,48,896]{2,1,0:T(8,128)(2,1)}), bf16[16,48,896]{2,1,0:T(8,128)(2,1)S(1)}, u32[]{:S(2)}, u32[]{:S(2)}) async-start(bf16[16,48,896]{2,1,0:T(8,128)(2,1)} %late.1.refs_4_), calls=%async_computation.3 | async-start | bytes 2752512 | tf_op jit(solution)/shard_map/all_to_all | solution.py:671
  133.6 19.2 %collective-permute-start.10 = (bf16[192,768]{1,0:T(8,128)(2,1)}, bf16[192,768]{1,0:T(8,128)(2,1)S(1)}, u32[]{:S(2)}, u32[]{:S(2)}) collective-permute-start(bf16[192,768]{1,0:T(8,128)(2,1)} %part.1), channel_id=1, source_target_pairs={{0,32},{1,3},{2,34},{3,5},{4,36},{5,7},{6,38},{7,1},{8,40},{9,11},... | collective-permute-start | bytes 884744 | tf_op jit(solution)/shard_map/ppermute | solution.py:96
  135.0 17.9 %collective-permute-start.11 = (bf16[192,768]{1,0:T(8,128)(2,1)}, bf16[192,768]{1,0:T(8,128)(2,1)S(1)}, u32[]{:S(2)}, u32[]{:S(2)}) collective-permute-start(bf16[192,768]{1,0:T(8,128)(2,1)} %part.1), channel_id=1, source_target_pairs={{0,96},{1,7},{2,98},{3,1},{4,100},{5,3},{6,102},{7,5},{8,104},{9,1... | collective-permute-start | bytes 884744 | tf_op jit(solution)/shard_map/ppermute | solution.py:96
  136.3 20.3 %collective-permute-start.12 = (bf16[192,768]{1,0:T(8,128)(2,1)}, bf16[192,768]{1,0:T(8,128)(2,1)S(1)}, u32[]{:S(2)}, u32[]{:S(2)}) collective-permute-start(bf16[192,768]{1,0:T(8,128)(2,1)} %part.1), channel_id=1, source_target_pairs={{0,64},{1,5},{2,66},{3,7},{4,68},{5,1},{6,70},{7,3},{8,72},{9,13},... | collective-permute-start | bytes 884744 | tf_op jit(solution)/shard_map/ppermute | solution.py:96
  152.9 9.4 %copy-start.12 = (bf16[192,768]{1,0:T(8,128)(2,1)}, bf16[192,768]{1,0:T(8,128)(2,1)S(1)}, u32[]{:S(2)}) copy-start(bf16[192,768]{1,0:T(8,128)(2,1)S(1)} %collective-permute-done.10.refs_1_) | copy-start | bytes 884740
  152.9 9.4 %copy-start.13 = (bf16[192,768]{1,0:T(8,128)(2,1)}, bf16[192,768]{1,0:T(8,128)(2,1)S(1)}, u32[]{:S(2)}) copy-start(bf16[192,768]{1,0:T(8,128)(2,1)S(1)} %collective-permute-done.11.refs_2_) | copy-start | bytes 884740
  156.6 5.6 %copy-start.14 = (bf16[192,768]{1,0:T(8,128)(2,1)}, bf16[192,768]{1,0:T(8,128)(2,1)S(1)}, u32[]{:S(2)}) copy-start(bf16[192,768]{1,0:T(8,128)(2,1)S(1)} %collective-permute-done.12.refs_3_) | copy-start | bytes 884740
  157.9 11.7 %copy-start.15 = (bf16[192,768]{1,0:T(8,128)(2,1)}, bf16[192,768]{1,0:T(8,128)(2,1)S(1)}, u32[]{:S(2)}) copy-start(bf16[192,768]{1,0:T(8,128)(2,1)S(1)} %add_convert_fusion.refs_1_) | copy-start | bytes 884740
  157.9 7.6 %collective-permute-start.16 = (bf16[192,768]{1,0:T(8,128)(2,1)S(1)}, bf16[192,768]{1,0:T(8,128)(2,1)S(1)}, u32[]{:S(2)}, u32[]{:S(2)}) collective-permute-start(bf16[192,768]{1,0:T(8,128)(2,1)S(1)} %add_convert_fusion.refs_1_), channel_id=1, source_target_pairs={{0,8},{1,33},{2,10},{3,35},{4,12},{5,37},{6,14},{7,39},{8,16},{9,4... | collective-permute-start | bytes 884744 | tf_op jit(solution)/shard_map/ppermute | solution.py:96
  158.2 9.7 %collective-permute-start.17 = (bf16[192,768]{1,0:T(8,128)(2,1)S(1)}, bf16[192,768]{1,0:T(8,128)(2,1)S(1)}, u32[]{:S(2)}, u32[]{:S(2)}) collective-permute-start(bf16[192,768]{1,0:T(8,128)(2,1)S(1)} %add_convert_fusion.refs_1_), channel_id=1, source_target_pairs={{0,24},{1,97},{2,26},{3,99},{4,28},{5,101},{6,30},{7,103},{8,0},{9... | collective-permute-start | bytes 884744 | tf_op jit(solution)/shard_map/ppermute | solution.py:96
  161.1 8.5 %collective-permute-start.18 = (bf16[192,768]{1,0:T(8,128)(2,1)S(1)}, bf16[192,768]{1,0:T(8,128)(2,1)}, u32[]{:S(2)}, u32[]{:S(2)}) collective-permute-start(bf16[192,768]{1,0:T(8,128)(2,1)S(1)} %add_convert_fusion.refs_1_), channel_id=1, source_target_pairs={{0,16},{1,65},{2,18},{3,67},{4,20},{5,69},{6,22},{7,71},{8,24},{9,... | collective-permute-start | bytes 884744 | tf_op jit(solution)/shard_map/ppermute | solution.py:96
  165.5 9.2 %copy-start.18 = (bf16[48,896]{1,0:T(8,128)(2,1)S(1)}, bf16[48,896]{1,0:T(8,128)(2,1)}, u32[]{:S(2)}) copy-start(bf16[48,896]{1,0:T(8,128)(2,1)} %strip.1.refs_5_.refs_0_) | copy-start | bytes 258052
  165.5 4.1 %copy-start.20 = (bf16[192,768]{1,0:T(8,128)(2,1)}, bf16[192,768]{1,0:T(8,128)(2,1)S(1)}, u32[]{:S(2)}) copy-start(bf16[192,768]{1,0:T(8,128)(2,1)S(1)} %collective-permute-done.16.refs_2_) | copy-start | bytes 884740
  172.0 5.4 %collective-permute-start.21 = (bf16[768,768]{1,0:T(8,128)(2,1)}, bf16[768,768]{1,0:T(8,128)(2,1)}, u32[]{:S(2)}, u32[]{:S(2)}) collective-permute-start(bf16[768,768]{1,0:T(8,128)(2,1)} %join.1.own_ref), channel_id=1, source_target_pairs={{0,1},{1,0},{2,3},{3,2},{4,5},{5,4},{6,7},{7,6},{8,9},{9,8},{10,11... | collective-permute-start | bytes 3538952 | tf_op jit(solution)/shard_map/ppermute | solution.py:100
  172.0 16.9 %collective-permute-start.19 = (bf16[768,768]{1,0:T(8,128)(2,1)}, bf16[768,768]{1,0:T(8,128)(2,1)}, u32[]{:S(2)}, u32[]{:S(2)}) collective-permute-start(bf16[768,768]{1,0:T(8,128)(2,1)} %join.1.own_ref), channel_id=1, source_target_pairs={{0,2},{1,9},{2,4},{3,11},{4,6},{5,13},{6,0},{7,15},{8,10},{9,17},{... | collective-permute-start | bytes 3538952 | tf_op jit(solution)/shard_map/ppermute | solution.py:96
  172.8 16.1 %collective-permute-start.20 = (bf16[768,768]{1,0:T(8,128)(2,1)}, bf16[768,768]{1,0:T(8,128)(2,1)S(1)}, u32[]{:S(2)}, u32[]{:S(2)}) collective-permute-start(bf16[768,768]{1,0:T(8,128)(2,1)} %join.1.own_ref), channel_id=1, source_target_pairs={{0,6},{1,25},{2,0},{3,27},{4,2},{5,29},{6,4},{7,31},{8,14},{9,1},{... | collective-permute-start | bytes 3538952 | tf_op jit(solution)/shard_map/ppermute | solution.py:96
  174.6 8.2 %collective-permute-start.13 = (bf16[48,896]{1,0:T(8,128)(2,1)S(1)}, bf16[48,896]{1,0:T(8,128)(2,1)S(1)}, u32[]{:S(2)}, u32[]{:S(2)}) collective-permute-start(bf16[48,896]{1,0:T(8,128)(2,1)S(1)} %copy-done.18), channel_id=1, source_target_pairs={{0,32},{1,33},{2,34},{3,35},{4,36},{5,37},{6,38},{7,39},{8,40},{9,... | collective-permute-start | bytes 258056 | tf_op jit(solution)/shard_map/ppermute | solution.py:96
  175.5 9.0 %collective-permute-start.14 = (bf16[48,896]{1,0:T(8,128)(2,1)S(1)}, bf16[48,896]{1,0:T(8,128)(2,1)S(1)}, u32[]{:S(2)}, u32[]{:S(2)}) collective-permute-start(bf16[48,896]{1,0:T(8,128)(2,1)S(1)} %copy-done.18), channel_id=1, source_target_pairs={{0,96},{1,97},{2,98},{3,99},{4,100},{5,101},{6,102},{7,103},{8,104... | collective-permute-start | bytes 258056 | tf_op jit(solution)/shard_map/ppermute | solution.py:96
  177.3 7.2 %collective-permute-start.15 = (bf16[48,896]{1,0:T(8,128)(2,1)S(1)}, bf16[48,896]{1,0:T(8,128)(2,1)S(1)}, u32[]{:S(2)}, u32[]{:S(2)}) collective-permute-start(bf16[48,896]{1,0:T(8,128)(2,1)S(1)} %copy-done.18), channel_id=1, source_target_pairs={{0,64},{1,65},{2,66},{3,67},{4,68},{5,69},{6,70},{7,71},{8,72},{9,... | collective-permute-start | bytes 258056 | tf_op jit(solution)/shard_map/ppermute | solution.py:96
  182.9 6.0 %copy-start.24 = (bf16[48,896]{1,0:T(8,128)(2,1)}, bf16[48,896]{1,0:T(8,128)(2,1)S(1)}, u32[]{:S(2)}) copy-start(bf16[48,896]{1,0:T(8,128)(2,1)S(1)} %collective-permute-done.13.refs_1_) | copy-start | bytes 258052
  182.9 6.0 %collective-permute-start.22 = (f32[8,128]{1,0:T(8,128)S(1)}, f32[8,128]{1,0:T(8,128)S(1)}, u32[]{:S(2)}, u32[]{:S(2)}) collective-permute-start(f32[8,128]{1,0:T(8,128)S(1)} %slice.13), channel_id=1, source_target_pairs={{0,1},{1,0},{2,3},{3,2},{4,5},{5,4},{6,7},{7,6},{8,9},{9,8},{10,11... | collective-permute-start | bytes 12296 | tf_op jit(solution)/shard_map/ppermute | solution.py:100
  184.5 4.3 %copy-start.25 = (bf16[48,896]{1,0:T(8,128)(2,1)}, bf16[48,896]{1,0:T(8,128)(2,1)S(1)}, u32[]{:S(2)}) copy-start(bf16[48,896]{1,0:T(8,128)(2,1)S(1)} %collective-permute-done.14.refs_2_) | copy-start | bytes 258052
  184.5 4.3 %copy-start.26 = (bf16[48,896]{1,0:T(8,128)(2,1)}, bf16[48,896]{1,0:T(8,128)(2,1)S(1)}, u32[]{:S(2)}) copy-start(bf16[48,896]{1,0:T(8,128)(2,1)S(1)} %collective-permute-done.15.refs_3_) | copy-start | bytes 258052
  192.6 30.1 %all-to-all-start.4 = ((bf16[16,48,896]{2,1,0:T(8,128)(2,1)}), bf16[16,48,896]{2,1,0:T(8,128)(2,1)S(1)}, u32[]{:S(2)}, u32[]{:S(2)}) async-start(bf16[16,48,896]{2,1,0:T(8,128)(2,1)} %copies.1), calls=%async_computation.4 | async-start | bytes 2752512 | tf_op jit(solution)/shard_map/all_to_all | solution.py:680
  199.5 6.7 %collective-permute-start.25 = (bf16[768,768]{1,0:T(8,128)(2,1)}, bf16[768,768]{1,0:T(8,128)(2,1)}, u32[]{:S(2)}, u32[]{:S(2)}) collective-permute-start(bf16[768,768]{1,0:T(8,128)(2,1)} %tie.8.own_ref), channel_id=1, source_target_pairs={{0,1},{1,0},{2,3},{3,2},{4,5},{5,4},{6,7},{7,6},{8,9},{9,8},{10,11... | collective-permute-start | bytes 3538952 | tf_op jit(solution)/shard_map/ppermute | solution.py:100
  203.4 7.1 %collective-permute-start.24 = (bf16[768,768]{1,0:T(8,128)(2,1)}, bf16[768,768]{1,0:T(8,128)(2,1)}, u32[]{:S(2)}, u32[]{:S(2)}) collective-permute-start(bf16[768,768]{1,0:T(8,128)(2,1)} %tie.7.own_ref), channel_id=1, source_target_pairs={{0,1},{1,0},{2,3},{3,2},{4,5},{5,4},{6,7},{7,6},{8,9},{9,8},{10,11... | collective-permute-start | bytes 3538952 | tf_op jit(solution)/shard_map/ppermute | solution.py:100
  203.4 17.5 %collective-permute-start.26 = (bf16[384,768]{1,0:T(8,128)(2,1)}, bf16[384,768]{1,0:T(8,128)(2,1)}, u32[]{:S(2)}, u32[]{:S(2)}) collective-permute-start(bf16[384,768]{1,0:T(8,128)(2,1)} %get-tuple-element.102.refs_0_), channel_id=1, source_target_pairs={{0,6},{1,25},{2,0},{3,27},{4,2},{5,29},{6,4},{7,31},{8,14},{9,1},{... | collective-permute-start | bytes 1769480 | tf_op jit(solution)/shard_map/ppermute | solution.py:96
  206.3 15.6 %collective-permute-start.23 = (bf16[384,768]{1,0:T(8,128)(2,1)}, bf16[384,768]{1,0:T(8,128)(2,1)S(1)}, u32[]{:S(2)}, u32[]{:S(2)}) collective-permute-start(bf16[384,768]{1,0:T(8,128)(2,1)} %get-tuple-element.101.refs_0_), channel_id=1, source_target_pairs={{0,2},{1,9},{2,4},{3,11},{4,6},{5,13},{6,0},{7,15},{8,10},{9,17},{... | collective-permute-start | bytes 1769480 | tf_op jit(solution)/shard_map/ppermute | solution.py:96
  222.7 2.7 %copy-start.5 = (bf16[384,768]{1,0:T(8,128)(2,1)S(1)}, bf16[384,768]{1,0:T(8,128)(2,1)}, u32[]{:S(2)}) copy-start(bf16[384,768]{1,0:T(8,128)(2,1)} %tie.9.refs_0_.own_ref) | copy-start | bytes 1769476
  223.8 13.0 %collective-permute-start.27 = (bf16[16,48,896]{2,1,0:T(8,128)(2,1)}, bf16[16,48,896]{2,1,0:T(8,128)(2,1)S(1)}, u32[]{:S(2)}, u32[]{:S(2)}) collective-permute-start(bf16[16,48,896]{2,1,0:T(8,128)(2,1)} %tie.11.refs_1_), channel_id=1, source_target_pairs={{0,1},{1,0},{2,3},{3,2},{4,5},{5,4},{6,7},{7,6},{8,9},{9,8},{10,11... | collective-permute-start | bytes 4128776 | tf_op jit(solution)/shard_map/ppermute | solution.py:100
  225.4 4.7 %collective-permute-start.29 = (bf16[384,768]{1,0:T(8,128)(2,1)}, bf16[384,768]{1,0:T(8,128)(2,1)}, u32[]{:S(2)}, u32[]{:S(2)}) collective-permute-start(bf16[384,768]{1,0:T(8,128)(2,1)} %tie.10.refs_1_.own_ref), channel_id=1, source_target_pairs={{0,1},{1,0},{2,3},{3,2},{4,5},{5,4},{6,7},{7,6},{8,9},{9,8},{10,11... | collective-permute-start | bytes 1769480 | tf_op jit(solution)/shard_map/ppermute | solution.py:100
  225.4 8.0 %collective-permute-start.28 = (bf16[384,768]{1,0:T(8,128)(2,1)S(1)}, bf16[384,768]{1,0:T(8,128)(2,1)}, u32[]{:S(2)}, u32[]{:S(2)}) collective-permute-start(bf16[384,768]{1,0:T(8,128)(2,1)S(1)} %copy-done.5), channel_id=1, source_target_pairs={{0,1},{1,0},{2,3},{3,2},{4,5},{5,4},{6,7},{7,6},{8,9},{9,8},{10,11... | collective-permute-start | bytes 1769480 | tf_op jit(solution)/shard_map/ppermute | solution.py:100
  (18 other events, 16.9 us)

commit v7 on v6

--- a/solution.py
+++ b/solution.py
@@ -68,7 +68,7 @@
 
 
 AXES = ("x", "y", "z", "c")
-ORDER = ((2, 1, 0, 0), (1, 0, 2, 0))
+ORDER = ((2, 1, 0, 0), (1, 0, 2, 2))
 FROM = (0, 3, 1, 2)
 
 
@@ -83,13 +83,20 @@
     return pairs
 
 
-def ring_groups(place):
+def groups_by(key):
     groups = {}
     for at in itertools.product(range(4), range(4), range(4), range(2)):
-        key = list(at)
-        key[ORDER[at[3]][place]] = -1
-        groups.setdefault(tuple(key), []).append(((at[0] * 4 + at[1]) * 4 + at[2]) * 2 + at[3])
+        groups.setdefault(key(at), []).append(((at[0] * 4 + at[1]) * 4 + at[2]) * 2 + at[3])
     return list(groups.values())
+
+
+def ring_groups(place):
+    return groups_by(lambda at: tuple(-1 if i == ORDER[at[3]][place] else v for i, v in enumerate(at)))
+
+
+def in_plane(v):
+    planes = groups_by(lambda at: (at[ORDER[at[3]][3]], at[3]))
+    return lax.all_to_all(v, AXES, 0, 0, axis_index_groups=planes, tiled=True)
 
 
 def send(v, place, shift):
@@ -642,7 +649,7 @@
     slabs = lax.all_to_all(packed, AXES, 0, 0, axis_index_groups=ring_groups(0), tiled=True)
 
     gq, right, right_send, kv_grads, kv_send = attend_back(at, kinds, xq, ga, o, lse, kv_all, key_cols, own_lanes, start_lanes, gb, after=(packed,))
-    shares = call(share_kernel, (kv_grads, swap(kv_send)), shapes(KV_HALF)[0], name="share", after=(slabs,))
+    shares = call(share_kernel, (kv_grads, swap(kv_send)), shapes(KV_HALF)[0], name="share", after=(slabs[0, :8, :128],))
     parts = lax.all_to_all(shares, ("y", "z"), 0, 0, tiled=True)
 
     pieces = pl.pallas_call(
@@ -668,7 +675,7 @@
                   [pltpu.VMEM((D, 128), f32)], name="late", after=ff_parts[1:])
     ff_part = call(part_kernel, ff_parts, shapes(QUARTER)[0], name="part", after=(shares,))
     ff_crossed = gather4(ff_part, 2)
-    late_parts = lax.all_to_all(shares, ("y", "z"), 0, 0, tiled=True)
+    late_parts = in_plane(shares)
     ff_totals = gather4(pair_sums(*ff_crossed), 1)
     strip = call(strip_kernel, (late_parts,), shapes(((STRIP, D + 128), bf16))[0], name="strip", after=ff_crossed[1:])
     u = call(join_kernel, (at,) + ff_totals, shapes(((D, D), bf16))[0], name="join", after=(strip,))
@@ -677,7 +684,7 @@
     mark = corner(kept[0])
     copies = call(copies_kernel, gather4(strip, 3), shapes(((CHIPS, STRIP, D + 128), bf16))[0], name="copies",
                   after=(before, after, mark))
-    late = lax.all_to_all(copies, ("y", "z"), 0, 0, tiled=True)
+    late = in_plane(copies)
     g_down, g_up, *rest = feed_forward_rest(at, before, after, kept, mark)
     late = tie(late, *rest)
     one = lambda n: ((n,), f32)

time: 244 us -> 238 us (0.975)
  Pallas kernels: 110 us -> 102 us
  starting transfers between devices: 63.2 us -> 69.8 us
  waiting for transfers between devices: 46.5 us -> 40.7 us
    ppermute x16, starting transfers between devices: 21.2 us -> 29.6 us  [send(): return lax.ppermute(v, AXES, ring(place, shift))]
    pallas_call x15, Pallas kernels: 74.4 us -> 66.9 us  [call(): pl.pallas_call(run, out_shape=outs, in_specs=[SMEM if v.dtype == jnp.int3...]
    ppermute x16, waiting for transfers between devices: 34.3 us -> 26.9 us  [send(): return lax.ppermute(v, AXES, ring(place, shift))]
    all_to_all x2, starting transfers between devices: 9.43 us -> 12.8 us  [in_plane(): return lax.all_to_all(v, AXES, 0, 0, axis_index_groups=planes, tiled=True)]
    all_to_all x1, waiting for transfers between devices: 0.01 us -> 3.38 us  [body(): lax.all_to_all(packed, AXES, 0, 0, axis_index_groups=ring_groups(0), tile...]
    all_to_all x1, starting transfers between devices: 6.52 us -> 3.88 us  [body(): parts = lax.all_to_all(shares, ('y', 'z'), 0, 0, tiled=True)]
    ppermute x14, starting transfers between devices: 13.5 us -> 11 us  [swap(): return lax.ppermute(v, 'c', [(0, 1), (1, 0)])]
  transfers between devices with their start and end apart: 35 -> 35, of which waited for: 15 -> 14; matrix products, arithmetic and copies ran while one was open for 4% -> 5% of each run, Pallas kernels for 25% -> 24%
where the time goes in v7:
time: 238 us; the launch traced here: 237 us
  Pallas kernels  102 us (43%)
  starting transfers between devices  69.8 us (29%)
  waiting for transfers between devices  40.7 us (17%)
  local copies, waits for them, and re-layouts  18.4 us (8%)
  other arithmetic  4.53 us (2%)
    pallas_call x15, Pallas kernels, call(): pl.pallas_call(run, out_shape=outs, in_specs=[SMEM if v.dtype == jnp.int3...  66.9 us
    ppermute x16, starting transfers between devices, send(): return lax.ppermute(v, AXES, ring(place, shift))  29.6 us
    ppermute x16, waiting for transfers between devices, send(): return lax.ppermute(v, AXES, ring(place, shift))  26.9 us
    pallas_call x5, Pallas kernels, place(): pl.pallas_call(place_kernel, grid_spec=pltpu.PrefetchScalarGridSpec(num_s...  19.3 us
    all_to_all x2, starting transfers between devices, in_plane(): return lax.all_to_all(v, AXES, 0, 0, axis_index_groups=planes, tiled=True)  12.8 us
    unnamed x62, local copies, waits for them, and re-layouts  12 us
    ppermute x14, starting transfers between devices, swap(): return lax.ppermute(v, 'c', [(0, 1), (1, 0)])  11 us
    pallas_call x1, Pallas kernels, body(): pl.pallas_call(middle_kernel, grid=(steps,), out_shape=shapes(narrow, ((R...  10.5 us
  transfers between devices with their start and end apart: 35, of which 14 were waited for; matrix products, arithmetic and copies ran while one was open for 5% of the time, Pallas kernels for 24%

profile of v7, /device:TPU:1, one launch (start us, length us, event | category | flops | bytes accessed | tf_op | source)
XLA Modules:
  0.0 236.7 jit_solution(757430380765900936)
XLA Ops:
  0.6 2.2 enter.1
  2.9 8.6 %all-to-all-start = ((bf16[16,128,128]{2,1,0:T(8,128)(2,1)}), bf16[16,128,128]{2,1,0:T(8,128)(2,1)S(1)}, u32[]{:S(2)}, u32[]{:S(2)}) async-start(bf16[16,128,128]{2,1,0:T(8,128)(2,1)} %get-tuple-element.71), calls=%async_computation | async-start | bytes 1048576 | tf_op jit(solution)/shard_map/all_to_all | solution.py:613
  17.1 2.2 broadcast_in_dim.28.refs_3_.refs_5_.refs_7_
  19.3 2.3 query.1.refs_0_.refs_2_
  22.6 2.1 collective-permute-start
  27.3 14.5 %attend.1 = (bf16[128,768]{1,0:T(8,128)(2,1)}, bf16[128,768]{1,0:T(8,128)(2,1)}, bf16[128,768]{1,0:T(8,128)(2,1)}, bf16[2,768,128]{2,1,0:T(8,128)(2,1)}, f32[2,7...) custom-call(s32[6]{0:T(128)} %stack.27.refs_0_.at_ref, s32[8]{0:T(128)} %select_n.94.refs_6_.refs_1_, ...), custom_call_target="tpu_custom_call" | custom-call | flops 1 | bytes 1 | tf_op jit(solution)/shard_map/attend/pallas_call | solution.py:475
  41.8 10.5 %middle.1 = (bf16[128,768]{1,0:T(8,128)(2,1)}, bf16[128,3072]{1,0:T(8,128)(2,1)}, bf16[128,3072]{1,0:T(8,128)(2,1)}, bf16[128,768]{1,0:T(8,128)(2,1)}, bf16[128,...) custom-call(s32[6]{0:T(128)} %stack.27.refs_0_.at_ref, ...), custom_call_target="tpu_custom_call" | custom-call | flops 1 | bytes 1 | tf_op jit(solution)/shard_map/middle/pallas_call | solution.py:629
  52.9 2.3 collective-permute-done.2.refs_3_
  56.1 3.4 %pack.1.refs_11_ = bf16[4,256,1536]{2,1,0:T(8,128)(2,1)} custom-call(bf16[128,3072]{1,0:T(8,128)(2,1)} %get-tuple-element.80.refs_0_, bf16[128,768]{1,0:T(8,128)(2,1)} %get-tuple-element.81.refs_1_, bf16[128,3072]{1,0:T(8,128)(2,1)} %copy-done.16, bf16[128,768]{1,0:T(8,128)(2,1)} %copy-done.22), custom_call_target="tpu_custom_call" | custom-call | flops 1 | bytes 1 | tf_op jit(solution)/shard_map/pack/pallas_call | solution.py:475
  59.5 3.9 %all-to-all-start.1 = ((bf16[4,256,1536]{2,1,0:T(8,128)(2,1)}), bf16[4,256,1536]{2,1,0:T(8,128)(2,1)S(1)}, u32[]{:S(2)}, u32[]{:S(2)}) async-start(bf16[4,256,1536]{2,1,0:T(8,128)(2,1)} %pack.1.refs_11_), calls=%async_computation.1 | async-start | bytes 6291456 | tf_op jit(solution)/shard_map/all_to_all | solution.py:649
  63.4 17.3 %attend_back.1 = (bf16[128,768]{1,0:T(8,128)(2,1)}, bf16[128,768]{1,0:T(8,128)(2,1)}, bf16[128,768]{1,0:T(8,128)(2,1)}, bf16[16,128,128]{2,1,0:T(8,128)(2,1)}, bf16[16,128,128]{2,1,0:T(8,128)(2,1)}) custom-call(s32[6]{0:T(128)} %stack.27.refs_0_.at_ref, s32[8]{0:T(128)} %select_n.94.refs_6_.refs_1_, bf16[2,768,128]{2,1,0:T(8,128)(2,1)} %get-tuple-element.74.refs_2_, ...), custom_call_target="tpu_custom_call" | custom-call | flops 1 | bytes 1 | tf_op jit(solution)/shard_map/attend_back/pallas_call | solution.py:475
  81.1 3.4 %all-to-all-done.1.slab_ref = bf16[4,256,1536]{2,1,0:T(8,128)(2,1)S(1)} async-done(((bf16[4,256,1536]{2,1,0:T(8,128)(2,1)}), bf16[4,256,1536]{2,1,0:T(8,128)(2,1)S(1)}, u32[]{:S(2)}, u32[]{:S(2)}) %all-to-all-start.1) | async-done | bytes 3145760 | tf_op jit(solution)/shard_map/all_to_all | solution.py:649
  84.4 1.7 copy-done.1
  86.7 2.1 share.1
  88.8 3.9 %all-to-all-start.2 = ((bf16[16,128,128]{2,1,0:T(8,128)(2,1)}), bf16[16,128,128]{2,1,0:T(8,128)(2,1)S(1)}, u32[]{:S(2)}, u32[]{:S(2)}) async-start(bf16[16,128,128]{2,1,0:T(8,128)(2,1)} %share.1), calls=%async_computation.2 | async-start | bytes 1048576 | tf_op jit(solution)/shard_map/all_to_all | solution.py:653
  92.7 5.3 %weights.1 = (bf16[192,768]{1,0:T(8,128)(2,1)}, bf16[192,768]{1,0:T(8,128)(2,1)}, bf16[192,768]{1,0:T(8,128)(2,1)}, bf16[192,768]{1,0:T(8,128)(2,1)}) custom-call(s32[6]{0:T(128)} %stack.27.refs_0_.at_ref, bf16[4,256,1536]{2,1,0:T(8,128)(2,1)} %copy-done.1), custom_call_target="tpu_custom_call" | custom-call | flops 1 | bytes 1 | tf_op jit(solution)/shard_map/weights/pallas_call | solution.py:655
  99.2 8.0 %collective-permute-start.8 = (bf16[192,768]{1,0:T(8,128)(2,1)}, bf16[192,768]{1,0:T(8,128)(2,1)S(1)}, u32[]{:S(2)}, u32[]{:S(2)}) collective-permute-start(bf16[192,768]{1,0:T(8,128)(2,1)} %get-tuple-element.98), channel_id=1, source_target_pairs={{0,24},{1,97},{2,26},{3,99},{4,28},{5,101},{6,30},{7,103},{8,0},{9... | collective-permute-start | bytes 884744 | tf_op jit(solution)/shard_map/ppermute | solution.py:103
  110.8 3.0 %square.1.refs_10_.refs_5_ = bf16[768,768]{1,0:T(8,128)(2,1)} custom-call(bf16[128,768]{1,0:T(8,128)(2,1)} %get-tuple-element.90.refs_0_.refs_1_, bf16[128,768]{1,0:T(8,128)(2,1)} %copy-done.17, bf16[128,768]{1,0:T(8,128)(2,1)} %get-tuple-element.92.refs_2_, bf16[128,768]{1,0:T(8,128)(2,1)} %copy-done.23), custom_call_target="tpu_custom_call" | custom-call | flops 1 | bytes 1 | tf_op jit(solution)/shard_map/square/pallas_call | solution.py:475
  114.6 3.3 %leave.1 = (f32[768,128]{1,0:T(8,128)}, f32[128,128]{1,0:T(8,128)}, f32[128,128]{1,0:T(8,128)}, f32[128,128]{1,0:T(8,128)}) custom-call(s32[6]{0:T(128)} %stack.27.refs_0_.at_ref, bf16[128,768]{1,0:T(8,128)(2,1)} %bitcast.61, bf16[768]{0:T(1024)(128)(2,1)} %refs_2_.5, bf16[768,768]{1,0:T(8,128)(2,1)} %refs_3_.3, bf16[768,128]{1,0:T(8,128)(2,1)} %refs_4_.3, ...), custom_call_target="tpu_custom_call" | custom-call | flops 1 | bytes 1 | tf_op jit(solution)/shard_map/leave/pallas_call | solution.py:475
  120.0 2.8 %late.1.refs_4_ = bf16[16,48,896]{2,1,0:T(8,128)(2,1)} custom-call(s32[6]{0:T(128)} %stack.27.refs_0_.at_ref, bf16[128,768]{1,0:T(8,128)(2,1)} %get-tuple-element.90.refs_0_.refs_1_, bf16[128,768]{1,0:T(8,128)(2,1)} %copy-done.17, f32[128,128]{1,0:T(8,128)} %get-tuple-element.95.refs_3_, f32[128,128]{1,0:T(8,128)} %copy-done.27, ...), custom_call_target="tpu_custom_call" | custom-call | flops 1 | bytes 1 | tf_op jit(solution)/shard_map/late/pallas_call | solution.py:475
  122.8 6.4 %all-to-all-start.3 = ((bf16[16,48,896]{2,1,0:T(8,128)(2,1)}), bf16[16,48,896]{2,1,0:T(8,128)(2,1)S(1)}, u32[]{:S(2)}, u32[]{:S(2)}) async-start(bf16[16,48,896]{2,1,0:T(8,128)(2,1)} %late.1.refs_4_), calls=%async_computation.3 | async-start | bytes 2752512 | tf_op jit(solution)/shard_map/all_to_all | solution.py:99
  129.2 2.1 part.1
  131.3 1.6 collective-permute-start.10
  134.1 1.8 collective-permute-start.12
  135.9 9.2 %collective-permute-done.10.refs_1_ = bf16[192,768]{1,0:T(8,128)(2,1)S(1)} collective-permute-done((bf16[192,768]{1,0:T(8,128)(2,1)}, bf16[192,768]{1,0:T(8,128)(2,1)S(1)}, u32[]{:S(2)}, u32[]{:S(2)}) %collective-permute-start.10) | collective-permute-done | bytes 294944 | tf_op jit(solution)/shard_map/ppermute | solution.py:103
  146.9 2.9 %collective-permute-start.17 = (bf16[192,768]{1,0:T(8,128)(2,1)S(1)}, bf16[192,768]{1,0:T(8,128)(2,1)S(1)}, u32[]{:S(2)}, u32[]{:S(2)}) collective-permute-start(bf16[192,768]{1,0:T(8,128)(2,1)S(1)} %add_convert_fusion.refs_1_), channel_id=1, source_target_pairs={{0,24},{1,97},{2,26},{3,99},{4,28},{5,101},{6,30},{7,103},{8,0},{9... | collective-permute-start | bytes 884744 | tf_op jit(solution)/shard_map/ppermute | solution.py:103
  152.0 2.1 strip.1.refs_5_.refs_0_
  154.2 2.5 %collective-permute-done.17.refs_3_ = bf16[192,768]{1,0:T(8,128)(2,1)S(1)} collective-permute-done((bf16[192,768]{1,0:T(8,128)(2,1)S(1)}, bf16[192,768]{1,0:T(8,128)(2,1)S(1)}, u32[]{:S(2)}, u32[]{:S(2)}) %collective-permute-start.17) | collective-permute-done | bytes 294944 | tf_op jit(solution)/shard_map/ppermute | solution.py:103
  156.6 1.9 collective-permute-done.18.refs_4_
  158.6 2.4 join.1.own_ref
  160.9 2.7 %collective-permute-start.21 = (bf16[768,768]{1,0:T(8,128)(2,1)}, bf16[768,768]{1,0:T(8,128)(2,1)}, u32[]{:S(2)}, u32[]{:S(2)}) collective-permute-start(bf16[768,768]{1,0:T(8,128)(2,1)} %join.1.own_ref), channel_id=1, source_target_pairs={{0,1},{1,0},{2,3},{3,2},{4,5},{5,4},{6,7},{7,6},{8,9},{9,8},{10,11... | collective-permute-start | bytes 3538952 | tf_op jit(solution)/shard_map/ppermute | solution.py:107
  164.8 1.9 collective-permute-start.20
  169.3 1.6 collective-permute-start.15
  170.9 4.2 %place.5 = (f32[3072,768]{1,0:T(8,128)}, f32[768,3072]{1,0:T(8,128)}) custom-call(s32[6]{0:T(128)} %stack.27.refs_0_.at_ref, bf16[768,768]{1,0:T(8,128)(2,1)} %join.1.own_ref, bf16[768,768]{1,0:T(8,128)(2,1)} %collective-permute-done.21.other_ref), custom_call_target="tpu_custom_call" | custom-call | flops 1 | bytes 1 | tf_op jit(solution)/shard_map/place/pallas_call | solution.py:397
  175.8 4.9 %collective-permute-done.19.refs_4_.refs_0_.v_ref = bf16[768,768]{1,0:T(8,128)(2,1)} collective-permute-done((bf16[768,768]{1,0:T(8,128)(2,1)}, bf16[768,768]{1,0:T(8,128)(2,1)}, u32[]{:S(2)}, u32[]{:S(2)}) %collective-permute-start.19) | collective-permute-done | bytes 1179680 | tf_op jit(solution)/shard_map/ppermute | solution.py:103
  182.4 2.2 copies.1
  184.6 6.4 %all-to-all-start.4 = ((bf16[16,48,896]{2,1,0:T(8,128)(2,1)}), bf16[16,48,896]{2,1,0:T(8,128)(2,1)S(1)}, u32[]{:S(2)}, u32[]{:S(2)}) async-start(bf16[16,48,896]{2,1,0:T(8,128)(2,1)} %copies.1), calls=%async_computation.4 | async-start | bytes 2752512 | tf_op jit(solution)/shard_map/all_to_all | solution.py:99
  191.0 2.7 %halves.1 = (bf16[384,768]{1,0:T(8,128)(2,1)}, bf16[384,768]{1,0:T(8,128)(2,1)}) custom-call(bf16[768,768]{1,0:T(8,128)(2,1)} %collective-permute-done.19.refs_4_.refs_0_.v_ref, bf16[768,768]{1,0:T(8,128)(2,1)} %copy-done, f32[8,128]{1,0:T(8,128)} %copy-done.28), custom_call_target="tpu_custom_call" | custom-call | flops 1 | bytes 1 | tf_op jit(solution)/shard_map/halves/pallas_call | solution.py:475
  193.7 3.7 %collective-permute-start.25 = (bf16[768,768]{1,0:T(8,128)(2,1)}, bf16[768,768]{1,0:T(8,128)(2,1)}, u32[]{:S(2)}, u32[]{:S(2)}) collective-permute-start(bf16[768,768]{1,0:T(8,128)(2,1)} %tie.8.own_ref), channel_id=1, source_target_pairs={{0,1},{1,0},{2,3},{3,2},{4,5},{5,4},{6,7},{7,6},{8,9},{9,8},{10,11... | collective-permute-start | bytes 3538952 | tf_op jit(solution)/shard_map/ppermute | solution.py:107
  197.4 2.9 %collective-permute-start.26 = (bf16[384,768]{1,0:T(8,128)(2,1)}, bf16[384,768]{1,0:T(8,128)(2,1)}, u32[]{:S(2)}, u32[]{:S(2)}) collective-permute-start(bf16[384,768]{1,0:T(8,128)(2,1)} %get-tuple-element.102.refs_0_), channel_id=1, source_target_pairs={{0,6},{1,25},{2,0},{3,27},{4,2},{5,29},{6,4},{7,31},{8,14},{9,1},{... | collective-permute-start | bytes 1769480 | tf_op jit(solution)/shard_map/ppermute | solution.py:103
  200.3 4.2 %place.6 = (f32[3072,768]{1,0:T(8,128)}, f32[768,3072]{1,0:T(8,128)}) custom-call(s32[6]{0:T(128)} %stack.27.refs_0_.at_ref, bf16[768,768]{1,0:T(8,128)(2,1)} %tie.8.own_ref, bf16[768,768]{1,0:T(8,128)(2,1)} %collective-permute-done.25.other_ref, f32[3072,768]{1,0:T(8,128)} %get-tuple-element.100.rest_0_, ...), custom_call_target="tpu_custom_call", output_to_operand_aliasing={{0}: (3, {}), {1}: (4, {})} | custom-call | flops 1 | bytes 1 | tf_op jit(solution)/shard_map/place/pallas_call | solution.py:397
  204.5 4.2 %place.7 = (f32[3072,768]{1,0:T(8,128)}, f32[768,3072]{1,0:T(8,128)}) custom-call(s32[6]{0:T(128)} %stack.27.refs_0_.at_ref, bf16[768,768]{1,0:T(8,128)(2,1)} %tie.7.own_ref, bf16[768,768]{1,0:T(8,128)(2,1)} %collective-permute-done.24.other_ref, f32[3072,768]{1,0:T(8,128)} %get-tuple-element.104.rest_0_, ...), custom_call_target="tpu_custom_call", output_to_operand_aliasing={{0}: (3, {}), {1}: (4, {})} | custom-call | flops 1 | bytes 1 | tf_op jit(solution)/shard_map/place/pallas_call | solution.py:397
  208.7 6.5 %collective-permute-done.26.v_ref = bf16[384,768]{1,0:T(8,128)(2,1)} collective-permute-done((bf16[384,768]{1,0:T(8,128)(2,1)}, bf16[384,768]{1,0:T(8,128)(2,1)}, u32[]{:S(2)}, u32[]{:S(2)}) %collective-permute-start.26) | collective-permute-done | bytes 589856 | tf_op jit(solution)/shard_map/ppermute | solution.py:103
  215.2 1.8 collective-permute-done.23.v_ref
  219.7 4.4 %collective-permute-done.29.other_ref = bf16[384,768]{1,0:T(8,128)(2,1)} collective-permute-done((bf16[384,768]{1,0:T(8,128)(2,1)}, bf16[384,768]{1,0:T(8,128)(2,1)}, u32[]{:S(2)}, u32[]{:S(2)}) %collective-permute-start.29) | collective-permute-done | bytes 589856 | tf_op jit(solution)/shard_map/ppermute | solution.py:107
  224.1 3.4 %place.8 = (f32[3072,768]{1,0:T(8,128)}, f32[768,3072]{1,0:T(8,128)}) custom-call(s32[6]{0:T(128)} %stack.27.refs_0_.at_ref, bf16[384,768]{1,0:T(8,128)(2,1)} %tie.10.refs_1_.own_ref, bf16[384,768]{1,0:T(8,128)(2,1)} %collective-permute-done.29.other_ref, ...), custom_call_target="tpu_custom_call", output_to_operand_aliasing={{0}: (3, {}), {1}: (4, {})} | custom-call | flops 1 | bytes 1 | tf_op jit(solution)/shard_map/place/pallas_call | solution.py:397
  227.5 3.4 %place.9 = (f32[3072,768]{1,0:T(8,128)}, f32[768,3072]{1,0:T(8,128)}) custom-call(s32[6]{0:T(128)} %stack.27.refs_0_.at_ref, bf16[384,768]{1,0:T(8,128)(2,1)} %tie.9.refs_0_.own_ref, bf16[384,768]{1,0:T(8,128)(2,1)} %collective-permute-done.28.other_ref, f32[3072,768]{1,0:T(8,128)} %get-tuple-element.118.rest_0_, ...), custom_call_target="tpu_custom_call", output_to_operand_aliasing={{0}: (3, {}), {1}: (4, {})} | custom-call | flops 1 | bytes 1 | tf_op jit(solution)/shard_map/place/pallas_call | solution.py:397
  232.0 4.6 %late_place.1 = (f32[768,768]{1,0:T(8,128)}, f32[768,768]{1,0:T(8,128)}, f32[768,128]{1,0:T(8,128)}, f32[64]{0:T(128)}, f32[768]{0:T(1024)}, /*index=5*/f32[768]...) custom-call(s32[6]{0:T(128)} %stack.27.refs_0_.at_ref, ...), custom_call_target="tpu_custom_call" | custom-call | flops 1 | bytes 1 | tf_op jit(solution)/shard_map/late_place/pallas_call | solution.py:475
  (142 shorter events, 34.4 us)
Async XLA Ops:
  2.9 18.9 %all-to-all-start = ((bf16[16,128,128]{2,1,0:T(8,128)(2,1)}), bf16[16,128,128]{2,1,0:T(8,128)(2,1)S(1)}, u32[]{:S(2)}, u32[]{:S(2)}) async-start(bf16[16,128,128]{2,1,0:T(8,128)(2,1)} %get-tuple-element.71), calls=%async_computation | async-start | bytes 1048576 | tf_op jit(solution)/shard_map/all_to_all | solution.py:613
  22.6 3.9 %collective-permute-start = (bf16[16,128,128]{2,1,0:T(8,128)(2,1)}, bf16[16,128,128]{2,1,0:T(8,128)(2,1)S(1)}, u32[]{:S(2)}, u32[]{:S(2)}) collective-permute-start(bf16[16,128,128]{2,1,0:T(8,128)(2,1)} %tie.6.refs_3_), channel_id=1, source_target_pairs={{0,1},{1,0},{2,3},{3,2},{4,5},{5,4},{6,7},{7,6},{8,9},{9,8},{10,11... | collective-permute-start | bytes 1572872 | tf_op jit(solution)/shard_map/ppermute | solution.py:107
  52.3 2.9 %collective-permute-start.1 = (bf16[128,3072]{1,0:T(8,128)(2,1)}, bf16[128,3072]{1,0:T(8,128)(2,1)S(1)}, u32[]{:S(2)}, u32[]{:S(2)}) collective-permute-start(bf16[128,3072]{1,0:T(8,128)(2,1)} %get-tuple-element.82), channel_id=1, source_target_pairs={{0,1},{1,0},{2,3},{3,2},{4,5},{5,4},{6,7},{7,6},{8,9},{9,8},{10,11... | collective-permute-start | bytes 2359304 | tf_op jit(solution)/shard_map/ppermute | solution.py:107
  52.8 2.4 %collective-permute-start.2 = (bf16[128,768]{1,0:T(8,128)(2,1)}, bf16[128,768]{1,0:T(8,128)(2,1)S(1)}, u32[]{:S(2)}, u32[]{:S(2)}) collective-permute-start(bf16[128,768]{1,0:T(8,128)(2,1)} %get-tuple-element.83), channel_id=1, source_target_pairs={{0,1},{1,0},{2,3},{3,2},{4,5},{5,4},{6,7},{7,6},{8,9},{9,8},{10,11... | collective-permute-start | bytes 589832 | tf_op jit(solution)/shard_map/ppermute | solution.py:107
  59.5 24.9 %all-to-all-start.1 = ((bf16[4,256,1536]{2,1,0:T(8,128)(2,1)}), bf16[4,256,1536]{2,1,0:T(8,128)(2,1)S(1)}, u32[]{:S(2)}, u32[]{:S(2)}) async-start(bf16[4,256,1536]{2,1,0:T(8,128)(2,1)} %pack.1.refs_11_), calls=%async_computation.1 | async-start | bytes 6291456 | tf_op jit(solution)/shard_map/all_to_all | solution.py:649
  80.7 6.0 %collective-permute-start.3 = (bf16[16,128,128]{2,1,0:T(8,128)(2,1)}, bf16[16,128,128]{2,1,0:T(8,128)(2,1)}, u32[]{:S(2)}, u32[]{:S(2)}) collective-permute-start(bf16[16,128,128]{2,1,0:T(8,128)(2,1)} %get-tuple-element.88), channel_id=1, source_target_pairs={{0,1},{1,0},{2,3},{3,2},{4,5},{5,4},{6,7},{7,6},{8,9},{9,8},{10,11... | collective-permute-start | bytes 1572872 | tf_op jit(solution)/shard_map/ppermute | solution.py:107
  84.4 1.7 copy-start.1
  88.8 19.6 %copy-start.29 = (bf16[128,768]{1,0:T(8,128)(2,1)S(1)}, bf16[128,768]{1,0:T(8,128)(2,1)}, u32[]{:S(2)}) copy-start(bf16[128,768]{1,0:T(8,128)(2,1)} %get-tuple-element.91) | copy-start | bytes 589828
  88.8 19.6 %copy-start.30 = (bf16[128,768]{1,0:T(8,128)(2,1)S(1)}, bf16[128,768]{1,0:T(8,128)(2,1)}, u32[]{:S(2)}) copy-start(bf16[128,768]{1,0:T(8,128)(2,1)} %get-tuple-element.93) | copy-start | bytes 589828
  88.8 25.0 %all-to-all-start.2 = ((bf16[16,128,128]{2,1,0:T(8,128)(2,1)}), bf16[16,128,128]{2,1,0:T(8,128)(2,1)S(1)}, u32[]{:S(2)}, u32[]{:S(2)}) async-start(bf16[16,128,128]{2,1,0:T(8,128)(2,1)} %share.1), calls=%async_computation.2 | async-start | bytes 1048576 | tf_op jit(solution)/shard_map/all_to_all | solution.py:653
  98.0 20.1 %collective-permute-start.7 = (bf16[192,768]{1,0:T(8,128)(2,1)}, bf16[192,768]{1,0:T(8,128)(2,1)S(1)}, u32[]{:S(2)}, u32[]{:S(2)}) collective-permute-start(bf16[192,768]{1,0:T(8,128)(2,1)} %get-tuple-element.97), channel_id=1, source_target_pairs={{0,8},{1,33},{2,10},{3,35},{4,12},{5,37},{6,14},{7,39},{8,16},{9,4... | collective-permute-start | bytes 884744 | tf_op jit(solution)/shard_map/ppermute | solution.py:103
  99.2 18.9 %collective-permute-start.8 = (bf16[192,768]{1,0:T(8,128)(2,1)}, bf16[192,768]{1,0:T(8,128)(2,1)S(1)}, u32[]{:S(2)}, u32[]{:S(2)}) collective-permute-start(bf16[192,768]{1,0:T(8,128)(2,1)} %get-tuple-element.98), channel_id=1, source_target_pairs={{0,24},{1,97},{2,26},{3,99},{4,28},{5,101},{6,30},{7,103},{8,0},{9... | collective-permute-start | bytes 884744 | tf_op jit(solution)/shard_map/ppermute | solution.py:103
  107.2 11.0 %collective-permute-start.9 = (bf16[192,768]{1,0:T(8,128)(2,1)}, bf16[192,768]{1,0:T(8,128)(2,1)S(1)}, u32[]{:S(2)}, u32[]{:S(2)}) collective-permute-start(bf16[192,768]{1,0:T(8,128)(2,1)} %get-tuple-element.99), channel_id=1, source_target_pairs={{0,16},{1,65},{2,18},{3,67},{4,20},{5,69},{6,22},{7,71},{8,24},{9,... | collective-permute-start | bytes 884744 | tf_op jit(solution)/shard_map/ppermute | solution.py:103
  108.4 1.4 collective-permute-start.4
  108.4 1.7 collective-permute-start.5
  117.9 1.5 collective-permute-start.6
  122.8 28.2 %all-to-all-start.3 = ((bf16[16,48,896]{2,1,0:T(8,128)(2,1)}), bf16[16,48,896]{2,1,0:T(8,128)(2,1)S(1)}, u32[]{:S(2)}, u32[]{:S(2)}) async-start(bf16[16,48,896]{2,1,0:T(8,128)(2,1)} %late.1.refs_4_), calls=%async_computation.3 | async-start | bytes 2752512 | tf_op jit(solution)/shard_map/all_to_all | solution.py:99
  131.3 13.8 %collective-permute-start.10 = (bf16[192,768]{1,0:T(8,128)(2,1)}, bf16[192,768]{1,0:T(8,128)(2,1)S(1)}, u32[]{:S(2)}, u32[]{:S(2)}) collective-permute-start(bf16[192,768]{1,0:T(8,128)(2,1)} %part.1), channel_id=1, source_target_pairs={{0,32},{1,3},{2,34},{3,5},{4,36},{5,7},{6,38},{7,1},{8,40},{9,11},... | collective-permute-start | bytes 884744 | tf_op jit(solution)/shard_map/ppermute | solution.py:103
  132.9 12.2 %collective-permute-start.11 = (bf16[192,768]{1,0:T(8,128)(2,1)}, bf16[192,768]{1,0:T(8,128)(2,1)S(1)}, u32[]{:S(2)}, u32[]{:S(2)}) collective-permute-start(bf16[192,768]{1,0:T(8,128)(2,1)} %part.1), channel_id=1, source_target_pairs={{0,96},{1,7},{2,98},{3,1},{4,100},{5,3},{6,102},{7,5},{8,104},{9,1... | collective-permute-start | bytes 884744 | tf_op jit(solution)/shard_map/ppermute | solution.py:103
  134.1 10.9 %collective-permute-start.12 = (bf16[192,768]{1,0:T(8,128)(2,1)}, bf16[192,768]{1,0:T(8,128)(2,1)S(1)}, u32[]{:S(2)}, u32[]{:S(2)}) collective-permute-start(bf16[192,768]{1,0:T(8,128)(2,1)} %part.1), channel_id=1, source_target_pairs={{0,64},{1,5},{2,66},{3,7},{4,68},{5,1},{6,70},{7,3},{8,72},{9,13},... | collective-permute-start | bytes 884744 | tf_op jit(solution)/shard_map/ppermute | solution.py:103
  145.1 5.9 %copy-start.12 = (bf16[192,768]{1,0:T(8,128)(2,1)}, bf16[192,768]{1,0:T(8,128)(2,1)S(1)}, u32[]{:S(2)}) copy-start(bf16[192,768]{1,0:T(8,128)(2,1)S(1)} %collective-permute-done.10.refs_1_) | copy-start | bytes 884740
  145.1 5.9 %copy-start.13 = (bf16[192,768]{1,0:T(8,128)(2,1)}, bf16[192,768]{1,0:T(8,128)(2,1)S(1)}, u32[]{:S(2)}) copy-start(bf16[192,768]{1,0:T(8,128)(2,1)S(1)} %collective-permute-done.11.refs_2_) | copy-start | bytes 884740
  145.1 5.9 %copy-start.14 = (bf16[192,768]{1,0:T(8,128)(2,1)}, bf16[192,768]{1,0:T(8,128)(2,1)S(1)}, u32[]{:S(2)}) copy-start(bf16[192,768]{1,0:T(8,128)(2,1)S(1)} %collective-permute-done.12.refs_3_) | copy-start | bytes 884740
  146.4 12.2 %copy-start.15 = (bf16[192,768]{1,0:T(8,128)(2,1)}, bf16[192,768]{1,0:T(8,128)(2,1)S(1)}, u32[]{:S(2)}) copy-start(bf16[192,768]{1,0:T(8,128)(2,1)S(1)} %add_convert_fusion.refs_1_) | copy-start | bytes 884740
  146.4 7.7 %collective-permute-start.16 = (bf16[192,768]{1,0:T(8,128)(2,1)S(1)}, bf16[192,768]{1,0:T(8,128)(2,1)S(1)}, u32[]{:S(2)}, u32[]{:S(2)}) collective-permute-start(bf16[192,768]{1,0:T(8,128)(2,1)S(1)} %add_convert_fusion.refs_1_), channel_id=1, source_target_pairs={{0,8},{1,33},{2,10},{3,35},{4,12},{5,37},{6,14},{7,39},{8,16},{9,4... | collective-permute-start | bytes 884744 | tf_op jit(solution)/shard_map/ppermute | solution.py:103
  146.9 9.8 %collective-permute-start.17 = (bf16[192,768]{1,0:T(8,128)(2,1)S(1)}, bf16[192,768]{1,0:T(8,128)(2,1)S(1)}, u32[]{:S(2)}, u32[]{:S(2)}) collective-permute-start(bf16[192,768]{1,0:T(8,128)(2,1)S(1)} %add_convert_fusion.refs_1_), channel_id=1, source_target_pairs={{0,24},{1,97},{2,26},{3,99},{4,28},{5,101},{6,30},{7,103},{8,0},{9... | collective-permute-start | bytes 884744 | tf_op jit(solution)/shard_map/ppermute | solution.py:103
  149.8 8.8 %collective-permute-start.18 = (bf16[192,768]{1,0:T(8,128)(2,1)S(1)}, bf16[192,768]{1,0:T(8,128)(2,1)}, u32[]{:S(2)}, u32[]{:S(2)}) collective-permute-start(bf16[192,768]{1,0:T(8,128)(2,1)S(1)} %add_convert_fusion.refs_1_), channel_id=1, source_target_pairs={{0,16},{1,65},{2,18},{3,67},{4,20},{5,69},{6,22},{7,71},{8,24},{9,... | collective-permute-start | bytes 884744 | tf_op jit(solution)/shard_map/ppermute | solution.py:103
  154.2 12.5 %copy-start.18 = (bf16[48,896]{1,0:T(8,128)(2,1)S(1)}, bf16[48,896]{1,0:T(8,128)(2,1)}, u32[]{:S(2)}) copy-start(bf16[48,896]{1,0:T(8,128)(2,1)} %strip.1.refs_5_.refs_0_) | copy-start | bytes 258052
  154.2 4.4 %copy-start.20 = (bf16[192,768]{1,0:T(8,128)(2,1)}, bf16[192,768]{1,0:T(8,128)(2,1)S(1)}, u32[]{:S(2)}) copy-start(bf16[192,768]{1,0:T(8,128)(2,1)S(1)} %collective-permute-done.16.refs_2_) | copy-start | bytes 884740
  156.6 1.9 copy-start.21
  160.9 8.4 %collective-permute-start.21 = (bf16[768,768]{1,0:T(8,128)(2,1)}, bf16[768,768]{1,0:T(8,128)(2,1)}, u32[]{:S(2)}, u32[]{:S(2)}) collective-permute-start(bf16[768,768]{1,0:T(8,128)(2,1)} %join.1.own_ref), channel_id=1, source_target_pairs={{0,1},{1,0},{2,3},{3,2},{4,5},{5,4},{6,7},{7,6},{8,9},{9,8},{10,11... | collective-permute-start | bytes 3538952 | tf_op jit(solution)/shard_map/ppermute | solution.py:107
  163.6 17.1 %collective-permute-start.19 = (bf16[768,768]{1,0:T(8,128)(2,1)}, bf16[768,768]{1,0:T(8,128)(2,1)}, u32[]{:S(2)}, u32[]{:S(2)}) collective-permute-start(bf16[768,768]{1,0:T(8,128)(2,1)} %join.1.own_ref), channel_id=1, source_target_pairs={{0,2},{1,9},{2,4},{3,11},{4,6},{5,13},{6,0},{7,15},{8,10},{9,17},{... | collective-permute-start | bytes 3538952 | tf_op jit(solution)/shard_map/ppermute | solution.py:103
  164.8 16.0 %collective-permute-start.20 = (bf16[768,768]{1,0:T(8,128)(2,1)}, bf16[768,768]{1,0:T(8,128)(2,1)S(1)}, u32[]{:S(2)}, u32[]{:S(2)}) collective-permute-start(bf16[768,768]{1,0:T(8,128)(2,1)} %join.1.own_ref), channel_id=1, source_target_pairs={{0,6},{1,25},{2,0},{3,27},{4,2},{5,29},{6,4},{7,31},{8,14},{9,1},{... | collective-permute-start | bytes 3538952 | tf_op jit(solution)/shard_map/ppermute | solution.py:103
  166.6 9.1 %collective-permute-start.13 = (bf16[48,896]{1,0:T(8,128)(2,1)S(1)}, bf16[48,896]{1,0:T(8,128)(2,1)S(1)}, u32[]{:S(2)}, u32[]{:S(2)}) collective-permute-start(bf16[48,896]{1,0:T(8,128)(2,1)S(1)} %copy-done.18), channel_id=1, source_target_pairs={{0,32},{1,3},{2,34},{3,5},{4,36},{5,7},{6,38},{7,1},{8,40},{9,11},... | collective-permute-start | bytes 258056 | tf_op jit(solution)/shard_map/ppermute | solution.py:103
  167.9 7.9 %collective-permute-start.14 = (bf16[48,896]{1,0:T(8,128)(2,1)S(1)}, bf16[48,896]{1,0:T(8,128)(2,1)S(1)}, u32[]{:S(2)}, u32[]{:S(2)}) collective-permute-start(bf16[48,896]{1,0:T(8,128)(2,1)S(1)} %copy-done.18), channel_id=1, source_target_pairs={{0,96},{1,7},{2,98},{3,1},{4,100},{5,3},{6,102},{7,5},{8,104},{9,1... | collective-permute-start | bytes 258056 | tf_op jit(solution)/shard_map/ppermute | solution.py:103
  169.3 6.5 %collective-permute-start.15 = (bf16[48,896]{1,0:T(8,128)(2,1)S(1)}, bf16[48,896]{1,0:T(8,128)(2,1)S(1)}, u32[]{:S(2)}, u32[]{:S(2)}) collective-permute-start(bf16[48,896]{1,0:T(8,128)(2,1)S(1)} %copy-done.18), channel_id=1, source_target_pairs={{0,64},{1,5},{2,66},{3,7},{4,68},{5,1},{6,70},{7,3},{8,72},{9,13},... | collective-permute-start | bytes 258056 | tf_op jit(solution)/shard_map/ppermute | solution.py:103
  175.8 5.0 %copy-start.24 = (bf16[48,896]{1,0:T(8,128)(2,1)}, bf16[48,896]{1,0:T(8,128)(2,1)S(1)}, u32[]{:S(2)}) copy-start(bf16[48,896]{1,0:T(8,128)(2,1)S(1)} %collective-permute-done.13.refs_1_) | copy-start | bytes 258052
  175.8 5.0 %collective-permute-start.22 = (f32[8,128]{1,0:T(8,128)S(1)}, f32[8,128]{1,0:T(8,128)S(1)}, u32[]{:S(2)}, u32[]{:S(2)}) collective-permute-start(f32[8,128]{1,0:T(8,128)S(1)} %slice.17), channel_id=1, source_target_pairs={{0,1},{1,0},{2,3},{3,2},{4,5},{5,4},{6,7},{7,6},{8,9},{9,8},{10,11... | collective-permute-start | bytes 12296 | tf_op jit(solution)/shard_map/ppermute | solution.py:107
  175.8 5.0 %copy-start.25 = (bf16[48,896]{1,0:T(8,128)(2,1)}, bf16[48,896]{1,0:T(8,128)(2,1)S(1)}, u32[]{:S(2)}) copy-start(bf16[48,896]{1,0:T(8,128)(2,1)S(1)} %collective-permute-done.14.refs_2_) | copy-start | bytes 258052
  175.8 5.0 %copy-start.26 = (bf16[48,896]{1,0:T(8,128)(2,1)}, bf16[48,896]{1,0:T(8,128)(2,1)S(1)}, u32[]{:S(2)}) copy-start(bf16[48,896]{1,0:T(8,128)(2,1)S(1)} %collective-permute-done.15.refs_3_) | copy-start | bytes 258052
  184.6 33.2 %all-to-all-start.4 = ((bf16[16,48,896]{2,1,0:T(8,128)(2,1)}), bf16[16,48,896]{2,1,0:T(8,128)(2,1)S(1)}, u32[]{:S(2)}, u32[]{:S(2)}) async-start(bf16[16,48,896]{2,1,0:T(8,128)(2,1)} %copies.1), calls=%async_computation.4 | async-start | bytes 2752512 | tf_op jit(solution)/shard_map/all_to_all | solution.py:99
  193.7 6.6 %collective-permute-start.25 = (bf16[768,768]{1,0:T(8,128)(2,1)}, bf16[768,768]{1,0:T(8,128)(2,1)}, u32[]{:S(2)}, u32[]{:S(2)}) collective-permute-start(bf16[768,768]{1,0:T(8,128)(2,1)} %tie.8.own_ref), channel_id=1, source_target_pairs={{0,1},{1,0},{2,3},{3,2},{4,5},{5,4},{6,7},{7,6},{8,9},{9,8},{10,11... | collective-permute-start | bytes 3538952 | tf_op jit(solution)/shard_map/ppermute | solution.py:107
  197.4 7.1 %collective-permute-start.24 = (bf16[768,768]{1,0:T(8,128)(2,1)}, bf16[768,768]{1,0:T(8,128)(2,1)}, u32[]{:S(2)}, u32[]{:S(2)}) collective-permute-start(bf16[768,768]{1,0:T(8,128)(2,1)} %tie.7.own_ref), channel_id=1, source_target_pairs={{0,1},{1,0},{2,3},{3,2},{4,5},{5,4},{6,7},{7,6},{8,9},{9,8},{10,11... | collective-permute-start | bytes 3538952 | tf_op jit(solution)/shard_map/ppermute | solution.py:107
  197.4 17.7 %collective-permute-start.26 = (bf16[384,768]{1,0:T(8,128)(2,1)}, bf16[384,768]{1,0:T(8,128)(2,1)}, u32[]{:S(2)}, u32[]{:S(2)}) collective-permute-start(bf16[384,768]{1,0:T(8,128)(2,1)} %get-tuple-element.102.refs_0_), channel_id=1, source_target_pairs={{0,6},{1,25},{2,0},{3,27},{4,2},{5,29},{6,4},{7,31},{8,14},{9,1},{... | collective-permute-start | bytes 1769480 | tf_op jit(solution)/shard_map/ppermute | solution.py:103
  200.3 16.7 %collective-permute-start.23 = (bf16[384,768]{1,0:T(8,128)(2,1)}, bf16[384,768]{1,0:T(8,128)(2,1)S(1)}, u32[]{:S(2)}, u32[]{:S(2)}) collective-permute-start(bf16[384,768]{1,0:T(8,128)(2,1)} %get-tuple-element.101.refs_0_), channel_id=1, source_target_pairs={{0,2},{1,9},{2,4},{3,11},{4,6},{5,13},{6,0},{7,15},{8,10},{9,17},{... | collective-permute-start | bytes 1769480 | tf_op jit(solution)/shard_map/ppermute | solution.py:103
  218.9 11.9 %collective-permute-start.27 = (bf16[16,48,896]{2,1,0:T(8,128)(2,1)}, bf16[16,48,896]{2,1,0:T(8,128)(2,1)S(1)}, u32[]{:S(2)}, u32[]{:S(2)}) collective-permute-start(bf16[16,48,896]{2,1,0:T(8,128)(2,1)} %tie.11.refs_1_), channel_id=1, source_target_pairs={{0,1},{1,0},{2,3},{3,2},{4,5},{5,4},{6,7},{7,6},{8,9},{9,8},{10,11... | collective-permute-start | bytes 4128776 | tf_op jit(solution)/shard_map/ppermute | solution.py:107
  219.2 4.9 %collective-permute-start.29 = (bf16[384,768]{1,0:T(8,128)(2,1)}, bf16[384,768]{1,0:T(8,128)(2,1)}, u32[]{:S(2)}, u32[]{:S(2)}) collective-permute-start(bf16[384,768]{1,0:T(8,128)(2,1)} %tie.10.refs_1_.own_ref), channel_id=1, source_target_pairs={{0,1},{1,0},{2,3},{3,2},{4,5},{5,4},{6,7},{7,6},{8,9},{9,8},{10,11... | collective-permute-start | bytes 1769480 | tf_op jit(solution)/shard_map/ppermute | solution.py:107
  219.4 8.0 %collective-permute-start.28 = (bf16[384,768]{1,0:T(8,128)(2,1)S(1)}, bf16[384,768]{1,0:T(8,128)(2,1)}, u32[]{:S(2)}, u32[]{:S(2)}) collective-permute-start(bf16[384,768]{1,0:T(8,128)(2,1)S(1)} %copy-done.5), channel_id=1, source_target_pairs={{0,1},{1,0},{2,3},{3,2},{4,5},{5,4},{6,7},{7,6},{8,9},{9,8},{10,11... | collective-permute-start | bytes 1769480 | tf_op jit(solution)/shard_map/ppermute | solution.py:107
  (18 other events, 17.0 us)

commit v8 on v7

--- a/solution.py
+++ b/solution.py
@@ -387,17 +387,17 @@
     down_ref[...] = jnp.where(first, own, other).astype(f32)
     up_ref[...] = jnp.where(first, other, own).astype(f32)
 
-def place(at, rel, own, other, kept, part=0):
+def place(at, rel, own, other, kept):
     tile = D // 2
     piece = pl.BlockSpec((tile, D), lambda i, at: (i, 0))
     outs = (
-        pl.BlockSpec((tile, D), lambda i, at: (((at[4] + rel) & 3) * 2 + part + i, 0)),
-        pl.BlockSpec((tile, D), lambda i, at: (part + i, (at[5] + rel) & 3)),
+        pl.BlockSpec((tile, D), lambda i, at: (((at[4] + rel) & 3) * 2 + i, 0)),
+        pl.BlockSpec((tile, D), lambda i, at: (i, (at[5] + rel) & 3)),
     )
     return pl.pallas_call(
         place_kernel,
         grid_spec=pltpu.PrefetchScalarGridSpec(
-            num_scalar_prefetch=1, grid=(own.shape[0] // tile,), in_specs=[piece, piece] + [ANY] * len(kept), out_specs=outs
+            num_scalar_prefetch=1, grid=(2,), in_specs=[piece, piece] + [ANY] * len(kept), out_specs=outs
         ),
         out_shape=shapes(((FF, D), f32), ((D, FF), f32)),
         input_output_aliases={3: 0, 4: 1} if kept else {},
@@ -556,7 +556,6 @@
 
 
 QUARTER = ((D // 4, D), bf16)
-HALF = ((D // 2, D), bf16)
 
 
 def pair_sums(a, b, c, d):
@@ -582,22 +581,6 @@
 
 def corner(v):
     return swap(v[:8, :128])
-
-
-def halves_kernel(before_ref, after_ref, low_ref, high_ref):
-    low_ref[...] = before_ref[D // 2 :, :]
-    high_ref[...] = after_ref[: D // 2, :]
-
-
-def feed_forward_rest(at, before, after, kept, mark):
-    low, high = call(halves_kernel, (before, after), shapes(HALF, HALF), name="halves", after=(mark,))
-    before, after = tie(before, low), tie(after, high)
-    low, high = send(low, 0, 1), send(high, 0, 3)
-    kept = place(at, 3, before, swap(before), kept)
-    kept = place(at, 1, after, swap(after), kept)
-    low, high = (tie(v, kept[0]) for v in (low, high))
-    kept = place(at, 2, high, swap(high), kept)
-    return *place(at, 2, low, swap(low), kept, part=1), low, high
 
 
 def body(block_input, file_lengths, file_splits, ln1_gain, ln1_bias, w_query, b_query, w_kv, b_value, w_out, b_out,
@@ -679,14 +662,17 @@
     ff_totals = gather4(pair_sums(*ff_crossed), 1)
     strip = call(strip_kernel, (late_parts,), shapes(((STRIP, D + 128), bf16))[0], name="strip", after=ff_crossed[1:])
     u = call(join_kernel, (at,) + ff_totals, shapes(((D, D), bf16))[0], name="join", after=(strip,))
-    before, after = send(u, 0, 1), send(u, 0, 3)
+    before, after, far = spread(0, u, u, u)
     kept = place(at, 0, u, swap(u), ())
     mark = corner(kept[0])
     copies = call(copies_kernel, gather4(strip, 3), shapes(((CHIPS, STRIP, D + 128), bf16))[0], name="copies",
-                  after=(before, after, mark))
+                  after=(before, after, far, mark))
     late = in_plane(copies)
-    g_down, g_up, *rest = feed_forward_rest(at, before, after, kept, mark)
-    late = tie(late, *rest)
+    before, after, far = (tie(v, copies) for v in (before, after, far))
+    kept = place(at, 3, before, swap(before), kept)
+    kept = place(at, 1, after, swap(after), kept)
+    g_down, g_up = place(at, 2, far, swap(far), kept)
+    late = tie(late, corner(g_down))
     one = lambda n: ((n,), f32)
     outs = call(
         late_place_kernel, (at, late, swap(late)),

time: 238 us -> 235 us (0.987)
  waiting for transfers between devices: 40.7 us -> 48.7 us
  Pallas kernels: 102 us -> 97 us
  starting transfers between devices: 69.8 us -> 65.6 us
    ppermute x16 -> x15, waiting for transfers between devices: 26.9 us -> 31.1 us  [send(): return lax.ppermute(v, AXES, ring(place, shift))]
    ppermute x16 -> x15, starting transfers between devices: 29.6 us -> 25.7 us  [send(): return lax.ppermute(v, AXES, ring(place, shift))]
    ppermute x14, starting transfers between devices: 11 us -> 13.7 us  [swap(): return lax.ppermute(v, 'c', [(0, 1), (1, 0)])]
    all_to_all x2, starting transfers between devices: 12.8 us -> 10.1 us  [in_plane(): return lax.all_to_all(v, AXES, 0, 0, axis_index_groups=planes, tiled=True)]
    pallas_call x15 -> x14, Pallas kernels: 66.9 us -> 64.3 us  [call(): pl.pallas_call(run, out_shape=outs, in_specs=[SMEM if v.dtype == jnp.int3...]
    pallas_call x5 -> x4, Pallas kernels: 19.3 us -> 16.8 us  [place(): pl.pallas_call(place_kernel, grid_spec=pltpu.PrefetchScalarGridSpec(num_s...]
    unnamed x62 -> x64, local copies, waits for them, and re-layouts: 12 us -> 11.8 us
  transfers between devices with their start and end apart: 35 -> 34, of which waited for: 14 -> 16; matrix products, arithmetic and copies ran while one was open for 5% -> 4% of each run, Pallas kernels for 24% -> 22%
where the time goes in v8:
time: 235 us; the launch traced here: 234 us
  Pallas kernels  97 us (41%)
  starting transfers between devices  65.6 us (28%)
  waiting for transfers between devices  48.7 us (21%)
  local copies, waits for them, and re-layouts  19 us (8%)
  other arithmetic  2.37 us (1%)
    pallas_call x14, Pallas kernels, call(): pl.pallas_call(run, out_shape=outs, in_specs=[SMEM if v.dtype == jnp.int3...  64.3 us
    ppermute x15, waiting for transfers between devices, send(): return lax.ppermute(v, AXES, ring(place, shift))  31.1 us
    ppermute x15, starting transfers between devices, send(): return lax.ppermute(v, AXES, ring(place, shift))  25.7 us
    pallas_call x4, Pallas kernels, place(): pl.pallas_call(place_kernel, grid_spec=pltpu.PrefetchScalarGridSpec(num_s...  16.8 us
    ppermute x14, starting transfers between devices, swap(): return lax.ppermute(v, 'c', [(0, 1), (1, 0)])  13.7 us
    ppermute x14, waiting for transfers between devices, swap(): return lax.ppermute(v, 'c', [(0, 1), (1, 0)])  11.9 us
    unnamed x64, local copies, waits for them, and re-layouts  11.8 us
    pallas_call x1, Pallas kernels, body(): pl.pallas_call(middle_kernel, grid=(steps,), out_shape=shapes(narrow, ((R...  10.5 us
  transfers between devices with their start and end apart: 34, of which 16 were waited for; matrix products, arithmetic and copies ran while one was open for 4% of the time, Pallas kernels for 22%

profile of v8, /device:TPU:1, one launch (start us, length us, event | category | flops | bytes accessed | tf_op | source)
XLA Modules:
  0.0 233.8 jit_solution(5879231434961034414)
XLA Ops:
  0.7 2.2 enter.1
  2.9 8.6 %all-to-all-start = ((bf16[16,128,128]{2,1,0:T(8,128)(2,1)}), bf16[16,128,128]{2,1,0:T(8,128)(2,1)S(1)}, u32[]{:S(2)}, u32[]{:S(2)}) async-start(bf16[16,128,128]{2,1,0:T(8,128)(2,1)} %get-tuple-element.67), calls=%async_computation | async-start | bytes 1048576 | tf_op jit(solution)/shard_map/all_to_all | solution.py:596
  15.0 2.2 broadcast_in_dim.28.refs_3_.refs_5_.refs_7_
  17.2 2.3 query.1.refs_0_.refs_2_
  19.5 2.3 all-to-all-done.v_ref
  22.6 2.1 collective-permute-start
  27.3 14.5 %attend.1 = (bf16[128,768]{1,0:T(8,128)(2,1)}, bf16[128,768]{1,0:T(8,128)(2,1)}, bf16[128,768]{1,0:T(8,128)(2,1)}, bf16[2,768,128]{2,1,0:T(8,128)(2,1)}, f32[2,7...) custom-call(s32[6]{0:T(128)} %stack.27.refs_0_.at_ref, s32[8]{0:T(128)} %select_n.94.refs_6_.refs_1_, ...), custom_call_target="tpu_custom_call" | custom-call | flops 1 | bytes 1 | tf_op jit(solution)/shard_map/attend/pallas_call | solution.py:475
  41.8 10.5 %middle.1 = (bf16[128,768]{1,0:T(8,128)(2,1)}, bf16[128,3072]{1,0:T(8,128)(2,1)}, bf16[128,3072]{1,0:T(8,128)(2,1)}, bf16[128,768]{1,0:T(8,128)(2,1)}, bf16[128,...) custom-call(s32[6]{0:T(128)} %stack.27.refs_0_.at_ref, ...), custom_call_target="tpu_custom_call" | custom-call | flops 1 | bytes 1 | tf_op jit(solution)/shard_map/middle/pallas_call | solution.py:612
  53.0 2.3 collective-permute-done.2.refs_3_
  56.2 3.4 %pack.1.refs_11_ = bf16[4,256,1536]{2,1,0:T(8,128)(2,1)} custom-call(bf16[128,3072]{1,0:T(8,128)(2,1)} %get-tuple-element.76.refs_0_, bf16[128,768]{1,0:T(8,128)(2,1)} %get-tuple-element.77.refs_1_, bf16[128,3072]{1,0:T(8,128)(2,1)} %copy-done.14, bf16[128,768]{1,0:T(8,128)(2,1)} %copy-done.20), custom_call_target="tpu_custom_call" | custom-call | flops 1 | bytes 1 | tf_op jit(solution)/shard_map/pack/pallas_call | solution.py:475
  59.5 3.9 %all-to-all-start.1 = ((bf16[4,256,1536]{2,1,0:T(8,128)(2,1)}), bf16[4,256,1536]{2,1,0:T(8,128)(2,1)S(1)}, u32[]{:S(2)}, u32[]{:S(2)}) async-start(bf16[4,256,1536]{2,1,0:T(8,128)(2,1)} %pack.1.refs_11_), calls=%async_computation.1 | async-start | bytes 6291456 | tf_op jit(solution)/shard_map/all_to_all | solution.py:632
  63.4 17.3 %attend_back.1 = (bf16[128,768]{1,0:T(8,128)(2,1)}, bf16[128,768]{1,0:T(8,128)(2,1)}, bf16[128,768]{1,0:T(8,128)(2,1)}, bf16[16,128,128]{2,1,0:T(8,128)(2,1)}, bf16[16,128,128]{2,1,0:T(8,128)(2,1)}) custom-call(s32[6]{0:T(128)} %stack.27.refs_0_.at_ref, s32[8]{0:T(128)} %select_n.94.refs_6_.refs_1_, bf16[2,768,128]{2,1,0:T(8,128)(2,1)} %get-tuple-element.70.refs_2_, ...), custom_call_target="tpu_custom_call" | custom-call | flops 1 | bytes 1 | tf_op jit(solution)/shard_map/attend_back/pallas_call | solution.py:475
  81.1 3.4 %all-to-all-done.1.slab_ref = bf16[4,256,1536]{2,1,0:T(8,128)(2,1)S(1)} async-done(((bf16[4,256,1536]{2,1,0:T(8,128)(2,1)}), bf16[4,256,1536]{2,1,0:T(8,128)(2,1)S(1)}, u32[]{:S(2)}, u32[]{:S(2)}) %all-to-all-start.1) | async-done | bytes 3145760 | tf_op jit(solution)/shard_map/all_to_all | solution.py:632
  84.5 1.7 copy-done
  86.7 2.1 share.1
  88.8 3.6 %all-to-all-start.2 = ((bf16[16,128,128]{2,1,0:T(8,128)(2,1)}), bf16[16,128,128]{2,1,0:T(8,128)(2,1)S(1)}, u32[]{:S(2)}, u32[]{:S(2)}) async-start(bf16[16,128,128]{2,1,0:T(8,128)(2,1)} %share.1), calls=%async_computation.2 | async-start | bytes 1048576 | tf_op jit(solution)/shard_map/all_to_all | solution.py:636
  92.4 5.3 %weights.1 = (bf16[192,768]{1,0:T(8,128)(2,1)}, bf16[192,768]{1,0:T(8,128)(2,1)}, bf16[192,768]{1,0:T(8,128)(2,1)}, bf16[192,768]{1,0:T(8,128)(2,1)}) custom-call(s32[6]{0:T(128)} %stack.27.refs_0_.at_ref, bf16[4,256,1536]{2,1,0:T(8,128)(2,1)} %copy-done), custom_call_target="tpu_custom_call" | custom-call | flops 1 | bytes 1 | tf_op jit(solution)/shard_map/weights/pallas_call | solution.py:638
  97.8 6.7 %collective-permute-start.7 = (bf16[192,768]{1,0:T(8,128)(2,1)}, bf16[192,768]{1,0:T(8,128)(2,1)S(1)}, u32[]{:S(2)}, u32[]{:S(2)}) collective-permute-start(bf16[192,768]{1,0:T(8,128)(2,1)} %get-tuple-element.93), channel_id=1, source_target_pairs={{0,8},{1,33},{2,10},{3,35},{4,12},{5,37},{6,14},{7,39},{8,16},{9,4... | collective-permute-start | bytes 884744 | tf_op jit(solution)/shard_map/ppermute | solution.py:103
  109.3 3.0 %square.1.refs_10_.refs_5_ = bf16[768,768]{1,0:T(8,128)(2,1)} custom-call(bf16[128,768]{1,0:T(8,128)(2,1)} %get-tuple-element.86.refs_0_.refs_1_, bf16[128,768]{1,0:T(8,128)(2,1)} %copy-done.15, bf16[128,768]{1,0:T(8,128)(2,1)} %get-tuple-element.88.refs_2_, bf16[128,768]{1,0:T(8,128)(2,1)} %copy-done.21), custom_call_target="tpu_custom_call" | custom-call | flops 1 | bytes 1 | tf_op jit(solution)/shard_map/square/pallas_call | solution.py:475
  113.2 3.3 %leave.1 = (f32[768,128]{1,0:T(8,128)}, f32[128,128]{1,0:T(8,128)}, f32[128,128]{1,0:T(8,128)}, f32[128,128]{1,0:T(8,128)}) custom-call(s32[6]{0:T(128)} %stack.27.refs_0_.at_ref, bf16[128,768]{1,0:T(8,128)(2,1)} %bitcast.61, bf16[768]{0:T(1024)(128)(2,1)} %refs_2_.5, bf16[768,768]{1,0:T(8,128)(2,1)} %refs_3_.3, bf16[768,128]{1,0:T(8,128)(2,1)} %refs_4_.3, ...), custom_call_target="tpu_custom_call" | custom-call | flops 1 | bytes 1 | tf_op jit(solution)/shard_map/leave/pallas_call | solution.py:475
  118.5 2.8 %late.1.refs_4_ = bf16[16,48,896]{2,1,0:T(8,128)(2,1)} custom-call(s32[6]{0:T(128)} %stack.27.refs_0_.at_ref, bf16[128,768]{1,0:T(8,128)(2,1)} %get-tuple-element.86.refs_0_.refs_1_, bf16[128,768]{1,0:T(8,128)(2,1)} %copy-done.15, f32[128,128]{1,0:T(8,128)} %get-tuple-element.91.refs_3_, f32[128,128]{1,0:T(8,128)} %copy-done.25, ...), custom_call_target="tpu_custom_call" | custom-call | flops 1 | bytes 1 | tf_op jit(solution)/shard_map/late/pallas_call | solution.py:475
  121.3 6.4 %all-to-all-start.3 = ((bf16[16,48,896]{2,1,0:T(8,128)(2,1)}), bf16[16,48,896]{2,1,0:T(8,128)(2,1)S(1)}, u32[]{:S(2)}, u32[]{:S(2)}) async-start(bf16[16,48,896]{2,1,0:T(8,128)(2,1)} %late.1.refs_4_), calls=%async_computation.3 | async-start | bytes 2752512 | tf_op jit(solution)/shard_map/all_to_all | solution.py:99
  127.7 2.1 part.1
  129.8 1.6 collective-permute-start.10
  132.7 1.8 collective-permute-start.12
  134.4 9.2 %collective-permute-done.10.refs_1_ = bf16[192,768]{1,0:T(8,128)(2,1)S(1)} collective-permute-done((bf16[192,768]{1,0:T(8,128)(2,1)}, bf16[192,768]{1,0:T(8,128)(2,1)S(1)}, u32[]{:S(2)}, u32[]{:S(2)}) %collective-permute-start.10) | collective-permute-done | bytes 294944 | tf_op jit(solution)/shard_map/ppermute | solution.py:103
  145.0 1.7 collective-permute-start.16
  146.7 1.6 collective-permute-start.17
  150.6 2.2 strip.1.refs_5_.refs_0_
  152.7 2.5 %collective-permute-done.17.refs_3_ = bf16[192,768]{1,0:T(8,128)(2,1)S(1)} collective-permute-done((bf16[192,768]{1,0:T(8,128)(2,1)S(1)}, bf16[192,768]{1,0:T(8,128)(2,1)S(1)}, u32[]{:S(2)}, u32[]{:S(2)}) %collective-permute-start.17) | collective-permute-done | bytes 294944 | tf_op jit(solution)/shard_map/ppermute | solution.py:103
  155.2 1.9 collective-permute-done.18.refs_4_
  157.1 2.4 %join.1.own_ref = bf16[768,768]{1,0:T(8,128)(2,1)} custom-call(s32[6]{0:T(128)} %stack.27.refs_0_.at_ref, bf16[192,768]{1,0:T(8,128)(2,1)} %copy-done.13, bf16[192,768]{1,0:T(8,128)(2,1)} %copy-done.18, bf16[192,768]{1,0:T(8,128)(2,1)} %copy-done.19, bf16[192,768]{1,0:T(8,128)(2,1)} %collective-permute-done.18.refs_4_, bf16[48,896]{1,0:T(8,128)(2,1)} %strip.1.refs_5_.refs_0_), custom_call_target="tpu_custom_call" | custom-call | flops 1 | bytes 1 | tf_op jit(solution)/shard_map/join/pallas_call | solution.py:475
  159.5 2.7 %collective-permute-start.22 = (bf16[768,768]{1,0:T(8,128)(2,1)}, bf16[768,768]{1,0:T(8,128)(2,1)}, u32[]{:S(2)}, u32[]{:S(2)}) collective-permute-start(bf16[768,768]{1,0:T(8,128)(2,1)} %join.1.own_ref), channel_id=1, source_target_pairs={{0,1},{1,0},{2,3},{3,2},{4,5},{5,4},{6,7},{7,6},{8,9},{9,8},{10,11... | collective-permute-start | bytes 3538952 | tf_op jit(solution)/shard_map/ppermute | solution.py:107
  163.3 1.5 collective-permute-start.20
  166.0 1.6 collective-permute-start.13
  167.7 4.5 %collective-permute-done.13.refs_1_ = bf16[48,896]{1,0:T(8,128)(2,1)S(1)} collective-permute-done((bf16[48,896]{1,0:T(8,128)(2,1)S(1)}, bf16[48,896]{1,0:T(8,128)(2,1)S(1)}, u32[]{:S(2)}, u32[]{:S(2)}) %collective-permute-start.13) | collective-permute-done | bytes 86048 | tf_op jit(solution)/shard_map/ppermute | solution.py:103
  174.2 4.2 %place.4 = (f32[3072,768]{1,0:T(8,128)}, f32[768,3072]{1,0:T(8,128)}) custom-call(s32[6]{0:T(128)} %stack.27.refs_0_.at_ref, bf16[768,768]{1,0:T(8,128)(2,1)} %join.1.own_ref, bf16[768,768]{1,0:T(8,128)(2,1)} %collective-permute-done.22.other_ref), custom_call_target="tpu_custom_call" | custom-call | flops 1 | bytes 1 | tf_op jit(solution)/shard_map/place/pallas_call | solution.py:397
  179.7 11.3 %collective-permute-done.20.refs_5_.v_ref = bf16[768,768]{1,0:T(8,128)(2,1)} collective-permute-done((bf16[768,768]{1,0:T(8,128)(2,1)}, bf16[768,768]{1,0:T(8,128)(2,1)}, u32[]{:S(2)}, u32[]{:S(2)}) %collective-permute-start.20) | collective-permute-done | bytes 1179680 | tf_op jit(solution)/shard_map/ppermute | solution.py:103
  191.0 1.8 collective-permute-done.21.refs_6_.v_ref
  194.4 2.2 copies.1.refs_0_
  196.6 3.7 %all-to-all-start.4 = ((bf16[16,48,896]{2,1,0:T(8,128)(2,1)}), bf16[16,48,896]{2,1,0:T(8,128)(2,1)S(1)}, u32[]{:S(2)}, u32[]{:S(2)}) async-start(bf16[16,48,896]{2,1,0:T(8,128)(2,1)} %copies.1.refs_0_), calls=%async_computation.4 | async-start | bytes 2752512 | tf_op jit(solution)/shard_map/all_to_all | solution.py:99
  200.3 5.1 %collective-permute-start.26 = (bf16[768,768]{1,0:T(8,128)(2,1)}, bf16[768,768]{1,0:T(8,128)(2,1)}, u32[]{:S(2)}, u32[]{:S(2)}) collective-permute-start(bf16[768,768]{1,0:T(8,128)(2,1)} %tie.8.own_ref), channel_id=1, source_target_pairs={{0,1},{1,0},{2,3},{3,2},{4,5},{5,4},{6,7},{7,6},{8,9},{9,8},{10,11... | collective-permute-start | bytes 3538952 | tf_op jit(solution)/shard_map/ppermute | solution.py:107
  205.9 2.3 collective-permute-done.26.other_ref
  208.2 4.2 %place.5 = (f32[3072,768]{1,0:T(8,128)}, f32[768,3072]{1,0:T(8,128)}) custom-call(s32[6]{0:T(128)} %stack.27.refs_0_.at_ref, bf16[768,768]{1,0:T(8,128)(2,1)} %tie.8.own_ref, bf16[768,768]{1,0:T(8,128)(2,1)} %collective-permute-done.26.other_ref, f32[3072,768]{1,0:T(8,128)} %get-tuple-element.96.rest_0_, ...), custom_call_target="tpu_custom_call", output_to_operand_aliasing={{0}: (3, {}), {1}: (4, {})} | custom-call | flops 1 | bytes 1 | tf_op jit(solution)/shard_map/place/pallas_call | solution.py:397
  212.3 4.2 %place.6 = (f32[3072,768]{1,0:T(8,128)}, f32[768,3072]{1,0:T(8,128)}) custom-call(s32[6]{0:T(128)} %stack.27.refs_0_.at_ref, bf16[768,768]{1,0:T(8,128)(2,1)} %tie.7.own_ref, bf16[768,768]{1,0:T(8,128)(2,1)} %collective-permute-done.25.other_ref, f32[3072,768]{1,0:T(8,128)} %get-tuple-element.98.rest_0_, ...), custom_call_target="tpu_custom_call", output_to_operand_aliasing={{0}: (3, {}), {1}: (4, {})} | custom-call | flops 1 | bytes 1 | tf_op jit(solution)/shard_map/place/pallas_call | solution.py:397
  216.5 4.2 %place.7 = (f32[3072,768]{1,0:T(8,128)}, f32[768,3072]{1,0:T(8,128)}) custom-call(s32[6]{0:T(128)} %stack.27.refs_0_.at_ref, bf16[768,768]{1,0:T(8,128)(2,1)} %tie.6.own_ref, bf16[768,768]{1,0:T(8,128)(2,1)} %collective-permute-done.24.other_ref, f32[3072,768]{1,0:T(8,128)} %get-tuple-element.100.rest_0_, ...), custom_call_target="tpu_custom_call", output_to_operand_aliasing={{0}: (3, {}), {1}: (4, {})} | custom-call | flops 1 | bytes 1 | tf_op jit(solution)/shard_map/place/pallas_call | solution.py:397
  225.0 3.0 %collective-permute-done.28.refs_2_ = bf16[16,48,896]{2,1,0:T(8,128)(2,1)S(1)} collective-permute-done((bf16[16,48,896]{2,1,0:T(8,128)(2,1)}, bf16[16,48,896]{2,1,0:T(8,128)(2,1)S(1)}, u32[]{:S(2)}, u32[]{:S(2)}) %collective-permute-start.28) | collective-permute-done | bytes 1376288 | tf_op jit(solution)/shard_map/ppermute | solution.py:107
  229.0 4.6 %late_place.1 = (f32[768,768]{1,0:T(8,128)}, f32[768,768]{1,0:T(8,128)}, f32[768,128]{1,0:T(8,128)}, f32[64]{0:T(128)}, f32[768]{0:T(1024)}, /*index=5*/f32[768]...) custom-call(s32[6]{0:T(128)} %stack.27.refs_0_.at_ref, ...), custom_call_target="tpu_custom_call" | custom-call | flops 1 | bytes 1 | tf_op jit(solution)/shard_map/late_place/pallas_call | solution.py:475
  (140 shorter events, 34.8 us)
Async XLA Ops:
  0.6 10.9 %copy-start.29 = (s32[1,8]{1,0:T(1,128)S(1)}, s32[1,8]{1,0:T(1,128)}, u32[]{:S(2)}) copy-start(s32[1,8]{1,0:T(1,128)} %param.19) | copy-start | bytes 100
  0.7 11.1 %copy-start.27 = (s32[1,8,2]{1,2,0:T(2,128)S(1)}, s32[1,8,2]{1,2,0:T(2,128)}, u32[]{:S(2)}) copy-start(s32[1,8,2]{1,2,0:T(2,128)} %param.20) | copy-start | bytes 196
  2.9 18.9 %all-to-all-start = ((bf16[16,128,128]{2,1,0:T(8,128)(2,1)}), bf16[16,128,128]{2,1,0:T(8,128)(2,1)S(1)}, u32[]{:S(2)}, u32[]{:S(2)}) async-start(bf16[16,128,128]{2,1,0:T(8,128)(2,1)} %get-tuple-element.67), calls=%async_computation | async-start | bytes 1048576 | tf_op jit(solution)/shard_map/all_to_all | solution.py:596
  22.6 3.9 %collective-permute-start = (bf16[16,128,128]{2,1,0:T(8,128)(2,1)}, bf16[16,128,128]{2,1,0:T(8,128)(2,1)S(1)}, u32[]{:S(2)}, u32[]{:S(2)}) collective-permute-start(bf16[16,128,128]{2,1,0:T(8,128)(2,1)} %tie.5.refs_3_), channel_id=1, source_target_pairs={{0,1},{1,0},{2,3},{3,2},{4,5},{5,4},{6,7},{7,6},{8,9},{9,8},{10,11... | collective-permute-start | bytes 1572872 | tf_op jit(solution)/shard_map/ppermute | solution.py:107
  52.4 2.9 %collective-permute-start.1 = (bf16[128,3072]{1,0:T(8,128)(2,1)}, bf16[128,3072]{1,0:T(8,128)(2,1)S(1)}, u32[]{:S(2)}, u32[]{:S(2)}) collective-permute-start(bf16[128,3072]{1,0:T(8,128)(2,1)} %get-tuple-element.78), channel_id=1, source_target_pairs={{0,1},{1,0},{2,3},{3,2},{4,5},{5,4},{6,7},{7,6},{8,9},{9,8},{10,11... | collective-permute-start | bytes 2359304 | tf_op jit(solution)/shard_map/ppermute | solution.py:107
  52.8 2.4 %collective-permute-start.2 = (bf16[128,768]{1,0:T(8,128)(2,1)}, bf16[128,768]{1,0:T(8,128)(2,1)S(1)}, u32[]{:S(2)}, u32[]{:S(2)}) collective-permute-start(bf16[128,768]{1,0:T(8,128)(2,1)} %get-tuple-element.79), channel_id=1, source_target_pairs={{0,1},{1,0},{2,3},{3,2},{4,5},{5,4},{6,7},{7,6},{8,9},{9,8},{10,11... | collective-permute-start | bytes 589832 | tf_op jit(solution)/shard_map/ppermute | solution.py:107
  59.5 24.9 %all-to-all-start.1 = ((bf16[4,256,1536]{2,1,0:T(8,128)(2,1)}), bf16[4,256,1536]{2,1,0:T(8,128)(2,1)S(1)}, u32[]{:S(2)}, u32[]{:S(2)}) async-start(bf16[4,256,1536]{2,1,0:T(8,128)(2,1)} %pack.1.refs_11_), calls=%async_computation.1 | async-start | bytes 6291456 | tf_op jit(solution)/shard_map/all_to_all | solution.py:632
  80.8 6.0 %collective-permute-start.3 = (bf16[16,128,128]{2,1,0:T(8,128)(2,1)}, bf16[16,128,128]{2,1,0:T(8,128)(2,1)}, u32[]{:S(2)}, u32[]{:S(2)}) collective-permute-start(bf16[16,128,128]{2,1,0:T(8,128)(2,1)} %get-tuple-element.84), channel_id=1, source_target_pairs={{0,1},{1,0},{2,3},{3,2},{4,5},{5,4},{6,7},{7,6},{8,9},{9,8},{10,11... | collective-permute-start | bytes 1572872 | tf_op jit(solution)/shard_map/ppermute | solution.py:107
  88.8 23.5 %all-to-all-start.2 = ((bf16[16,128,128]{2,1,0:T(8,128)(2,1)}), bf16[16,128,128]{2,1,0:T(8,128)(2,1)S(1)}, u32[]{:S(2)}, u32[]{:S(2)}) async-start(bf16[16,128,128]{2,1,0:T(8,128)(2,1)} %share.1), calls=%async_computation.2 | async-start | bytes 1048576 | tf_op jit(solution)/shard_map/all_to_all | solution.py:636
  92.4 14.5 %copy-start.30 = (bf16[128,768]{1,0:T(8,128)(2,1)S(1)}, bf16[128,768]{1,0:T(8,128)(2,1)}, u32[]{:S(2)}) copy-start(bf16[128,768]{1,0:T(8,128)(2,1)} %get-tuple-element.87) | copy-start | bytes 589828
  92.4 14.5 %copy-start.31 = (bf16[128,768]{1,0:T(8,128)(2,1)S(1)}, bf16[128,768]{1,0:T(8,128)(2,1)}, u32[]{:S(2)}) copy-start(bf16[128,768]{1,0:T(8,128)(2,1)} %get-tuple-element.89) | copy-start | bytes 589828
  97.8 18.9 %collective-permute-start.7 = (bf16[192,768]{1,0:T(8,128)(2,1)}, bf16[192,768]{1,0:T(8,128)(2,1)S(1)}, u32[]{:S(2)}, u32[]{:S(2)}) collective-permute-start(bf16[192,768]{1,0:T(8,128)(2,1)} %get-tuple-element.93), channel_id=1, source_target_pairs={{0,8},{1,33},{2,10},{3,35},{4,12},{5,37},{6,14},{7,39},{8,16},{9,4... | collective-permute-start | bytes 884744 | tf_op jit(solution)/shard_map/ppermute | solution.py:103
  104.5 12.2 %collective-permute-start.8 = (bf16[192,768]{1,0:T(8,128)(2,1)}, bf16[192,768]{1,0:T(8,128)(2,1)S(1)}, u32[]{:S(2)}, u32[]{:S(2)}) collective-permute-start(bf16[192,768]{1,0:T(8,128)(2,1)} %get-tuple-element.94), channel_id=1, source_target_pairs={{0,24},{1,97},{2,26},{3,99},{4,28},{5,101},{6,30},{7,103},{8,0},{9... | collective-permute-start | bytes 884744 | tf_op jit(solution)/shard_map/ppermute | solution.py:103
  105.7 11.0 %collective-permute-start.9 = (bf16[192,768]{1,0:T(8,128)(2,1)}, bf16[192,768]{1,0:T(8,128)(2,1)S(1)}, u32[]{:S(2)}, u32[]{:S(2)}) collective-permute-start(bf16[192,768]{1,0:T(8,128)(2,1)} %get-tuple-element.95), channel_id=1, source_target_pairs={{0,16},{1,65},{2,18},{3,67},{4,20},{5,69},{6,22},{7,71},{8,24},{9,... | collective-permute-start | bytes 884744 | tf_op jit(solution)/shard_map/ppermute | solution.py:103
  106.9 1.4 collective-permute-start.4
  106.9 1.7 collective-permute-start.5
  116.4 1.5 collective-permute-start.6
  121.3 28.2 %all-to-all-start.3 = ((bf16[16,48,896]{2,1,0:T(8,128)(2,1)}), bf16[16,48,896]{2,1,0:T(8,128)(2,1)S(1)}, u32[]{:S(2)}, u32[]{:S(2)}) async-start(bf16[16,48,896]{2,1,0:T(8,128)(2,1)} %late.1.refs_4_), calls=%async_computation.3 | async-start | bytes 2752512 | tf_op jit(solution)/shard_map/all_to_all | solution.py:99
  129.8 13.8 %collective-permute-start.10 = (bf16[192,768]{1,0:T(8,128)(2,1)}, bf16[192,768]{1,0:T(8,128)(2,1)S(1)}, u32[]{:S(2)}, u32[]{:S(2)}) collective-permute-start(bf16[192,768]{1,0:T(8,128)(2,1)} %part.1), channel_id=1, source_target_pairs={{0,32},{1,3},{2,34},{3,5},{4,36},{5,7},{6,38},{7,1},{8,40},{9,11},... | collective-permute-start | bytes 884744 | tf_op jit(solution)/shard_map/ppermute | solution.py:103
  131.5 12.2 %collective-permute-start.11 = (bf16[192,768]{1,0:T(8,128)(2,1)}, bf16[192,768]{1,0:T(8,128)(2,1)S(1)}, u32[]{:S(2)}, u32[]{:S(2)}) collective-permute-start(bf16[192,768]{1,0:T(8,128)(2,1)} %part.1), channel_id=1, source_target_pairs={{0,96},{1,7},{2,98},{3,1},{4,100},{5,3},{6,102},{7,5},{8,104},{9,1... | collective-permute-start | bytes 884744 | tf_op jit(solution)/shard_map/ppermute | solution.py:103
  132.7 10.9 %collective-permute-start.12 = (bf16[192,768]{1,0:T(8,128)(2,1)}, bf16[192,768]{1,0:T(8,128)(2,1)S(1)}, u32[]{:S(2)}, u32[]{:S(2)}) collective-permute-start(bf16[192,768]{1,0:T(8,128)(2,1)} %part.1), channel_id=1, source_target_pairs={{0,64},{1,5},{2,66},{3,7},{4,68},{5,1},{6,70},{7,3},{8,72},{9,13},... | collective-permute-start | bytes 884744 | tf_op jit(solution)/shard_map/ppermute | solution.py:103
  143.6 5.9 %copy-start.10 = (bf16[192,768]{1,0:T(8,128)(2,1)}, bf16[192,768]{1,0:T(8,128)(2,1)S(1)}, u32[]{:S(2)}) copy-start(bf16[192,768]{1,0:T(8,128)(2,1)S(1)} %collective-permute-done.10.refs_1_) | copy-start | bytes 884740
  143.6 5.9 %copy-start.11 = (bf16[192,768]{1,0:T(8,128)(2,1)}, bf16[192,768]{1,0:T(8,128)(2,1)S(1)}, u32[]{:S(2)}) copy-start(bf16[192,768]{1,0:T(8,128)(2,1)S(1)} %collective-permute-done.11.refs_2_) | copy-start | bytes 884740
  143.6 5.9 %copy-start.12 = (bf16[192,768]{1,0:T(8,128)(2,1)}, bf16[192,768]{1,0:T(8,128)(2,1)S(1)}, u32[]{:S(2)}) copy-start(bf16[192,768]{1,0:T(8,128)(2,1)S(1)} %collective-permute-done.12.refs_3_) | copy-start | bytes 884740
  145.0 12.2 %copy-start.13 = (bf16[192,768]{1,0:T(8,128)(2,1)}, bf16[192,768]{1,0:T(8,128)(2,1)S(1)}, u32[]{:S(2)}) copy-start(bf16[192,768]{1,0:T(8,128)(2,1)S(1)} %add_convert_fusion.refs_1_) | copy-start | bytes 884740
  145.0 7.7 %collective-permute-start.16 = (bf16[192,768]{1,0:T(8,128)(2,1)S(1)}, bf16[192,768]{1,0:T(8,128)(2,1)S(1)}, u32[]{:S(2)}, u32[]{:S(2)}) collective-permute-start(bf16[192,768]{1,0:T(8,128)(2,1)S(1)} %add_convert_fusion.refs_1_), channel_id=1, source_target_pairs={{0,8},{1,33},{2,10},{3,35},{4,12},{5,37},{6,14},{7,39},{8,16},{9,4... | collective-permute-start | bytes 884744 | tf_op jit(solution)/shard_map/ppermute | solution.py:103
  146.7 8.5 %collective-permute-start.17 = (bf16[192,768]{1,0:T(8,128)(2,1)S(1)}, bf16[192,768]{1,0:T(8,128)(2,1)S(1)}, u32[]{:S(2)}, u32[]{:S(2)}) collective-permute-start(bf16[192,768]{1,0:T(8,128)(2,1)S(1)} %add_convert_fusion.refs_1_), channel_id=1, source_target_pairs={{0,24},{1,97},{2,26},{3,99},{4,28},{5,101},{6,30},{7,103},{8,0},{9... | collective-permute-start | bytes 884744 | tf_op jit(solution)/shard_map/ppermute | solution.py:103
  148.4 8.8 %collective-permute-start.18 = (bf16[192,768]{1,0:T(8,128)(2,1)S(1)}, bf16[192,768]{1,0:T(8,128)(2,1)}, u32[]{:S(2)}, u32[]{:S(2)}) collective-permute-start(bf16[192,768]{1,0:T(8,128)(2,1)S(1)} %add_convert_fusion.refs_1_), channel_id=1, source_target_pairs={{0,16},{1,65},{2,18},{3,67},{4,20},{5,69},{6,22},{7,71},{8,24},{9,... | collective-permute-start | bytes 884744 | tf_op jit(solution)/shard_map/ppermute | solution.py:103
  152.7 13.3 %copy-start.16 = (bf16[48,896]{1,0:T(8,128)(2,1)S(1)}, bf16[48,896]{1,0:T(8,128)(2,1)}, u32[]{:S(2)}) copy-start(bf16[48,896]{1,0:T(8,128)(2,1)} %strip.1.refs_5_.refs_0_) | copy-start | bytes 258052
  152.7 4.4 %copy-start.18 = (bf16[192,768]{1,0:T(8,128)(2,1)}, bf16[192,768]{1,0:T(8,128)(2,1)S(1)}, u32[]{:S(2)}) copy-start(bf16[192,768]{1,0:T(8,128)(2,1)S(1)} %collective-permute-done.16.refs_2_) | copy-start | bytes 884740
  155.2 1.9 copy-start.19
  159.5 14.1 %collective-permute-start.22 = (bf16[768,768]{1,0:T(8,128)(2,1)}, bf16[768,768]{1,0:T(8,128)(2,1)}, u32[]{:S(2)}, u32[]{:S(2)}) collective-permute-start(bf16[768,768]{1,0:T(8,128)(2,1)} %join.1.own_ref), channel_id=1, source_target_pairs={{0,1},{1,0},{2,3},{3,2},{4,5},{5,4},{6,7},{7,6},{8,9},{9,8},{10,11... | collective-permute-start | bytes 3538952 | tf_op jit(solution)/shard_map/ppermute | solution.py:107
  162.2 17.5 %collective-permute-start.19 = (bf16[768,768]{1,0:T(8,128)(2,1)}, bf16[768,768]{1,0:T(8,128)(2,1)}, u32[]{:S(2)}, u32[]{:S(2)}) collective-permute-start(bf16[768,768]{1,0:T(8,128)(2,1)} %join.1.own_ref), channel_id=1, source_target_pairs={{0,2},{1,9},{2,4},{3,11},{4,6},{5,13},{6,0},{7,15},{8,10},{9,17},{... | collective-permute-start | bytes 3538952 | tf_op jit(solution)/shard_map/ppermute | solution.py:103
  163.3 27.7 %collective-permute-start.20 = (bf16[768,768]{1,0:T(8,128)(2,1)}, bf16[768,768]{1,0:T(8,128)(2,1)}, u32[]{:S(2)}, u32[]{:S(2)}) collective-permute-start(bf16[768,768]{1,0:T(8,128)(2,1)} %join.1.own_ref), channel_id=1, source_target_pairs={{0,6},{1,25},{2,0},{3,27},{4,2},{5,29},{6,4},{7,31},{8,14},{9,1},{... | collective-permute-start | bytes 3538952 | tf_op jit(solution)/shard_map/ppermute | solution.py:103
  164.9 27.9 %collective-permute-start.21 = (bf16[768,768]{1,0:T(8,128)(2,1)}, bf16[768,768]{1,0:T(8,128)(2,1)S(1)}, u32[]{:S(2)}, u32[]{:S(2)}) collective-permute-start(bf16[768,768]{1,0:T(8,128)(2,1)} %join.1.own_ref), channel_id=1, source_target_pairs={{0,4},{1,17},{2,6},{3,19},{4,0},{5,21},{6,2},{7,23},{8,12},{9,25},... | collective-permute-start | bytes 3538952 | tf_op jit(solution)/shard_map/ppermute | solution.py:103
  166.0 6.1 %collective-permute-start.13 = (bf16[48,896]{1,0:T(8,128)(2,1)S(1)}, bf16[48,896]{1,0:T(8,128)(2,1)S(1)}, u32[]{:S(2)}, u32[]{:S(2)}) collective-permute-start(bf16[48,896]{1,0:T(8,128)(2,1)S(1)} %copy-done.16), channel_id=1, source_target_pairs={{0,32},{1,3},{2,34},{3,5},{4,36},{5,7},{6,38},{7,1},{8,40},{9,11},... | collective-permute-start | bytes 258056 | tf_op jit(solution)/shard_map/ppermute | solution.py:103
  172.1 20.6 %copy-start.22 = (bf16[48,896]{1,0:T(8,128)(2,1)}, bf16[48,896]{1,0:T(8,128)(2,1)S(1)}, u32[]{:S(2)}) copy-start(bf16[48,896]{1,0:T(8,128)(2,1)S(1)} %collective-permute-done.13.refs_1_) | copy-start | bytes 258052
  172.1 6.9 %collective-permute-start.14 = (bf16[48,896]{1,0:T(8,128)(2,1)S(1)}, bf16[48,896]{1,0:T(8,128)(2,1)S(1)}, u32[]{:S(2)}, u32[]{:S(2)}) collective-permute-start(bf16[48,896]{1,0:T(8,128)(2,1)S(1)} %copy-done.16), channel_id=1, source_target_pairs={{0,96},{1,7},{2,98},{3,1},{4,100},{5,3},{6,102},{7,5},{8,104},{9,1... | collective-permute-start | bytes 258056 | tf_op jit(solution)/shard_map/ppermute | solution.py:103
  173.6 6.1 %collective-permute-start.15 = (bf16[48,896]{1,0:T(8,128)(2,1)S(1)}, bf16[48,896]{1,0:T(8,128)(2,1)S(1)}, u32[]{:S(2)}, u32[]{:S(2)}) collective-permute-start(bf16[48,896]{1,0:T(8,128)(2,1)S(1)} %copy-done.16), channel_id=1, source_target_pairs={{0,64},{1,5},{2,66},{3,7},{4,68},{5,1},{6,70},{7,3},{8,72},{9,13},... | collective-permute-start | bytes 258056 | tf_op jit(solution)/shard_map/ppermute | solution.py:103
  179.1 13.7 %copy-start.23 = (bf16[48,896]{1,0:T(8,128)(2,1)}, bf16[48,896]{1,0:T(8,128)(2,1)S(1)}, u32[]{:S(2)}) copy-start(bf16[48,896]{1,0:T(8,128)(2,1)S(1)} %collective-permute-done.14.refs_2_) | copy-start | bytes 258052
  179.1 13.7 %collective-permute-start.23 = (f32[8,128]{1,0:T(8,128)S(1)}, f32[8,128]{1,0:T(8,128)S(1)}, u32[]{:S(2)}, u32[]{:S(2)}) collective-permute-start(f32[8,128]{1,0:T(8,128)S(1)} %slice.20), channel_id=1, source_target_pairs={{0,1},{1,0},{2,3},{3,2},{4,5},{5,4},{6,7},{7,6},{8,9},{9,8},{10,11... | collective-permute-start | bytes 12296 | tf_op jit(solution)/shard_map/ppermute | solution.py:107
  179.7 13.1 %copy-start.24 = (bf16[48,896]{1,0:T(8,128)(2,1)}, bf16[48,896]{1,0:T(8,128)(2,1)S(1)}, u32[]{:S(2)}) copy-start(bf16[48,896]{1,0:T(8,128)(2,1)S(1)} %collective-permute-done.15.refs_3_) | copy-start | bytes 258052
  196.6 26.1 %all-to-all-start.4 = ((bf16[16,48,896]{2,1,0:T(8,128)(2,1)}), bf16[16,48,896]{2,1,0:T(8,128)(2,1)S(1)}, u32[]{:S(2)}, u32[]{:S(2)}) async-start(bf16[16,48,896]{2,1,0:T(8,128)(2,1)} %copies.1.refs_0_), calls=%async_computation.4 | async-start | bytes 2752512 | tf_op jit(solution)/shard_map/all_to_all | solution.py:99
  200.3 7.9 %collective-permute-start.26 = (bf16[768,768]{1,0:T(8,128)(2,1)}, bf16[768,768]{1,0:T(8,128)(2,1)}, u32[]{:S(2)}, u32[]{:S(2)}) collective-permute-start(bf16[768,768]{1,0:T(8,128)(2,1)} %tie.8.own_ref), channel_id=1, source_target_pairs={{0,1},{1,0},{2,3},{3,2},{4,5},{5,4},{6,7},{7,6},{8,9},{9,8},{10,11... | collective-permute-start | bytes 3538952 | tf_op jit(solution)/shard_map/ppermute | solution.py:107
  205.3 7.0 %collective-permute-start.25 = (bf16[768,768]{1,0:T(8,128)(2,1)}, bf16[768,768]{1,0:T(8,128)(2,1)}, u32[]{:S(2)}, u32[]{:S(2)}) collective-permute-start(bf16[768,768]{1,0:T(8,128)(2,1)} %tie.7.own_ref), channel_id=1, source_target_pairs={{0,1},{1,0},{2,3},{3,2},{4,5},{5,4},{6,7},{7,6},{8,9},{9,8},{10,11... | collective-permute-start | bytes 3538952 | tf_op jit(solution)/shard_map/ppermute | solution.py:107
  205.4 11.1 %collective-permute-start.24 = (bf16[768,768]{1,0:T(8,128)(2,1)}, bf16[768,768]{1,0:T(8,128)(2,1)}, u32[]{:S(2)}, u32[]{:S(2)}) collective-permute-start(bf16[768,768]{1,0:T(8,128)(2,1)} %tie.6.own_ref), channel_id=1, source_target_pairs={{0,1},{1,0},{2,3},{3,2},{4,5},{5,4},{6,7},{7,6},{8,9},{9,8},{10,11... | collective-permute-start | bytes 3538952 | tf_op jit(solution)/shard_map/ppermute | solution.py:107
  221.4 1.2 collective-permute-start.27
  224.3 3.6 %collective-permute-start.28 = (bf16[16,48,896]{2,1,0:T(8,128)(2,1)}, bf16[16,48,896]{2,1,0:T(8,128)(2,1)S(1)}, u32[]{:S(2)}, u32[]{:S(2)}) collective-permute-start(bf16[16,48,896]{2,1,0:T(8,128)(2,1)} %tie.9.refs_1_), channel_id=1, source_target_pairs={{0,1},{1,0},{2,3},{3,2},{4,5},{5,4},{6,7},{7,6},{8,9},{9,8},{10,11... | collective-permute-start | bytes 4128776 | tf_op jit(solution)/shard_map/ppermute | solution.py:107
  (18 other events, 16.8 us)

commit v9 on v8

--- a/solution.py
+++ b/solution.py
@@ -666,13 +666,14 @@
     kept = place(at, 0, u, swap(u), ())
     mark = corner(kept[0])
     copies = call(copies_kernel, gather4(strip, 3), shapes(((CHIPS, STRIP, D + 128), bf16))[0], name="copies",
-                  after=(before, after, far, mark))
+                  after=(mark,))
     late = in_plane(copies)
-    before, after, far = (tie(v, copies) for v in (before, after, far))
+    far = tie(far, copies)
+    before, after = tie(before, far), tie(after, far)
     kept = place(at, 3, before, swap(before), kept)
     kept = place(at, 1, after, swap(after), kept)
     g_down, g_up = place(at, 2, far, swap(far), kept)
-    late = tie(late, corner(g_down))
+    late = tie(late, corner(kept[0]))
     one = lambda n: ((n,), f32)
     outs = call(
         late_place_kernel, (at, late, swap(late)),

time: 235 us -> 236 us (level)
  Pallas kernels: 97 us -> 101 us
  waiting for transfers between devices: 48.7 us -> 46.3 us
    pallas_call x14, Pallas kernels: 64.3 us -> 68 us  [call(): pl.pallas_call(run, out_shape=outs, in_specs=[SMEM if v.dtype == jnp.int3...]
    ppermute x15, waiting for transfers between devices: 31.1 us -> 27.8 us  [send(): return lax.ppermute(v, AXES, ring(place, shift))]
    ppermute x14, waiting for transfers between devices: 11.9 us -> 14.8 us  [swap(): return lax.ppermute(v, 'c', [(0, 1), (1, 0)])]
    unnamed x64 -> x68, local copies, waits for them, and re-layouts: 11.8 us -> 12.7 us
  transfers between devices with their start and end apart: 34 -> 34, of which waited for: 16 -> 15; matrix products, arithmetic and copies ran while one was open for 4% -> 4% of each run, Pallas kernels for 22% -> 24%
where the time goes in v9:
time: 236 us; the launch traced here: 235 us
  Pallas kernels  101 us (43%)
  starting transfers between devices  64.3 us (27%)
  waiting for transfers between devices  46.3 us (20%)
  local copies, waits for them, and re-layouts  19.8 us (8%)
  other arithmetic  2.37 us (1%)
    pallas_call x14, Pallas kernels, call(): pl.pallas_call(run, out_shape=outs, in_specs=[SMEM if v.dtype == jnp.int3...  68 us
    ppermute x15, waiting for transfers between devices, send(): return lax.ppermute(v, AXES, ring(place, shift))  27.8 us
    ppermute x15, starting transfers between devices, send(): return lax.ppermute(v, AXES, ring(place, shift))  25.1 us
    pallas_call x4, Pallas kernels, place(): pl.pallas_call(place_kernel, grid_spec=pltpu.PrefetchScalarGridSpec(num_s...  16.8 us
    ppermute x14, waiting for transfers between devices, swap(): return lax.ppermute(v, 'c', [(0, 1), (1, 0)])  14.8 us
    unnamed x68, local copies, waits for them, and re-layouts  12.7 us
    ppermute x14, starting transfers between devices, swap(): return lax.ppermute(v, 'c', [(0, 1), (1, 0)])  12 us
    all_to_all x2, starting transfers between devices, in_plane(): return lax.all_to_all(v, AXES, 0, 0, axis_index_groups=planes, tiled=True)  11.1 us
  transfers between devices with their start and end apart: 34, of which 15 were waited for; matrix products, arithmetic and copies ran while one was open for 4% of the time, Pallas kernels for 24%

profile of v9, /device:TPU:1, one launch (start us, length us, event | category | flops | bytes accessed | tf_op | source)
XLA Modules:
  0.0 234.6 jit_solution(9625364711846721756)
XLA Ops:
  0.7 2.2 enter.1
  2.9 8.6 %all-to-all-start = ((bf16[16,128,128]{2,1,0:T(8,128)(2,1)}), bf16[16,128,128]{2,1,0:T(8,128)(2,1)S(1)}, u32[]{:S(2)}, u32[]{:S(2)}) async-start(bf16[16,128,128]{2,1,0:T(8,128)(2,1)} %get-tuple-element.67), calls=%async_computation | async-start | bytes 1048576 | tf_op jit(solution)/shard_map/all_to_all | solution.py:596
  14.9 2.2 broadcast_in_dim.28.refs_3_.refs_5_.refs_7_
  17.1 2.3 query.1.refs_0_.refs_2_
  19.4 2.4 %all-to-all-done.v_ref = bf16[16,128,128]{2,1,0:T(8,128)(2,1)S(1)} async-done(((bf16[16,128,128]{2,1,0:T(8,128)(2,1)}), bf16[16,128,128]{2,1,0:T(8,128)(2,1)S(1)}, u32[]{:S(2)}, u32[]{:S(2)}) %all-to-all-start) | async-done | bytes 524320 | tf_op jit(solution)/shard_map/all_to_all | solution.py:596
  22.6 2.1 collective-permute-start
  27.3 16.2 %attend.1 = (bf16[128,768]{1,0:T(8,128)(2,1)}, bf16[128,768]{1,0:T(8,128)(2,1)}, bf16[128,768]{1,0:T(8,128)(2,1)}, bf16[2,768,128]{2,1,0:T(8,128)(2,1)}, f32[2,7...) custom-call(s32[6]{0:T(128)} %stack.27.refs_0_.at_ref, s32[8]{0:T(128)} %select_n.94.refs_6_.refs_1_, ...), custom_call_target="tpu_custom_call" | custom-call | flops 1 | bytes 1 | tf_op jit(solution)/shard_map/attend/pallas_call | solution.py:475
  43.5 10.5 %middle.1 = (bf16[128,768]{1,0:T(8,128)(2,1)}, bf16[128,3072]{1,0:T(8,128)(2,1)}, bf16[128,3072]{1,0:T(8,128)(2,1)}, bf16[128,768]{1,0:T(8,128)(2,1)}, bf16[128,...) custom-call(s32[6]{0:T(128)} %stack.27.refs_0_.at_ref, ...), custom_call_target="tpu_custom_call" | custom-call | flops 1 | bytes 1 | tf_op jit(solution)/shard_map/middle/pallas_call | solution.py:612
  54.7 2.3 collective-permute-done.2.refs_3_
  57.9 3.4 %pack.1.refs_11_ = bf16[4,256,1536]{2,1,0:T(8,128)(2,1)} custom-call(bf16[128,3072]{1,0:T(8,128)(2,1)} %get-tuple-element.76.refs_0_, bf16[128,768]{1,0:T(8,128)(2,1)} %get-tuple-element.77.refs_1_, bf16[128,3072]{1,0:T(8,128)(2,1)} %copy-done.16, bf16[128,768]{1,0:T(8,128)(2,1)} %copy-done.22), custom_call_target="tpu_custom_call" | custom-call | flops 1 | bytes 1 | tf_op jit(solution)/shard_map/pack/pallas_call | solution.py:475
  61.3 3.9 %all-to-all-start.1 = ((bf16[4,256,1536]{2,1,0:T(8,128)(2,1)}), bf16[4,256,1536]{2,1,0:T(8,128)(2,1)S(1)}, u32[]{:S(2)}, u32[]{:S(2)}) async-start(bf16[4,256,1536]{2,1,0:T(8,128)(2,1)} %pack.1.refs_11_), calls=%async_computation.1 | async-start | bytes 6291456 | tf_op jit(solution)/shard_map/all_to_all | solution.py:632
  65.1 19.4 %attend_back.1 = (bf16[128,768]{1,0:T(8,128)(2,1)}, bf16[128,768]{1,0:T(8,128)(2,1)}, bf16[128,768]{1,0:T(8,128)(2,1)}, bf16[16,128,128]{2,1,0:T(8,128)(2,1)}, bf16[16,128,128]{2,1,0:T(8,128)(2,1)}) custom-call(s32[6]{0:T(128)} %stack.27.refs_0_.at_ref, s32[8]{0:T(128)} %select_n.94.refs_6_.refs_1_, bf16[2,768,128]{2,1,0:T(8,128)(2,1)} %get-tuple-element.70.refs_2_, ...), custom_call_target="tpu_custom_call" | custom-call | flops 1 | bytes 1 | tf_op jit(solution)/shard_map/attend_back/pallas_call | solution.py:475
  84.9 1.3 all-to-all-done.1.slab_ref
  86.2 1.7 copy-done.2
  88.4 2.1 share.1
  90.6 3.6 %all-to-all-start.2 = ((bf16[16,128,128]{2,1,0:T(8,128)(2,1)}), bf16[16,128,128]{2,1,0:T(8,128)(2,1)S(1)}, u32[]{:S(2)}, u32[]{:S(2)}) async-start(bf16[16,128,128]{2,1,0:T(8,128)(2,1)} %share.1), calls=%async_computation.2 | async-start | bytes 1048576 | tf_op jit(solution)/shard_map/all_to_all | solution.py:636
  94.2 5.4 %weights.1 = (bf16[192,768]{1,0:T(8,128)(2,1)}, bf16[192,768]{1,0:T(8,128)(2,1)}, bf16[192,768]{1,0:T(8,128)(2,1)}, bf16[192,768]{1,0:T(8,128)(2,1)}) custom-call(s32[6]{0:T(128)} %stack.27.refs_0_.at_ref, bf16[4,256,1536]{2,1,0:T(8,128)(2,1)} %copy-done.2), custom_call_target="tpu_custom_call" | custom-call | flops 1 | bytes 1 | tf_op jit(solution)/shard_map/weights/pallas_call | solution.py:638
  99.6 4.9 %collective-permute-start.7 = (bf16[192,768]{1,0:T(8,128)(2,1)}, bf16[192,768]{1,0:T(8,128)(2,1)S(1)}, u32[]{:S(2)}, u32[]{:S(2)}) collective-permute-start(bf16[192,768]{1,0:T(8,128)(2,1)} %get-tuple-element.93), channel_id=1, source_target_pairs={{0,8},{1,33},{2,10},{3,35},{4,12},{5,37},{6,14},{7,39},{8,16},{9,4... | collective-permute-start | bytes 884744 | tf_op jit(solution)/shard_map/ppermute | solution.py:103
  109.3 3.0 %square.1.refs_10_.refs_5_ = bf16[768,768]{1,0:T(8,128)(2,1)} custom-call(bf16[128,768]{1,0:T(8,128)(2,1)} %get-tuple-element.86.refs_0_.refs_1_, bf16[128,768]{1,0:T(8,128)(2,1)} %copy-done.17, bf16[128,768]{1,0:T(8,128)(2,1)} %get-tuple-element.88.refs_2_, bf16[128,768]{1,0:T(8,128)(2,1)} %copy-done.23), custom_call_target="tpu_custom_call" | custom-call | flops 1 | bytes 1 | tf_op jit(solution)/shard_map/square/pallas_call | solution.py:475
  113.2 3.3 %leave.1 = (f32[768,128]{1,0:T(8,128)}, f32[128,128]{1,0:T(8,128)}, f32[128,128]{1,0:T(8,128)}, f32[128,128]{1,0:T(8,128)}) custom-call(s32[6]{0:T(128)} %stack.27.refs_0_.at_ref, bf16[128,768]{1,0:T(8,128)(2,1)} %bitcast.61, bf16[768]{0:T(1024)(128)(2,1)} %refs_2_.5, bf16[768,768]{1,0:T(8,128)(2,1)} %refs_3_.3, bf16[768,128]{1,0:T(8,128)(2,1)} %refs_4_.3, ...), custom_call_target="tpu_custom_call" | custom-call | flops 1 | bytes 1 | tf_op jit(solution)/shard_map/leave/pallas_call | solution.py:475
  118.5 2.8 %late.1.refs_4_ = bf16[16,48,896]{2,1,0:T(8,128)(2,1)} custom-call(s32[6]{0:T(128)} %stack.27.refs_0_.at_ref, bf16[128,768]{1,0:T(8,128)(2,1)} %get-tuple-element.86.refs_0_.refs_1_, bf16[128,768]{1,0:T(8,128)(2,1)} %copy-done.17, f32[128,128]{1,0:T(8,128)} %get-tuple-element.91.refs_3_, f32[128,128]{1,0:T(8,128)} %copy-done.27, ...), custom_call_target="tpu_custom_call" | custom-call | flops 1 | bytes 1 | tf_op jit(solution)/shard_map/late/pallas_call | solution.py:475
  121.3 6.4 %all-to-all-start.3 = ((bf16[16,48,896]{2,1,0:T(8,128)(2,1)}), bf16[16,48,896]{2,1,0:T(8,128)(2,1)S(1)}, u32[]{:S(2)}, u32[]{:S(2)}) async-start(bf16[16,48,896]{2,1,0:T(8,128)(2,1)} %late.1.refs_4_), calls=%async_computation.3 | async-start | bytes 2752512 | tf_op jit(solution)/shard_map/all_to_all | solution.py:99
  127.7 2.1 part.1
  129.8 1.6 collective-permute-start.10
  132.7 1.8 collective-permute-start.12
  134.4 9.2 %collective-permute-done.10.refs_1_ = bf16[192,768]{1,0:T(8,128)(2,1)S(1)} collective-permute-done((bf16[192,768]{1,0:T(8,128)(2,1)}, bf16[192,768]{1,0:T(8,128)(2,1)S(1)}, u32[]{:S(2)}, u32[]{:S(2)}) %collective-permute-start.10) | collective-permute-done | bytes 294944 | tf_op jit(solution)/shard_map/ppermute | solution.py:103
  143.6 1.3 add_convert_fusion.refs_1_
  145.0 1.8 collective-permute-start.16
  146.8 1.6 collective-permute-start.17
  150.6 2.1 strip.1.refs_5_.refs_0_
  152.7 2.5 %collective-permute-done.17.refs_3_ = bf16[192,768]{1,0:T(8,128)(2,1)S(1)} collective-permute-done((bf16[192,768]{1,0:T(8,128)(2,1)S(1)}, bf16[192,768]{1,0:T(8,128)(2,1)S(1)}, u32[]{:S(2)}, u32[]{:S(2)}) %collective-permute-start.17) | collective-permute-done | bytes 294944 | tf_op jit(solution)/shard_map/ppermute | solution.py:103
  155.2 1.9 collective-permute-done.18.refs_4_
  157.1 2.3 join.1.own_ref
  159.5 2.7 %collective-permute-start.19 = (bf16[768,768]{1,0:T(8,128)(2,1)}, bf16[768,768]{1,0:T(8,128)(2,1)}, u32[]{:S(2)}, u32[]{:S(2)}) collective-permute-start(bf16[768,768]{1,0:T(8,128)(2,1)} %join.1.own_ref), channel_id=1, source_target_pairs={{0,1},{1,0},{2,3},{3,2},{4,5},{5,4},{6,7},{7,6},{8,9},{9,8},{10,11... | collective-permute-start | bytes 3538952 | tf_op jit(solution)/shard_map/ppermute | solution.py:107
  162.1 1.6 collective-permute-start.22
  163.8 1.6 collective-permute-start.24
  167.4 14.2 %collective-permute-done.13.refs_1_ = bf16[48,896]{1,0:T(8,128)(2,1)S(1)} collective-permute-done((bf16[48,896]{1,0:T(8,128)(2,1)S(1)}, bf16[48,896]{1,0:T(8,128)(2,1)S(1)}, u32[]{:S(2)}, u32[]{:S(2)}) %collective-permute-start.13) | collective-permute-done | bytes 86048 | tf_op jit(solution)/shard_map/ppermute | solution.py:103
  181.6 3.4 %collective-permute-start.15 = (bf16[48,896]{1,0:T(8,128)(2,1)S(1)}, bf16[48,896]{1,0:T(8,128)(2,1)S(1)}, u32[]{:S(2)}, u32[]{:S(2)}) collective-permute-start(bf16[48,896]{1,0:T(8,128)(2,1)S(1)} %copy-done.18), channel_id=1, source_target_pairs={{0,64},{1,5},{2,66},{3,7},{4,68},{5,1},{6,70},{7,3},{8,72},{9,13},... | collective-permute-start | bytes 258056 | tf_op jit(solution)/shard_map/ppermute | solution.py:103
  185.0 4.2 %place.4 = (f32[3072,768]{1,0:T(8,128)}, f32[768,3072]{1,0:T(8,128)}) custom-call(s32[6]{0:T(128)} %stack.27.refs_0_.at_ref, bf16[768,768]{1,0:T(8,128)(2,1)} %join.1.own_ref, bf16[768,768]{1,0:T(8,128)(2,1)} %collective-permute-done.19.other_ref), custom_call_target="tpu_custom_call" | custom-call | flops 1 | bytes 1 | tf_op jit(solution)/shard_map/place/pallas_call | solution.py:397
  191.7 2.2 copies.1.refs_0_
  193.9 4.7 %all-to-all-start.4 = ((bf16[16,48,896]{2,1,0:T(8,128)(2,1)}), bf16[16,48,896]{2,1,0:T(8,128)(2,1)}, u32[]{:S(2)}, u32[]{:S(2)}) async-start(bf16[16,48,896]{2,1,0:T(8,128)(2,1)} %copies.1.refs_0_), calls=%async_computation.4 | async-start | bytes 2752512 | tf_op jit(solution)/shard_map/all_to_all | solution.py:99
  200.1 2.5 %collective-permute-done.25.other_ref = bf16[768,768]{1,0:T(8,128)(2,1)S(1)} collective-permute-done((bf16[768,768]{1,0:T(8,128)(2,1)}, bf16[768,768]{1,0:T(8,128)(2,1)S(1)}, u32[]{:S(2)}, u32[]{:S(2)}) %collective-permute-start.25) | collective-permute-done | bytes 1179680 | tf_op jit(solution)/shard_map/ppermute | solution.py:107
  203.7 4.2 %place.5 = (f32[3072,768]{1,0:T(8,128)}, f32[768,3072]{1,0:T(8,128)}) custom-call(s32[6]{0:T(128)} %stack.27.refs_0_.at_ref, bf16[768,768]{1,0:T(8,128)(2,1)} %tie.8.own_ref, bf16[768,768]{1,0:T(8,128)(2,1)} %copy-done.7, f32[3072,768]{1,0:T(8,128)} %get-tuple-element.96.rest_0_, ...), custom_call_target="tpu_custom_call", output_to_operand_aliasing={{0}: (3, {}), {1}: (4, {})} | custom-call | flops 1 | bytes 1 | tf_op jit(solution)/shard_map/place/pallas_call | solution.py:397
  207.9 4.2 %place.6 = (f32[3072,768]{1,0:T(8,128)}, f32[768,3072]{1,0:T(8,128)}) custom-call(s32[6]{0:T(128)} %stack.27.refs_0_.at_ref, bf16[768,768]{1,0:T(8,128)(2,1)} %tie.7.own_ref, bf16[768,768]{1,0:T(8,128)(2,1)} %collective-permute-done.23.other_ref, f32[3072,768]{1,0:T(8,128)} %get-tuple-element.98.rest_0_, ...), custom_call_target="tpu_custom_call", output_to_operand_aliasing={{0}: (3, {}), {1}: (4, {})} | custom-call | flops 1 | bytes 1 | tf_op jit(solution)/shard_map/place/pallas_call | solution.py:397
  214.5 4.6 %collective-permute-start.27 = (bf16[16,48,896]{2,1,0:T(8,128)(2,1)}, bf16[16,48,896]{2,1,0:T(8,128)(2,1)S(1)}, u32[]{:S(2)}, u32[]{:S(2)}) collective-permute-start(bf16[16,48,896]{2,1,0:T(8,128)(2,1)} %tie.9.refs_1_), channel_id=1, source_target_pairs={{0,1},{1,0},{2,3},{3,2},{4,5},{5,4},{6,7},{7,6},{8,9},{9,8},{10,11... | collective-permute-start | bytes 4128776 | tf_op jit(solution)/shard_map/ppermute | solution.py:107
  219.2 4.4 %collective-permute-done.28.other_ref = bf16[768,768]{1,0:T(8,128)(2,1)S(1)} collective-permute-done((bf16[768,768]{1,0:T(8,128)(2,1)S(1)}, bf16[768,768]{1,0:T(8,128)(2,1)S(1)}, u32[]{:S(2)}, u32[]{:S(2)}) %collective-permute-start.28) | collective-permute-done | bytes 1179680 | tf_op jit(solution)/shard_map/ppermute | solution.py:107
  224.6 4.2 %place.7 = (f32[3072,768]{1,0:T(8,128)}, f32[768,3072]{1,0:T(8,128)}) custom-call(s32[6]{0:T(128)} %stack.27.refs_0_.at_ref, bf16[768,768]{1,0:T(8,128)(2,1)} %tie.6.refs_0_.own_ref, bf16[768,768]{1,0:T(8,128)(2,1)} %copy-done.8, f32[3072,768]{1,0:T(8,128)} %get-tuple-element.100.rest_0_, ...), custom_call_target="tpu_custom_call", output_to_operand_aliasing={{0}: (3, {}), {1}: (4, {})} | custom-call | flops 1 | bytes 1 | tf_op jit(solution)/shard_map/place/pallas_call | solution.py:397
  229.9 4.6 %late_place.1 = (f32[768,768]{1,0:T(8,128)}, f32[768,768]{1,0:T(8,128)}, f32[768,128]{1,0:T(8,128)}, f32[64]{0:T(128)}, f32[768]{0:T(1024)}, /*index=5*/f32[768]...) custom-call(s32[6]{0:T(128)} %stack.27.refs_0_.at_ref, ...), custom_call_target="tpu_custom_call" | custom-call | flops 1 | bytes 1 | tf_op jit(solution)/shard_map/late_place/pallas_call | solution.py:475
  (144 shorter events, 32.0 us)
Async XLA Ops:
  0.6 10.9 %copy-start.31 = (s32[1,8]{1,0:T(1,128)S(1)}, s32[1,8]{1,0:T(1,128)}, u32[]{:S(2)}) copy-start(s32[1,8]{1,0:T(1,128)} %param.19) | copy-start | bytes 100
  0.7 11.1 %copy-start.30 = (s32[1,8,2]{1,2,0:T(2,128)S(1)}, s32[1,8,2]{1,2,0:T(2,128)}, u32[]{:S(2)}) copy-start(s32[1,8,2]{1,2,0:T(2,128)} %param.20) | copy-start | bytes 196
  2.9 18.9 %all-to-all-start = ((bf16[16,128,128]{2,1,0:T(8,128)(2,1)}), bf16[16,128,128]{2,1,0:T(8,128)(2,1)S(1)}, u32[]{:S(2)}, u32[]{:S(2)}) async-start(bf16[16,128,128]{2,1,0:T(8,128)(2,1)} %get-tuple-element.67), calls=%async_computation | async-start | bytes 1048576 | tf_op jit(solution)/shard_map/all_to_all | solution.py:596
  22.6 3.9 %collective-permute-start = (bf16[16,128,128]{2,1,0:T(8,128)(2,1)}, bf16[16,128,128]{2,1,0:T(8,128)(2,1)S(1)}, u32[]{:S(2)}, u32[]{:S(2)}) collective-permute-start(bf16[16,128,128]{2,1,0:T(8,128)(2,1)} %tie.5.refs_3_), channel_id=1, source_target_pairs={{0,1},{1,0},{2,3},{3,2},{4,5},{5,4},{6,7},{7,6},{8,9},{9,8},{10,11... | collective-permute-start | bytes 1572872 | tf_op jit(solution)/shard_map/ppermute | solution.py:107
  54.1 2.9 %collective-permute-start.1 = (bf16[128,3072]{1,0:T(8,128)(2,1)}, bf16[128,3072]{1,0:T(8,128)(2,1)S(1)}, u32[]{:S(2)}, u32[]{:S(2)}) collective-permute-start(bf16[128,3072]{1,0:T(8,128)(2,1)} %get-tuple-element.78), channel_id=1, source_target_pairs={{0,1},{1,0},{2,3},{3,2},{4,5},{5,4},{6,7},{7,6},{8,9},{9,8},{10,11... | collective-permute-start | bytes 2359304 | tf_op jit(solution)/shard_map/ppermute | solution.py:107
  54.5 2.4 %collective-permute-start.2 = (bf16[128,768]{1,0:T(8,128)(2,1)}, bf16[128,768]{1,0:T(8,128)(2,1)S(1)}, u32[]{:S(2)}, u32[]{:S(2)}) collective-permute-start(bf16[128,768]{1,0:T(8,128)(2,1)} %get-tuple-element.79), channel_id=1, source_target_pairs={{0,1},{1,0},{2,3},{3,2},{4,5},{5,4},{6,7},{7,6},{8,9},{9,8},{10,11... | collective-permute-start | bytes 589832 | tf_op jit(solution)/shard_map/ppermute | solution.py:107
  61.3 24.9 %all-to-all-start.1 = ((bf16[4,256,1536]{2,1,0:T(8,128)(2,1)}), bf16[4,256,1536]{2,1,0:T(8,128)(2,1)S(1)}, u32[]{:S(2)}, u32[]{:S(2)}) async-start(bf16[4,256,1536]{2,1,0:T(8,128)(2,1)} %pack.1.refs_11_), calls=%async_computation.1 | async-start | bytes 6291456 | tf_op jit(solution)/shard_map/all_to_all | solution.py:632
  84.5 3.9 %collective-permute-start.3 = (bf16[16,128,128]{2,1,0:T(8,128)(2,1)}, bf16[16,128,128]{2,1,0:T(8,128)(2,1)}, u32[]{:S(2)}, u32[]{:S(2)}) collective-permute-start(bf16[16,128,128]{2,1,0:T(8,128)(2,1)} %get-tuple-element.84), channel_id=1, source_target_pairs={{0,1},{1,0},{2,3},{3,2},{4,5},{5,4},{6,7},{7,6},{8,9},{9,8},{10,11... | collective-permute-start | bytes 1572872 | tf_op jit(solution)/shard_map/ppermute | solution.py:107
  86.2 1.7 copy-start.2
  90.6 21.8 %all-to-all-start.2 = ((bf16[16,128,128]{2,1,0:T(8,128)(2,1)}), bf16[16,128,128]{2,1,0:T(8,128)(2,1)S(1)}, u32[]{:S(2)}, u32[]{:S(2)}) async-start(bf16[16,128,128]{2,1,0:T(8,128)(2,1)} %share.1), calls=%async_computation.2 | async-start | bytes 1048576 | tf_op jit(solution)/shard_map/all_to_all | solution.py:636
  94.2 12.8 %copy-start.32 = (bf16[128,768]{1,0:T(8,128)(2,1)S(1)}, bf16[128,768]{1,0:T(8,128)(2,1)}, u32[]{:S(2)}) copy-start(bf16[128,768]{1,0:T(8,128)(2,1)} %get-tuple-element.87) | copy-start | bytes 589828
  94.2 12.8 %copy-start.33 = (bf16[128,768]{1,0:T(8,128)(2,1)S(1)}, bf16[128,768]{1,0:T(8,128)(2,1)}, u32[]{:S(2)}) copy-start(bf16[128,768]{1,0:T(8,128)(2,1)} %get-tuple-element.89) | copy-start | bytes 589828
  99.6 17.1 %collective-permute-start.7 = (bf16[192,768]{1,0:T(8,128)(2,1)}, bf16[192,768]{1,0:T(8,128)(2,1)S(1)}, u32[]{:S(2)}, u32[]{:S(2)}) collective-permute-start(bf16[192,768]{1,0:T(8,128)(2,1)} %get-tuple-element.93), channel_id=1, source_target_pairs={{0,8},{1,33},{2,10},{3,35},{4,12},{5,37},{6,14},{7,39},{8,16},{9,4... | collective-permute-start | bytes 884744 | tf_op jit(solution)/shard_map/ppermute | solution.py:103
  104.5 12.2 %collective-permute-start.8 = (bf16[192,768]{1,0:T(8,128)(2,1)}, bf16[192,768]{1,0:T(8,128)(2,1)S(1)}, u32[]{:S(2)}, u32[]{:S(2)}) collective-permute-start(bf16[192,768]{1,0:T(8,128)(2,1)} %get-tuple-element.94), channel_id=1, source_target_pairs={{0,24},{1,97},{2,26},{3,99},{4,28},{5,101},{6,30},{7,103},{8,0},{9... | collective-permute-start | bytes 884744 | tf_op jit(solution)/shard_map/ppermute | solution.py:103
  105.8 11.0 %collective-permute-start.9 = (bf16[192,768]{1,0:T(8,128)(2,1)}, bf16[192,768]{1,0:T(8,128)(2,1)S(1)}, u32[]{:S(2)}, u32[]{:S(2)}) collective-permute-start(bf16[192,768]{1,0:T(8,128)(2,1)} %get-tuple-element.95), channel_id=1, source_target_pairs={{0,16},{1,65},{2,18},{3,67},{4,20},{5,69},{6,22},{7,71},{8,24},{9,... | collective-permute-start | bytes 884744 | tf_op jit(solution)/shard_map/ppermute | solution.py:103
  106.9 1.4 collective-permute-start.4
  107.0 1.7 collective-permute-start.5
  116.5 1.5 collective-permute-start.6
  121.3 28.2 %all-to-all-start.3 = ((bf16[16,48,896]{2,1,0:T(8,128)(2,1)}), bf16[16,48,896]{2,1,0:T(8,128)(2,1)S(1)}, u32[]{:S(2)}, u32[]{:S(2)}) async-start(bf16[16,48,896]{2,1,0:T(8,128)(2,1)} %late.1.refs_4_), calls=%async_computation.3 | async-start | bytes 2752512 | tf_op jit(solution)/shard_map/all_to_all | solution.py:99
  129.8 13.8 %collective-permute-start.10 = (bf16[192,768]{1,0:T(8,128)(2,1)}, bf16[192,768]{1,0:T(8,128)(2,1)S(1)}, u32[]{:S(2)}, u32[]{:S(2)}) collective-permute-start(bf16[192,768]{1,0:T(8,128)(2,1)} %part.1), channel_id=1, source_target_pairs={{0,32},{1,3},{2,34},{3,5},{4,36},{5,7},{6,38},{7,1},{8,40},{9,11},... | collective-permute-start | bytes 884744 | tf_op jit(solution)/shard_map/ppermute | solution.py:103
  131.5 12.2 %collective-permute-start.11 = (bf16[192,768]{1,0:T(8,128)(2,1)}, bf16[192,768]{1,0:T(8,128)(2,1)S(1)}, u32[]{:S(2)}, u32[]{:S(2)}) collective-permute-start(bf16[192,768]{1,0:T(8,128)(2,1)} %part.1), channel_id=1, source_target_pairs={{0,96},{1,7},{2,98},{3,1},{4,100},{5,3},{6,102},{7,5},{8,104},{9,1... | collective-permute-start | bytes 884744 | tf_op jit(solution)/shard_map/ppermute | solution.py:103
  132.7 10.9 %collective-permute-start.12 = (bf16[192,768]{1,0:T(8,128)(2,1)}, bf16[192,768]{1,0:T(8,128)(2,1)S(1)}, u32[]{:S(2)}, u32[]{:S(2)}) collective-permute-start(bf16[192,768]{1,0:T(8,128)(2,1)} %part.1), channel_id=1, source_target_pairs={{0,64},{1,5},{2,66},{3,7},{4,68},{5,1},{6,70},{7,3},{8,72},{9,13},... | collective-permute-start | bytes 884744 | tf_op jit(solution)/shard_map/ppermute | solution.py:103
  143.6 5.9 %copy-start.12 = (bf16[192,768]{1,0:T(8,128)(2,1)}, bf16[192,768]{1,0:T(8,128)(2,1)S(1)}, u32[]{:S(2)}) copy-start(bf16[192,768]{1,0:T(8,128)(2,1)S(1)} %collective-permute-done.10.refs_1_) | copy-start | bytes 884740
  143.6 5.9 %copy-start.13 = (bf16[192,768]{1,0:T(8,128)(2,1)}, bf16[192,768]{1,0:T(8,128)(2,1)S(1)}, u32[]{:S(2)}) copy-start(bf16[192,768]{1,0:T(8,128)(2,1)S(1)} %collective-permute-done.11.refs_2_) | copy-start | bytes 884740
  143.6 5.9 %copy-start.14 = (bf16[192,768]{1,0:T(8,128)(2,1)}, bf16[192,768]{1,0:T(8,128)(2,1)S(1)}, u32[]{:S(2)}) copy-start(bf16[192,768]{1,0:T(8,128)(2,1)S(1)} %collective-permute-done.12.refs_3_) | copy-start | bytes 884740
  145.0 12.2 %copy-start.15 = (bf16[192,768]{1,0:T(8,128)(2,1)}, bf16[192,768]{1,0:T(8,128)(2,1)S(1)}, u32[]{:S(2)}) copy-start(bf16[192,768]{1,0:T(8,128)(2,1)S(1)} %add_convert_fusion.refs_1_) | copy-start | bytes 884740
  145.0 7.7 %collective-permute-start.16 = (bf16[192,768]{1,0:T(8,128)(2,1)S(1)}, bf16[192,768]{1,0:T(8,128)(2,1)S(1)}, u32[]{:S(2)}, u32[]{:S(2)}) collective-permute-start(bf16[192,768]{1,0:T(8,128)(2,1)S(1)} %add_convert_fusion.refs_1_), channel_id=1, source_target_pairs={{0,8},{1,33},{2,10},{3,35},{4,12},{5,37},{6,14},{7,39},{8,16},{9,4... | collective-permute-start | bytes 884744 | tf_op jit(solution)/shard_map/ppermute | solution.py:103
  146.8 8.4 %collective-permute-start.17 = (bf16[192,768]{1,0:T(8,128)(2,1)S(1)}, bf16[192,768]{1,0:T(8,128)(2,1)S(1)}, u32[]{:S(2)}, u32[]{:S(2)}) collective-permute-start(bf16[192,768]{1,0:T(8,128)(2,1)S(1)} %add_convert_fusion.refs_1_), channel_id=1, source_target_pairs={{0,24},{1,97},{2,26},{3,99},{4,28},{5,101},{6,30},{7,103},{8,0},{9... | collective-permute-start | bytes 884744 | tf_op jit(solution)/shard_map/ppermute | solution.py:103
  148.4 8.8 %collective-permute-start.18 = (bf16[192,768]{1,0:T(8,128)(2,1)S(1)}, bf16[192,768]{1,0:T(8,128)(2,1)}, u32[]{:S(2)}, u32[]{:S(2)}) collective-permute-start(bf16[192,768]{1,0:T(8,128)(2,1)S(1)} %add_convert_fusion.refs_1_), channel_id=1, source_target_pairs={{0,16},{1,65},{2,18},{3,67},{4,20},{5,69},{6,22},{7,71},{8,24},{9,... | collective-permute-start | bytes 884744 | tf_op jit(solution)/shard_map/ppermute | solution.py:103
  152.7 13.7 %copy-start.18 = (bf16[48,896]{1,0:T(8,128)(2,1)S(1)}, bf16[48,896]{1,0:T(8,128)(2,1)}, u32[]{:S(2)}) copy-start(bf16[48,896]{1,0:T(8,128)(2,1)} %strip.1.refs_5_.refs_0_) | copy-start | bytes 258052
  152.7 4.4 %copy-start.20 = (bf16[192,768]{1,0:T(8,128)(2,1)}, bf16[192,768]{1,0:T(8,128)(2,1)S(1)}, u32[]{:S(2)}) copy-start(bf16[192,768]{1,0:T(8,128)(2,1)S(1)} %collective-permute-done.16.refs_2_) | copy-start | bytes 884740
  155.2 1.9 copy-start.21
  159.5 22.2 %collective-permute-start.19 = (bf16[768,768]{1,0:T(8,128)(2,1)}, bf16[768,768]{1,0:T(8,128)(2,1)}, u32[]{:S(2)}, u32[]{:S(2)}) collective-permute-start(bf16[768,768]{1,0:T(8,128)(2,1)} %join.1.own_ref), channel_id=1, source_target_pairs={{0,1},{1,0},{2,3},{3,2},{4,5},{5,4},{6,7},{7,6},{8,9},{9,8},{10,11... | collective-permute-start | bytes 3538952 | tf_op jit(solution)/shard_map/ppermute | solution.py:107
  162.1 36.4 %collective-permute-start.22 = (bf16[768,768]{1,0:T(8,128)(2,1)}, bf16[768,768]{1,0:T(8,128)(2,1)S(1)}, u32[]{:S(2)}, u32[]{:S(2)}) collective-permute-start(bf16[768,768]{1,0:T(8,128)(2,1)} %join.1.own_ref), channel_id=1, source_target_pairs={{0,4},{1,17},{2,6},{3,19},{4,0},{5,21},{6,2},{7,23},{8,12},{9,25},... | collective-permute-start | bytes 3538952 | tf_op jit(solution)/shard_map/ppermute | solution.py:103
  163.8 35.8 %collective-permute-start.24 = (bf16[768,768]{1,0:T(8,128)(2,1)}, bf16[768,768]{1,0:T(8,128)(2,1)}, u32[]{:S(2)}, u32[]{:S(2)}) collective-permute-start(bf16[768,768]{1,0:T(8,128)(2,1)} %join.1.own_ref), channel_id=1, source_target_pairs={{0,2},{1,9},{2,4},{3,11},{4,6},{5,13},{6,0},{7,15},{8,10},{9,17},{... | collective-permute-start | bytes 3538952 | tf_op jit(solution)/shard_map/ppermute | solution.py:103
  165.4 34.5 %collective-permute-start.21 = (bf16[768,768]{1,0:T(8,128)(2,1)}, bf16[768,768]{1,0:T(8,128)(2,1)}, u32[]{:S(2)}, u32[]{:S(2)}) collective-permute-start(bf16[768,768]{1,0:T(8,128)(2,1)} %join.1.own_ref), channel_id=1, source_target_pairs={{0,6},{1,25},{2,0},{3,27},{4,2},{5,29},{6,4},{7,31},{8,14},{9,1},{... | collective-permute-start | bytes 3538952 | tf_op jit(solution)/shard_map/ppermute | solution.py:103
  166.5 15.2 %collective-permute-start.13 = (bf16[48,896]{1,0:T(8,128)(2,1)S(1)}, bf16[48,896]{1,0:T(8,128)(2,1)S(1)}, u32[]{:S(2)}, u32[]{:S(2)}) collective-permute-start(bf16[48,896]{1,0:T(8,128)(2,1)S(1)} %copy-done.18), channel_id=1, source_target_pairs={{0,32},{1,3},{2,34},{3,5},{4,36},{5,7},{6,38},{7,1},{8,40},{9,11},... | collective-permute-start | bytes 258056 | tf_op jit(solution)/shard_map/ppermute | solution.py:103
  181.6 9.4 %copy-start.24 = (bf16[48,896]{1,0:T(8,128)(2,1)}, bf16[48,896]{1,0:T(8,128)(2,1)S(1)}, u32[]{:S(2)}) copy-start(bf16[48,896]{1,0:T(8,128)(2,1)S(1)} %collective-permute-done.13.refs_1_) | copy-start | bytes 258052
  181.6 8.3 %collective-permute-start.14 = (bf16[48,896]{1,0:T(8,128)(2,1)S(1)}, bf16[48,896]{1,0:T(8,128)(2,1)S(1)}, u32[]{:S(2)}, u32[]{:S(2)}) collective-permute-start(bf16[48,896]{1,0:T(8,128)(2,1)S(1)} %copy-done.18), channel_id=1, source_target_pairs={{0,96},{1,7},{2,98},{3,1},{4,100},{5,3},{6,102},{7,5},{8,104},{9,1... | collective-permute-start | bytes 258056 | tf_op jit(solution)/shard_map/ppermute | solution.py:103
  181.6 8.3 %collective-permute-start.15 = (bf16[48,896]{1,0:T(8,128)(2,1)S(1)}, bf16[48,896]{1,0:T(8,128)(2,1)S(1)}, u32[]{:S(2)}, u32[]{:S(2)}) collective-permute-start(bf16[48,896]{1,0:T(8,128)(2,1)S(1)} %copy-done.18), channel_id=1, source_target_pairs={{0,64},{1,5},{2,66},{3,7},{4,68},{5,1},{6,70},{7,3},{8,72},{9,13},... | collective-permute-start | bytes 258056 | tf_op jit(solution)/shard_map/ppermute | solution.py:103
  189.9 1.2 collective-permute-start.20
  193.9 20.1 %all-to-all-start.4 = ((bf16[16,48,896]{2,1,0:T(8,128)(2,1)}), bf16[16,48,896]{2,1,0:T(8,128)(2,1)}, u32[]{:S(2)}, u32[]{:S(2)}) async-start(bf16[16,48,896]{2,1,0:T(8,128)(2,1)} %copies.1.refs_0_), calls=%async_computation.4 | async-start | bytes 2752512 | tf_op jit(solution)/shard_map/all_to_all | solution.py:99
  199.6 3.1 %collective-permute-start.25 = (bf16[768,768]{1,0:T(8,128)(2,1)}, bf16[768,768]{1,0:T(8,128)(2,1)S(1)}, u32[]{:S(2)}, u32[]{:S(2)}) collective-permute-start(bf16[768,768]{1,0:T(8,128)(2,1)} %tie.8.own_ref), channel_id=1, source_target_pairs={{0,1},{1,0},{2,3},{3,2},{4,5},{5,4},{6,7},{7,6},{8,9},{9,8},{10,11... | collective-permute-start | bytes 3538952 | tf_op jit(solution)/shard_map/ppermute | solution.py:107
  199.9 8.0 %collective-permute-start.23 = (bf16[768,768]{1,0:T(8,128)(2,1)}, bf16[768,768]{1,0:T(8,128)(2,1)}, u32[]{:S(2)}, u32[]{:S(2)}) collective-permute-start(bf16[768,768]{1,0:T(8,128)(2,1)} %tie.7.own_ref), channel_id=1, source_target_pairs={{0,1},{1,0},{2,3},{3,2},{4,5},{5,4},{6,7},{7,6},{8,9},{9,8},{10,11... | collective-permute-start | bytes 3538952 | tf_op jit(solution)/shard_map/ppermute | solution.py:107
  212.8 6.4 %copy-start.1 = (bf16[768,768]{1,0:T(8,128)(2,1)S(1)}, bf16[768,768]{1,0:T(8,128)(2,1)}, u32[]{:S(2)}) copy-start(bf16[768,768]{1,0:T(8,128)(2,1)} %tie.6.refs_0_.own_ref) | copy-start | bytes 3538948
  212.8 1.2 collective-permute-start.26
  214.5 14.3 %collective-permute-start.27 = (bf16[16,48,896]{2,1,0:T(8,128)(2,1)}, bf16[16,48,896]{2,1,0:T(8,128)(2,1)S(1)}, u32[]{:S(2)}, u32[]{:S(2)}) collective-permute-start(bf16[16,48,896]{2,1,0:T(8,128)(2,1)} %tie.9.refs_1_), channel_id=1, source_target_pairs={{0,1},{1,0},{2,3},{3,2},{4,5},{5,4},{6,7},{7,6},{8,9},{9,8},{10,11... | collective-permute-start | bytes 4128776 | tf_op jit(solution)/shard_map/ppermute | solution.py:107
  219.1 4.4 %collective-permute-start.28 = (bf16[768,768]{1,0:T(8,128)(2,1)S(1)}, bf16[768,768]{1,0:T(8,128)(2,1)S(1)}, u32[]{:S(2)}, u32[]{:S(2)}) collective-permute-start(bf16[768,768]{1,0:T(8,128)(2,1)S(1)} %copy-done.1), channel_id=1, source_target_pairs={{0,1},{1,0},{2,3},{3,2},{4,5},{5,4},{6,7},{7,6},{8,9},{9,8},{10,11... | collective-permute-start | bytes 3538952 | tf_op jit(solution)/shard_map/ppermute | solution.py:107
  (20 other events, 18.4 us)

commit v10 on v9

--- a/solution.py
+++ b/solution.py
@@ -661,15 +661,15 @@
     late_parts = in_plane(shares)
     ff_totals = gather4(pair_sums(*ff_crossed), 1)
     strip = call(strip_kernel, (late_parts,), shapes(((STRIP, D + 128), bf16))[0], name="strip", after=ff_crossed[1:])
-    u = call(join_kernel, (at,) + ff_totals, shapes(((D, D), bf16))[0], name="join", after=(strip,))
+    strips = gather4(strip, 3)
+    u = call(join_kernel, (at,) + ff_totals, shapes(((D, D), bf16))[0], name="join", after=strips[1:])
     before, after, far = spread(0, u, u, u)
     kept = place(at, 0, u, swap(u), ())
     mark = corner(kept[0])
-    copies = call(copies_kernel, gather4(strip, 3), shapes(((CHIPS, STRIP, D + 128), bf16))[0], name="copies",
+    copies = call(copies_kernel, strips, shapes(((CHIPS, STRIP, D + 128), bf16))[0], name="copies",
                   after=(mark,))
     late = in_plane(copies)
-    far = tie(far, copies)
-    before, after = tie(before, far), tie(after, far)
+    before, after, far = (tie(v, copies) for v in (before, after, far))
     kept = place(at, 3, before, swap(before), kept)
     kept = place(at, 1, after, swap(after), kept)
     g_down, g_up = place(at, 2, far, swap(far), kept)

time: 236 us -> 232 us (0.983)
  starting transfers between devices: 64.3 us -> 76.1 us
  waiting for transfers between devices: 46.3 us -> 35.1 us
  Pallas kernels: 101 us -> 96.8 us
    ppermute x14, starting transfers between devices: 12 us -> 24.4 us  [swap(): return lax.ppermute(v, 'c', [(0, 1), (1, 0)])]
    ppermute x15, waiting for transfers between devices: 27.8 us -> 18.7 us  [send(): return lax.ppermute(v, AXES, ring(place, shift))]
    ppermute x14, waiting for transfers between devices: 14.8 us -> 10.6 us  [swap(): return lax.ppermute(v, 'c', [(0, 1), (1, 0)])]
    pallas_call x14, Pallas kernels: 68 us -> 64.2 us  [call(): pl.pallas_call(run, out_shape=outs, in_specs=[SMEM if v.dtype == jnp.int3...]
    unnamed x68 -> x62, local copies, waits for them, and re-layouts: 12.7 us -> 12.4 us
  transfers between devices with their start and end apart: 34 -> 34, of which waited for: 15 -> 17; matrix products, arithmetic and copies ran while one was open for 4% -> 4% of each run, Pallas kernels for 24% -> 24%
where the time goes in v10:
time: 232 us; the launch traced here: 231 us
  Pallas kernels  96.8 us (42%)
  starting transfers between devices  76.1 us (33%)
  waiting for transfers between devices  35.1 us (15%)
  local copies, waits for them, and re-layouts  19.6 us (8%)
  other arithmetic  2.37 us (1%)
    pallas_call x14, Pallas kernels, call(): pl.pallas_call(run, out_shape=outs, in_specs=[SMEM if v.dtype == jnp.int3...  64.2 us
    ppermute x15, starting transfers between devices, send(): return lax.ppermute(v, AXES, ring(place, shift))  25.8 us
    ppermute x14, starting transfers between devices, swap(): return lax.ppermute(v, 'c', [(0, 1), (1, 0)])  24.4 us
    ppermute x15, waiting for transfers between devices, send(): return lax.ppermute(v, AXES, ring(place, shift))  18.7 us
    pallas_call x4, Pallas kernels, place(): pl.pallas_call(place_kernel, grid_spec=pltpu.PrefetchScalarGridSpec(num_s...  16.8 us
    unnamed x62, local copies, waits for them, and re-layouts  12.4 us
    ppermute x14, waiting for transfers between devices, swap(): return lax.ppermute(v, 'c', [(0, 1), (1, 0)])  10.6 us
    pallas_call x1, Pallas kernels, body(): pl.pallas_call(middle_kernel, grid=(steps,), out_shape=shapes(narrow, ((R...  10.5 us
  transfers between devices with their start and end apart: 34, of which 17 were waited for; matrix products, arithmetic and copies ran while one was open for 4% of the time, Pallas kernels for 24%

profile of v10, /device:TPU:1, one launch (start us, length us, event | category | flops | bytes accessed | tf_op | source)
XLA Modules:
  0.0 231.0 jit_solution(16318859834142893694)
XLA Ops:
  0.7 2.2 enter.1
  2.9 8.6 %all-to-all-start = ((bf16[16,128,128]{2,1,0:T(8,128)(2,1)}), bf16[16,128,128]{2,1,0:T(8,128)(2,1)S(1)}, u32[]{:S(2)}, u32[]{:S(2)}) async-start(bf16[16,128,128]{2,1,0:T(8,128)(2,1)} %get-tuple-element.67), calls=%async_computation | async-start | bytes 1048576 | tf_op jit(solution)/shard_map/all_to_all | solution.py:596
  15.0 2.2 broadcast_in_dim.28.refs_3_.refs_5_.refs_7_
  17.2 2.3 query.1.refs_0_.refs_2_
  19.5 2.4 %all-to-all-done.v_ref = bf16[16,128,128]{2,1,0:T(8,128)(2,1)S(1)} async-done(((bf16[16,128,128]{2,1,0:T(8,128)(2,1)}), bf16[16,128,128]{2,1,0:T(8,128)(2,1)S(1)}, u32[]{:S(2)}, u32[]{:S(2)}) %all-to-all-start) | async-done | bytes 524320 | tf_op jit(solution)/shard_map/all_to_all | solution.py:596
  22.6 2.1 collective-permute-start
  27.3 14.4 %attend.1 = (bf16[128,768]{1,0:T(8,128)(2,1)}, bf16[128,768]{1,0:T(8,128)(2,1)}, bf16[128,768]{1,0:T(8,128)(2,1)}, bf16[2,768,128]{2,1,0:T(8,128)(2,1)}, f32[2,7...) custom-call(s32[6]{0:T(128)} %stack.27.refs_0_.at_ref, s32[8]{0:T(128)} %select_n.94.refs_6_.refs_1_, ...), custom_call_target="tpu_custom_call" | custom-call | flops 1 | bytes 1 | tf_op jit(solution)/shard_map/attend/pallas_call | solution.py:475
  41.8 10.5 %middle.1 = (bf16[128,768]{1,0:T(8,128)(2,1)}, bf16[128,3072]{1,0:T(8,128)(2,1)}, bf16[128,3072]{1,0:T(8,128)(2,1)}, bf16[128,768]{1,0:T(8,128)(2,1)}, bf16[128,...) custom-call(s32[6]{0:T(128)} %stack.27.refs_0_.at_ref, ...), custom_call_target="tpu_custom_call" | custom-call | flops 1 | bytes 1 | tf_op jit(solution)/shard_map/middle/pallas_call | solution.py:612
  52.9 2.3 collective-permute-done.2.refs_3_
  56.1 3.4 %pack.1.refs_11_ = bf16[4,256,1536]{2,1,0:T(8,128)(2,1)} custom-call(bf16[128,3072]{1,0:T(8,128)(2,1)} %get-tuple-element.76.refs_0_, bf16[128,768]{1,0:T(8,128)(2,1)} %get-tuple-element.77.refs_1_, bf16[128,3072]{1,0:T(8,128)(2,1)} %copy-done.14, bf16[128,768]{1,0:T(8,128)(2,1)} %copy-done.22), custom_call_target="tpu_custom_call" | custom-call | flops 1 | bytes 1 | tf_op jit(solution)/shard_map/pack/pallas_call | solution.py:475
  59.5 3.9 %all-to-all-start.1 = ((bf16[4,256,1536]{2,1,0:T(8,128)(2,1)}), bf16[4,256,1536]{2,1,0:T(8,128)(2,1)S(1)}, u32[]{:S(2)}, u32[]{:S(2)}) async-start(bf16[4,256,1536]{2,1,0:T(8,128)(2,1)} %pack.1.refs_11_), calls=%async_computation.1 | async-start | bytes 6291456 | tf_op jit(solution)/shard_map/all_to_all | solution.py:632
  63.4 17.3 %attend_back.1 = (bf16[128,768]{1,0:T(8,128)(2,1)}, bf16[128,768]{1,0:T(8,128)(2,1)}, bf16[128,768]{1,0:T(8,128)(2,1)}, bf16[16,128,128]{2,1,0:T(8,128)(2,1)}, bf16[16,128,128]{2,1,0:T(8,128)(2,1)}) custom-call(s32[6]{0:T(128)} %stack.27.refs_0_.at_ref, s32[8]{0:T(128)} %select_n.94.refs_6_.refs_1_, bf16[2,768,128]{2,1,0:T(8,128)(2,1)} %get-tuple-element.70.refs_2_, ...), custom_call_target="tpu_custom_call" | custom-call | flops 1 | bytes 1 | tf_op jit(solution)/shard_map/attend_back/pallas_call | solution.py:475
  81.0 3.4 %all-to-all-done.1.slab_ref = bf16[4,256,1536]{2,1,0:T(8,128)(2,1)S(1)} async-done(((bf16[4,256,1536]{2,1,0:T(8,128)(2,1)}), bf16[4,256,1536]{2,1,0:T(8,128)(2,1)S(1)}, u32[]{:S(2)}, u32[]{:S(2)}) %all-to-all-start.1) | async-done | bytes 3145760 | tf_op jit(solution)/shard_map/all_to_all | solution.py:632
  84.4 1.7 copy-done
  86.7 2.1 share.1
  88.8 3.6 %all-to-all-start.2 = ((bf16[16,128,128]{2,1,0:T(8,128)(2,1)}), bf16[16,128,128]{2,1,0:T(8,128)(2,1)S(1)}, u32[]{:S(2)}, u32[]{:S(2)}) async-start(bf16[16,128,128]{2,1,0:T(8,128)(2,1)} %share.1), calls=%async_computation.2 | async-start | bytes 1048576 | tf_op jit(solution)/shard_map/all_to_all | solution.py:636
  92.4 5.3 %weights.1 = (bf16[192,768]{1,0:T(8,128)(2,1)}, bf16[192,768]{1,0:T(8,128)(2,1)}, bf16[192,768]{1,0:T(8,128)(2,1)}, bf16[192,768]{1,0:T(8,128)(2,1)}) custom-call(s32[6]{0:T(128)} %stack.27.refs_0_.at_ref, bf16[4,256,1536]{2,1,0:T(8,128)(2,1)} %copy-done), custom_call_target="tpu_custom_call" | custom-call | flops 1 | bytes 1 | tf_op jit(solution)/shard_map/weights/pallas_call | solution.py:638
  98.9 6.8 %collective-permute-start.8 = (bf16[192,768]{1,0:T(8,128)(2,1)}, bf16[192,768]{1,0:T(8,128)(2,1)S(1)}, u32[]{:S(2)}, u32[]{:S(2)}) collective-permute-start(bf16[192,768]{1,0:T(8,128)(2,1)} %get-tuple-element.94), channel_id=1, source_target_pairs={{0,24},{1,97},{2,26},{3,99},{4,28},{5,101},{6,30},{7,103},{8,0},{9... | collective-permute-start | bytes 884744 | tf_op jit(solution)/shard_map/ppermute | solution.py:103
  105.7 1.7 collective-permute-start.9
  109.8 3.0 %square.1.refs_10_.refs_5_ = bf16[768,768]{1,0:T(8,128)(2,1)} custom-call(bf16[128,768]{1,0:T(8,128)(2,1)} %get-tuple-element.86.refs_0_.refs_1_, bf16[128,768]{1,0:T(8,128)(2,1)} %copy-done.15, bf16[128,768]{1,0:T(8,128)(2,1)} %get-tuple-element.88.refs_2_, bf16[128,768]{1,0:T(8,128)(2,1)} %copy-done.23), custom_call_target="tpu_custom_call" | custom-call | flops 1 | bytes 1 | tf_op jit(solution)/shard_map/square/pallas_call | solution.py:475
  113.6 3.3 %leave.1 = (f32[768,128]{1,0:T(8,128)}, f32[128,128]{1,0:T(8,128)}, f32[128,128]{1,0:T(8,128)}, f32[128,128]{1,0:T(8,128)}) custom-call(s32[6]{0:T(128)} %stack.27.refs_0_.at_ref, bf16[128,768]{1,0:T(8,128)(2,1)} %bitcast.61, bf16[768]{0:T(1024)(128)(2,1)} %refs_2_.5, bf16[768,768]{1,0:T(8,128)(2,1)} %refs_3_.3, bf16[768,128]{1,0:T(8,128)(2,1)} %refs_4_.3, ...), custom_call_target="tpu_custom_call" | custom-call | flops 1 | bytes 1 | tf_op jit(solution)/shard_map/leave/pallas_call | solution.py:475
  119.0 2.8 %late.1.refs_4_ = bf16[16,48,896]{2,1,0:T(8,128)(2,1)} custom-call(s32[6]{0:T(128)} %stack.27.refs_0_.at_ref, bf16[128,768]{1,0:T(8,128)(2,1)} %get-tuple-element.86.refs_0_.refs_1_, bf16[128,768]{1,0:T(8,128)(2,1)} %copy-done.15, f32[128,128]{1,0:T(8,128)} %get-tuple-element.91.refs_3_, f32[128,128]{1,0:T(8,128)} %copy-done.24, ...), custom_call_target="tpu_custom_call" | custom-call | flops 1 | bytes 1 | tf_op jit(solution)/shard_map/late/pallas_call | solution.py:475
  121.8 6.1 %all-to-all-start.3 = ((bf16[16,48,896]{2,1,0:T(8,128)(2,1)}), bf16[16,48,896]{2,1,0:T(8,128)(2,1)S(1)}, u32[]{:S(2)}, u32[]{:S(2)}) async-start(bf16[16,48,896]{2,1,0:T(8,128)(2,1)} %late.1.refs_4_), calls=%async_computation.3 | async-start | bytes 2752512 | tf_op jit(solution)/shard_map/all_to_all | solution.py:99
  127.9 2.1 part.1
  130.0 1.6 collective-permute-start.10
  132.9 1.8 collective-permute-start.12
  134.6 9.5 %collective-permute-done.10.refs_1_ = bf16[192,768]{1,0:T(8,128)(2,1)S(1)} collective-permute-done((bf16[192,768]{1,0:T(8,128)(2,1)}, bf16[192,768]{1,0:T(8,128)(2,1)S(1)}, u32[]{:S(2)}, u32[]{:S(2)}) %collective-permute-start.10) | collective-permute-done | bytes 294944 | tf_op jit(solution)/shard_map/ppermute | solution.py:103
  144.2 1.3 add_convert_fusion.refs_1_
  145.8 2.7 %collective-permute-start.17 = (bf16[192,768]{1,0:T(8,128)(2,1)S(1)}, bf16[192,768]{1,0:T(8,128)(2,1)S(1)}, u32[]{:S(2)}, u32[]{:S(2)}) collective-permute-start(bf16[192,768]{1,0:T(8,128)(2,1)S(1)} %add_convert_fusion.refs_1_), channel_id=1, source_target_pairs={{0,24},{1,97},{2,26},{3,99},{4,28},{5,101},{6,30},{7,103},{8,0},{9... | collective-permute-start | bytes 884744 | tf_op jit(solution)/shard_map/ppermute | solution.py:103
  149.6 2.1 strip.1.refs_0_
  151.8 1.9 collective-permute-start.13
  154.4 1.3 collective-permute-done.16.refs_2_
  157.6 3.2 %collective-permute-done.15.refs_7_.refs_3_ = bf16[48,896]{1,0:T(8,128)(2,1)S(1)} collective-permute-done((bf16[48,896]{1,0:T(8,128)(2,1)}, bf16[48,896]{1,0:T(8,128)(2,1)S(1)}, u32[]{:S(2)}, u32[]{:S(2)}) %collective-permute-start.15) | collective-permute-done | bytes 86048 | tf_op jit(solution)/shard_map/ppermute | solution.py:103
  161.5 2.3 %join.1.own_ref = bf16[768,768]{1,0:T(8,128)(2,1)} custom-call(s32[6]{0:T(128)} %stack.27.refs_0_.at_ref, bf16[192,768]{1,0:T(8,128)(2,1)} %copy-done.13, bf16[192,768]{1,0:T(8,128)(2,1)} %copy-done.20, bf16[192,768]{1,0:T(8,128)(2,1)} %copy-done.21, bf16[192,768]{1,0:T(8,128)(2,1)} %collective-permute-done.18.refs_4_, bf16[48,896]{1,0:T(8,128)(2,1)} %copy-done.17, ...), custom_call_target="tpu_custom_call" | custom-call | flops 1 | bytes 1 | tf_op jit(solution)/shard_map/join/pallas_call | solution.py:475
  163.8 4.8 %collective-permute-start.19 = (bf16[768,768]{1,0:T(8,128)(2,1)}, bf16[768,768]{1,0:T(8,128)(2,1)S(1)}, u32[]{:S(2)}, u32[]{:S(2)}) collective-permute-start(bf16[768,768]{1,0:T(8,128)(2,1)} %join.1.own_ref), channel_id=1, source_target_pairs={{0,1},{1,0},{2,3},{3,2},{4,5},{5,4},{6,7},{7,6},{8,9},{9,8},{10,11... | collective-permute-start | bytes 3538952 | tf_op jit(solution)/shard_map/ppermute | solution.py:107
  168.9 2.4 %collective-permute-start.21 = (bf16[768,768]{1,0:T(8,128)(2,1)}, bf16[768,768]{1,0:T(8,128)(2,1)}, u32[]{:S(2)}, u32[]{:S(2)}) collective-permute-start(bf16[768,768]{1,0:T(8,128)(2,1)} %join.1.own_ref), channel_id=1, source_target_pairs={{0,6},{1,25},{2,0},{3,27},{4,2},{5,29},{6,4},{7,31},{8,14},{9,1},{... | collective-permute-start | bytes 3538952 | tf_op jit(solution)/shard_map/ppermute | solution.py:103
  172.3 4.2 %place.4 = (f32[3072,768]{1,0:T(8,128)}, f32[768,3072]{1,0:T(8,128)}) custom-call(s32[6]{0:T(128)} %stack.27.refs_0_.at_ref, bf16[768,768]{1,0:T(8,128)(2,1)} %join.1.own_ref, bf16[768,768]{1,0:T(8,128)(2,1)} %copy-done.12), custom_call_target="tpu_custom_call" | custom-call | flops 1 | bytes 1 | tf_op jit(solution)/shard_map/place/pallas_call | solution.py:397
  179.1 2.2 copies.1.refs_0_
  181.3 3.7 %all-to-all-start.4 = ((bf16[16,48,896]{2,1,0:T(8,128)(2,1)}), bf16[16,48,896]{2,1,0:T(8,128)(2,1)S(1)}, u32[]{:S(2)}, u32[]{:S(2)}) async-start(bf16[16,48,896]{2,1,0:T(8,128)(2,1)} %copies.1.refs_0_), calls=%async_computation.4 | async-start | bytes 2752512 | tf_op jit(solution)/shard_map/all_to_all | solution.py:99
  185.5 2.1 collective-permute-start.24
  187.7 3.1 %collective-permute-start.27 = (bf16[768,768]{1,0:T(8,128)(2,1)}, bf16[768,768]{1,0:T(8,128)(2,1)}, u32[]{:S(2)}, u32[]{:S(2)}) collective-permute-start(bf16[768,768]{1,0:T(8,128)(2,1)} %join.1.own_ref), channel_id=1, source_target_pairs={{0,4},{1,17},{2,6},{3,19},{4,0},{5,21},{6,2},{7,23},{8,12},{9,25},... | collective-permute-start | bytes 3538952 | tf_op jit(solution)/shard_map/ppermute | solution.py:103
  190.9 4.2 %place.5 = (f32[3072,768]{1,0:T(8,128)}, f32[768,3072]{1,0:T(8,128)}) custom-call(s32[6]{0:T(128)} %stack.27.refs_0_.at_ref, bf16[768,768]{1,0:T(8,128)(2,1)} %tie.7.own_ref, bf16[768,768]{1,0:T(8,128)(2,1)} %collective-permute-done.24.other_ref, f32[3072,768]{1,0:T(8,128)} %get-tuple-element.96.rest_0_, ...), custom_call_target="tpu_custom_call", output_to_operand_aliasing={{0}: (3, {}), {1}: (4, {})} | custom-call | flops 1 | bytes 1 | tf_op jit(solution)/shard_map/place/pallas_call | solution.py:397
  195.1 4.2 %place.6 = (f32[3072,768]{1,0:T(8,128)}, f32[768,3072]{1,0:T(8,128)}) custom-call(s32[6]{0:T(128)} %stack.27.refs_0_.at_ref, bf16[768,768]{1,0:T(8,128)(2,1)} %tie.6.own_ref, bf16[768,768]{1,0:T(8,128)(2,1)} %collective-permute-done.22.other_ref, f32[3072,768]{1,0:T(8,128)} %get-tuple-element.98.rest_0_, ...), custom_call_target="tpu_custom_call", output_to_operand_aliasing={{0}: (3, {}), {1}: (4, {})} | custom-call | flops 1 | bytes 1 | tf_op jit(solution)/shard_map/place/pallas_call | solution.py:397
  203.2 12.3 %collective-permute-start.26 = (bf16[16,48,896]{2,1,0:T(8,128)(2,1)}, bf16[16,48,896]{2,1,0:T(8,128)(2,1)S(1)}, u32[]{:S(2)}, u32[]{:S(2)}) collective-permute-start(bf16[16,48,896]{2,1,0:T(8,128)(2,1)} %tie.8.refs_1_), channel_id=1, source_target_pairs={{0,1},{1,0},{2,3},{3,2},{4,5},{5,4},{6,7},{7,6},{8,9},{9,8},{10,11... | collective-permute-start | bytes 4128776 | tf_op jit(solution)/shard_map/ppermute | solution.py:107
  215.5 2.4 %collective-permute-done.27.v_ref = bf16[768,768]{1,0:T(8,128)(2,1)} collective-permute-done((bf16[768,768]{1,0:T(8,128)(2,1)}, bf16[768,768]{1,0:T(8,128)(2,1)}, u32[]{:S(2)}, u32[]{:S(2)}) %collective-permute-start.27) | collective-permute-done | bytes 1179680 | tf_op jit(solution)/shard_map/ppermute | solution.py:103
  217.8 3.2 %collective-permute-done.28.other_ref = bf16[768,768]{1,0:T(8,128)(2,1)} collective-permute-done((bf16[768,768]{1,0:T(8,128)(2,1)}, bf16[768,768]{1,0:T(8,128)(2,1)}, u32[]{:S(2)}, u32[]{:S(2)}) %collective-permute-start.28) | collective-permute-done | bytes 1179680 | tf_op jit(solution)/shard_map/ppermute | solution.py:107
  221.0 4.2 %place.7 = (f32[3072,768]{1,0:T(8,128)}, f32[768,3072]{1,0:T(8,128)}) custom-call(s32[6]{0:T(128)} %stack.27.refs_0_.at_ref, bf16[768,768]{1,0:T(8,128)(2,1)} %tie.9.own_ref, bf16[768,768]{1,0:T(8,128)(2,1)} %collective-permute-done.28.other_ref, f32[3072,768]{1,0:T(8,128)} %get-tuple-element.100.rest_0_, ...), custom_call_target="tpu_custom_call", output_to_operand_aliasing={{0}: (3, {}), {1}: (4, {})} | custom-call | flops 1 | bytes 1 | tf_op jit(solution)/shard_map/place/pallas_call | solution.py:397
  226.3 4.6 %late_place.1 = (f32[768,768]{1,0:T(8,128)}, f32[768,768]{1,0:T(8,128)}, f32[768,128]{1,0:T(8,128)}, f32[64]{0:T(128)}, f32[768]{0:T(1024)}, /*index=5*/f32[768]...) custom-call(s32[6]{0:T(128)} %stack.27.refs_0_.at_ref, ...), custom_call_target="tpu_custom_call" | custom-call | flops 1 | bytes 1 | tf_op jit(solution)/shard_map/late_place/pallas_call | solution.py:475
  (138 shorter events, 31.0 us)
Async XLA Ops:
  0.6 10.9 %copy-start.28 = (s32[1,8]{1,0:T(1,128)S(1)}, s32[1,8]{1,0:T(1,128)}, u32[]{:S(2)}) copy-start(s32[1,8]{1,0:T(1,128)} %param.19) | copy-start | bytes 100
  0.7 11.1 %copy-start.27 = (s32[1,8,2]{1,2,0:T(2,128)S(1)}, s32[1,8,2]{1,2,0:T(2,128)}, u32[]{:S(2)}) copy-start(s32[1,8,2]{1,2,0:T(2,128)} %param.20) | copy-start | bytes 196
  2.9 18.9 %all-to-all-start = ((bf16[16,128,128]{2,1,0:T(8,128)(2,1)}), bf16[16,128,128]{2,1,0:T(8,128)(2,1)S(1)}, u32[]{:S(2)}, u32[]{:S(2)}) async-start(bf16[16,128,128]{2,1,0:T(8,128)(2,1)} %get-tuple-element.67), calls=%async_computation | async-start | bytes 1048576 | tf_op jit(solution)/shard_map/all_to_all | solution.py:596
  22.6 3.9 %collective-permute-start = (bf16[16,128,128]{2,1,0:T(8,128)(2,1)}, bf16[16,128,128]{2,1,0:T(8,128)(2,1)S(1)}, u32[]{:S(2)}, u32[]{:S(2)}) collective-permute-start(bf16[16,128,128]{2,1,0:T(8,128)(2,1)} %tie.5.refs_3_), channel_id=1, source_target_pairs={{0,1},{1,0},{2,3},{3,2},{4,5},{5,4},{6,7},{7,6},{8,9},{9,8},{10,11... | collective-permute-start | bytes 1572872 | tf_op jit(solution)/shard_map/ppermute | solution.py:107
  52.3 2.9 %collective-permute-start.1 = (bf16[128,3072]{1,0:T(8,128)(2,1)}, bf16[128,3072]{1,0:T(8,128)(2,1)S(1)}, u32[]{:S(2)}, u32[]{:S(2)}) collective-permute-start(bf16[128,3072]{1,0:T(8,128)(2,1)} %get-tuple-element.78), channel_id=1, source_target_pairs={{0,1},{1,0},{2,3},{3,2},{4,5},{5,4},{6,7},{7,6},{8,9},{9,8},{10,11... | collective-permute-start | bytes 2359304 | tf_op jit(solution)/shard_map/ppermute | solution.py:107
  52.8 2.4 %collective-permute-start.2 = (bf16[128,768]{1,0:T(8,128)(2,1)}, bf16[128,768]{1,0:T(8,128)(2,1)S(1)}, u32[]{:S(2)}, u32[]{:S(2)}) collective-permute-start(bf16[128,768]{1,0:T(8,128)(2,1)} %get-tuple-element.79), channel_id=1, source_target_pairs={{0,1},{1,0},{2,3},{3,2},{4,5},{5,4},{6,7},{7,6},{8,9},{9,8},{10,11... | collective-permute-start | bytes 589832 | tf_op jit(solution)/shard_map/ppermute | solution.py:107
  59.5 24.9 %all-to-all-start.1 = ((bf16[4,256,1536]{2,1,0:T(8,128)(2,1)}), bf16[4,256,1536]{2,1,0:T(8,128)(2,1)S(1)}, u32[]{:S(2)}, u32[]{:S(2)}) async-start(bf16[4,256,1536]{2,1,0:T(8,128)(2,1)} %pack.1.refs_11_), calls=%async_computation.1 | async-start | bytes 6291456 | tf_op jit(solution)/shard_map/all_to_all | solution.py:632
  80.6 6.0 %collective-permute-start.3 = (bf16[16,128,128]{2,1,0:T(8,128)(2,1)}, bf16[16,128,128]{2,1,0:T(8,128)(2,1)}, u32[]{:S(2)}, u32[]{:S(2)}) collective-permute-start(bf16[16,128,128]{2,1,0:T(8,128)(2,1)} %get-tuple-element.84), channel_id=1, source_target_pairs={{0,1},{1,0},{2,3},{3,2},{4,5},{5,4},{6,7},{7,6},{8,9},{9,8},{10,11... | collective-permute-start | bytes 1572872 | tf_op jit(solution)/shard_map/ppermute | solution.py:107
  84.4 1.7 copy-start
  88.8 24.1 %all-to-all-start.2 = ((bf16[16,128,128]{2,1,0:T(8,128)(2,1)}), bf16[16,128,128]{2,1,0:T(8,128)(2,1)S(1)}, u32[]{:S(2)}, u32[]{:S(2)}) async-start(bf16[16,128,128]{2,1,0:T(8,128)(2,1)} %share.1), calls=%async_computation.2 | async-start | bytes 1048576 | tf_op jit(solution)/shard_map/all_to_all | solution.py:636
  92.4 15.1 %copy-start.29 = (bf16[128,768]{1,0:T(8,128)(2,1)S(1)}, bf16[128,768]{1,0:T(8,128)(2,1)}, u32[]{:S(2)}) copy-start(bf16[128,768]{1,0:T(8,128)(2,1)} %get-tuple-element.87) | copy-start | bytes 589828
  92.4 15.1 %copy-start.30 = (bf16[128,768]{1,0:T(8,128)(2,1)S(1)}, bf16[128,768]{1,0:T(8,128)(2,1)}, u32[]{:S(2)}) copy-start(bf16[128,768]{1,0:T(8,128)(2,1)} %get-tuple-element.89) | copy-start | bytes 589828
  97.7 19.4 %collective-permute-start.7 = (bf16[192,768]{1,0:T(8,128)(2,1)}, bf16[192,768]{1,0:T(8,128)(2,1)S(1)}, u32[]{:S(2)}, u32[]{:S(2)}) collective-permute-start(bf16[192,768]{1,0:T(8,128)(2,1)} %get-tuple-element.93), channel_id=1, source_target_pairs={{0,8},{1,33},{2,10},{3,35},{4,12},{5,37},{6,14},{7,39},{8,16},{9,4... | collective-permute-start | bytes 884744 | tf_op jit(solution)/shard_map/ppermute | solution.py:103
  98.9 18.2 %collective-permute-start.8 = (bf16[192,768]{1,0:T(8,128)(2,1)}, bf16[192,768]{1,0:T(8,128)(2,1)S(1)}, u32[]{:S(2)}, u32[]{:S(2)}) collective-permute-start(bf16[192,768]{1,0:T(8,128)(2,1)} %get-tuple-element.94), channel_id=1, source_target_pairs={{0,24},{1,97},{2,26},{3,99},{4,28},{5,101},{6,30},{7,103},{8,0},{9... | collective-permute-start | bytes 884744 | tf_op jit(solution)/shard_map/ppermute | solution.py:103
  105.7 11.5 %collective-permute-start.9 = (bf16[192,768]{1,0:T(8,128)(2,1)}, bf16[192,768]{1,0:T(8,128)(2,1)S(1)}, u32[]{:S(2)}, u32[]{:S(2)}) collective-permute-start(bf16[192,768]{1,0:T(8,128)(2,1)} %get-tuple-element.95), channel_id=1, source_target_pairs={{0,16},{1,65},{2,18},{3,67},{4,20},{5,69},{6,22},{7,71},{8,24},{9,... | collective-permute-start | bytes 884744 | tf_op jit(solution)/shard_map/ppermute | solution.py:103
  107.4 1.4 collective-permute-start.4
  107.4 1.7 collective-permute-start.5
  116.9 1.5 collective-permute-start.6
  117.2 1.2 copy-start.6
  121.8 26.7 %all-to-all-start.3 = ((bf16[16,48,896]{2,1,0:T(8,128)(2,1)}), bf16[16,48,896]{2,1,0:T(8,128)(2,1)S(1)}, u32[]{:S(2)}, u32[]{:S(2)}) async-start(bf16[16,48,896]{2,1,0:T(8,128)(2,1)} %late.1.refs_4_), calls=%async_computation.3 | async-start | bytes 2752512 | tf_op jit(solution)/shard_map/all_to_all | solution.py:99
  130.0 14.1 %collective-permute-start.10 = (bf16[192,768]{1,0:T(8,128)(2,1)}, bf16[192,768]{1,0:T(8,128)(2,1)S(1)}, u32[]{:S(2)}, u32[]{:S(2)}) collective-permute-start(bf16[192,768]{1,0:T(8,128)(2,1)} %part.1), channel_id=1, source_target_pairs={{0,32},{1,3},{2,34},{3,5},{4,36},{5,7},{6,38},{7,1},{8,40},{9,11},... | collective-permute-start | bytes 884744 | tf_op jit(solution)/shard_map/ppermute | solution.py:103
  131.7 12.5 %collective-permute-start.11 = (bf16[192,768]{1,0:T(8,128)(2,1)}, bf16[192,768]{1,0:T(8,128)(2,1)S(1)}, u32[]{:S(2)}, u32[]{:S(2)}) collective-permute-start(bf16[192,768]{1,0:T(8,128)(2,1)} %part.1), channel_id=1, source_target_pairs={{0,96},{1,7},{2,98},{3,1},{4,100},{5,3},{6,102},{7,5},{8,104},{9,1... | collective-permute-start | bytes 884744 | tf_op jit(solution)/shard_map/ppermute | solution.py:103
  132.9 11.3 %collective-permute-start.12 = (bf16[192,768]{1,0:T(8,128)(2,1)}, bf16[192,768]{1,0:T(8,128)(2,1)S(1)}, u32[]{:S(2)}, u32[]{:S(2)}) collective-permute-start(bf16[192,768]{1,0:T(8,128)(2,1)} %part.1), channel_id=1, source_target_pairs={{0,64},{1,5},{2,66},{3,7},{4,68},{5,1},{6,70},{7,3},{8,72},{9,13},... | collective-permute-start | bytes 884744 | tf_op jit(solution)/shard_map/ppermute | solution.py:103
  144.2 4.4 %copy-start.9 = (bf16[192,768]{1,0:T(8,128)(2,1)}, bf16[192,768]{1,0:T(8,128)(2,1)S(1)}, u32[]{:S(2)}) copy-start(bf16[192,768]{1,0:T(8,128)(2,1)S(1)} %collective-permute-done.10.refs_1_) | copy-start | bytes 884740
  144.2 4.4 %copy-start.10 = (bf16[192,768]{1,0:T(8,128)(2,1)}, bf16[192,768]{1,0:T(8,128)(2,1)S(1)}, u32[]{:S(2)}) copy-start(bf16[192,768]{1,0:T(8,128)(2,1)S(1)} %collective-permute-done.11.refs_2_) | copy-start | bytes 884740
  144.2 4.4 %copy-start.11 = (bf16[192,768]{1,0:T(8,128)(2,1)}, bf16[192,768]{1,0:T(8,128)(2,1)S(1)}, u32[]{:S(2)}) copy-start(bf16[192,768]{1,0:T(8,128)(2,1)S(1)} %collective-permute-done.12.refs_3_) | copy-start | bytes 884740
  145.5 15.3 %copy-start.13 = (bf16[192,768]{1,0:T(8,128)(2,1)}, bf16[192,768]{1,0:T(8,128)(2,1)S(1)}, u32[]{:S(2)}) copy-start(bf16[192,768]{1,0:T(8,128)(2,1)S(1)} %add_convert_fusion.refs_1_) | copy-start | bytes 884740
  145.5 10.2 %collective-permute-start.16 = (bf16[192,768]{1,0:T(8,128)(2,1)S(1)}, bf16[192,768]{1,0:T(8,128)(2,1)S(1)}, u32[]{:S(2)}, u32[]{:S(2)}) collective-permute-start(bf16[192,768]{1,0:T(8,128)(2,1)S(1)} %add_convert_fusion.refs_1_), channel_id=1, source_target_pairs={{0,8},{1,33},{2,10},{3,35},{4,12},{5,37},{6,14},{7,39},{8,16},{9,4... | collective-permute-start | bytes 884744 | tf_op jit(solution)/shard_map/ppermute | solution.py:103
  145.8 9.9 %collective-permute-start.17 = (bf16[192,768]{1,0:T(8,128)(2,1)S(1)}, bf16[192,768]{1,0:T(8,128)(2,1)S(1)}, u32[]{:S(2)}, u32[]{:S(2)}) collective-permute-start(bf16[192,768]{1,0:T(8,128)(2,1)S(1)} %add_convert_fusion.refs_1_), channel_id=1, source_target_pairs={{0,24},{1,97},{2,26},{3,99},{4,28},{5,101},{6,30},{7,103},{8,0},{9... | collective-permute-start | bytes 884744 | tf_op jit(solution)/shard_map/ppermute | solution.py:103
  148.5 7.3 %collective-permute-start.18 = (bf16[192,768]{1,0:T(8,128)(2,1)S(1)}, bf16[192,768]{1,0:T(8,128)(2,1)}, u32[]{:S(2)}, u32[]{:S(2)}) collective-permute-start(bf16[192,768]{1,0:T(8,128)(2,1)S(1)} %add_convert_fusion.refs_1_), channel_id=1, source_target_pairs={{0,16},{1,65},{2,18},{3,67},{4,20},{5,69},{6,22},{7,71},{8,24},{9,... | collective-permute-start | bytes 884744 | tf_op jit(solution)/shard_map/ppermute | solution.py:103
  151.8 5.2 %collective-permute-start.13 = (bf16[48,896]{1,0:T(8,128)(2,1)}, bf16[48,896]{1,0:T(8,128)(2,1)S(1)}, u32[]{:S(2)}, u32[]{:S(2)}) collective-permute-start(bf16[48,896]{1,0:T(8,128)(2,1)} %strip.1.refs_0_), channel_id=1, source_target_pairs={{0,32},{1,3},{2,34},{3,5},{4,36},{5,7},{6,38},{7,1},{8,40},{9,11},... | collective-permute-start | bytes 258056 | tf_op jit(solution)/shard_map/ppermute | solution.py:103
  153.6 3.9 %collective-permute-start.14 = (bf16[48,896]{1,0:T(8,128)(2,1)}, bf16[48,896]{1,0:T(8,128)(2,1)S(1)}, u32[]{:S(2)}, u32[]{:S(2)}) collective-permute-start(bf16[48,896]{1,0:T(8,128)(2,1)} %strip.1.refs_0_), channel_id=1, source_target_pairs={{0,96},{1,7},{2,98},{3,1},{4,100},{5,3},{6,102},{7,5},{8,104},{9,1... | collective-permute-start | bytes 258056 | tf_op jit(solution)/shard_map/ppermute | solution.py:103
  155.8 5.1 %copy-start.20 = (bf16[192,768]{1,0:T(8,128)(2,1)}, bf16[192,768]{1,0:T(8,128)(2,1)S(1)}, u32[]{:S(2)}) copy-start(bf16[192,768]{1,0:T(8,128)(2,1)S(1)} %collective-permute-done.16.refs_2_) | copy-start | bytes 884740
  155.8 5.1 %collective-permute-start.15 = (bf16[48,896]{1,0:T(8,128)(2,1)}, bf16[48,896]{1,0:T(8,128)(2,1)S(1)}, u32[]{:S(2)}, u32[]{:S(2)}) collective-permute-start(bf16[48,896]{1,0:T(8,128)(2,1)} %strip.1.refs_0_), channel_id=1, source_target_pairs={{0,64},{1,5},{2,66},{3,7},{4,68},{5,1},{6,70},{7,3},{8,72},{9,13},... | collective-permute-start | bytes 258056 | tf_op jit(solution)/shard_map/ppermute | solution.py:103
  155.8 5.0 %copy-start.21 = (bf16[192,768]{1,0:T(8,128)(2,1)}, bf16[192,768]{1,0:T(8,128)(2,1)S(1)}, u32[]{:S(2)}) copy-start(bf16[192,768]{1,0:T(8,128)(2,1)S(1)} %collective-permute-done.17.refs_3_) | copy-start | bytes 884740
  156.9 3.9 %copy-start.17 = (bf16[48,896]{1,0:T(8,128)(2,1)}, bf16[48,896]{1,0:T(8,128)(2,1)S(1)}, u32[]{:S(2)}) copy-start(bf16[48,896]{1,0:T(8,128)(2,1)S(1)} %collective-permute-done.13.refs_5_.refs_1_) | copy-start | bytes 258052
  157.6 3.3 %copy-start.18 = (bf16[48,896]{1,0:T(8,128)(2,1)}, bf16[48,896]{1,0:T(8,128)(2,1)S(1)}, u32[]{:S(2)}) copy-start(bf16[48,896]{1,0:T(8,128)(2,1)S(1)} %collective-permute-done.14.refs_6_.refs_2_) | copy-start | bytes 258052
  163.8 7.4 %collective-permute-start.19 = (bf16[768,768]{1,0:T(8,128)(2,1)}, bf16[768,768]{1,0:T(8,128)(2,1)S(1)}, u32[]{:S(2)}, u32[]{:S(2)}) collective-permute-start(bf16[768,768]{1,0:T(8,128)(2,1)} %join.1.own_ref), channel_id=1, source_target_pairs={{0,1},{1,0},{2,3},{3,2},{4,5},{5,4},{6,7},{7,6},{8,9},{9,8},{10,11... | collective-permute-start | bytes 3538952 | tf_op jit(solution)/shard_map/ppermute | solution.py:107
  168.6 16.9 %collective-permute-start.23 = (bf16[768,768]{1,0:T(8,128)(2,1)}, bf16[768,768]{1,0:T(8,128)(2,1)}, u32[]{:S(2)}, u32[]{:S(2)}) collective-permute-start(bf16[768,768]{1,0:T(8,128)(2,1)} %join.1.own_ref), channel_id=1, source_target_pairs={{0,2},{1,9},{2,4},{3,11},{4,6},{5,13},{6,0},{7,15},{8,10},{9,17},{... | collective-permute-start | bytes 3538952 | tf_op jit(solution)/shard_map/ppermute | solution.py:103
  168.9 18.7 %collective-permute-start.21 = (bf16[768,768]{1,0:T(8,128)(2,1)}, bf16[768,768]{1,0:T(8,128)(2,1)}, u32[]{:S(2)}, u32[]{:S(2)}) collective-permute-start(bf16[768,768]{1,0:T(8,128)(2,1)} %join.1.own_ref), channel_id=1, source_target_pairs={{0,6},{1,25},{2,0},{3,27},{4,2},{5,29},{6,4},{7,31},{8,14},{9,1},{... | collective-permute-start | bytes 3538952 | tf_op jit(solution)/shard_map/ppermute | solution.py:103
  177.2 1.4 collective-permute-start.20
  181.3 20.1 %all-to-all-start.4 = ((bf16[16,48,896]{2,1,0:T(8,128)(2,1)}), bf16[16,48,896]{2,1,0:T(8,128)(2,1)S(1)}, u32[]{:S(2)}, u32[]{:S(2)}) async-start(bf16[16,48,896]{2,1,0:T(8,128)(2,1)} %copies.1.refs_0_), calls=%async_computation.4 | async-start | bytes 2752512 | tf_op jit(solution)/shard_map/all_to_all | solution.py:99
  185.5 5.4 %collective-permute-start.24 = (bf16[768,768]{1,0:T(8,128)(2,1)}, bf16[768,768]{1,0:T(8,128)(2,1)}, u32[]{:S(2)}, u32[]{:S(2)}) collective-permute-start(bf16[768,768]{1,0:T(8,128)(2,1)} %tie.7.own_ref), channel_id=1, source_target_pairs={{0,1},{1,0},{2,3},{3,2},{4,5},{5,4},{6,7},{7,6},{8,9},{9,8},{10,11... | collective-permute-start | bytes 3538952 | tf_op jit(solution)/shard_map/ppermute | solution.py:107
  187.6 7.5 %collective-permute-start.22 = (bf16[768,768]{1,0:T(8,128)(2,1)}, bf16[768,768]{1,0:T(8,128)(2,1)}, u32[]{:S(2)}, u32[]{:S(2)}) collective-permute-start(bf16[768,768]{1,0:T(8,128)(2,1)} %tie.6.own_ref), channel_id=1, source_target_pairs={{0,1},{1,0},{2,3},{3,2},{4,5},{5,4},{6,7},{7,6},{8,9},{9,8},{10,11... | collective-permute-start | bytes 3538952 | tf_op jit(solution)/shard_map/ppermute | solution.py:107
  187.7 30.1 %collective-permute-start.27 = (bf16[768,768]{1,0:T(8,128)(2,1)}, bf16[768,768]{1,0:T(8,128)(2,1)}, u32[]{:S(2)}, u32[]{:S(2)}) collective-permute-start(bf16[768,768]{1,0:T(8,128)(2,1)} %join.1.own_ref), channel_id=1, source_target_pairs={{0,4},{1,17},{2,6},{3,19},{4,0},{5,21},{6,2},{7,23},{8,12},{9,25},... | collective-permute-start | bytes 3538952 | tf_op jit(solution)/shard_map/ppermute | solution.py:103
  200.0 1.5 collective-permute-start.25
  203.2 22.0 %collective-permute-start.26 = (bf16[16,48,896]{2,1,0:T(8,128)(2,1)}, bf16[16,48,896]{2,1,0:T(8,128)(2,1)S(1)}, u32[]{:S(2)}, u32[]{:S(2)}) collective-permute-start(bf16[16,48,896]{2,1,0:T(8,128)(2,1)} %tie.8.refs_1_), channel_id=1, source_target_pairs={{0,1},{1,0},{2,3},{3,2},{4,5},{5,4},{6,7},{7,6},{8,9},{9,8},{10,11... | collective-permute-start | bytes 4128776 | tf_op jit(solution)/shard_map/ppermute | solution.py:107
  217.8 3.2 %collective-permute-start.28 = (bf16[768,768]{1,0:T(8,128)(2,1)}, bf16[768,768]{1,0:T(8,128)(2,1)}, u32[]{:S(2)}, u32[]{:S(2)}) collective-permute-start(bf16[768,768]{1,0:T(8,128)(2,1)} %tie.9.own_ref), channel_id=1, source_target_pairs={{0,1},{1,0},{2,3},{3,2},{4,5},{5,4},{6,7},{7,6},{8,9},{9,8},{10,11... | collective-permute-start | bytes 3538952 | tf_op jit(solution)/shard_map/ppermute | solution.py:107
  (17 other events, 14.5 us)
